TPU v7x, 32 devices: a whole 2x2x4 slice. The times are simulated.
32 devices in a mesh: member: 2 (over x), patch: 8 (over z, y), feat: 2 (over core).
Axes of the slice: x: 2, y: 2, z: 4, core: 2. Of those that a mesh axis runs over, the one named last changes fastest.
Arguments:
- node_latent: bfloat16 [10240, 512], P(('member', 'patch')), parts along dimension 0, may hold values from -6 to 6
- edge_latent: bfloat16 [65536, 512], P(('member', 'patch')), parts along dimension 0, may hold values from -6 to 6
- edge_senders: int32 [65536], P(('member', 'patch')), parts along dimension 0, may hold values from 0 to 1151
- edge_receivers: int32 [65536], P(('member', 'patch')), parts along dimension 0, may hold values from 0 to 1151
- halo_rows: int32 [32, 128], P(('member', 'patch')), parts along dimension 0, may hold values from 0 to 639
- coarse_rows: int32 [512], P(('member', 'patch')), parts along dimension 0, may hold values from 0 to 639
- edge_counts: int32 [16], P(('member', 'patch')), parts along dimension 0, may hold values from 1024 to 4096, as said below
- edge_w1: bfloat16 [1536, 512], P(None, 'feat'), may hold values from -0.15625 to 0.15625
- edge_w2: bfloat16 [512, 512], P('feat'), may hold values from -0.25 to 0.25
- edge_gain: bfloat16 [512], replicated, may hold values from 0.099609375 to 1.8984375
- node_w1: bfloat16 [1024, 512], P(None, 'feat'), may hold values from -0.1875 to 0.1875
- node_w2: bfloat16 [512, 512], P('feat'), may hold values from -0.25 to 0.25
- node_gain: bfloat16 [512], replicated, may hold values from 0.099609375 to 1.8984375
Outputs:
- nodes_out: bfloat16 [10240, 512], P(('member', 'patch'), 'feat'), parts along dimension 0
- edges_out: bfloat16 [65536, 512], P(('member', 'patch'), 'feat'), parts along dimension 0
There are 2 independent parts, one for each index of `member`. A program takes and returns all parts, laid end to end along the dimension named above; an argument that names none is the same for every part. Nothing has to cross between parts.
Inputs may be any that keep to these rules, and one draw needn't show every extreme that they name: `edge_counts`: every patch has at least 1024 live edges; at least one patch is full in every draw.
All inputs are finite; a program needn't handle non-finite values.
Results may differ from a plain program's by a relative error of at most 0.0055.
Values may be sent and summed in bfloat16 or wider, within the bound.
No kernel may reach another device: no remote copies, remote signals or barrier semaphores. Data moves between devices by JAX's collectives and lax.ppermute only.
A program may use at most 128 MiB of HBM per device.

v0:
```python
import jax
import jax.numpy as jnp
from jax import lax
from jax.sharding import PartitionSpec as P

EPSILON = 1e-05


def extended(block, sides, width):
    for axis, dim in sides:
        count = lax.axis_size(axis)
        forward = [(i, i + 1) for i in range(count - 1)]
        backward = [(target, source) for source, target in forward]
        low = lax.ppermute(
            lax.slice_in_dim(block, block.shape[dim] - width, None, axis=dim), axis, forward
        )
        high = lax.ppermute(lax.slice_in_dim(block, 0, width, axis=dim), axis, backward)
        block = jnp.concatenate([low, block, high], axis=dim)
    return block


def normalize(values, gain_vector):
    center = jnp.mean(values, axis=1, keepdims=True)
    square = jnp.mean(values * values, axis=1, keepdims=True)
    return (
        (values - center)
        * lax.rsqrt(square - center * center + EPSILON)
        * gain_vector.astype(jnp.float32)
    )


def normalized_share(partial_out, gain_vector):
    share_out = lax.psum_scatter(partial_out, "feat", scatter_dimension=1, tiled=True)
    columns = share_out.shape[1]
    model_width = columns * lax.axis_size("feat")
    totals = lax.psum((jnp.sum(share_out, axis=1), jnp.sum(share_out * share_out, axis=1)), "feat")
    center = totals[0][:, None] / model_width
    square = totals[1][:, None] / model_width
    gain_share = lax.dynamic_slice_in_dim(
        gain_vector, lax.axis_index("feat") * columns, columns
    ).astype(jnp.float32)
    return (share_out - center) * lax.rsqrt(square - center * center + EPSILON) * gain_share


def first_layer(latent, lookup, senders, receivers, weight):
    model_width = latent.shape[1]
    total = jnp.dot(latent, weight[:model_width], preferred_element_type=jnp.float32)
    total = total + jnp.dot(
        lookup[senders], weight[model_width : 2 * model_width], preferred_element_type=jnp.float32
    )
    return total + jnp.dot(
        lookup[receivers], weight[2 * model_width :], preferred_element_type=jnp.float32
    )


def on_device(
    node_latent,
    edge_latent,
    edge_senders,
    edge_receivers,
    halo_rows,
    coarse_rows,
    edge_counts,
    edge_w1,
    edge_w2,
    edge_gain,
    node_w1,
    node_w2,
    node_gain,
):
    node_count, model_width = node_latent.shape
    halo_count = halo_rows.shape[1]
    edge_count = edge_latent.shape[0]
    feat_ways = lax.axis_size("feat")
    column_share = model_width // feat_ways
    position = lax.axis_index("feat")
    outgoing = jnp.concatenate([node_latent[halo_rows[1]], node_latent[halo_rows[0]]], axis=0)
    widened = extended(outgoing, (("patch", 0),), halo_count)
    coarse_all = lax.all_gather(node_latent[coarse_rows], "patch", axis=0, tiled=True)
    lookup = jnp.concatenate(
        [node_latent, widened[:halo_count], widened[3 * halo_count :], coarse_all], axis=0
    )
    slot_count = lookup.shape[0]
    live_limit = edge_counts[0]
    row_share = edge_count // feat_ways
    row_start = position * row_share
    latent_rows = lax.dynamic_slice_in_dim(edge_latent, row_start, row_share, 0)
    sender_rows = lax.dynamic_slice_in_dim(edge_senders, row_start, row_share, 0)
    receiver_rows = lax.dynamic_slice_in_dim(edge_receivers, row_start, row_share, 0)
    weight_in, weight_out = (
        lax.all_gather(edge_w1, "feat", axis=1, tiled=True),
        lax.all_gather(edge_w2, "feat", axis=0, tiled=True),
    )
    hidden = jax.nn.silu(
        first_layer(latent_rows, lookup, sender_rows, receiver_rows, weight_in)
    ).astype(jnp.bfloat16)
    update = normalize(jnp.dot(hidden, weight_out, preferred_element_type=jnp.float32), edge_gain)
    live_rows = row_start + jnp.arange(row_share) < live_limit
    before = latent_rows.astype(jnp.float32)
    fresh_rows = jnp.where(live_rows[:, None], before + update, before).astype(jnp.bfloat16)
    fresh_edges = lax.all_to_all(fresh_rows, "feat", split_axis=1, concat_axis=0, tiled=True)
    live_all = jnp.arange(edge_count) < live_limit
    message = jnp.where(live_all[:, None], fresh_edges, jnp.zeros_like(fresh_edges)).astype(
        jnp.float32
    )
    target = jnp.where(live_all, edge_receivers, slot_count)
    summed = jax.ops.segment_sum(message, target, num_segments=slot_count + 1)[:slot_count]
    returned = extended(
        summed[node_count : node_count + 2 * halo_count].astype(jnp.bfloat16),
        (("patch", 0),),
        halo_count,
    ).astype(jnp.float32)
    coarse_back = lax.psum_scatter(
        summed[node_count + 2 * halo_count :].astype(jnp.bfloat16),
        "patch",
        scatter_dimension=0,
        tiled=True,
    ).astype(jnp.float32)
    gathered = summed[:node_count].at[halo_rows[0]].add(returned[3 * halo_count :])
    gathered = gathered.at[halo_rows[1]].add(returned[:halo_count]).at[coarse_rows].add(coarse_back)
    message_sum = lax.all_gather(gathered.astype(jnp.bfloat16), "feat", axis=1, tiled=True)
    pre_active = jnp.dot(node_latent, node_w1[:model_width], preferred_element_type=jnp.float32)
    pre_active = pre_active + jnp.dot(
        message_sum, node_w1[model_width:], preferred_element_type=jnp.float32
    )
    hidden_nodes = jax.nn.silu(pre_active).astype(jnp.bfloat16)
    update_nodes = normalized_share(
        jnp.dot(hidden_nodes, node_w2, preferred_element_type=jnp.float32), node_gain
    )
    own_columns = lax.dynamic_slice_in_dim(
        node_latent, position * column_share, column_share, 1
    ).astype(jnp.float32)
    return ((own_columns + update_nodes).astype(jnp.bfloat16), fresh_edges)


def solution(mesh):
    placed = (
        P(("member", "patch"), None),
        P(("member", "patch"), None),
        P(("member", "patch")),
        P(("member", "patch")),
        P(("member", "patch"), None),
        P(("member", "patch")),
        P(("member", "patch")),
        P(None, "feat"),
        P("feat", None),
        P(),
        P(None, "feat"),
        P("feat", None),
        P(),
    )
    return jax.shard_map(
        on_device,
        mesh=mesh,
        in_specs=placed,
        out_specs=(P(("member", "patch"), "feat"), P(("member", "patch"), "feat")),
        check_vma=False,
    )
```

profile of v0, /device:TPU:0, one launch (start us, length us, event | category | flops | bytes accessed | tf_op | source)
XLA Modules:
  0.0 241.3 jit_solution(15873917387522191220)
XLA Ops:
  8.1 2.0 gather_fusion
  10.1 5.0 %collective-permute-start = (bf16[128,512]{1,0:T(8,128)(2,1)S(1)}, bf16[128,512]{1,0:T(8,128)(2,1)S(1)}, u32[]{:S(2)}, u32[]{:S(2)}) collective-permute-start(bf16[128,512]{1,0:T(8,128)(2,1)S(1)} %gather_fusion), channel_id=1, source_target_pairs={{0,2},{2,4},{4,6},{6,8},{8,10},{10,12},{12,14},{1,3},{3,5},{5,7},{... | collective-permute-start | bytes 393224 | tf_op jit(solution)/shard_map/ppermute | solution.py:14
  15.2 2.0 gather_fusion.1
  17.2 1.3 collective-permute-start.1
  21.2 33.1 %all-gather = bf16[256,512]{1,0:T(8,128)(2,1)S(1)} all-gather(bf16[32,512]{1,0:T(8,128)(2,1)S(1)} %gather_fusion.2), channel_id=2, replica_groups=mesh['member'=2,'patch'=8,'feat'=2] {'patch'}, dimensions={0}, use_global_device_ids=true | all-gather | bytes 294912 | tf_op jit(solution)/shard_map/all_gather | solution.py:79
  54.3 2.2 all_gather.14
  57.1 3.0 %constant_dynamic-slice_fusion = bf16[2048,512]{1,0:T(8,128)(2,1)} fusion(bf16[4096,512]{1,0:T(8,128)(2,1)} %param.14, s32[]{:T(128)S(6)} %select_n.55), kind=kLoop, calls=%fused_computation.72 | loop fusion | bytes 4194308
  60.2 4.0 %copy.19 = bf16[2048,512]{0,1:T(8,128)(2,1)} copy(bf16[2048,512]{1,0:T(8,128)(2,1)} %constant_dynamic-slice_fusion) | data formatting | bytes 4194304
  65.7 9.2 %gather_fusion.3 = bf16[2048,512]{1,0:T(8,128)(2,1)} fusion(bf16[1152,512]{1,0:T(8,128)(2,1)S(1)} %constant_dynamic-update-slice_fusion, s32[2048]{0:T(1024)S(1)} %copy-done.8), kind=kCustom, calls=%fused_computation.3 | custom fusion | bytes 4202496 | tf_op jit(solution)/shard_map/gather | solution.py:49
  74.9 9.2 %gather_fusion.4 = bf16[2048,512]{1,0:T(8,128)(2,1)} fusion(bf16[1152,512]{1,0:T(8,128)(2,1)S(1)} %constant_dynamic-update-slice_fusion, s32[2048]{0:T(1024)S(1)} %copy-done.9), kind=kCustom, calls=%fused_computation.4 | custom fusion | bytes 4202496 | tf_op jit(solution)/shard_map/gather | solution.py:52
  84.1 5.1 %fusion.13 = f32[2048,512]{1,0:T(8,128)} fusion(bf16[2048,512]{1,0:T(8,128)(2,1)} %constant_dynamic-slice_fusion, bf16[1536,512]{1,0:T(8,128)(2,1)} %all-gather.3.cloned.1.call-done), kind=kOutput, calls=%fused_computation.28 | convolution fusion | flops 1073741824 | bytes 6815744 | tf_op jit(solution)/shard_map/dot_general | solution.py:47
  89.1 4.3 %fusion.11 = f32[2048,512]{1,0:T(8,128)} fusion(bf16[2048,512]{1,0:T(8,128)(2,1)S(1)} %copy-done.2, bf16[1536,512]{1,0:T(8,128)(2,1)} %all-gather.3.cloned.1.call-done), kind=kOutput, calls=%fused_computation.26 | convolution fusion | flops 1073741824 | bytes 6815744 | tf_op jit(solution)/shard_map/dot_general | solution.py:48
  93.4 9.8 %fusion.38 = (f32[2048]{0:T(1024)S(1)}, f32[2048]{0:T(1024)}, f32[2048,512]{0,1:T(8,128)}) fusion(bf16[512,512]{1,0:T(8,128)(2,1)S(1)} %all_gather.14, f32[2048,512]{1,0:T(8,128)} %fusion.13, f32[2048,512]{1,0:T(8,128)} %fusion.11, bf16[2048,512]{1,0:T(8,128)(2,1)} %gather_fusion.4, bf16[1536,512]{1,0:T(8,128)(2,1)} %all-gather.3.cloned.1.call-done), kind=kOutput, calls=%fused_computation.75 | convolution fusion | flops 2157965312 | bytes 15745024 | tf_op jit(solution)/shard_map/dot_general | solution.py:97
  103.9 3.3 %fusion = bf16[2048,512]{0,1:T(8,128)(2,1)S(1)} fusion(f32[2048,512]{0,1:T(8,128)} %get-tuple-element.18, bf16[2048,512]{0,1:T(8,128)(2,1)S(1)} %copy-done.4, f32[512]{0:T(512)} %convert_element_type.41, f32[2048]{0:T(1024)S(1)} %get-tuple-element.13, f32[2048]{0:T(1024)S(1)} %get-tuple-element.12, pred[2048]{0:T(1024)(128)(4,1)S(1)} %add_compare_fusion), kind=kLoop, calls=%fused_computation.10 | loop fusion | flops 7340032 | bytes 8409088 | tf_op jit(solution)/shard_map/convert_element_type | solution.py:100
  107.2 6.3 %all_to_all.19 = bf16[2048,2,256]{0,2,1:T(8,128)(2,1)} all-to-all(bf16[2048,2,256]{0,2,1:T(8,128)(2,1)S(1)} %bitcast.25), channel_id=1, replica_groups=mesh['member'=2,'patch'=8,'feat'=2] {'feat'}, dimensions={1} | all-to-all | bytes 4194304 | tf_op jit(solution)/shard_map/all_to_all | solution.py:101
  113.5 2.8 %copy.18 = bf16[2,2048,256]{2,1,0:T(8,128)(2,1)S(1)} copy(bf16[2,2048,256]{1,2,0:T(8,128)(2,1)} %bitcast.24) | data formatting | bytes 4194304 | tf_op jit(solution)/shard_map/all_to_all | solution.py:101
  116.4 26.1 %scatter_custom_fusion = f32[1153,256]{1,0:T(8,128)} fusion(s32[4096]{0:T(1024)} %broadcast_select_fusion, bf16[4096,256]{1,0:T(8,128)(2,1)S(1)} %bitcast.22, pred[4096]{0:T(1024)(128)(4,1)S(1)} %iota_compare_fusion, bf16[]{:T(256)} %constant.9.clone.1, f32[]{:T(128)} %constant.17.clone.1), kind=kCustom, calls=%fused_computation.11 | custom fusion | flops 3145728 | bytes 3282944 | tf_op jit(solution)/shard_map/scatter-add | solution.py:107
  142.5 1.3 convert.4
  144.5 7.6 %collective-permute-start.2 = (bf16[128,256]{1,0:T(8,128)(2,1)S(1)}, bf16[128,256]{1,0:T(8,128)(2,1)S(1)}, u32[]{:S(2)}, u32[]{:S(2)}) collective-permute-start(bf16[128,256]{1,0:T(8,128)(2,1)S(1)} %get-tuple-element.10), channel_id=1, source_target_pairs={{0,2},{2,4},{4,6},{6,8},{8,10},{10,12},{12,14},{1,3},{3,5},{5,7},{... | collective-permute-start | bytes 196616 | tf_op jit(solution)/shard_map/ppermute | solution.py:14
  152.1 1.3 collective-permute-start.3
  153.5 1.3 fusion.18
  154.8 3.5 %collective-permute-done.3 = bf16[128,256]{1,0:T(8,128)(2,1)S(1)} collective-permute-done((bf16[128,256]{1,0:T(8,128)(2,1)S(1)}, bf16[128,256]{1,0:T(8,128)(2,1)S(1)}, u32[]{:S(2)}, u32[]{:S(2)}) %collective-permute-start.3) | collective-permute-done | bytes 65568 | tf_op jit(solution)/shard_map/ppermute | solution.py:17
  158.3 1.8 scatter_custom_fusion.1
  160.1 1.7 scatter_custom_fusion.2
  161.8 53.7 %reduce-scatter.3.cloned.1.call-done = bf16[32,256]{1,0:T(8,128)(2,1)} async-done(((bf16[256,256]{1,0:T(8,128)(2,1)}), bf16[32,256]{1,0:T(8,128)(2,1)}) %reduce-scatter.3.cloned.1.call-update) | async-done | bytes 16400 | tf_op jit(solution)/shard_map/reduce_scatter | solution.py:113
  215.5 1.2 scatter_custom_fusion.3
  216.8 2.3 all_gather.15
  219.0 1.9 fusion.7
  221.0 7.9 %reduce-scatter.5.cloned.1.call-done = f32[640,256]{1,0:T(8,128)} async-done(((f32[640,512]{1,0:T(8,128)}), f32[640,256]{1,0:T(8,128)}) %reduce-scatter.5.cloned.1.call-update) | async-done | bytes 655376 | tf_op jit(solution)/shard_map/reduce_scatter | solution.py:33
  228.9 1.3 fusion.39
  230.2 2.5 %all-reduce = (f32[640]{0:T(1024)S(1)}, f32[640]{0:T(1024)S(1)}) all-reduce(f32[640]{0:T(1024)S(1)} %get-tuple-element.5, f32[640]{0:T(1024)S(1)} %get-tuple-element.4), channel_id=1, replica_groups=mesh['member'=2,'patch'=8,'feat'=2] {'feat'}, use_global_device_ids=true, to_apply=%region_11.12 | all-reduce | flops 1280 | bytes 10240 | tf_op jit(solution)/shard_map/psum | solution.py:36
  232.7 2.1 add_convert_fusion
  (68 shorter events, 6.6 us)
Async XLA Ops:
  7.2 211.9 %copy-start = (bf16[256,512]{1,0:T(8,128)(2,1)S(1)}, bf16[256,512]{1,0:T(8,128)(2,1)}, u32[]{:S(2)}) copy-start(bf16[256,512]{1,0:T(8,128)(2,1)} %param.24) | copy-start | bytes 786436
  7.2 12.1 %copy-start.1 = (bf16[640,512]{1,0:T(8,128)(2,1)S(1)}, bf16[640,512]{1,0:T(8,128)(2,1)}, u32[]{:S(2)}) copy-start(bf16[640,512]{1,0:T(8,128)(2,1)} %param.13) | copy-start | bytes 1966084
  7.2 11.4 %copy-start.16 = (s32[32]{0:T(128)S(1)}, s32[32]{0:T(128)}, u32[]{:S(2)}) copy-start(s32[32]{0:T(128)} %param.18) | copy-start | bytes 388
  7.2 11.4 %copy-start.10 = (s32[4096]{0:T(1024)S(1)}, s32[4096]{0:T(1024)}, u32[]{:S(2)}) copy-start(s32[4096]{0:T(1024)} %param.15) | copy-start | bytes 49156
  7.2 13.3 %copy-start.7 = (s32[4096]{0:T(1024)S(1)}, s32[4096]{0:T(1024)}, u32[]{:S(2)}) copy-start(s32[4096]{0:T(1024)} %param.16) | copy-start | bytes 49156
  7.2 76.8 %all-gather.3.cloned.1.call-start = ((), (), s32[]{:S(2)}) async-start(), calls=%async_computation.3 | async-start | bytes 2359296 | tf_op jit(solution)/shard_map/all_gather | solution.py:91
  8.0 7.1 %copy-start.11 = (s32[128]{0:T(128)}, s32[128]{0:T(128)S(1)}, u32[]{:S(2)}) copy-start(s32[128]{0:T(128)S(1)} %get-tuple-element.16) | copy-start | bytes 1540
  8.0 7.1 %copy-start.12 = (s32[128]{0:T(128)}, s32[128]{0:T(128)S(1)}, u32[]{:S(2)}) copy-start(s32[128]{0:T(128)S(1)} %get-tuple-element.17) | copy-start | bytes 1540
  10.1 44.2 %copy-start.5 = (bf16[256,512]{1,0:T(8,128)(2,1)S(1)}, bf16[256,512]{1,0:T(8,128)(2,1)}, u32[]{:S(2)}) copy-start(bf16[256,512]{1,0:T(8,128)(2,1)} %param.21) | copy-start | bytes 786436
  10.1 54.6 %collective-permute-start = (bf16[128,512]{1,0:T(8,128)(2,1)S(1)}, bf16[128,512]{1,0:T(8,128)(2,1)S(1)}, u32[]{:S(2)}, u32[]{:S(2)}) collective-permute-start(bf16[128,512]{1,0:T(8,128)(2,1)S(1)} %gather_fusion), channel_id=1, source_target_pairs={{0,2},{2,4},{4,6},{6,8},{8,10},{10,12},{12,14},{1,3},{3,5},{5,7},{... | collective-permute-start | bytes 393224 | tf_op jit(solution)/shard_map/ppermute | solution.py:14
  17.2 47.5 %collective-permute-start.1 = (bf16[128,512]{1,0:T(8,128)(2,1)S(1)}, bf16[128,512]{1,0:T(8,128)(2,1)}, u32[]{:S(2)}, u32[]{:S(2)}) collective-permute-start(bf16[128,512]{1,0:T(8,128)(2,1)S(1)} %gather_fusion.1), channel_id=1, source_target_pairs={{2,0},{4,2},{6,4},{8,6},{10,8},{12,10},{14,12},{3,1},{5,3},{7,5},{... | collective-permute-start | bytes 393224 | tf_op jit(solution)/shard_map/ppermute | solution.py:17
  18.5 197.0 %reduce-scatter.3.cloned.1.call-start = ((), (), s32[]{:S(2)}) async-start(), calls=%async_computation.4 | async-start | bytes 147456 | tf_op jit(solution)/shard_map/reduce_scatter | solution.py:113
  18.6 35.6 %copy-start.14 = (s32[32]{0:T(128)}, s32[32]{0:T(128)S(1)}, u32[]{:S(2)}) copy-start(s32[32]{0:T(128)S(1)} %compare_select_fusion.2) | copy-start | bytes 388
  60.2 4.0 %copy-start.13 = (bf16[512]{0:T(512)(128)(2,1)S(1)}, bf16[512]{0:T(512)(128)(2,1)}, u32[]{:S(2)}) copy-start(bf16[512]{0:T(512)(128)(2,1)} %param.22) | copy-start | bytes 3076
  60.2 5.5 %copy-start.8 = (s32[2048]{0:T(1024)S(1)}, s32[2048]{0:T(1024)}, u32[]{:S(2)}) copy-start(s32[2048]{0:T(1024)} %fusion.32) | copy-start | bytes 24580
  65.7 9.2 %copy-start.9 = (s32[2048]{0:T(1024)S(1)}, s32[2048]{0:T(1024)}, u32[]{:S(2)}) copy-start(s32[2048]{0:T(1024)} %fusion.33) | copy-start | bytes 24580
  84.1 5.1 %copy-start.2 = (bf16[2048,512]{1,0:T(8,128)(2,1)S(1)}, bf16[2048,512]{1,0:T(8,128)(2,1)}, u32[]{:S(2)}) copy-start(bf16[2048,512]{1,0:T(8,128)(2,1)} %gather_fusion.3) | copy-start | bytes 6291460
  93.4 10.5 %copy-start.4 = (bf16[2048,512]{0,1:T(8,128)(2,1)S(1)}, bf16[2048,512]{0,1:T(8,128)(2,1)}, u32[]{:S(2)}) copy-start(bf16[2048,512]{0,1:T(8,128)(2,1)} %copy.19) | copy-start | bytes 6291460
  116.4 27.5 %copy-start.3 = (bf16[2,2048,256]{2,1,0:T(8,128)(2,1)}, bf16[2,2048,256]{2,1,0:T(8,128)(2,1)S(1)}, u32[]{:S(2)}) copy-start(bf16[2,2048,256]{2,1,0:T(8,128)(2,1)S(1)} %copy.18) | copy-start | bytes 6291460
  144.5 13.8 %slice-start = ((f32[1153,256]{1,0:T(8,128)}), f32[640,256]{1,0:T(8,128)S(1)}, s32[]{:S(2)}) async-start(f32[1153,256]{1,0:T(8,128)} %scatter_custom_fusion), calls=%async_computation.6 | async-start | bytes 1310720 | tf_op jit(solution)/shard_map/slice | solution.py:119
  144.5 10.3 %collective-permute-start.2 = (bf16[128,256]{1,0:T(8,128)(2,1)S(1)}, bf16[128,256]{1,0:T(8,128)(2,1)S(1)}, u32[]{:S(2)}, u32[]{:S(2)}) collective-permute-start(bf16[128,256]{1,0:T(8,128)(2,1)S(1)} %get-tuple-element.10), channel_id=1, source_target_pairs={{0,2},{2,4},{4,6},{6,8},{8,10},{10,12},{12,14},{1,3},{3,5},{5,7},{... | collective-permute-start | bytes 196616 | tf_op jit(solution)/shard_map/ppermute | solution.py:14
  152.1 6.2 %collective-permute-start.3 = (bf16[128,256]{1,0:T(8,128)(2,1)S(1)}, bf16[128,256]{1,0:T(8,128)(2,1)S(1)}, u32[]{:S(2)}, u32[]{:S(2)}) collective-permute-start(bf16[128,256]{1,0:T(8,128)(2,1)S(1)} %get-tuple-element.11), channel_id=1, source_target_pairs={{2,0},{4,2},{6,4},{8,6},{10,8},{12,10},{14,12},{3,1},{5,3},{7,5},{... | collective-permute-start | bytes 196616 | tf_op jit(solution)/shard_map/ppermute | solution.py:17
  153.5 75.4 %reduce-scatter.5.cloned.1.call-start = ((), (), s32[]{:S(2)}) async-start(), calls=%async_computation.5 | async-start | bytes 1966080 | tf_op jit(solution)/shard_map/reduce_scatter | solution.py:33
  158.3 60.8 %copy-start.6 = (bf16[1024,256]{1,0:T(8,128)(2,1)S(1)}, bf16[1024,256]{1,0:T(8,128)(2,1)}, u32[]{:S(2)}) copy-start(bf16[1024,256]{1,0:T(8,128)(2,1)} %param.23) | copy-start | bytes 1572868
  219.0 1.9 copy-start.15
Sparse Core Ops, SparseCore 0:
  18.7 12.6 all-gather.2
  153.6 61.8 reduce-scatter.2
  221.1 7.7 reduce-scatter.4
where the time goes:
time: 242 us; the launch traced here: 241 us
  waiting for transfers between devices  65.1 us (27%)
  blocking collectives  46.3 us (19%)
  other arithmetic  42.9 us (18%)
  local copies, waits for them, and re-layouts  34.7 us (14%)
  matrix products  22.3 us (9%)
  starting transfers between devices  15.3 us (6%)
  between operations  14.7 us (6%)
    reduce_scatter x1, waiting for transfers between devices, on_device(): lax.psum_scatter(summed[node_count + 2 * halo_count:].astype(jnp.bfloat16...  53.7 us
    all_gather x1, blocking collectives, on_device(): lax.all_gather(node_latent[coarse_rows], 'patch', axis=0, tiled=True)  33.1 us
    scatter-add x1, other arithmetic, on_device(): jax.ops.segment_sum(message, target, num_segments=slot_count + 1)  26.1 us
    ppermute x2, starting transfers between devices, extended(): lax.ppermute(lax.slice_in_dim(block, block.shape[dim] - width, None, axis...  12.6 us
    dot_general x1, matrix products, on_device(): jnp.dot(hidden, weight_out, preferred_element_type=jnp.float32)  9.81 us
    gather x1, local copies, waits for them, and re-layouts, first_layer(): lookup[senders]  9.19 us
    gather x1, local copies, waits for them, and re-layouts, first_layer(): lookup[receivers]  9.16 us
    unnamed x39, local copies, waits for them, and re-layouts  8.05 us
  transfers between devices with their start and end apart: 7, of which 3 were waited for; matrix products, arithmetic and copies ran while one was open for 15% of the time, Pallas kernels for 0%

commit v1 on v0

v1 whole, which is shorter than its diff:
```python
import functools

import jax
import jax.numpy as jnp
from jax import lax
from jax.experimental import pallas as pl
from jax.experimental.pallas import tpu as pltpu
from jax.sharding import PartitionSpec as P

EPSILON = 1e-05
F32 = jnp.float32
BF16 = jnp.bfloat16
MIB = 1024 * 1024
FEAT_SWAP = [(0, 1), (1, 0)]


def silu(v):
    return 0.5 * v * (1.0 + jnp.tanh(0.5 * v))


def dot(a, b):
    return jnp.dot(a, b, preferred_element_type=F32)


def layer_norm(pre, gain):
    width = pre.shape[1]
    center = jnp.sum(pre, axis=1, keepdims=True) / width
    square = jnp.sum(pre * pre, axis=1, keepdims=True) / width
    return (pre - center) * lax.rsqrt(square - center * center + EPSILON) * gain


def one_hot_rows(index_row, first, count):
    entries = index_row.shape[1]
    column = jnp.transpose(jnp.broadcast_to(index_row, (128, entries))) - first
    lanes = lax.broadcasted_iota(jnp.int32, (entries, 128), 1)
    return jnp.concatenate(
        [(column == lanes + 128 * j).astype(F32).astype(BF16) for j in range(count // 128)], axis=1
    )


def one_hot_columns(index_row, first, count):
    entries = index_row.shape[1]
    rows = lax.broadcasted_iota(jnp.int32, (count, entries), 0) + first
    return (rows == jnp.broadcast_to(index_row, (count, entries))).astype(F32).astype(BF16)


def lend_kernel(feat_ref, node_ref, halo_ref, coarse_ref, out_ref):
    node_count = node_ref.shape[0]
    halo = jnp.where(feat_ref[0] == 0, halo_ref[0:1, :], halo_ref[1:2, :])
    index_row = jnp.concatenate([halo, coarse_ref[...]], axis=1)
    picks = one_hot_columns(index_row, 0, node_count)
    out_ref[...] = lax.dot_general(
        picks, node_ref[...], (((0,), (0,)), ((), ())), preferred_element_type=F32
    ).astype(BF16)


def local_kernel(
    feat_ref, node_ref, lent_ref, wa_ref, wb_ref, latent_ref, index_ref, out_ref, table, local_slots, coarse
):
    node_count, width = node_ref.shape
    half = wa_ref.shape[1]
    halves = ((wa_ref, 0), (wb_ref, half))

    @pl.when(pl.program_id(0) == 0)
    def _():
        for side in range(2):
            base = side * local_slots
            rows = slice((side + 1) * width, (side + 2) * width)
            for weight, col in halves:
                cols = slice(col, col + half)
                table[base : base + node_count, cols] = dot(node_ref[...], weight[rows, :]).astype(BF16)
                table[base + node_count : base + node_count + coarse, cols] = dot(
                    lent_ref[lent_ref.shape[0] - coarse :, :], weight[rows, :]
                ).astype(BF16)
            table[base + node_count + coarse : base + local_slots, :] = jnp.zeros(
                (local_slots - node_count - coarse, 2 * half), BF16
            )

    picks = jnp.concatenate(
        [one_hot_rows(index_ref[side : side + 1, :], 0, local_slots) for side in range(2)], axis=1
    )
    for weight, col in halves:
        cols = slice(col, col + half)
        out_ref[:, cols] = dot(latent_ref[...], weight[:width, :]) + dot(picks, table[:, cols])


def edge_kernel(
    feat_ref,
    limit_ref,
    pre_ref,
    latent_ref,
    index_ref,
    mine_ref,
    theirs_ref,
    wa_ref,
    wb_ref,
    va_ref,
    vb_ref,
    gain_ref,
    out_mine_ref,
    out_other_ref,
    group_mine_ref,
    group_other_ref,
    local_ref,
    table,
    sums,
    local_slots,
):
    step = pl.program_id(0)
    steps = pl.num_programs(0)
    block, width = latent_ref.shape
    half = wa_ref.shape[1]
    group = mine_ref.shape[0]
    used = local_ref.shape[0]
    feat = feat_ref[0]

    @pl.when(step == 0)
    def _():
        for side in range(2):
            rows = slice((side + 1) * width, (side + 2) * width)
            for weight, col in ((wa_ref, 0), (wb_ref, half)):
                cols = slice(col, col + half)
                base = side * 2 * group
                at_mine = pl.multiple_of(base + feat * group, group)
                at_theirs = pl.multiple_of(base + (1 - feat) * group, group)
                table[pl.ds(at_mine, group), cols] = dot(mine_ref[...], weight[rows, :]).astype(BF16)
                table[pl.ds(at_theirs, group), cols] = dot(theirs_ref[...], weight[rows, :]).astype(BF16)
        sums[...] = jnp.zeros_like(sums)
        local_ref[...] = jnp.zeros_like(local_ref)

    picks = jnp.concatenate(
        [one_hot_rows(index_ref[side : side + 1, :], local_slots, 2 * group) for side in range(2)], axis=1
    )
    hidden = silu(pre_ref[...] + dot(picks, table[...])).astype(BF16)
    pre = dot(hidden[:, :half], va_ref[...]) + dot(hidden[:, half:], vb_ref[...])
    update = layer_norm(pre, gain_ref[...].astype(F32))
    before = latent_ref[...]
    row = lax.broadcasted_iota(jnp.int32, (block, 1), 0) + (feat * steps + step) * block
    fresh = jnp.where(row < limit_ref[0], before.astype(F32) + update, before.astype(F32)).astype(BF16)
    low, high = fresh[:, : width // 2], fresh[:, width // 2 :]
    out_mine_ref[...] = jnp.where(feat == 0, low, high)
    out_other_ref[...] = jnp.where(feat == 0, high, low)
    receivers = index_ref[1:2, :]
    local_ref[...] += dot(one_hot_columns(receivers, 0, used), fresh)
    sums[...] += dot(one_hot_columns(receivers, local_slots, 2 * group), fresh)

    @pl.when(step == steps - 1)
    def _():
        group_mine_ref[...] = sums[pl.ds(pl.multiple_of(feat * group, group), group), :]
        group_other_ref[...] = sums[pl.ds(pl.multiple_of((1 - feat) * group, group), group), :].astype(BF16)


def merge_kernel(mine_ref, theirs_ref, *out_refs):
    at = 0
    for out_ref in out_refs:
        rows = out_ref.shape[0]
        part = slice(at, at + rows)
        out_ref[...] = (mine_ref[part, :] + theirs_ref[part, :].astype(F32)).astype(BF16)
        at += rows


def place_kernel(feat_ref, block_ref, whole_ref, out_ref):
    out_ref[...] = block_ref[...]


def node_kernel(
    feat_ref,
    node_ref,
    halo_ref,
    coarse_ref,
    own_ref,
    partner_ref,
    mine_ref,
    theirs_ref,
    wa_ref,
    wb_ref,
    va_ref,
    vb_ref,
    gain_ref,
    out_ref,
):
    node_count, width = node_ref.shape
    half = wa_ref.shape[1]
    group = mine_ref.shape[0]
    coarse = coarse_ref.shape[1]
    feat = feat_ref[0]
    low, high = halo_ref[0:1, :], halo_ref[1:2, :]
    coarse_row = coarse_ref[...]
    repeat = (group - low.shape[1]) // coarse
    index_row = jnp.concatenate(
        [jnp.where(feat == 0, low, high)]
        + [coarse_row] * repeat
        + [jnp.where(feat == 0, high, low)]
        + [coarse_row] * (repeat + 2),
        axis=1,
    )
    returned = jnp.concatenate(
        [mine_ref[...], theirs_ref[...], own_ref[node_count:, :].astype(BF16), partner_ref[node_count:, :]], axis=0
    )
    received = (
        own_ref[:node_count, :]
        + partner_ref[:node_count, :].astype(F32)
        + dot(one_hot_columns(index_row, 0, node_count), returned)
    ).astype(BF16)
    total = None
    for weight, second in ((wa_ref, va_ref), (wb_ref, vb_ref)):
        pre = dot(node_ref[...], weight[:width, :]) + dot(received, weight[width:, :])
        part = dot(silu(pre).astype(BF16), second[...])
        total = part if total is None else total + part
    update = layer_norm(total, gain_ref[...].astype(F32))
    fresh = (node_ref[...].astype(F32) + update).astype(BF16)
    out_ref[...] = jnp.where(feat == 0, fresh[:, : width // 2], fresh[:, width // 2 :])


def whole(shape):
    return pl.BlockSpec(shape, lambda *_: (0,) * len(shape))


def call(kernel, grid, scalars, in_specs, out_specs, out_shape, operands, flops, scratch=(), aliases=None):
    return pl.pallas_call(
        kernel,
        grid_spec=pltpu.PrefetchScalarGridSpec(
            num_scalar_prefetch=len(scalars),
            grid=grid,
            in_specs=in_specs,
            out_specs=out_specs,
            scratch_shapes=list(scratch),
        ),
        out_shape=out_shape,
        input_output_aliases=aliases or {},
        cost_estimate=pl.CostEstimate(flops=flops, bytes_accessed=4 * MIB, transcendentals=0),
        compiler_params=pltpu.CompilerParams(vmem_limit_bytes=40 * MIB),
    )(*scalars, *operands)


def hops(count, distance, wrap):
    pairs = []
    for patch in range(count):
        for feat, step in ((0, distance), (1, -distance)):
            target = patch + step
            if wrap or 0 <= target < count:
                pairs.append((2 * patch + feat, 2 * (target % count) + feat))
    return pairs


def exchange_pairs(count):
    middle = count // 2
    pairs = [hops(count, 1, False)] + [hops(count, k, True) for k in range(2, middle)]
    last = [(2 * patch, 2 * ((patch + middle) % count)) for patch in range(count)]
    return pairs + [last + [(1, 2 * count - 1), (2 * count - 1, 1)]]


def relative_slots(rows, patch, patches, node_count, halo, coarse, local_slots, group):
    at = rows - (node_count + 2 * halo)
    owner, entry = at // coarse, at % coarse
    below = (patch - owner) % patches
    middle = patches // 2
    first, second = local_slots, local_slots + group
    ends = ((patch == 0) & (owner == patches - 1)) | ((patch == patches - 1) & (owner == 0))
    place = jnp.where(
        below <= middle,
        first + halo + coarse * (below - 1),
        second + halo + coarse * (patches - below - 1),
    )
    place = jnp.where(ends, second + halo + coarse * (middle - 1), place)
    place = jnp.where(below == 0, node_count, place) + entry
    place = jnp.where(rows < node_count + 2 * halo, second + rows - (node_count + halo), place)
    place = jnp.where(rows < node_count + halo, first + rows - node_count, place)
    return jnp.where(rows < node_count, rows, place)


def on_device(
    node_latent,
    edge_latent,
    edge_senders,
    edge_receivers,
    halo_rows,
    coarse_rows,
    edge_counts,
    edge_w1,
    edge_w2,
    edge_gain,
    node_w1,
    node_w2,
    node_gain,
):
    node_count, width = node_latent.shape
    half = width // 2
    edge_count = edge_latent.shape[0]
    halo, coarse = halo_rows.shape[1], coarse_rows.shape[0]
    patches = lax.axis_size("patch")
    feat = lax.axis_index("feat")
    patch = lax.axis_index("patch")
    both = ("patch", "feat")
    group = halo + coarse * (patches // 2)
    used = node_count + coarse
    local_slots = -(-used // 256) * 256
    share = edge_count // 2
    block = 512
    steps = share // block
    feat_scalar = feat.astype(jnp.int32).reshape(1)
    coarse_row = coarse_rows.reshape(1, coarse)
    edge_gain, node_gain = edge_gain.reshape(1, width), node_gain.reshape(1, width)

    def shape(rows, columns, kind):
        return jax.ShapeDtypeStruct((rows, columns), kind)

    lent = call(
        lend_kernel,
        (1,),
        (feat_scalar,),
        [whole((node_count, width)), whole((2, halo)), whole((1, coarse))],
        whole((halo + coarse, width)),
        shape(halo + coarse, width, BF16),
        (node_latent, halo_rows, coarse_row),
        2 * node_count * (halo + coarse) * width,
    )
    pairs = exchange_pairs(patches)
    arrived = [lax.ppermute(lent, both, pairs[0])]
    for some in pairs[1:]:
        arrived.append(lax.ppermute(lent[halo:], both, some))
    table_mine = jnp.concatenate(arrived, axis=0)
    table_theirs = lax.ppermute(table_mine, "feat", FEAT_SWAP)

    edge_w1_b = lax.ppermute(edge_w1, "feat", FEAT_SWAP)
    edge_w2_b = lax.ppermute(edge_w2, "feat", FEAT_SWAP)
    node_w1_b = lax.ppermute(node_w1, "feat", FEAT_SWAP)
    node_w2_b = lax.ppermute(node_w2, "feat", FEAT_SWAP)

    live = jnp.arange(edge_count) < edge_counts[0]
    slots = jnp.stack(
        [
            jnp.where(
                live,
                relative_slots(rows, patch, patches, node_count, halo, coarse, local_slots, group),
                -1,
            )
            for rows in (edge_senders, edge_receivers)
        ]
    )

    my_rows = lambda i, f, *_: (f[0] * steps + i, 0)
    other_rows = lambda i, f, *_: ((1 - f[0]) * steps + i, 0)
    my_slots = lambda i, f, *_: (0, f[0] * steps + i)
    step_rows = lambda i, *_: (i, 0)

    pre = call(
        functools.partial(local_kernel, local_slots=local_slots, coarse=coarse),
        (steps,),
        (feat_scalar,),
        [
            whole((node_count, width)),
            whole((halo + coarse, width)),
            whole((3 * width, half)),
            whole((3 * width, half)),
            pl.BlockSpec((block, width), my_rows),
            pl.BlockSpec((2, block), my_slots),
        ],
        pl.BlockSpec((block, width), step_rows),
        shape(share, width, F32),
        (node_latent, lent, edge_w1, edge_w1_b, edge_latent, slots),
        2 * width * width * share + 4 * used * width * width + 4 * share * local_slots * width,
        scratch=[pltpu.VMEM((2 * local_slots, width), BF16)],
    )

    edges, edges_other, group_mine, group_other, local_sums = call(
        functools.partial(edge_kernel, local_slots=local_slots),
        (steps,),
        (feat_scalar, edge_counts),
        [
            pl.BlockSpec((block, width), step_rows),
            pl.BlockSpec((block, width), my_rows),
            pl.BlockSpec((2, block), my_slots),
            whole((group, width)),
            whole((group, width)),
            whole((3 * width, half)),
            whole((3 * width, half)),
            whole((half, width)),
            whole((half, width)),
            whole((1, width)),
        ],
        [
            pl.BlockSpec((block, half), my_rows),
            pl.BlockSpec((block, half), step_rows),
            whole((group, width)),
            whole((group, width)),
            whole((used, width)),
        ],
        [
            shape(edge_count, half, BF16),
            shape(share, half, BF16),
            shape(group, width, F32),
            shape(group, width, BF16),
            shape(used, width, F32),
        ],
        (pre, edge_latent, slots, table_mine, table_theirs, edge_w1, edge_w1_b, edge_w2, edge_w2_b, edge_gain),
        2 * share * width * (width + 6 * group + used) + 8 * group * width * width,
        scratch=[pltpu.VMEM((4 * group, width), BF16), pltpu.VMEM((2 * group, width), F32)],
    )

    group_theirs = lax.ppermute(group_other, "feat", FEAT_SWAP)
    sizes = [halo + coarse] + [coarse] * (len(pairs) - 1)
    outgoing = call(
        merge_kernel,
        (1,),
        (),
        [whole((group, width))] * 2,
        [whole((rows, width)) for rows in sizes],
        [shape(rows, width, BF16) for rows in sizes],
        (group_mine, group_theirs),
        group * width,
    )
    back = [
        lax.ppermute(part, both, [(target, source) for source, target in some])
        for part, some in zip(outgoing, pairs)
    ]
    back_mine = jnp.concatenate(back, axis=0)
    back_theirs = lax.ppermute(back_mine, "feat", FEAT_SWAP)
    local_theirs = lax.ppermute(local_sums.astype(BF16), "feat", FEAT_SWAP)
    edges_theirs = lax.ppermute(edges_other, "feat", FEAT_SWAP)
    edges_out = call(
        place_kernel,
        (steps,),
        (feat_scalar,),
        [pl.BlockSpec((block, half), step_rows), pl.BlockSpec(memory_space=pl.ANY)],
        pl.BlockSpec((block, half), other_rows),
        shape(edge_count, half, BF16),
        (edges_theirs, edges),
        share * half,
        aliases={2: 0},
    )
    nodes_out = call(
        node_kernel,
        (1,),
        (feat_scalar,),
        [
            whole((node_count, width)),
            whole((2, halo)),
            whole((1, coarse)),
            whole((used, width)),
            whole((used, width)),
            whole((group, width)),
            whole((group, width)),
            whole((2 * width, half)),
            whole((2 * width, half)),
            whole((half, width)),
            whole((half, width)),
            whole((1, width)),
        ],
        whole((node_count, half)),
        shape(node_count, half, BF16),
        (
            node_latent,
            halo_rows,
            coarse_row,
            local_sums,
            local_theirs,
            back_mine,
            back_theirs,
            node_w1,
            node_w1_b,
            node_w2,
            node_w2_b,
            node_gain,
        ),
        2 * node_count * width * (3 * width + 2 * group),
    )
    return nodes_out, edges_out


def solution(mesh):
    placed = (
        P(("member", "patch"), None),
        P(("member", "patch"), None),
        P(("member", "patch")),
        P(("member", "patch")),
        P(("member", "patch"), None),
        P(("member", "patch")),
        P(("member", "patch")),
        P(None, "feat"),
        P("feat", None),
        P(),
        P(None, "feat"),
        P("feat", None),
        P(),
    )
    return jax.shard_map(
        on_device,
        mesh=mesh,
        in_specs=placed,
        out_specs=(P(("member", "patch"), "feat"), P(("member", "patch"), "feat")),
        check_vma=False,
    )
```

time: 242 us -> 74.2 us (0.31)
  the two profiles are of different devices: /device:TPU:0 before, /device:TPU:25 now
where the time goes in v1:
time: 74.2 us; the launch traced here: 73.7 us
  starting transfers between devices  33.3 us (45%)
  Pallas kernels  21.1 us (28%)
  waiting for transfers between devices  9.21 us (12%)
  local copies, waits for them, and re-layouts  7.61 us (10%)
  between operations  1.55 us (2%)
  other arithmetic  0.94 us (1%)
    pallas_call x6, Pallas kernels, call(): pl.pallas_call(kernel, grid_spec=pltpu.PrefetchScalarGridSpec(num_scalar_...  21.1 us
    ppermute x1, starting transfers between devices, on_device(): back_theirs = lax.ppermute(back_mine, 'feat', FEAT_SWAP)  12.1 us
    ppermute x4, starting transfers between devices, on_device(): lax.ppermute(part, both, [(target, source) for source, target in some])  7.59 us
    ppermute x4, waiting for transfers between devices, on_device(): lax.ppermute(part, both, [(target, source) for source, target in some])  7.02 us
    unnamed x36, local copies, waits for them, and re-layouts  6.9 us
    ppermute x1, starting transfers between devices, on_device(): edge_w1_b = lax.ppermute(edge_w1, 'feat', FEAT_SWAP)  5.14 us
    ppermute x1, starting transfers between devices, on_device(): arrived = [lax.ppermute(lent, both, pairs[0])]  3.03 us
    ppermute x1, starting transfers between devices, on_device(): table_theirs = lax.ppermute(table_mine, 'feat', FEAT_SWAP)  2.48 us
  transfers between devices with their start and end apart: 17, of which 5 were waited for; matrix products, arithmetic and copies ran while one was open for 2% of the time, Pallas kernels for 12%

profile of v1, /device:TPU:25, one launch (start us, length us, event | category | flops | bytes accessed | tf_op | source)
XLA Modules:
  0.0 73.7 jit_solution(3026969188075099352)
XLA Ops:
  0.6 1.1 %copy-done = bf16[640,512]{1,0:T(8,128)(2,1)S(1)} copy-done((bf16[640,512]{1,0:T(8,128)(2,1)S(1)}, bf16[640,512]{1,0:T(8,128)(2,1)}, u32[]{:S(2)}) %copy-start) | copy-done | bytes 655384
  1.7 0.7 copy-done.5
  2.4 0.7 copy-done.7
  3.1 0.3 shard_map.140.lent_ref
  3.4 3.0 %collective-permute-start.1 = (bf16[160,512]{1,0:T(8,128)(2,1)S(1)}, bf16[160,512]{1,0:T(8,128)(2,1)S(1)}, u32[]{:S(2)}, u32[]{:S(2)}) collective-permute-start(bf16[160,512]{1,0:T(8,128)(2,1)S(1)} %shard_map.140.lent_ref), channel_id=1, source_target_pairs={{0,2},{2,4},{3,1},{4,6},{5,3},{6,8},{7,5},{8,10},{9,7},{10,12},{11... | collective-permute-start | bytes 491528 | tf_op jit(solution)/shard_map/ppermute | solution.py:319
  6.4 0.2 collective-permute-start.2
  6.7 0.7 collective-permute-start.4
  7.3 5.1 %collective-permute-start = (bf16[1536,256]{1,0:T(8,128)(2,1)}, bf16[1536,256]{1,0:T(8,128)(2,1)S(1)}, u32[]{:S(2)}, u32[]{:S(2)}) collective-permute-start(bf16[1536,256]{1,0:T(8,128)(2,1)} %wa_ref.4), channel_id=1, source_target_pairs={{0,1},{1,0},{2,3},{3,2},{4,5},{5,4},{6,7},{7,6},{8,9},{9,8},{10,11... | collective-permute-start | bytes 2359304 | tf_op jit(solution)/shard_map/ppermute | solution.py:325
  13.1 0.8 %fusion.8 = (s32[4096]{0:T(1024)S(1)}, s32[4096]{0:T(1024)S(1)}) fusion(s32[4096]{0:T(1024)} %param.15, s32[]{:T(128)S(6)} %axis_index.25, s32[]{:T(128)} %bitcast.5, pred[]{:T(512)S(6)} %eq.34, pred[]{:T(512)S(6)} %eq.32, s32[4096]{0:T(1024)} %param.16), kind=kLoop, calls=%fused_computation.35 | loop fusion | flops 479232 | bytes 65546 | tf_op jit(solution)/shard_map/jit(_where)/select_n | solution.py:333
  14.0 0.7 reshape.18.gain_ref
  14.8 2.5 %collective-permute-start.5 = (bf16[256,512]{1,0:T(8,128)(2,1)S(1)}, bf16[256,512]{1,0:T(8,128)(2,1)S(1)}, u32[]{:S(2)}, u32[]{:S(2)}) collective-permute-start(bf16[256,512]{1,0:T(8,128)(2,1)S(1)} %constant_dynamic-update-slice_fusion.mine_ref), channel_id=1, source_target_pairs={{0,1},{1,0},{2,3},{3,2},{4,5},{5,4},{6,7},{7,6},{8,9},{9,8},{10,11... | collective-permute-start | bytes 786440 | tf_op jit(solution)/shard_map/ppermute | solution.py:323
  17.3 1.1 %copy-done.1 = bf16[640,512]{1,0:T(8,128)(2,1)S(1)} copy-done((bf16[640,512]{1,0:T(8,128)(2,1)S(1)}, bf16[640,512]{1,0:T(8,128)(2,1)}, u32[]{:S(2)}) %copy-start.1) | copy-done | bytes 655384
  18.4 2.2 %copy-done.9 = bf16[4096,512]{1,0:T(8,128)(2,1)S(1)} copy-done((bf16[4096,512]{1,0:T(8,128)(2,1)S(1)}, bf16[4096,512]{1,0:T(8,128)(2,1)}, u32[]{:S(2)}) %copy-start.9) | copy-done | bytes 4194328
  20.5 1.1 %copy-done.11 = bf16[1536,256]{1,0:T(8,128)(2,1)S(1)} copy-done((bf16[1536,256]{1,0:T(8,128)(2,1)S(1)}, bf16[1536,256]{1,0:T(8,128)(2,1)}, u32[]{:S(2)}) %copy-start.11) | copy-done | bytes 786456
  21.7 6.2 %shard_map.141.pre_ref = f32[2048,512]{1,0:T(8,128)S(1)} custom-call(s32[1]{0:T(128)} %bitcast.feat_ref, bf16[640,512]{1,0:T(8,128)(2,1)S(1)} %copy-done.1, bf16[160,512]{1,0:T(8,128)(2,1)S(1)} %shard_map.140.lent_ref, bf16[1536,256]{1,0:T(8,128)(2,1)S(1)} %copy-done.11, bf16[1536,256]{1,0:T(8,128)(2,1)S(1)} %collective-permute-done.wb_ref, ...), custom_call_target="tpu_custom_call" | custom-call | flops 4999610368 | bytes 4194304 | tf_op jit(solution)/shard_map/pallas_call | solution.py:220
  27.9 10.2 %shard_map.142 = (bf16[4096,256]{1,0:T(8,128)(2,1)}, bf16[2048,256]{1,0:T(8,128)(2,1)S(1)}, f32[256,512]{1,0:T(8,128)S(1)}, bf16[256,512]{1,0:T(8,128)(2,1)S(1)}, f32[672,512]{1,0:T(8,128)S(1)}) custom-call(s32[1]{0:T(128)} %bitcast.feat_ref, s32[1]{0:T(128)} %copy.23.limit_ref, f32[2048,512]{1,0:T(8,128)S(1)} %shard_map.141.pre_ref, ...), custom_call_target="tpu_custom_call" | custom-call | flops 6241124352 | bytes 4194304 | tf_op jit(solution)/shard_map/pallas_call | solution.py:220
  38.2 0.5 collective-permute-start.16
  38.7 1.0 %collective-permute-done.8.theirs_ref = bf16[256,512]{1,0:T(8,128)(2,1)S(1)} collective-permute-done((bf16[256,512]{1,0:T(8,128)(2,1)S(1)}, bf16[256,512]{1,0:T(8,128)(2,1)S(1)}, u32[]{:S(2)}, u32[]{:S(2)}) %collective-permute-start.8) | collective-permute-done | bytes 262176 | tf_op jit(solution)/shard_map/ppermute | solution.py:401
  39.8 2.3 %collective-permute-start.9 = (bf16[160,512]{1,0:T(8,128)(2,1)S(1)}, bf16[160,512]{1,0:T(8,128)(2,1)S(1)}, u32[]{:S(2)}, u32[]{:S(2)}) collective-permute-start(bf16[160,512]{1,0:T(8,128)(2,1)S(1)} %get-tuple-element.14), channel_id=1, source_target_pairs={{2,0},{4,2},{1,3},{6,4},{3,5},{8,6},{5,7},{10,8},{7,9},{12,10},{9,... | collective-permute-start | bytes 491528 | tf_op jit(solution)/shard_map/ppermute | solution.py:414
  42.0 0.9 %collective-permute-start.14 = (bf16[1024,256]{1,0:T(8,128)(2,1)S(1)}, bf16[1024,256]{1,0:T(8,128)(2,1)S(1)}, u32[]{:S(2)}, u32[]{:S(2)}) collective-permute-start(bf16[1024,256]{1,0:T(8,128)(2,1)S(1)} %copy-done.3), channel_id=1, source_target_pairs={{0,1},{1,0},{2,3},{3,2},{4,5},{5,4},{6,7},{7,6},{8,9},{9,8},{10,11... | collective-permute-start | bytes 1572872 | tf_op jit(solution)/shard_map/ppermute | solution.py:327
  42.9 0.1 collective-permute-start.15
  43.0 0.1 convert_element_type.3
  43.1 0.5 collective-permute-start.7
  43.6 3.2 %collective-permute-done.9 = bf16[160,512]{1,0:T(8,128)(2,1)S(1)} collective-permute-done((bf16[160,512]{1,0:T(8,128)(2,1)S(1)}, bf16[160,512]{1,0:T(8,128)(2,1)S(1)}, u32[]{:S(2)}, u32[]{:S(2)}) %collective-permute-start.9) | collective-permute-done | bytes 163872 | tf_op jit(solution)/shard_map/ppermute | solution.py:414
  46.9 2.7 %collective-permute-done.10 = bf16[32,512]{1,0:T(8,128)(2,1)S(1)} collective-permute-done((bf16[32,512]{1,0:T(8,128)(2,1)S(1)}, bf16[32,512]{1,0:T(8,128)(2,1)S(1)}, u32[]{:S(2)}, u32[]{:S(2)}) %collective-permute-start.10) | collective-permute-done | bytes 32800 | tf_op jit(solution)/shard_map/ppermute | solution.py:414
  49.6 4.7 %collective-permute-start.11 = (bf16[32,512]{1,0:T(8,128)(2,1)S(1)}, bf16[32,512]{1,0:T(8,128)(2,1)S(1)}, u32[]{:S(2)}, u32[]{:S(2)}) collective-permute-start(bf16[32,512]{1,0:T(8,128)(2,1)S(1)} %get-tuple-element.16), channel_id=1, source_target_pairs={{6,0},{11,1},{8,2},{13,3},{10,4},{15,5},{12,6},{1,7},{14,8},{3,9},... | collective-permute-start | bytes 98312 | tf_op jit(solution)/shard_map/ppermute | solution.py:414
  54.3 1.0 %collective-permute-done.11 = bf16[32,512]{1,0:T(8,128)(2,1)S(1)} collective-permute-done((bf16[32,512]{1,0:T(8,128)(2,1)S(1)}, bf16[32,512]{1,0:T(8,128)(2,1)S(1)}, u32[]{:S(2)}, u32[]{:S(2)}) %collective-permute-start.11) | collective-permute-done | bytes 32800 | tf_op jit(solution)/shard_map/ppermute | solution.py:414
  55.3 0.7 collective-permute-start.12
  56.0 12.1 %collective-permute-start.13 = (bf16[256,512]{1,0:T(8,128)(2,1)S(1)}, bf16[256,512]{1,0:T(8,128)(2,1)S(1)}, u32[]{:S(2)}, u32[]{:S(2)}) collective-permute-start(bf16[256,512]{1,0:T(8,128)(2,1)S(1)} %constant_dynamic-update-slice_fusion.4.mine_ref), channel_id=1, source_target_pairs={{0,1},{1,0},{2,3},{3,2},{4,5},{5,4},{6,7},{7,6},{8,9},{9,8},{10,11... | collective-permute-start | bytes 786440 | tf_op jit(solution)/shard_map/ppermute | solution.py:418
  68.2 1.1 %collective-permute-done.13.theirs_ref = bf16[256,512]{1,0:T(8,128)(2,1)S(1)} collective-permute-done((bf16[256,512]{1,0:T(8,128)(2,1)S(1)}, bf16[256,512]{1,0:T(8,128)(2,1)S(1)}, u32[]{:S(2)}, u32[]{:S(2)}) %collective-permute-start.13) | collective-permute-done | bytes 262176 | tf_op jit(solution)/shard_map/ppermute | solution.py:418
  69.3 2.9 %shard_map.144 = bf16[640,256]{1,0:T(8,128)(2,1)} custom-call(s32[1]{0:T(128)} %bitcast.feat_ref, bf16[640,512]{1,0:T(8,128)(2,1)S(1)} %copy-done.2, s32[2,128]{1,0:T(2,128)S(1)} %copy-done.6, s32[1,32]{1,0:T(1,128)S(1)} %bitcast.7, f32[672,512]{1,0:T(8,128)S(1)} %get-tuple-element.11.own_ref, bf16[672,512]{1,0:T(8,128)(2,1)S(1)} %collective-permute-done.7.partner_ref, ...), custom_call_target="tpu_custom_call" | custom-call | flops 1342177280 | bytes 4194304 | tf_op jit(solution)/shard_map/pallas_call | solution.py:220
  72.2 1.5 %shard_map.145 = bf16[4096,256]{1,0:T(8,128)(2,1)} custom-call(s32[1]{0:T(128)} %bitcast.feat_ref, bf16[2048,256]{1,0:T(8,128)(2,1)S(1)} %collective-permute-done.16.block_ref, bf16[4096,256]{1,0:T(8,128)(2,1)} %get-tuple-element.19.whole_ref), custom_call_target="tpu_custom_call", output_to_operand_aliasing={{}: (2, {})} | custom-call | flops 524288 | bytes 4194304 | tf_op jit(solution)/shard_map/pallas_call | solution.py:220
  (52 shorter events, 0.3 us)
Async XLA Ops:
  0.6 1.1 %copy-start = (bf16[640,512]{1,0:T(8,128)(2,1)S(1)}, bf16[640,512]{1,0:T(8,128)(2,1)}, u32[]{:S(2)}) copy-start(bf16[640,512]{1,0:T(8,128)(2,1)} %node_ref.5) | copy-start | bytes 1966084
  1.7 0.7 copy-start.5
  2.4 0.7 copy-start.7
  3.4 11.3 %collective-permute-start.1 = (bf16[160,512]{1,0:T(8,128)(2,1)S(1)}, bf16[160,512]{1,0:T(8,128)(2,1)S(1)}, u32[]{:S(2)}, u32[]{:S(2)}) collective-permute-start(bf16[160,512]{1,0:T(8,128)(2,1)S(1)} %shard_map.140.lent_ref), channel_id=1, source_target_pairs={{0,2},{2,4},{3,1},{4,6},{5,3},{6,8},{7,5},{8,10},{9,7},{10,12},{11... | collective-permute-start | bytes 491528 | tf_op jit(solution)/shard_map/ppermute | solution.py:319
  6.4 8.3 %collective-permute-start.2 = (bf16[32,512]{1,0:T(8,128)(2,1)S(1)}, bf16[32,512]{1,0:T(8,128)(2,1)S(1)}, u32[]{:S(2)}, u32[]{:S(2)}) collective-permute-start(bf16[32,512]{1,0:T(8,128)(2,1)S(1)} %slice.6), channel_id=1, source_target_pairs={{0,4},{1,13},{2,6},{3,15},{4,8},{5,1},{6,10},{7,3},{8,12},{9,5},{1... | collective-permute-start | bytes 98312 | tf_op jit(solution)/shard_map/ppermute | solution.py:321
  6.7 8.1 %collective-permute-start.3 = (bf16[32,512]{1,0:T(8,128)(2,1)S(1)}, bf16[32,512]{1,0:T(8,128)(2,1)S(1)}, u32[]{:S(2)}, u32[]{:S(2)}) collective-permute-start(bf16[32,512]{1,0:T(8,128)(2,1)S(1)} %slice.6), channel_id=1, source_target_pairs={{0,6},{1,11},{2,8},{3,13},{4,10},{5,15},{6,12},{7,1},{8,14},{9,3},... | collective-permute-start | bytes 98312 | tf_op jit(solution)/shard_map/ppermute | solution.py:321
  6.7 8.1 %collective-permute-start.4 = (bf16[32,512]{1,0:T(8,128)(2,1)S(1)}, bf16[32,512]{1,0:T(8,128)(2,1)S(1)}, u32[]{:S(2)}, u32[]{:S(2)}) collective-permute-start(bf16[32,512]{1,0:T(8,128)(2,1)S(1)} %slice.6), channel_id=1, source_target_pairs={{0,8},{2,10},{4,12},{6,14},{8,0},{10,2},{12,4},{14,6},{1,15},{15,1... | collective-permute-start | bytes 98312 | tf_op jit(solution)/shard_map/ppermute | solution.py:321
  7.3 9.9 %collective-permute-start = (bf16[1536,256]{1,0:T(8,128)(2,1)}, bf16[1536,256]{1,0:T(8,128)(2,1)S(1)}, u32[]{:S(2)}, u32[]{:S(2)}) collective-permute-start(bf16[1536,256]{1,0:T(8,128)(2,1)} %wa_ref.4), channel_id=1, source_target_pairs={{0,1},{1,0},{2,3},{3,2},{4,5},{5,4},{6,7},{7,6},{8,9},{9,8},{10,11... | collective-permute-start | bytes 2359304 | tf_op jit(solution)/shard_map/ppermute | solution.py:325
  14.7 13.2 %collective-permute-start.6 = (bf16[256,512]{1,0:T(8,128)(2,1)}, bf16[256,512]{1,0:T(8,128)(2,1)S(1)}, u32[]{:S(2)}, u32[]{:S(2)}) collective-permute-start(bf16[256,512]{1,0:T(8,128)(2,1)} %va_ref.2), channel_id=1, source_target_pairs={{0,1},{1,0},{2,3},{3,2},{4,5},{5,4},{6,7},{7,6},{8,9},{9,8},{10,11... | collective-permute-start | bytes 786440 | tf_op jit(solution)/shard_map/ppermute | solution.py:326
  14.8 13.1 %collective-permute-start.5 = (bf16[256,512]{1,0:T(8,128)(2,1)S(1)}, bf16[256,512]{1,0:T(8,128)(2,1)S(1)}, u32[]{:S(2)}, u32[]{:S(2)}) collective-permute-start(bf16[256,512]{1,0:T(8,128)(2,1)S(1)} %constant_dynamic-update-slice_fusion.mine_ref), channel_id=1, source_target_pairs={{0,1},{1,0},{2,3},{3,2},{4,5},{5,4},{6,7},{7,6},{8,9},{9,8},{10,11... | collective-permute-start | bytes 786440 | tf_op jit(solution)/shard_map/ppermute | solution.py:323
  17.3 1.1 %copy-start.1 = (bf16[640,512]{1,0:T(8,128)(2,1)S(1)}, bf16[640,512]{1,0:T(8,128)(2,1)}, u32[]{:S(2)}) copy-start(bf16[640,512]{1,0:T(8,128)(2,1)} %node_ref.5) | copy-start | bytes 1966084
  18.4 2.2 %copy-start.9 = (bf16[4096,512]{1,0:T(8,128)(2,1)S(1)}, bf16[4096,512]{1,0:T(8,128)(2,1)}, u32[]{:S(2)}) copy-start(bf16[4096,512]{1,0:T(8,128)(2,1)} %latent_ref.3) | copy-start | bytes 12582916
  20.5 1.1 %copy-start.11 = (bf16[1536,256]{1,0:T(8,128)(2,1)S(1)}, bf16[1536,256]{1,0:T(8,128)(2,1)}, u32[]{:S(2)}) copy-start(bf16[1536,256]{1,0:T(8,128)(2,1)} %wa_ref.4) | copy-start | bytes 2359300
  21.7 6.2 %copy-start.10 = (bf16[4096,512]{1,0:T(8,128)(2,1)S(1)}, bf16[4096,512]{1,0:T(8,128)(2,1)}, u32[]{:S(2)}) copy-start(bf16[4096,512]{1,0:T(8,128)(2,1)} %latent_ref.3) | copy-start | bytes 12582916
  21.7 6.2 %copy-start.12 = (bf16[1536,256]{1,0:T(8,128)(2,1)S(1)}, bf16[1536,256]{1,0:T(8,128)(2,1)}, u32[]{:S(2)}) copy-start(bf16[1536,256]{1,0:T(8,128)(2,1)} %wa_ref.4) | copy-start | bytes 2359300
  21.7 6.2 %copy-start.13 = (bf16[256,512]{1,0:T(8,128)(2,1)S(1)}, bf16[256,512]{1,0:T(8,128)(2,1)}, u32[]{:S(2)}) copy-start(bf16[256,512]{1,0:T(8,128)(2,1)} %va_ref.2) | copy-start | bytes 786436
  27.9 14.2 %copy-start.3 = (bf16[1024,256]{1,0:T(8,128)(2,1)S(1)}, bf16[1024,256]{1,0:T(8,128)(2,1)}, u32[]{:S(2)}) copy-start(bf16[1024,256]{1,0:T(8,128)(2,1)} %wa_ref.5) | copy-start | bytes 1572868
  27.9 15.1 %copy-start.4 = (bf16[256,512]{1,0:T(8,128)(2,1)S(1)}, bf16[256,512]{1,0:T(8,128)(2,1)}, u32[]{:S(2)}) copy-start(bf16[256,512]{1,0:T(8,128)(2,1)} %va_ref.3) | copy-start | bytes 786436
  38.1 30.0 %copy-start.14 = (bf16[512]{0:T(512)(128)(2,1)S(1)}, bf16[512]{0:T(512)(128)(2,1)}, u32[]{:S(2)}) copy-start(bf16[512]{0:T(512)(128)(2,1)} %param.25) | copy-start | bytes 3076
  38.1 31.2 %copy-start.2 = (bf16[640,512]{1,0:T(8,128)(2,1)S(1)}, bf16[640,512]{1,0:T(8,128)(2,1)}, u32[]{:S(2)}) copy-start(bf16[640,512]{1,0:T(8,128)(2,1)} %node_ref.5) | copy-start | bytes 1966084
  38.1 31.2 %copy-start.6 = (s32[2,128]{1,0:T(2,128)S(1)}, s32[2,128]{1,0:T(2,128)}, u32[]{:S(2)}) copy-start(s32[2,128]{1,0:T(2,128)} %halo_ref.3) | copy-start | bytes 3076
  38.1 31.2 %copy-start.8 = (s32[32]{0:T(128)S(1)}, s32[32]{0:T(128)}, u32[]{:S(2)}) copy-start(s32[32]{0:T(128)} %param.18) | copy-start | bytes 388
  38.1 1.6 %collective-permute-start.8 = (bf16[256,512]{1,0:T(8,128)(2,1)S(1)}, bf16[256,512]{1,0:T(8,128)(2,1)S(1)}, u32[]{:S(2)}, u32[]{:S(2)}) collective-permute-start(bf16[256,512]{1,0:T(8,128)(2,1)S(1)} %get-tuple-element.13), channel_id=1, source_target_pairs={{0,1},{1,0},{2,3},{3,2},{4,5},{5,4},{6,7},{7,6},{8,9},{9,8},{10,11... | collective-permute-start | bytes 786440 | tf_op jit(solution)/shard_map/ppermute | solution.py:401
  38.2 34.0 %collective-permute-start.16 = (bf16[2048,256]{1,0:T(8,128)(2,1)S(1)}, bf16[2048,256]{1,0:T(8,128)(2,1)S(1)}, u32[]{:S(2)}, u32[]{:S(2)}) collective-permute-start(bf16[2048,256]{1,0:T(8,128)(2,1)S(1)} %get-tuple-element.18), channel_id=1, source_target_pairs={{0,1},{1,0},{2,3},{3,2},{4,5},{5,4},{6,7},{7,6},{8,9},{9,8},{10,11... | collective-permute-start | bytes 3145736 | tf_op jit(solution)/shard_map/ppermute | solution.py:420
  39.8 7.1 %collective-permute-start.9 = (bf16[160,512]{1,0:T(8,128)(2,1)S(1)}, bf16[160,512]{1,0:T(8,128)(2,1)S(1)}, u32[]{:S(2)}, u32[]{:S(2)}) collective-permute-start(bf16[160,512]{1,0:T(8,128)(2,1)S(1)} %get-tuple-element.14), channel_id=1, source_target_pairs={{2,0},{4,2},{1,3},{6,4},{3,5},{8,6},{5,7},{10,8},{7,9},{12,10},{9,... | collective-permute-start | bytes 491528 | tf_op jit(solution)/shard_map/ppermute | solution.py:414
  42.0 26.1 %collective-permute-start.14 = (bf16[1024,256]{1,0:T(8,128)(2,1)S(1)}, bf16[1024,256]{1,0:T(8,128)(2,1)S(1)}, u32[]{:S(2)}, u32[]{:S(2)}) collective-permute-start(bf16[1024,256]{1,0:T(8,128)(2,1)S(1)} %copy-done.3), channel_id=1, source_target_pairs={{0,1},{1,0},{2,3},{3,2},{4,5},{5,4},{6,7},{7,6},{8,9},{9,8},{10,11... | collective-permute-start | bytes 1572872 | tf_op jit(solution)/shard_map/ppermute | solution.py:327
  42.9 25.2 %collective-permute-start.15 = (bf16[256,512]{1,0:T(8,128)(2,1)S(1)}, bf16[256,512]{1,0:T(8,128)(2,1)S(1)}, u32[]{:S(2)}, u32[]{:S(2)}) collective-permute-start(bf16[256,512]{1,0:T(8,128)(2,1)S(1)} %copy-done.4), channel_id=1, source_target_pairs={{0,1},{1,0},{2,3},{3,2},{4,5},{5,4},{6,7},{7,6},{8,9},{9,8},{10,11... | collective-permute-start | bytes 786440 | tf_op jit(solution)/shard_map/ppermute | solution.py:328
  43.1 26.2 %collective-permute-start.7 = (bf16[672,512]{1,0:T(8,128)(2,1)S(1)}, bf16[672,512]{1,0:T(8,128)(2,1)S(1)}, u32[]{:S(2)}, u32[]{:S(2)}) collective-permute-start(bf16[672,512]{1,0:T(8,128)(2,1)S(1)} %convert_element_type.3), channel_id=1, source_target_pairs={{0,1},{1,0},{2,3},{3,2},{4,5},{5,4},{6,7},{7,6},{8,9},{9,8},{10,11... | collective-permute-start | bytes 2064392 | tf_op jit(solution)/shard_map/ppermute | solution.py:419
  46.8 2.8 %collective-permute-start.10 = (bf16[32,512]{1,0:T(8,128)(2,1)S(1)}, bf16[32,512]{1,0:T(8,128)(2,1)S(1)}, u32[]{:S(2)}, u32[]{:S(2)}) collective-permute-start(bf16[32,512]{1,0:T(8,128)(2,1)S(1)} %get-tuple-element.15), channel_id=1, source_target_pairs={{4,0},{13,1},{6,2},{15,3},{8,4},{1,5},{10,6},{3,7},{12,8},{5,9},{1... | collective-permute-start | bytes 98312 | tf_op jit(solution)/shard_map/ppermute | solution.py:414
  49.6 5.7 %collective-permute-start.11 = (bf16[32,512]{1,0:T(8,128)(2,1)S(1)}, bf16[32,512]{1,0:T(8,128)(2,1)S(1)}, u32[]{:S(2)}, u32[]{:S(2)}) collective-permute-start(bf16[32,512]{1,0:T(8,128)(2,1)S(1)} %get-tuple-element.16), channel_id=1, source_target_pairs={{6,0},{11,1},{8,2},{13,3},{10,4},{15,5},{12,6},{1,7},{14,8},{3,9},... | collective-permute-start | bytes 98312 | tf_op jit(solution)/shard_map/ppermute | solution.py:414
  55.3 0.7 collective-permute-start.12
  56.0 13.3 %collective-permute-start.13 = (bf16[256,512]{1,0:T(8,128)(2,1)S(1)}, bf16[256,512]{1,0:T(8,128)(2,1)S(1)}, u32[]{:S(2)}, u32[]{:S(2)}) collective-permute-start(bf16[256,512]{1,0:T(8,128)(2,1)S(1)} %constant_dynamic-update-slice_fusion.4.mine_ref), channel_id=1, source_target_pairs={{0,1},{1,0},{2,3},{3,2},{4,5},{5,4},{6,7},{7,6},{8,9},{9,8},{10,11... | collective-permute-start | bytes 786440 | tf_op jit(solution)/shard_map/ppermute | solution.py:418

commit v2 on v1

v2 whole, which is shorter than its diff:
```python
import functools

import jax
import jax.numpy as jnp
from jax import lax
from jax.experimental import pallas as pl
from jax.experimental.pallas import tpu as pltpu
from jax.sharding import PartitionSpec as P

EPSILON = 1e-05
F32 = jnp.float32
BF16 = jnp.bfloat16
MIB = 1024 * 1024
LIMIT = 28
FEAT_SWAP = [(0, 1), (1, 0)]


def silu(v):
    return 0.5 * v * (1.0 + jnp.tanh(0.5 * v))


def dot(a, b):
    return jnp.dot(a, b, preferred_element_type=F32)


def layer_norm(pre, gain):
    width = pre.shape[1]
    center = jnp.sum(pre, axis=1, keepdims=True) / width
    square = jnp.sum(pre * pre, axis=1, keepdims=True) / width
    return (pre - center) * lax.rsqrt(square - center * center + EPSILON) * gain


def one_hot_rows(index, first, count):
    lanes = lax.broadcasted_iota(jnp.int32, (128, 128), 1)
    blocks = []
    for j in range(index.shape[0]):
        column = jnp.transpose(jnp.broadcast_to(index[j : j + 1, :], (128, 128))) - first
        blocks.append(
            jnp.concatenate(
                [(column == lanes + at).astype(F32).astype(BF16) for at in range(0, count, 128)], axis=1
            )
        )
    return jnp.concatenate(blocks, axis=0)


def one_hot_columns(index_row, first, count):
    entries = index_row.shape[1]
    rows = lax.broadcasted_iota(jnp.int32, (count, entries), 0) + first
    return (rows == jnp.broadcast_to(index_row, (count, entries))).astype(F32).astype(BF16)


def flat_row(index):
    return jnp.concatenate([index[j : j + 1, :] for j in range(index.shape[0])], axis=1)


def load_all(pairs, sems):
    copies = [pltpu.make_async_copy(source, target, sems.at[i]) for i, (source, target) in enumerate(pairs)]
    for copy in copies:
        copy.start()
    return copies


class Layout:
    def __init__(self, patches, node_count, halo, coarse):
        self.patches, self.node_count, self.halo, self.coarse = patches, node_count, halo, coarse
        self.group = halo + coarse * (patches // 2)
        self.used = node_count + coarse
        self.local_slots = -(-self.used // 256) * 256

    def slots(self, rows, patch, live):
        node_count, halo, coarse, group = self.node_count, self.halo, self.coarse, self.group
        at = rows - (node_count + 2 * halo)
        owner, entry = lax.shift_right_arithmetic(at, coarse.bit_length() - 1), at & (coarse - 1)
        distance = patch ^ owner
        odd = patch & 1
        place = self.local_slots + (distance & 1) * group + halo + coarse * lax.shift_right_arithmetic(distance, 1)
        place = jnp.where(distance == 0, node_count, place)
        place = jnp.where(distance == 1, self.local_slots + halo, place) + entry
        lower = self.local_slots + (1 - odd) * group - node_count + rows
        upper = self.local_slots + odd * group - (node_count + halo) + rows
        lower = jnp.where(patch == 0, -1, lower)
        upper = jnp.where(patch == self.patches - 1, -1, upper)
        place = jnp.where(rows < node_count + 2 * halo, upper, place)
        place = jnp.where(rows < node_count + halo, lower, place)
        place = jnp.where(rows < node_count, rows, place)
        return jnp.where(live, place, -1)

    def edge_slots(self, index_ref, step, where_ref, edges_per_core, block):
        feat, patch, limit = where_ref[0], where_ref[1], where_ref[2]
        count = block // 128
        start = feat * (edges_per_core // 128) + step * count
        rows = index_ref[pl.ds(start, count), :]
        shape = (count, 128)
        edge = (
            lax.broadcasted_iota(jnp.int32, shape, 0) * 128 + lax.broadcasted_iota(jnp.int32, shape, 1) + start * 128
        )
        return self.slots(rows, patch, edge < limit)


def lend_kernel(where_ref, node_ref, halo_ref, coarse_ref, out_ref, node, halo, coarse, sems):
    for copy in load_all(((node_ref, node), (halo_ref, halo), (coarse_ref, coarse)), sems):
        copy.wait()
    node_count = node.shape[0]
    lists = halo[...]
    which = (where_ref[0] + where_ref[1]) & 1
    index_row = jnp.concatenate(
        [jnp.where(which == 0, lists[0:1], lists[1:2]), coarse[...].reshape(1, -1)], axis=1
    )
    picks = one_hot_columns(index_row, 0, node_count)
    out_ref[...] = lax.dot_general(
        picks, node[...], (((0,), (0,)), ((), ())), preferred_element_type=F32
    ).astype(BF16)


def local_kernel(
    where_ref, node_ref, wa_ref, lent_ref, wb_ref, latent_ref, send_ref, recv_ref, out_ref, table, node, wa, sems, layout, share
):
    step = pl.program_id(0)
    node_count, width = node.shape
    half = wa.shape[1]
    block = latent_ref.shape[0]
    local_slots, used = layout.local_slots, layout.used

    @pl.when(step == 0)
    def _():
        for copy in load_all(((node_ref, node), (wa_ref, wa)), sems):
            copy.wait()
        rows_in = jnp.concatenate([node[...], lent_ref[lent_ref.shape[0] - layout.coarse :, :]], axis=0)
        for side in range(2):
            base = side * local_slots
            rows = slice((side + 1) * width, (side + 2) * width)
            for weight, col in ((wa, 0), (wb_ref, half)):
                table[base : base + used, col : col + half] = dot(rows_in, weight[rows, :]).astype(BF16)
            table[base + used : base + local_slots, :] = jnp.zeros((local_slots - used, 2 * half), BF16)

    picks = jnp.concatenate(
        [
            one_hot_rows(layout.edge_slots(index_ref, step, where_ref, share, block), 0, local_slots)
            for index_ref in (send_ref, recv_ref)
        ],
        axis=1,
    )
    for weight, col in ((wa, 0), (wb_ref, half)):
        cols = slice(col, col + half)
        out_ref[:, cols] = dot(latent_ref[...], weight[:width, :]) + dot(picks, table[:, cols])


def edge_kernel(
    where_ref,
    pre_ref,
    latent_ref,
    send_ref,
    recv_ref,
    mine_ref,
    theirs_ref,
    wa_ref,
    wb_ref,
    va_ref,
    vb_ref,
    gain_ref,
    fresh_ref,
    out_mine_ref,
    out_other_ref,
    group_mine_ref,
    group_other_ref,
    table,
    sums,
    wa,
    va,
    sems,
    layout,
    share,
):
    step = pl.program_id(0)
    steps = pl.num_programs(0)
    block, width = latent_ref.shape
    half = wa.shape[1]
    group = layout.group
    feat = where_ref[0]

    @pl.when(step == 0)
    def _():
        for copy in load_all(((wa_ref, wa), (va_ref, va)), sems):
            copy.wait()
        for side in range(2):
            rows = slice((side + 1) * width, (side + 2) * width)
            for weight, col in ((wa, 0), (wb_ref, half)):
                cols = slice(col, col + half)
                base = side * 2 * group
                at_mine = pl.multiple_of(base + feat * group, group)
                at_theirs = pl.multiple_of(base + (1 - feat) * group, group)
                table[pl.ds(at_mine, group), cols] = dot(mine_ref[...], weight[rows, :]).astype(BF16)
                table[pl.ds(at_theirs, group), cols] = dot(theirs_ref[...], weight[rows, :]).astype(BF16)
        sums[...] = jnp.zeros_like(sums)

    senders, receivers = [
        layout.edge_slots(index_ref, step, where_ref, share, block) for index_ref in (send_ref, recv_ref)
    ]
    picks = jnp.concatenate(
        [one_hot_rows(index, layout.local_slots, 2 * group) for index in (senders, receivers)], axis=1
    )
    hidden = silu(pre_ref[...] + dot(picks, table[...])).astype(BF16)
    pre = dot(hidden[:, :half], va[...]) + dot(hidden[:, half:], vb_ref[...])
    update = layer_norm(pre, gain_ref[...].astype(F32).reshape(1, width))
    before = latent_ref[...]
    row = lax.broadcasted_iota(jnp.int32, (block, 1), 0) + (feat * steps + step) * block
    fresh = jnp.where(row < where_ref[2], before.astype(F32) + update, before.astype(F32)).astype(BF16)
    fresh_ref[...] = fresh
    low, high = fresh[:, : width // 2], fresh[:, width // 2 :]
    out_mine_ref[...] = jnp.where(feat == 0, low, high)
    out_other_ref[...] = jnp.where(feat == 0, high, low)
    sums[...] += dot(one_hot_columns(flat_row(receivers), layout.local_slots, 2 * group), fresh)

    @pl.when(step == steps - 1)
    def _():
        group_mine_ref[...] = sums[pl.ds(pl.multiple_of(feat * group, group), group), :]
        group_other_ref[...] = sums[pl.ds(pl.multiple_of((1 - feat) * group, group), group), :].astype(BF16)


def merge_kernel(mine_ref, theirs_ref, *out_refs):
    at = 0
    for out_ref in out_refs:
        rows = out_ref.shape[0]
        part = slice(at, at + rows)
        out_ref[...] = (mine_ref[part, :] + theirs_ref[part, :].astype(F32)).astype(BF16)
        at += rows


def local_sums_kernel(
    where_ref, fresh_ref, recv_ref, node_ref, wa_ref, wb_ref, sums_ref, pre_ref, node, wa, sems, layout, share
):
    step = pl.program_id(0)
    node_count, width = node.shape
    half = wa.shape[1]
    used = sums_ref.shape[0]
    block = fresh_ref.shape[0]

    @pl.when(step == 0)
    def _():
        load_all(((node_ref, node), (wa_ref.at[pl.ds(0, width), :], wa)), sems)
        sums_ref[...] = jnp.zeros_like(sums_ref)

    receivers = layout.edge_slots(recv_ref, step, where_ref, share, block)
    sums_ref[...] += dot(one_hot_columns(flat_row(receivers), 0, used), fresh_ref[...])

    @pl.when(step == pl.num_programs(0) - 1)
    def _():
        pltpu.make_async_copy(node_ref, node, sems.at[0]).wait()
        pltpu.make_async_copy(wa_ref.at[pl.ds(0, width), :], wa, sems.at[1]).wait()
        pre_ref[:, :half] = dot(node[...], wa[...])
        pre_ref[:, half:] = dot(node[...], wb_ref[...])


def receive_kernel(where_ref, sums_ref, halo_ref, coarse_ref, *refs):
    *parts, own_ref, rounded_ref = refs
    node_count = own_ref.shape[0]
    coarse = coarse_ref.shape[0]
    lists = halo_ref[...]
    which = (where_ref[0] + where_ref[1]) & 1
    coarse_row = coarse_ref[...].reshape(1, coarse)
    index_row = jnp.concatenate(
        [jnp.where(which == 0, lists[0:1], lists[1:2])] + [coarse_row] * (len(parts) + 1), axis=1
    )
    returned = jnp.concatenate([part[...] for part in parts] + [sums_ref[node_count:, :].astype(BF16)], axis=0)
    own = sums_ref[:node_count, :] + dot(one_hot_columns(index_row, 0, node_count), returned)
    own_ref[...] = own
    rounded_ref[...] = own.astype(BF16)


def node_kernel(
    where_ref,
    node_ref,
    own_ref,
    partner_ref,
    pre_ref,
    wa_ref,
    wb_ref,
    va_ref,
    vb_ref,
    gain_ref,
    edges_in_ref,
    edges_ref,
    out_ref,
    edges_out_ref,
    sems,
):
    node_count, width = node_ref.shape
    half = wa_ref.shape[1]
    share = edges_ref.shape[0]
    feat = where_ref[0]
    copy = pltpu.make_async_copy(
        edges_ref, edges_out_ref.at[pl.ds(pl.multiple_of((1 - feat) * share, share), share), :], sems.at[0]
    )
    copy.start()
    received = (own_ref[...] + partner_ref[...].astype(F32)).astype(BF16)
    total = None
    for weight, second, col in ((wa_ref, va_ref, 0), (wb_ref, vb_ref, half)):
        pre = pre_ref[:, col : col + half] + dot(received, weight[...])
        part = dot(silu(pre).astype(BF16), second[...])
        total = part if total is None else total + part
    update = layer_norm(total, gain_ref[...].astype(F32).reshape(1, width))
    fresh = (node_ref[...].astype(F32) + update).astype(BF16)
    out_ref[...] = jnp.where(feat == 0, fresh[:, : width // 2], fresh[:, width // 2 :])
    copy.wait()


def whole(shape):
    return pl.BlockSpec(shape, lambda *_: (0,) * len(shape))


def in_hbm(array):
    return pltpu.with_memory_space_constraint(array, pltpu.HBM)


def call(kernel, grid, where, in_specs, out_specs, out_shape, operands, flops, limit, scratch=(), aliases=None):
    return pl.pallas_call(
        kernel,
        grid_spec=pltpu.PrefetchScalarGridSpec(
            num_scalar_prefetch=len(where),
            grid=grid,
            in_specs=in_specs,
            out_specs=out_specs,
            scratch_shapes=list(scratch),
        ),
        out_shape=out_shape,
        input_output_aliases=aliases or {},
        cost_estimate=pl.CostEstimate(flops=flops, bytes_accessed=4 * MIB, transcendentals=0),
        compiler_params=pltpu.CompilerParams(vmem_limit_bytes=limit * MIB),
    )(*where, *operands)


def exchange_pairs(count):
    across = [(p + 1 if p % 2 else p - 1) % count for p in range(count)]
    rounds = [([p ^ 1 for p in range(count)], across)]
    for distance in range(2, count, 2):
        rounds.append(([p ^ distance for p in range(count)], [p ^ (distance + 1) for p in range(count)]))
    return [
        [(2 * p + feat, 2 * targets[p] + feat) for p in range(count) for feat, targets in enumerate(some)]
        for some in rounds
    ]


def on_device(
    node_latent,
    edge_latent,
    edge_senders,
    edge_receivers,
    halo_rows,
    coarse_rows,
    edge_counts,
    edge_w1,
    edge_w2,
    edge_gain,
    node_w1,
    node_w2,
    node_gain,
):
    node_count, width = node_latent.shape
    half = width // 2
    edge_count = edge_latent.shape[0]
    halo, coarse = halo_rows.shape[1], coarse_rows.shape[0]
    patches = lax.axis_size("patch")
    both = ("patch", "feat")
    layout = Layout(patches, node_count, halo, coarse)
    group, used, local_slots = layout.group, layout.used, layout.local_slots
    share = edge_count // 2
    block = 512
    steps = share // block
    where = (
        jnp.stack(
            [
                lax.axis_index("feat").astype(jnp.int32),
                lax.axis_index("patch").astype(jnp.int32),
                edge_counts[0],
            ]
        ),
    )
    anywhere = pl.BlockSpec(memory_space=pl.ANY)
    dma = pltpu.SemaphoreType.DMA
    index_rows = edge_count // 128

    def shape(rows, columns, kind):
        return jax.ShapeDtypeStruct((rows, columns), kind)

    def swap(values):
        return lax.ppermute(values, "feat", FEAT_SWAP)

    edge_w1_b, edge_w2_b, node_w1_b, node_w2_b = [swap(w) for w in (edge_w1, edge_w2, node_w1, node_w2)]
    node_latent, edge_latent, halo_rows, coarse_rows, edge_w1, edge_w2, node_w1, node_w2, edge_gain, node_gain = [
        in_hbm(array)
        for array in (
            node_latent,
            edge_latent,
            halo_rows,
            coarse_rows,
            edge_w1,
            edge_w2,
            node_w1,
            node_w2,
            edge_gain,
            node_gain,
        )
    ]
    senders, receivers = [in_hbm(rows.reshape(index_rows, 128)) for rows in (edge_senders, edge_receivers)]

    lent = call(
        lend_kernel,
        (1,),
        where,
        [anywhere] * 3,
        whole((halo + coarse, width)),
        shape(halo + coarse, width, BF16),
        (node_latent, halo_rows, coarse_rows),
        2 * node_count * (halo + coarse) * width,
        8,
        scratch=[
            pltpu.VMEM((node_count, width), BF16),
            pltpu.VMEM((2, halo), jnp.int32),
            pltpu.VMEM((coarse,), jnp.int32),
            dma((3,)),
        ],
    )
    pairs = exchange_pairs(patches)
    arrived = [lax.ppermute(lent, both, pairs[0])]
    for some in pairs[1:]:
        arrived.append(lax.ppermute(lent[halo:], both, some))
    table_mine = jnp.concatenate(arrived, axis=0)
    table_theirs = swap(table_mine)

    my_rows = lambda i, where: (where[0] * steps + i, 0)
    step_rows = lambda i, where: (i, 0)

    pre = call(
        functools.partial(local_kernel, layout=layout, share=share),
        (steps,),
        where,
        [
            anywhere,
            anywhere,
            whole((halo + coarse, width)),
            whole((3 * width, half)),
            pl.BlockSpec((block, width), my_rows),
            whole((index_rows, 128)),
            whole((index_rows, 128)),
        ],
        pl.BlockSpec((block, width), step_rows),
        shape(share, width, F32),
        (node_latent, edge_w1, lent, edge_w1_b, edge_latent, senders, receivers),
        2 * width * width * share + 4 * used * width * width + 4 * share * local_slots * width,
        LIMIT,
        scratch=[
            pltpu.VMEM((2 * local_slots, width), BF16),
            pltpu.VMEM((node_count, width), BF16),
            pltpu.VMEM((3 * width, half), BF16),
            dma((2,)),
        ],
    )

    fresh, edges, edges_other, group_mine, group_other = call(
        functools.partial(edge_kernel, layout=layout, share=share),
        (steps,),
        where,
        [
            pl.BlockSpec((block, width), step_rows),
            pl.BlockSpec((block, width), my_rows),
            whole((index_rows, 128)),
            whole((index_rows, 128)),
            whole((group, width)),
            whole((group, width)),
            anywhere,
            whole((3 * width, half)),
            anywhere,
            whole((half, width)),
            whole((width,)),
        ],
        [
            pl.BlockSpec((block, width), step_rows),
            pl.BlockSpec((block, half), my_rows),
            pl.BlockSpec((block, half), step_rows),
            whole((group, width)),
            whole((group, width)),
        ],
        [
            shape(share, width, BF16),
            shape(edge_count, half, BF16),
            shape(share, half, BF16),
            shape(group, width, F32),
            shape(group, width, BF16),
        ],
        (
            pre,
            edge_latent,
            senders,
            receivers,
            table_mine,
            table_theirs,
            edge_w1,
            edge_w1_b,
            edge_w2,
            edge_w2_b,
            edge_gain,
        ),
        2 * share * width * (width + 6 * group) + 8 * group * width * width,
        LIMIT,
        scratch=[
            pltpu.VMEM((4 * group, width), BF16),
            pltpu.VMEM((2 * group, width), F32),
            pltpu.VMEM((3 * width, half), BF16),
            pltpu.VMEM((half, width), BF16),
            dma((2,)),
        ],
    )

    group_theirs = swap(group_other)
    sizes = [halo + coarse] + [coarse] * (len(pairs) - 1)
    outgoing = call(
        merge_kernel,
        (1,),
        (),
        [whole((group, width))] * 2,
        [whole((rows, width)) for rows in sizes],
        [shape(rows, width, BF16) for rows in sizes],
        (group_mine, group_theirs),
        group * width,
        8,
    )
    *outgoing, edges_other, fresh = lax.optimization_barrier((*outgoing, edges_other, fresh))
    back = [lax.ppermute(part, both, some) for part, some in zip(outgoing, pairs)]
    edges_theirs = swap(edges_other)
    local_sums, node_pre = call(
        functools.partial(local_sums_kernel, layout=layout, share=share),
        (steps,),
        where,
        [
            pl.BlockSpec((block, width), step_rows),
            whole((index_rows, 128)),
            anywhere,
            anywhere,
            whole((width, half)),
        ],
        [whole((used, width)), whole((node_count, width))],
        [shape(used, width, F32), shape(node_count, width, F32)],
        (fresh, receivers, node_latent, node_w1, node_w1_b),
        2 * share * width * used + 2 * node_count * width * width,
        16,
        scratch=[
            pltpu.VMEM((node_count, width), BF16),
            pltpu.VMEM((width, half), BF16),
            dma((2,)),
        ],
    )
    own, rounded = call(
        receive_kernel,
        (1,),
        where,
        [whole((used, width)), whole((2, halo)), whole((coarse,))] + [whole((rows, width)) for rows in sizes],
        [whole((node_count, width))] * 2,
        [shape(node_count, width, F32), shape(node_count, width, BF16)],
        (local_sums, halo_rows, coarse_rows, *back),
        2 * node_count * width * (group + coarse),
        16,
    )
    partner = swap(rounded)
    upper_half = pl.BlockSpec((width, half), lambda *_: (1, 0))
    nodes_out, edges_out = call(
        node_kernel,
        (1,),
        where,
        [
            whole((node_count, width)),
            whole((node_count, width)),
            whole((node_count, width)),
            whole((node_count, width)),
            upper_half,
            upper_half,
            whole((half, width)),
            whole((half, width)),
            whole((width,)),
            anywhere,
            anywhere,
        ],
        [whole((node_count, half)), anywhere],
        [shape(node_count, half, BF16), shape(edge_count, half, BF16)],
        (
            node_latent,
            own,
            partner,
            node_pre,
            node_w1,
            node_w1_b,
            node_w2,
            node_w2_b,
            node_gain,
            edges,
            edges_theirs,
        ),
        4 * node_count * width * width,
        16,
        scratch=[dma((1,))],
        aliases={10: 1},
    )
    return nodes_out, edges_out


def solution(mesh):
    placed = (
        P(("member", "patch"), None),
        P(("member", "patch"), None),
        P(("member", "patch")),
        P(("member", "patch")),
        P(("member", "patch"), None),
        P(("member", "patch")),
        P(("member", "patch")),
        P(None, "feat"),
        P("feat", None),
        P(),
        P(None, "feat"),
        P("feat", None),
        P(),
    )
    return jax.shard_map(
        on_device,
        mesh=mesh,
        in_specs=placed,
        out_specs=(P(("member", "patch"), "feat"), P(("member", "patch"), "feat")),
        check_vma=False,
    )
```

time: 74.2 us -> 57.9 us (0.78)
  the two profiles are of different devices: /device:TPU:25 before, /device:TPU:0 now
where the time goes in v2:
time: 57.9 us; the launch traced here: 57.6 us
  Pallas kernels  32.9 us (57%)
  starting transfers between devices  16.1 us (28%)
  waiting for transfers between devices  7.15 us (12%)
  between operations  1.39 us (2%)
    pallas_call x7, Pallas kernels, call(): pl.pallas_call(kernel, grid_spec=pltpu.PrefetchScalarGridSpec(num_scalar_...  32.9 us
    ppermute x4, starting transfers between devices, on_device(): lax.ppermute(part, both, some)  4.95 us
    ppermute x3, starting transfers between devices, on_device(): arrived.append(lax.ppermute(lent[halo:], both, some))  4.39 us
    ppermute x8, starting transfers between devices, swap(): return lax.ppermute(values, 'feat', FEAT_SWAP)  4.15 us
    ppermute x8, waiting for transfers between devices, swap(): return lax.ppermute(values, 'feat', FEAT_SWAP)  3.24 us
    ppermute x3, waiting for transfers between devices, on_device(): arrived.append(lax.ppermute(lent[halo:], both, some))  2.8 us
    ppermute x1, starting transfers between devices, on_device(): arrived = [lax.ppermute(lent, both, pairs[0])]  2.59 us
  transfers between devices with their start and end apart: 16, of which 5 were waited for; matrix products, arithmetic and copies ran while one was open for 0% of the time, Pallas kernels for 50%

profile of v2, /device:TPU:0, one launch (start us, length us, event | category | flops | bytes accessed | tf_op | source)
XLA Modules:
  0.0 57.6 jit_solution(8168819185775156765)
XLA Ops:
  0.6 0.5 collective-permute-start
  1.8 0.1 pad_add_fusion.where_ref
  1.9 2.0 %shard_map.140.lent_ref = bf16[160,512]{1,0:T(8,128)(2,1)S(1)} custom-call(s32[3]{0:T(128)S(1)} %pad_add_fusion.where_ref, bf16[640,512]{1,0:T(8,128)(2,1)} %node_ref.7, s32[2,128]{1,0:T(2,128)} %halo_ref.3, s32[32]{0:T(128)} %coarse_ref.3), custom_call_target="tpu_custom_call" | custom-call | flops 104857600 | bytes 4194304 | tf_op jit(solution)/shard_map/pallas_call | solution.py:316
  3.9 2.6 %collective-permute-start.1 = (bf16[160,512]{1,0:T(8,128)(2,1)S(1)}, bf16[160,512]{1,0:T(8,128)(2,1)S(1)}, u32[]{:S(2)}, u32[]{:S(2)}) collective-permute-start(bf16[160,512]{1,0:T(8,128)(2,1)S(1)} %shard_map.140.lent_ref), channel_id=1, source_target_pairs={{0,2},{1,15},{2,0},{3,5},{4,6},{5,3},{6,4},{7,9},{8,10},{9,7},{10,... | collective-permute-start | bytes 491528 | tf_op jit(solution)/shard_map/ppermute | solution.py:424
  6.5 1.6 %collective-permute-start.2 = (bf16[32,512]{1,0:T(8,128)(2,1)S(1)}, bf16[32,512]{1,0:T(8,128)(2,1)S(1)}, u32[]{:S(2)}, u32[]{:S(2)}) collective-permute-start(bf16[32,512]{1,0:T(8,128)(2,1)S(1)} %slice.6), channel_id=1, source_target_pairs={{0,4},{1,7},{2,6},{3,5},{4,0},{5,3},{6,2},{7,1},{8,12},{9,15},{10,... | collective-permute-start | bytes 98312 | tf_op jit(solution)/shard_map/ppermute | solution.py:426
  8.0 2.6 %collective-permute-start.3 = (bf16[32,512]{1,0:T(8,128)(2,1)S(1)}, bf16[32,512]{1,0:T(8,128)(2,1)S(1)}, u32[]{:S(2)}, u32[]{:S(2)}) collective-permute-start(bf16[32,512]{1,0:T(8,128)(2,1)S(1)} %slice.6), channel_id=1, source_target_pairs={{0,8},{1,11},{2,10},{3,9},{4,12},{5,15},{6,14},{7,13},{8,0},{9,3},... | collective-permute-start | bytes 98312 | tf_op jit(solution)/shard_map/ppermute | solution.py:426
  10.6 0.2 collective-permute-start.4
  10.9 0.6 %collective-permute-done.1 = bf16[160,512]{1,0:T(8,128)(2,1)S(1)} collective-permute-done((bf16[160,512]{1,0:T(8,128)(2,1)S(1)}, bf16[160,512]{1,0:T(8,128)(2,1)S(1)}, u32[]{:S(2)}, u32[]{:S(2)}) %collective-permute-start.1) | collective-permute-done | bytes 163872 | tf_op jit(solution)/shard_map/ppermute | solution.py:424
  11.5 1.7 %collective-permute-start.6 = (bf16[256,512]{1,0:T(8,128)(2,1)}, bf16[256,512]{1,0:T(8,128)(2,1)S(1)}, u32[]{:S(2)}, u32[]{:S(2)}) collective-permute-start(bf16[256,512]{1,0:T(8,128)(2,1)} %va_ref.2), channel_id=1, source_target_pairs={{0,1},{1,0},{2,3},{3,2},{4,5},{5,4},{6,7},{7,6},{8,9},{9,8},{10,11... | collective-permute-start | bytes 786440 | tf_op jit(solution)/shard_map/ppermute | solution.py:386
  13.1 0.0 collective-permute-done.2
  13.1 0.4 collective-permute-start.8
  13.6 0.0 collective-permute-done.3
  13.6 2.8 %collective-permute-done.4 = bf16[32,512]{1,0:T(8,128)(2,1)S(1)} collective-permute-done((bf16[32,512]{1,0:T(8,128)(2,1)S(1)}, bf16[32,512]{1,0:T(8,128)(2,1)S(1)}, u32[]{:S(2)}, u32[]{:S(2)}) %collective-permute-start.4) | collective-permute-done | bytes 32800 | tf_op jit(solution)/shard_map/ppermute | solution.py:426
  16.4 0.2 collective-permute-start.5
  16.5 9.2 %shard_map.141.pre_ref = f32[2048,512]{1,0:T(8,128)S(1)} custom-call(s32[3]{0:T(128)S(1)} %pad_add_fusion.where_ref, bf16[640,512]{1,0:T(8,128)(2,1)} %node_ref.7, bf16[1536,256]{1,0:T(8,128)(2,1)} %wa_ref.5, bf16[160,512]{1,0:T(8,128)(2,1)S(1)} %shard_map.140.lent_ref, bf16[1536,256]{1,0:T(8,128)(2,1)S(1)} %collective-permute-done.wb_ref, ...), custom_call_target="tpu_custom_call" | custom-call | flops 4999610368 | bytes 4194304 | tf_op jit(solution)/shard_map/pallas_call | solution.py:316
  25.7 0.0 collective-permute-done.6.vb_ref
  25.8 11.7 %shard_map.142 = (bf16[2048,512]{1,0:T(8,128)(2,1)S(1)}, bf16[4096,256]{1,0:T(8,128)(2,1)}, bf16[2048,256]{1,0:T(8,128)(2,1)S(1)}, f32[256,512]{1,0:T(8,128)S(1)}, bf16[256,512]{1,0:T(8,128)(2,1)S(1)}) custom-call(s32[3]{0:T(128)S(1)} %pad_add_fusion.where_ref, f32[2048,512]{1,0:T(8,128)S(1)} %shard_map.141.pre_ref, bf16[4096,512]{1,0:T(8,128)(2,1)} %latent_ref.3, ...), custom_call_target="tpu_custom_call" | custom-call | flops 4831838208 | bytes 4194304 | tf_op jit(solution)/shard_map/pallas_call | solution.py:316
  37.4 0.4 collective-permute-start.7
  37.8 1.2 %collective-permute-done.7.theirs_ref = bf16[256,512]{1,0:T(8,128)(2,1)S(1)} collective-permute-done((bf16[256,512]{1,0:T(8,128)(2,1)S(1)}, bf16[256,512]{1,0:T(8,128)(2,1)S(1)}, u32[]{:S(2)}, u32[]{:S(2)}) %collective-permute-start.7) | collective-permute-done | bytes 262176 | tf_op jit(solution)/shard_map/ppermute | solution.py:386
  39.1 0.0 copy-start
  39.1 0.4 collective-permute-start.15
  39.5 0.6 collective-permute-start.9
  40.0 0.3 collective-permute-start.10
  40.3 2.9 %collective-permute-start.11 = (bf16[32,512]{1,0:T(8,128)(2,1)S(1)}, bf16[32,512]{1,0:T(8,128)(2,1)S(1)}, u32[]{:S(2)}, u32[]{:S(2)}) collective-permute-start(bf16[32,512]{1,0:T(8,128)(2,1)S(1)} %get-tuple-element.33), channel_id=1, source_target_pairs={{0,8},{1,11},{2,10},{3,9},{4,12},{5,15},{6,14},{7,13},{8,0},{9,3},... | collective-permute-start | bytes 98312 | tf_op jit(solution)/shard_map/ppermute | solution.py:528
  43.3 1.2 %collective-permute-start.12 = (bf16[32,512]{1,0:T(8,128)(2,1)S(1)}, bf16[32,512]{1,0:T(8,128)(2,1)S(1)}, u32[]{:S(2)}, u32[]{:S(2)}) collective-permute-start(bf16[32,512]{1,0:T(8,128)(2,1)S(1)} %get-tuple-element.34), channel_id=1, source_target_pairs={{0,12},{1,15},{2,14},{3,13},{4,8},{5,11},{6,10},{7,9},{8,4},{9,7},... | collective-permute-start | bytes 98312 | tf_op jit(solution)/shard_map/ppermute | solution.py:528
  44.4 4.0 %shard_map.144 = (f32[672,512]{1,0:T(8,128)S(1)}, f32[640,512]{1,0:T(8,128)S(1)}) custom-call(s32[3]{0:T(128)S(1)} %pad_add_fusion.where_ref, bf16[2048,512]{1,0:T(8,128)(2,1)S(1)} %get-tuple-element.29.fresh_ref, s32[32,128]{1,0:T(8,128)} %bitcast.8, bf16[640,512]{1,0:T(8,128)(2,1)} %node_ref.7, bf16[1024,256]{1,0:T(8,128)(2,1)} %wa_ref.7, ...), custom_call_target="tpu_custom_call" | custom-call | flops 1744830464 | bytes 4194304 | tf_op jit(solution)/shard_map/pallas_call | solution.py:316
  48.5 0.5 collective-permute-done.12.refs_3_
  49.0 1.8 %shard_map.145 = (f32[640,512]{1,0:T(8,128)S(1)}, bf16[640,512]{1,0:T(8,128)(2,1)S(1)}) custom-call(s32[3]{0:T(128)S(1)} %pad_add_fusion.where_ref, f32[672,512]{1,0:T(8,128)S(1)} %get-tuple-element.30.sums_ref, s32[2,128]{1,0:T(2,128)} %halo_ref.3, s32[32]{0:T(128)} %coarse_ref.3, bf16[160,512]{1,0:T(8,128)(2,1)S(1)} %collective-permute-done.9.refs_0_, ...), custom_call_target="tpu_custom_call" | custom-call | flops 188743680 | bytes 4194304 | tf_op jit(solution)/shard_map/pallas_call | solution.py:316
  50.8 0.5 collective-permute-start.13
  51.3 0.1 collective-permute-start.14
  51.4 2.0 %collective-permute-done.14.vb_ref = bf16[256,512]{1,0:T(8,128)(2,1)S(1)} collective-permute-done((bf16[256,512]{1,0:T(8,128)(2,1)S(1)}, bf16[256,512]{1,0:T(8,128)(2,1)S(1)}, u32[]{:S(2)}, u32[]{:S(2)}) %collective-permute-start.14) | collective-permute-done | bytes 262176 | tf_op jit(solution)/shard_map/ppermute | solution.py:386
  53.4 4.2 %shard_map.146 = (bf16[640,256]{1,0:T(8,128)(2,1)}, bf16[4096,256]{1,0:T(8,128)(2,1)}) custom-call(s32[3]{0:T(128)S(1)} %pad_add_fusion.where_ref, bf16[640,512]{1,0:T(8,128)(2,1)} %node_ref.7, f32[640,512]{1,0:T(8,128)S(1)} %get-tuple-element.35.own_ref, bf16[640,512]{1,0:T(8,128)(2,1)S(1)} %collective-permute-done.13.partner_ref, ...), custom_call_target="tpu_custom_call", output_to_operand_aliasing={{1}: (10, {})} | custom-call | flops 671088640 | bytes 4194304 | tf_op jit(solution)/shard_map/pallas_call | solution.py:316
  (15 shorter events, 0.1 us)
Async XLA Ops:
  0.6 15.9 %collective-permute-start = (bf16[1536,256]{1,0:T(8,128)(2,1)}, bf16[1536,256]{1,0:T(8,128)(2,1)S(1)}, u32[]{:S(2)}, u32[]{:S(2)}) collective-permute-start(bf16[1536,256]{1,0:T(8,128)(2,1)} %wa_ref.5), channel_id=1, source_target_pairs={{0,1},{1,0},{2,3},{3,2},{4,5},{5,4},{6,7},{7,6},{8,9},{9,8},{10,11... | collective-permute-start | bytes 2359304 | tf_op jit(solution)/shard_map/ppermute | solution.py:386
  3.9 7.6 %collective-permute-start.1 = (bf16[160,512]{1,0:T(8,128)(2,1)S(1)}, bf16[160,512]{1,0:T(8,128)(2,1)S(1)}, u32[]{:S(2)}, u32[]{:S(2)}) collective-permute-start(bf16[160,512]{1,0:T(8,128)(2,1)S(1)} %shard_map.140.lent_ref), channel_id=1, source_target_pairs={{0,2},{1,15},{2,0},{3,5},{4,6},{5,3},{6,4},{7,9},{8,10},{9,7},{10,... | collective-permute-start | bytes 491528 | tf_op jit(solution)/shard_map/ppermute | solution.py:424
  6.5 6.7 %collective-permute-start.2 = (bf16[32,512]{1,0:T(8,128)(2,1)S(1)}, bf16[32,512]{1,0:T(8,128)(2,1)S(1)}, u32[]{:S(2)}, u32[]{:S(2)}) collective-permute-start(bf16[32,512]{1,0:T(8,128)(2,1)S(1)} %slice.6), channel_id=1, source_target_pairs={{0,4},{1,7},{2,6},{3,5},{4,0},{5,3},{6,2},{7,1},{8,12},{9,15},{10,... | collective-permute-start | bytes 98312 | tf_op jit(solution)/shard_map/ppermute | solution.py:426
  8.0 5.5 %collective-permute-start.3 = (bf16[32,512]{1,0:T(8,128)(2,1)S(1)}, bf16[32,512]{1,0:T(8,128)(2,1)S(1)}, u32[]{:S(2)}, u32[]{:S(2)}) collective-permute-start(bf16[32,512]{1,0:T(8,128)(2,1)S(1)} %slice.6), channel_id=1, source_target_pairs={{0,8},{1,11},{2,10},{3,9},{4,12},{5,15},{6,14},{7,13},{8,0},{9,3},... | collective-permute-start | bytes 98312 | tf_op jit(solution)/shard_map/ppermute | solution.py:426
  10.6 5.7 %collective-permute-start.4 = (bf16[32,512]{1,0:T(8,128)(2,1)S(1)}, bf16[32,512]{1,0:T(8,128)(2,1)S(1)}, u32[]{:S(2)}, u32[]{:S(2)}) collective-permute-start(bf16[32,512]{1,0:T(8,128)(2,1)S(1)} %slice.6), channel_id=1, source_target_pairs={{0,12},{1,15},{2,14},{3,13},{4,8},{5,11},{6,10},{7,9},{8,4},{9,7},... | collective-permute-start | bytes 98312 | tf_op jit(solution)/shard_map/ppermute | solution.py:426
  11.5 14.3 %collective-permute-start.6 = (bf16[256,512]{1,0:T(8,128)(2,1)}, bf16[256,512]{1,0:T(8,128)(2,1)S(1)}, u32[]{:S(2)}, u32[]{:S(2)}) collective-permute-start(bf16[256,512]{1,0:T(8,128)(2,1)} %va_ref.2), channel_id=1, source_target_pairs={{0,1},{1,0},{2,3},{3,2},{4,5},{5,4},{6,7},{7,6},{8,9},{9,8},{10,11... | collective-permute-start | bytes 786440 | tf_op jit(solution)/shard_map/ppermute | solution.py:386
  13.1 30.1 %collective-permute-start.8 = (bf16[1024,256]{1,0:T(8,128)(2,1)}, bf16[1024,256]{1,0:T(8,128)(2,1)S(1)}, u32[]{:S(2)}, u32[]{:S(2)}) collective-permute-start(bf16[1024,256]{1,0:T(8,128)(2,1)} %wa_ref.7), channel_id=1, source_target_pairs={{0,1},{1,0},{2,3},{3,2},{4,5},{5,4},{6,7},{7,6},{8,9},{9,8},{10,11... | collective-permute-start | bytes 1572872 | tf_op jit(solution)/shard_map/ppermute | solution.py:386
  16.4 9.4 %collective-permute-start.5 = (bf16[256,512]{1,0:T(8,128)(2,1)S(1)}, bf16[256,512]{1,0:T(8,128)(2,1)S(1)}, u32[]{:S(2)}, u32[]{:S(2)}) collective-permute-start(bf16[256,512]{1,0:T(8,128)(2,1)S(1)} %constant_dynamic-update-slice_fusion.mine_ref), channel_id=1, source_target_pairs={{0,1},{1,0},{2,3},{3,2},{4,5},{5,4},{6,7},{7,6},{8,9},{9,8},{10,11... | collective-permute-start | bytes 786440 | tf_op jit(solution)/shard_map/ppermute | solution.py:386
  37.4 1.6 %collective-permute-start.7 = (bf16[256,512]{1,0:T(8,128)(2,1)S(1)}, bf16[256,512]{1,0:T(8,128)(2,1)S(1)}, u32[]{:S(2)}, u32[]{:S(2)}) collective-permute-start(bf16[256,512]{1,0:T(8,128)(2,1)S(1)} %get-tuple-element.22), channel_id=1, source_target_pairs={{0,1},{1,0},{2,3},{3,2},{4,5},{5,4},{6,7},{7,6},{8,9},{9,8},{10,11... | collective-permute-start | bytes 786440 | tf_op jit(solution)/shard_map/ppermute | solution.py:386
  39.1 12.2 %copy-start = (bf16[256,512]{1,0:T(8,128)(2,1)S(1)}, bf16[256,512]{1,0:T(8,128)(2,1)}, u32[]{:S(2)}) copy-start(bf16[256,512]{1,0:T(8,128)(2,1)} %va_ref.3) | copy-start | bytes 786436
  39.1 14.3 %collective-permute-start.15 = (bf16[2048,256]{1,0:T(8,128)(2,1)S(1)}, bf16[2048,256]{1,0:T(8,128)(2,1)S(1)}, u32[]{:S(2)}, u32[]{:S(2)}) collective-permute-start(bf16[2048,256]{1,0:T(8,128)(2,1)S(1)} %get-tuple-element.39), channel_id=1, source_target_pairs={{0,1},{1,0},{2,3},{3,2},{4,5},{5,4},{6,7},{7,6},{8,9},{9,8},{10,11... | collective-permute-start | bytes 3145736 | tf_op jit(solution)/shard_map/ppermute | solution.py:386
  39.5 9.5 %collective-permute-start.9 = (bf16[160,512]{1,0:T(8,128)(2,1)S(1)}, bf16[160,512]{1,0:T(8,128)(2,1)S(1)}, u32[]{:S(2)}, u32[]{:S(2)}) collective-permute-start(bf16[160,512]{1,0:T(8,128)(2,1)S(1)} %get-tuple-element.31), channel_id=1, source_target_pairs={{0,2},{1,15},{2,0},{3,5},{4,6},{5,3},{6,4},{7,9},{8,10},{9,7},{10,... | collective-permute-start | bytes 491528 | tf_op jit(solution)/shard_map/ppermute | solution.py:528
  40.0 8.4 %collective-permute-start.10 = (bf16[32,512]{1,0:T(8,128)(2,1)S(1)}, bf16[32,512]{1,0:T(8,128)(2,1)S(1)}, u32[]{:S(2)}, u32[]{:S(2)}) collective-permute-start(bf16[32,512]{1,0:T(8,128)(2,1)S(1)} %get-tuple-element.32), channel_id=1, source_target_pairs={{0,4},{1,7},{2,6},{3,5},{4,0},{5,3},{6,2},{7,1},{8,12},{9,15},{10,... | collective-permute-start | bytes 98312 | tf_op jit(solution)/shard_map/ppermute | solution.py:528
  40.3 8.1 %collective-permute-start.11 = (bf16[32,512]{1,0:T(8,128)(2,1)S(1)}, bf16[32,512]{1,0:T(8,128)(2,1)S(1)}, u32[]{:S(2)}, u32[]{:S(2)}) collective-permute-start(bf16[32,512]{1,0:T(8,128)(2,1)S(1)} %get-tuple-element.33), channel_id=1, source_target_pairs={{0,8},{1,11},{2,10},{3,9},{4,12},{5,15},{6,14},{7,13},{8,0},{9,3},... | collective-permute-start | bytes 98312 | tf_op jit(solution)/shard_map/ppermute | solution.py:528
  43.3 5.7 %collective-permute-start.12 = (bf16[32,512]{1,0:T(8,128)(2,1)S(1)}, bf16[32,512]{1,0:T(8,128)(2,1)S(1)}, u32[]{:S(2)}, u32[]{:S(2)}) collective-permute-start(bf16[32,512]{1,0:T(8,128)(2,1)S(1)} %get-tuple-element.34), channel_id=1, source_target_pairs={{0,12},{1,15},{2,14},{3,13},{4,8},{5,11},{6,10},{7,9},{8,4},{9,7},... | collective-permute-start | bytes 98312 | tf_op jit(solution)/shard_map/ppermute | solution.py:528
  50.8 2.6 %collective-permute-start.13 = (bf16[640,512]{1,0:T(8,128)(2,1)S(1)}, bf16[640,512]{1,0:T(8,128)(2,1)S(1)}, u32[]{:S(2)}, u32[]{:S(2)}) collective-permute-start(bf16[640,512]{1,0:T(8,128)(2,1)S(1)} %get-tuple-element.36), channel_id=1, source_target_pairs={{0,1},{1,0},{2,3},{3,2},{4,5},{5,4},{6,7},{7,6},{8,9},{9,8},{10,11... | collective-permute-start | bytes 1966088 | tf_op jit(solution)/shard_map/ppermute | solution.py:386
  51.3 2.1 %collective-permute-start.14 = (bf16[256,512]{1,0:T(8,128)(2,1)S(1)}, bf16[256,512]{1,0:T(8,128)(2,1)S(1)}, u32[]{:S(2)}, u32[]{:S(2)}) collective-permute-start(bf16[256,512]{1,0:T(8,128)(2,1)S(1)} %copy-done), channel_id=1, source_target_pairs={{0,1},{1,0},{2,3},{3,2},{4,5},{5,4},{6,7},{7,6},{8,9},{9,8},{10,11... | collective-permute-start | bytes 786440 | tf_op jit(solution)/shard_map/ppermute | solution.py:386

commit v3 on v0

v3 whole, which is shorter than its diff:
```python
import functools

import jax
import jax.numpy as jnp
from jax import lax
from jax.experimental import pallas as pl
from jax.experimental.pallas import tpu as pltpu
from jax.sharding import PartitionSpec as P

EPSILON = 1e-05
F32 = jnp.float32
BF16 = jnp.bfloat16
MIB = 1024 * 1024
LIMIT = 30
DEAD = -1
NOWHERE = -2
FEAT_SWAP = [(0, 1), (1, 0)]


def silu_of_double(half_v):
    return half_v + half_v * jnp.tanh(half_v)


def dot(a, b):
    return jnp.dot(a, b, preferred_element_type=F32)


def layer_norm(pre, gain, keep=None):
    width = pre.shape[1]
    center = jnp.sum(pre, axis=1, keepdims=True) * (1.0 / width)
    square = jnp.sum(pre * pre, axis=1, keepdims=True) * (1.0 / width)
    scale = lax.rsqrt(square - center * center + EPSILON)
    if keep is not None:
        scale = jnp.where(keep, scale, 0.0)
    return (pre - center) * scale * gain


def index_columns(index):
    return [
        jnp.transpose(jnp.broadcast_to(index[j : j + 1, :], (128, 128))) for j in range(index.shape[0])
    ]


def one_hot_rows(columns, first, count):
    lanes = lax.broadcasted_iota(jnp.int32, (128, 128), 1) + first
    return jnp.concatenate(
        [
            jnp.concatenate(
                [(column == lanes + at).astype(F32).astype(BF16) for at in range(0, count, 128)], axis=1
            )
            for column in columns
        ],
        axis=0,
    )


def one_hot_columns(index_row, first, count):
    entries = index_row.shape[1]
    rows = lax.broadcasted_iota(jnp.int32, (count, entries), 0) + first
    return (rows == jnp.broadcast_to(index_row, (count, entries))).astype(F32).astype(BF16)


def flat_row(index):
    return jnp.concatenate([index[j : j + 1, :] for j in range(index.shape[0])], axis=1)


def copies(pairs, sems):
    made = [pltpu.make_async_copy(source, target, sems.at[i]) for i, (source, target) in enumerate(pairs)]
    for copy in made:
        copy.start()
    return made


class Layout:
    def __init__(self, patches, node_count, halo, coarse):
        self.patches, self.node_count, self.halo, self.coarse = patches, node_count, halo, coarse
        self.group = halo + coarse * (patches // 2)
        self.used = node_count + coarse
        self.local_slots = -(-self.used // 256) * 256

    def slots(self, rows, patch):
        node_count, halo, coarse, group = self.node_count, self.halo, self.coarse, self.group
        at = rows - (node_count + 2 * halo)
        owner, entry = lax.shift_right_arithmetic(at, coarse.bit_length() - 1), at & (coarse - 1)
        distance = patch ^ owner
        odd = patch & 1
        place = self.local_slots + (distance & 1) * group + halo + coarse * lax.shift_right_arithmetic(distance, 1)
        place = jnp.where(distance == 0, node_count, place)
        place = jnp.where(distance == 1, self.local_slots + halo, place) + entry
        lower = self.local_slots + (1 - odd) * group - node_count + rows
        upper = self.local_slots + odd * group - (node_count + halo) + rows
        lower = jnp.where(patch == 0, NOWHERE, lower)
        upper = jnp.where(patch == self.patches - 1, NOWHERE, upper)
        place = jnp.where(rows < node_count + 2 * halo, upper, place)
        place = jnp.where(rows < node_count + halo, lower, place)
        return jnp.where(rows < node_count, rows, place)


def lent_list(lists):
    which = (lax.axis_index("feat") + lax.axis_index("patch")) & 1
    return jnp.where(which == 0, lists[0:1], lists[1:2])


def lend_kernel(node_ref, halo_ref, coarse_ref, lent_ref, node, halo, coarse, sems):
    for copy in copies(((halo_ref, halo), (coarse_ref, coarse), (node_ref, node)), sems):
        copy.wait()
    index_row = jnp.concatenate([lent_list(halo[...]), coarse[...].reshape(1, -1)], axis=1)
    lent_ref[...] = lax.dot_general(
        one_hot_columns(index_row, 0, node.shape[0]),
        node[...],
        (((0,), (0,)), ((), ())),
        preferred_element_type=F32,
    ).astype(BF16)


def local_kernel(
    node,
    lent_ref,
    wb_ref,
    limit,
    latent_hbm,
    send_hbm,
    recv_hbm,
    wa_hbm,
    *refs,
    layout,
    block,
):
    count = (len(refs) - 8) // 2
    more_hbm, refs = refs[:count], refs[count:]
    pre_ref, latent, send, recv, wa, *more = refs[: 5 + count]
    table, sems, block_sems = refs[5 + count :]
    share, width = latent.shape
    half = wa.shape[1]
    feat, patch = lax.axis_index("feat"), lax.axis_index("patch")
    local_slots, used = layout.local_slots, layout.used
    rows128 = share // 128
    mine = pl.ds(pl.multiple_of(feat * rows128, rows128), rows128)
    first = copies(
        (
            (wa_hbm, wa),
            (send_hbm.at[mine, :], send),
            (recv_hbm.at[mine, :], recv),
        ),
        sems,
    )
    blocks = copies(
        [
            (
                latent_hbm.at[pl.ds(pl.multiple_of(feat * share + at, block), block), :],
                latent.at[pl.ds(at, block), :],
            )
            for at in range(0, share, block)
        ],
        block_sems,
    )
    rest = copies(list(zip(more_hbm, more)), sems.at[pl.ds(3, count)])
    for copy in first:
        copy.wait()
    rows_in = jnp.concatenate([node[...], lent_ref[lent_ref.shape[0] - layout.coarse :, :]], axis=0)
    for side in range(2):
        base = side * local_slots
        rows = slice((side + 1) * width, (side + 2) * width)
        for weight, col in ((wa, 0), (wb_ref, half)):
            table[base : base + used, col : col + half] = dot(rows_in, weight[rows, :]).astype(BF16)
        table[base + used : base + local_slots, :] = jnp.zeros((local_slots - used, 2 * half), BF16)
    shape = (rows128, 128)
    edge = lax.broadcasted_iota(jnp.int32, shape, 0) * 128 + lax.broadcasted_iota(jnp.int32, shape, 1) + feat * share
    live = edge < limit[0]
    for index in (send, recv):
        index[...] = jnp.where(live, layout.slots(index[...], patch), DEAD)
    for i, copy in enumerate(blocks):
        part = slice(i * block, (i + 1) * block)
        some = slice(i * block // 128, (i + 1) * block // 128)
        picks = jnp.concatenate(
            [one_hot_rows(index_columns(index[some, :]), 0, local_slots) for index in (send, recv)], axis=1
        )
        copy.wait()
        for weight, col in ((wa, 0), (wb_ref, half)):
            cols = slice(col, col + half)
            pre_ref[part, cols] = 0.5 * (dot(latent[part, :], weight[:width, :]) + dot(picks, table[:, cols]))
    for copy in rest:
        copy.wait()


def edge_kernel(
    pre_ref,
    latent_ref,
    send_ref,
    recv_ref,
    mine_ref,
    theirs_ref,
    wa_ref,
    wb_ref,
    va_ref,
    vb_ref,
    gain_ref,
    out_mine_ref,
    out_other_ref,
    group_mine_ref,
    group_other_ref,
    table,
    sums,
    layout,
    block,
):
    share, width = latent_ref.shape
    half = wa_ref.shape[1]
    group = layout.group
    feat = lax.axis_index("feat")
    for side in range(2):
        rows = slice((side + 1) * width, (side + 2) * width)
        for weight, col in ((wa_ref, 0), (wb_ref, half)):
            cols = slice(col, col + half)
            base = side * 2 * group
            for source, owner in ((mine_ref, feat), (theirs_ref, 1 - feat)):
                at = pl.multiple_of(base + owner * group, group)
                table[pl.ds(at, group), cols] = (0.5 * dot(source[...], weight[rows, :])).astype(BF16)
    gain = gain_ref[...].astype(F32).reshape(1, width)
    for at in range(0, share, block):
        part = slice(at, at + block)
        some = slice(at // 128, (at + block) // 128)
        receivers = recv_ref[some, :]
        columns = [index_columns(send_ref[some, :]), index_columns(receivers)]
        picks = jnp.concatenate([one_hot_rows(column, layout.local_slots, 2 * group) for column in columns], axis=1)
        hidden = silu_of_double(pre_ref[part, :] + dot(picks, table[...])).astype(BF16)
        pre = dot(hidden[:, :half], va_ref[...]) + dot(hidden[:, half:], vb_ref[...])
        live = jnp.concatenate([column[:, :1] for column in columns[1]], axis=0) != DEAD
        fresh = (latent_ref[part, :].astype(F32) + layer_norm(pre, gain, live)).astype(BF16)
        low, high = fresh[:, : width // 2], fresh[:, width // 2 :]
        out_mine_ref[part, :] = jnp.where(feat == 0, low, high)
        out_other_ref[part, :] = jnp.where(feat == 0, high, low)
        added = dot(one_hot_columns(flat_row(receivers), layout.local_slots, 2 * group), fresh)
        sums[...] = added if at == 0 else sums[...] + added
    group_mine_ref[...] = sums[pl.ds(pl.multiple_of(feat * group, group), group), :]
    group_other_ref[...] = sums[pl.ds(pl.multiple_of((1 - feat) * group, group), group), :].astype(BF16)


def merge_kernel(mine_ref, theirs_ref, *out_refs):
    at = 0
    for out_ref in out_refs:
        rows = out_ref.shape[0]
        part = slice(at, at + rows)
        out_ref[...] = (mine_ref[part, :] + theirs_ref[part, :].astype(F32)).astype(BF16)
        at += rows


def local_sums_kernel(mine_ref, other_ref, recv_ref, node_ref, wa_ref, wb_ref, sums_ref, pre_ref, block):
    width = node_ref.shape[1]
    share, half = mine_ref.shape
    used = sums_ref.shape[0]
    feat = lax.axis_index("feat")
    mine = other = None
    for at in range(0, share, block):
        part = slice(at, at + block)
        picks = one_hot_columns(flat_row(recv_ref[at // 128 : (at + block) // 128, :]), 0, used)
        new_mine, new_other = dot(picks, mine_ref[part, :]), dot(picks, other_ref[part, :])
        mine = new_mine if mine is None else mine + new_mine
        other = new_other if other is None else other + new_other
    sums_ref[:, :half] = jnp.where(feat == 0, mine, other)
    sums_ref[:, half:] = jnp.where(feat == 0, other, mine)
    pre_ref[:, :half] = dot(node_ref[...], wa_ref[:width, :])
    pre_ref[:, half:] = dot(node_ref[...], wb_ref[:width, :])


def receive_kernel(sums_ref, halo_ref, coarse_ref, *refs):
    *parts, own_ref, rounded_ref = refs
    node_count = own_ref.shape[0]
    coarse = coarse_ref.shape[0]
    coarse_row = coarse_ref[...].reshape(1, coarse)
    index_row = jnp.concatenate([lent_list(halo_ref[...])] + [coarse_row] * (len(parts) + 1), axis=1)
    returned = jnp.concatenate([part[...] for part in parts] + [sums_ref[node_count:, :].astype(BF16)], axis=0)
    own = sums_ref[:node_count, :] + dot(one_hot_columns(index_row, 0, node_count), returned)
    own_ref[...] = own
    rounded_ref[...] = own.astype(BF16)


def node_kernel(
    node_ref,
    own_ref,
    partner_ref,
    pre_ref,
    wa_ref,
    wb_ref,
    va_ref,
    vb_ref,
    gain_ref,
    mine_ref,
    theirs_ref,
    out_ref,
    edges_ref,
    sems,
):
    node_count, width = node_ref.shape
    half = wa_ref.shape[1]
    share = mine_ref.shape[0]
    feat = lax.axis_index("feat")
    placed = copies(
        [
            (source, edges_ref.at[pl.ds(pl.multiple_of(owner * share, share), share), :])
            for source, owner in ((mine_ref, feat), (theirs_ref, 1 - feat))
        ],
        sems,
    )
    received = (own_ref[...] + partner_ref[...].astype(F32)).astype(BF16)
    total = None
    for weight, second, col in ((wa_ref, va_ref, 0), (wb_ref, vb_ref, half)):
        pre = pre_ref[:, col : col + half] + dot(received, weight[width:, :])
        part = dot(silu_of_double(0.5 * pre).astype(BF16), second[...])
        total = part if total is None else total + part
    update = layer_norm(total, gain_ref[...].astype(F32).reshape(1, width))
    fresh = (node_ref[...].astype(F32) + update).astype(BF16)
    out_ref[...] = jnp.where(feat == 0, fresh[:, : width // 2], fresh[:, width // 2 :])
    for copy in placed:
        copy.wait()


def in_hbm(array):
    return pltpu.with_memory_space_constraint(array, pltpu.HBM)


VMEM_SPEC = pl.BlockSpec(memory_space=pltpu.VMEM)
ANY_SPEC = pl.BlockSpec(memory_space=pl.ANY)


def call(kernel, operands, in_specs, outputs, out_specs, flops, limit, scratch=()):
    return pl.pallas_call(
        kernel,
        in_specs=in_specs,
        out_specs=out_specs,
        out_shape=outputs,
        scratch_shapes=list(scratch),
        cost_estimate=pl.CostEstimate(flops=flops, bytes_accessed=4 * MIB, transcendentals=0),
        compiler_params=pltpu.CompilerParams(vmem_limit_bytes=limit * MIB),
    )(*operands)


def exchange_pairs(count):
    across = [(p + 1 if p % 2 else p - 1) % count for p in range(count)]
    rounds = [([p ^ 1 for p in range(count)], across)]
    for distance in range(2, count, 2):
        rounds.append(([p ^ distance for p in range(count)], [p ^ (distance + 1) for p in range(count)]))
    return [
        [(2 * p + feat, 2 * targets[p] + feat) for p in range(count) for feat, targets in enumerate(some)]
        for some in rounds
    ]


def on_device(
    node_latent,
    edge_latent,
    edge_senders,
    edge_receivers,
    halo_rows,
    coarse_rows,
    edge_counts,
    edge_w1,
    edge_w2,
    edge_gain,
    node_w1,
    node_w2,
    node_gain,
):
    node_count, width = node_latent.shape
    half = width // 2
    edge_count = edge_latent.shape[0]
    halo, coarse = halo_rows.shape[1], coarse_rows.shape[0]
    patches = lax.axis_size("patch")
    both = ("patch", "feat")
    layout = Layout(patches, node_count, halo, coarse)
    group, used, local_slots = layout.group, layout.used, layout.local_slots
    share = edge_count // 2
    block = 512
    dma = pltpu.SemaphoreType.DMA

    def shape(rows, columns, kind=BF16):
        return jax.ShapeDtypeStruct((rows, columns), kind)

    def like(array):
        return jax.ShapeDtypeStruct(array.shape, array.dtype)

    def swap(values):
        return lax.ppermute(values, "feat", FEAT_SWAP)

    edge_w1_b, edge_w2_b = swap(edge_w1), swap(edge_w2)

    lent, node, halo_lists, coarse_list = call(
        lend_kernel,
        [in_hbm(array) for array in (node_latent, halo_rows, coarse_rows)],
        [ANY_SPEC] * 3,
        [shape(halo + coarse, width), like(node_latent), like(halo_rows), like(coarse_rows)],
        [VMEM_SPEC] * 4,
        2 * node_count * (halo + coarse) * width,
        8,
        scratch=[dma((3,))],
    )
    pairs = exchange_pairs(patches)
    arrived = [lax.ppermute(lent, both, pairs[0])]
    for some in pairs[1:]:
        arrived.append(lax.ppermute(lent[halo:], both, some))

    index_rows = (edge_count // 128, 128)
    more = (edge_w2, edge_gain, node_w1, node_w2, node_gain)
    pre, latent, send, recv, w1, w2, e_gain, n_w1, n_w2, n_gain = call(
        functools.partial(local_kernel, layout=layout, block=block),
        [node, lent, edge_w1_b, edge_counts]
        + [
            in_hbm(array)
            for array in (
                edge_latent,
                edge_senders.reshape(index_rows),
                edge_receivers.reshape(index_rows),
                edge_w1,
                *more,
            )
        ],
        [VMEM_SPEC] * 3 + [pl.BlockSpec(memory_space=pltpu.SMEM)] + [ANY_SPEC] * (4 + len(more)),
        [
            shape(share, width, F32),
            shape(share, width),
            shape(share // 128, 128, jnp.int32),
            shape(share // 128, 128, jnp.int32),
            like(edge_w1),
        ]
        + [like(array) for array in more],
        [VMEM_SPEC] * (5 + len(more)),
        2 * width * width * share + 4 * used * width * width + 4 * share * local_slots * width,
        LIMIT,
        scratch=[
            pltpu.VMEM((2 * local_slots, width), BF16),
            dma((3 + len(more),)),
            dma((share // block,)),
        ],
    )
    *arrived, pre = lax.optimization_barrier((*arrived, pre))
    table_mine = jnp.concatenate(arrived, axis=0)
    table_theirs = swap(table_mine)
    node_w1_b, node_w2_b = swap(n_w1), swap(n_w2)

    mine, other, group_mine, group_other = call(
        functools.partial(edge_kernel, layout=layout, block=block),
        (pre, latent, send, recv, table_mine, table_theirs, w1, edge_w1_b, w2, edge_w2_b, e_gain),
        [VMEM_SPEC] * 11,
        [shape(share, half), shape(share, half), shape(group, width, F32), shape(group, width)],
        [VMEM_SPEC] * 4,
        2 * share * width * (width + 6 * group) + 8 * group * width * width,
        LIMIT,
        scratch=[pltpu.VMEM((4 * group, width), BF16), pltpu.VMEM((2 * group, width), F32)],
    )

    group_theirs = swap(group_other)
    sizes = [halo + coarse] + [coarse] * (len(pairs) - 1)
    outgoing = call(
        merge_kernel,
        (group_mine, group_theirs),
        [VMEM_SPEC] * 2,
        [shape(rows, width) for rows in sizes],
        [VMEM_SPEC] * len(sizes),
        group * width,
        8,
    )
    *outgoing, mine, other = lax.optimization_barrier((*outgoing, mine, other))
    back = [lax.ppermute(part, both, some) for part, some in zip(outgoing, pairs)]
    edges_theirs = swap(other)
    local_sums, node_pre = call(
        functools.partial(local_sums_kernel, block=block),
        (mine, other, recv, node, n_w1, node_w1_b),
        [VMEM_SPEC] * 6,
        [shape(used, width, F32), shape(node_count, width, F32)],
        [VMEM_SPEC] * 2,
        2 * share * width * used + 2 * node_count * width * width,
        16,
    )
    own, rounded = call(
        receive_kernel,
        (local_sums, halo_lists, coarse_list, *back),
        [VMEM_SPEC] * (3 + len(sizes)),
        [shape(node_count, width, F32), shape(node_count, width)],
        [VMEM_SPEC] * 2,
        2 * node_count * width * (group + coarse),
        16,
    )
    partner = swap(rounded)
    nodes_out, edges_out = call(
        node_kernel,
        (node, own, partner, node_pre, n_w1, node_w1_b, n_w2, node_w2_b, n_gain, mine, edges_theirs),
        [VMEM_SPEC] * 9 + [ANY_SPEC] * 2,
        [shape(node_count, half), shape(edge_count, half)],
        [VMEM_SPEC, ANY_SPEC],
        4 * node_count * width * width,
        16,
        scratch=[dma((2,))],
    )
    return nodes_out, edges_out


def solution(mesh):
    placed = (
        P(("member", "patch"), None),
        P(("member", "patch"), None),
        P(("member", "patch")),
        P(("member", "patch")),
        P(("member", "patch"), None),
        P(("member", "patch")),
        P(("member", "patch")),
        P(None, "feat"),
        P("feat", None),
        P(),
        P(None, "feat"),
        P("feat", None),
        P(),
    )
    return jax.shard_map(
        on_device,
        mesh=mesh,
        in_specs=placed,
        out_specs=(P(("member", "patch"), "feat"), P(("member", "patch"), "feat")),
        check_vma=False,
    )
```

time: 242 us -> 47.1 us (0.19)
  waiting for transfers between devices: 65.1 us -> 6.39 us
  blocking collectives: 46.3 us -> 0 us
  other arithmetic: 42.9 us -> 0 us
  local copies, waits for them, and re-layouts: 34.7 us -> 0.03 us
  matrix products: 22.3 us -> 0 us
  Pallas kernels: 0 us -> 21.6 us
  between operations: 14.7 us -> 1.59 us
    reduce_scatter x2 -> x0, waiting for transfers between devices: 61.6 us -> none  [the longest x1 53.7 us: on_device(): lax.psum_scatter(summed[node_count + 2 * halo_count:].astype(jnp.bfloat16...]
    all_gather x3 -> x0, blocking collectives: 37.5 us -> none  [the longest x1 33.1 us: on_device(): lax.all_gather(node_latent[coarse_rows], 'patch', axis=0, tiled=True)]
    scatter-add x4 -> x0, other arithmetic: 30.8 us -> none  [the longest x1 26.1 us: on_device(): jax.ops.segment_sum(message, target, num_segments=slot_count + 1)]
    gather x5 -> x0, local copies, waits for them, and re-layouts: 23.1 us -> none  [the longest x1 9.19 us: first_layer(): lookup[senders]]
    dot_general x5 -> x0, matrix products: 22.3 us -> none  [the longest x1 9.81 us: on_device(): jnp.dot(hidden, weight_out, preferred_element_type=jnp.float32)]
    pallas_call x0 -> x7, Pallas kernels: none -> 21.6 us  [call(): pl.pallas_call(kernel, in_specs=in_specs, out_specs=out_specs, out_shape=...]
    unnamed x39 -> x3, local copies, waits for them, and re-layouts: 8.05 us -> 0.02 us
    all_to_all x1 -> x0, blocking collectives: 6.29 us -> none  [on_device(): lax.all_to_all(fresh_rows, 'feat', split_axis=1, concat_axis=0, tiled=True)]
  transfers between devices with their start and end apart: 7 -> 16, of which waited for: 3 -> 4; matrix products, arithmetic and copies ran while one was open for 15% -> 0% of each run, Pallas kernels for 0% -> 40%
where the time goes in v3:
time: 47.1 us; the launch traced here: 46.9 us
  Pallas kernels  21.6 us (46%)
  starting transfers between devices  17.3 us (37%)
  waiting for transfers between devices  6.39 us (14%)
  between operations  1.59 us (3%)
    pallas_call x7, Pallas kernels, call(): pl.pallas_call(kernel, in_specs=in_specs, out_specs=out_specs, out_shape=...  21.6 us
    ppermute x8, starting transfers between devices, swap(): return lax.ppermute(values, 'feat', FEAT_SWAP)  5.93 us
    ppermute x3, starting transfers between devices, on_device(): arrived.append(lax.ppermute(lent[halo:], both, some))  5.32 us
    ppermute x8, waiting for transfers between devices, swap(): return lax.ppermute(values, 'feat', FEAT_SWAP)  4.45 us
    ppermute x4, starting transfers between devices, on_device(): lax.ppermute(part, both, some)  4.39 us
    ppermute x4, waiting for transfers between devices, on_device(): lax.ppermute(part, both, some)  1.93 us
    ppermute x1, starting transfers between devices, on_device(): arrived = [lax.ppermute(lent, both, pairs[0])]  1.66 us
  transfers between devices with their start and end apart: 16, of which 4 were waited for; matrix products, arithmetic and copies ran while one was open for 0% of the time, Pallas kernels for 40%

profile of v3, /device:TPU:0, one launch (start us, length us, event | category | flops | bytes accessed | tf_op | source)
XLA Modules:
  0.0 46.9 jit_solution(11058125128561321833)
XLA Ops:
  0.6 0.5 %collective-permute-start.4 = (bf16[1536,256]{1,0:T(8,128)(2,1)}, bf16[1536,256]{1,0:T(8,128)(2,1)S(1)}, u32[]{:S(2)}, u32[]{:S(2)}) collective-permute-start(bf16[1536,256]{1,0:T(8,128)(2,1)} %wa_hbm.1), channel_id=1, source_target_pairs={{0,1},{1,0},{2,3},{3,2},{4,5},{5,4},{6,7},{7,6},{8,9},{9,8},{10,11... | collective-permute-start | bytes 2359304 | tf_op jit(solution)/shard_map/ppermute | solution.py:383
  1.1 1.5 %shard_map.140 = (bf16[160,512]{1,0:T(8,128)(2,1)S(1)}, bf16[640,512]{1,0:T(8,128)(2,1)S(1)}, s32[2,128]{1,0:T(2,128)S(1)}, s32[32]{0:T(128)S(1)}) custom-call(bf16[640,512]{1,0:T(8,128)(2,1)} %node_ref.1, s32[2,128]{1,0:T(2,128)} %halo_ref.1, s32[32]{0:T(128)} %coarse_ref.1), custom_call_target="tpu_custom_call" | custom-call | flops 104857600 | bytes 4194304 | tf_op jit(solution)/shard_map/pallas_call | solution.py:327
  2.7 4.7 %collective-permute-start.3 = (bf16[32,512]{1,0:T(8,128)(2,1)S(1)}, bf16[32,512]{1,0:T(8,128)(2,1)S(1)}, u32[]{:S(2)}, u32[]{:S(2)}) collective-permute-start(bf16[32,512]{1,0:T(8,128)(2,1)S(1)} %slice.2), channel_id=1, source_target_pairs={{0,12},{1,15},{2,14},{3,13},{4,8},{5,11},{6,10},{7,9},{8,4},{9,7},... | collective-permute-start | bytes 98312 | tf_op jit(solution)/shard_map/ppermute | solution.py:400
  7.3 0.0 collective-permute-start.2
  7.3 0.6 %collective-permute-start.1 = (bf16[32,512]{1,0:T(8,128)(2,1)S(1)}, bf16[32,512]{1,0:T(8,128)(2,1)S(1)}, u32[]{:S(2)}, u32[]{:S(2)}) collective-permute-start(bf16[32,512]{1,0:T(8,128)(2,1)S(1)} %slice.2), channel_id=1, source_target_pairs={{0,4},{1,7},{2,6},{3,5},{4,0},{5,3},{6,2},{7,1},{8,12},{9,15},{10,... | collective-permute-start | bytes 98312 | tf_op jit(solution)/shard_map/ppermute | solution.py:400
  8.0 1.7 %collective-permute-start = (bf16[160,512]{1,0:T(8,128)(2,1)S(1)}, bf16[160,512]{1,0:T(8,128)(2,1)S(1)}, u32[]{:S(2)}, u32[]{:S(2)}) collective-permute-start(bf16[160,512]{1,0:T(8,128)(2,1)S(1)} %get-tuple-element.40.lent_ref), channel_id=1, source_target_pairs={{0,2},{1,15},{2,0},{3,5},{4,6},{5,3},{6,4},{7,9},{8,10},{9,7},{10,... | collective-permute-start | bytes 491528 | tf_op jit(solution)/shard_map/ppermute | solution.py:398
  10.3 0.0 collective-permute-done.4.wb_ref
  10.3 3.3 %collective-permute-start.6 = (bf16[256,512]{1,0:T(8,128)(2,1)}, bf16[256,512]{1,0:T(8,128)(2,1)S(1)}, u32[]{:S(2)}, u32[]{:S(2)}) collective-permute-start(bf16[256,512]{1,0:T(8,128)(2,1)} %refs_0_.1), channel_id=1, source_target_pairs={{0,1},{1,0},{2,3},{3,2},{4,5},{5,4},{6,7},{7,6},{8,9},{9,8},{10,11... | collective-permute-start | bytes 786440 | tf_op jit(solution)/shard_map/ppermute | solution.py:383
  13.6 7.8 %shard_map.141 = (f32[2048,512]{1,0:T(8,128)S(1)}, bf16[2048,512]{1,0:T(8,128)(2,1)S(1)}, s32[16,128]{1,0:T(8,128)S(1)}, s32[16,128]{1,0:T(8,128)S(1)}, bf16[153...) custom-call(bf16[640,512]{1,0:T(8,128)(2,1)S(1)} %get-tuple-element., ...), custom_call_target="tpu_custom_call" | custom-call | flops 4999610368 | bytes 4194304 | tf_op jit(solution)/shard_map/pallas_call | solution.py:327
  21.4 0.0 collective-permute-done.3
  21.4 0.0 collective-permute-done.1
  21.5 0.0 collective-permute-done
  21.5 0.1 collective-permute-start.5
  21.6 0.5 %collective-permute-start.8 = (bf16[1024,256]{1,0:T(8,128)(2,1)S(1)}, bf16[1024,256]{1,0:T(8,128)(2,1)S(1)}, u32[]{:S(2)}, u32[]{:S(2)}) collective-permute-start(bf16[1024,256]{1,0:T(8,128)(2,1)S(1)} %get-tuple-element.63.wa_ref), channel_id=1, source_target_pairs={{0,1},{1,0},{2,3},{3,2},{4,5},{5,4},{6,7},{7,6},{8,9},{9,8},{10,11... | collective-permute-start | bytes 1572872 | tf_op jit(solution)/shard_map/ppermute | solution.py:383
  22.1 1.0 %collective-permute-done.5.theirs_ref = bf16[256,512]{1,0:T(8,128)(2,1)S(1)} collective-permute-done((bf16[256,512]{1,0:T(8,128)(2,1)S(1)}, bf16[256,512]{1,0:T(8,128)(2,1)S(1)}, u32[]{:S(2)}, u32[]{:S(2)}) %collective-permute-start.5) | collective-permute-done | bytes 262176 | tf_op jit(solution)/shard_map/ppermute | solution.py:383
  23.1 6.8 %shard_map.142 = (bf16[2048,256]{1,0:T(8,128)(2,1)S(1)}, bf16[2048,256]{1,0:T(8,128)(2,1)S(1)}, f32[256,512]{1,0:T(8,128)S(1)}, bf16[256,512]{1,0:T(8,128)(2,1)S(1)}) custom-call(f32[2048,512]{1,0:T(8,128)S(1)} %get-tuple-element.42.pre_ref, bf16[2048,512]{1,0:T(8,128)(2,1)S(1)} %get-tuple-element.43.latent_ref, s32[16,128]{1,0:T(8,128)S(1)} %get-tuple-element.44.send_ref, ...), custom_call_target="tpu_custom_call" | custom-call | flops 4831838208 | bytes 4194304 | tf_op jit(solution)/shard_map/pallas_call | solution.py:327
  29.9 0.2 collective-permute-start.7
  30.2 1.4 %collective-permute-done.7.theirs_ref = bf16[256,512]{1,0:T(8,128)(2,1)S(1)} collective-permute-done((bf16[256,512]{1,0:T(8,128)(2,1)S(1)}, bf16[256,512]{1,0:T(8,128)(2,1)S(1)}, u32[]{:S(2)}, u32[]{:S(2)}) %collective-permute-start.7) | collective-permute-done | bytes 262176 | tf_op jit(solution)/shard_map/ppermute | solution.py:383
  31.6 0.2 collective-permute-start.15
  31.8 1.3 %collective-permute-start.11 = (bf16[32,512]{1,0:T(8,128)(2,1)S(1)}, bf16[32,512]{1,0:T(8,128)(2,1)S(1)}, u32[]{:S(2)}, u32[]{:S(2)}) collective-permute-start(bf16[32,512]{1,0:T(8,128)(2,1)S(1)} %get-tuple-element.69), channel_id=1, source_target_pairs={{0,8},{1,11},{2,10},{3,9},{4,12},{5,15},{6,14},{7,13},{8,0},{9,3},... | collective-permute-start | bytes 98312 | tf_op jit(solution)/shard_map/ppermute | solution.py:463
  33.1 1.0 %collective-permute-start.9 = (bf16[160,512]{1,0:T(8,128)(2,1)S(1)}, bf16[160,512]{1,0:T(8,128)(2,1)S(1)}, u32[]{:S(2)}, u32[]{:S(2)}) collective-permute-start(bf16[160,512]{1,0:T(8,128)(2,1)S(1)} %get-tuple-element.67), channel_id=1, source_target_pairs={{0,2},{1,15},{2,0},{3,5},{4,6},{5,3},{6,4},{7,9},{8,10},{9,7},{10,... | collective-permute-start | bytes 491528 | tf_op jit(solution)/shard_map/ppermute | solution.py:463
  34.1 2.1 %collective-permute-start.12 = (bf16[32,512]{1,0:T(8,128)(2,1)S(1)}, bf16[32,512]{1,0:T(8,128)(2,1)S(1)}, u32[]{:S(2)}, u32[]{:S(2)}) collective-permute-start(bf16[32,512]{1,0:T(8,128)(2,1)S(1)} %get-tuple-element.70), channel_id=1, source_target_pairs={{0,12},{1,15},{2,14},{3,13},{4,8},{5,11},{6,10},{7,9},{8,4},{9,7},... | collective-permute-start | bytes 98312 | tf_op jit(solution)/shard_map/ppermute | solution.py:463
  36.2 2.1 %shard_map.144 = (f32[672,512]{1,0:T(8,128)S(1)}, f32[640,512]{1,0:T(8,128)S(1)}) custom-call(bf16[2048,256]{1,0:T(8,128)(2,1)S(1)} %get-tuple-element.61.mine_ref, bf16[2048,256]{1,0:T(8,128)(2,1)S(1)} %get-tuple-element.62.other_ref, s32[16,128]{1,0:T(8,128)S(1)} %get-tuple-element.45.recv_ref, bf16[640,512]{1,0:T(8,128)(2,1)S(1)} %get-tuple-element.39.node.node_ref, ...), custom_call_target="tpu_custom_call" | custom-call | flops 1744830464 | bytes 4194304 | tf_op jit(solution)/shard_map/pallas_call | solution.py:327
  38.3 1.9 %collective-permute-done.12.refs_3_ = bf16[32,512]{1,0:T(8,128)(2,1)S(1)} collective-permute-done((bf16[32,512]{1,0:T(8,128)(2,1)S(1)}, bf16[32,512]{1,0:T(8,128)(2,1)S(1)}, u32[]{:S(2)}, u32[]{:S(2)}) %collective-permute-start.12) | collective-permute-done | bytes 32800 | tf_op jit(solution)/shard_map/ppermute | solution.py:463
  40.3 0.0 collective-permute-done.9.refs_0_
  40.3 0.5 %shard_map.145 = (f32[640,512]{1,0:T(8,128)S(1)}, bf16[640,512]{1,0:T(8,128)(2,1)S(1)}) custom-call(f32[672,512]{1,0:T(8,128)S(1)} %get-tuple-element.64.sums_ref, s32[2,128]{1,0:T(2,128)S(1)} %get-tuple-element.65.halo_ref, s32[32]{0:T(128)S(1)} %get-tuple-element.66.coarse_ref, bf16[160,512]{1,0:T(8,128)(2,1)S(1)} %collective-permute-done.9.refs_0_, ...), custom_call_target="tpu_custom_call" | custom-call | flops 188743680 | bytes 4194304 | tf_op jit(solution)/shard_map/pallas_call | solution.py:327
  40.8 1.0 %collective-permute-start.13 = (bf16[640,512]{1,0:T(8,128)(2,1)S(1)}, bf16[640,512]{1,0:T(8,128)(2,1)S(1)}, u32[]{:S(2)}, u32[]{:S(2)}) collective-permute-start(bf16[640,512]{1,0:T(8,128)(2,1)S(1)} %get-tuple-element.72), channel_id=1, source_target_pairs={{0,1},{1,0},{2,3},{3,2},{4,5},{5,4},{6,7},{7,6},{8,9},{9,8},{10,11... | collective-permute-start | bytes 1966088 | tf_op jit(solution)/shard_map/ppermute | solution.py:383
  41.8 0.1 collective-permute-start.14
  41.9 2.0 %collective-permute-done.14.vb_ref = bf16[256,512]{1,0:T(8,128)(2,1)S(1)} collective-permute-done((bf16[256,512]{1,0:T(8,128)(2,1)S(1)}, bf16[256,512]{1,0:T(8,128)(2,1)S(1)}, u32[]{:S(2)}, u32[]{:S(2)}) %collective-permute-start.14) | collective-permute-done | bytes 262176 | tf_op jit(solution)/shard_map/ppermute | solution.py:383
  43.9 0.0 collective-permute-done.13.partner_ref
  43.9 0.0 collective-permute-done.15.theirs_ref
  44.0 2.8 %shard_map.146 = (bf16[640,256]{1,0:T(8,128)(2,1)}, bf16[4096,256]{1,0:T(8,128)(2,1)}) custom-call(bf16[640,512]{1,0:T(8,128)(2,1)S(1)} %get-tuple-element.39.node.node_ref, f32[640,512]{1,0:T(8,128)S(1)} %get-tuple-element.71.own_ref, bf16[640,512]{1,0:T(8,128)(2,1)S(1)} %collective-permute-done.13.partner_ref, f32[640,512]{1,0:T(8,128)S(1)} %get-tuple-element.73.pre_ref, ...), custom_call_target="tpu_custom_call" | custom-call | flops 671088640 | bytes 4194304 | tf_op jit(solution)/shard_map/pallas_call | solution.py:327
  (12 shorter events, 0.1 us)
Async XLA Ops:
  0.6 9.7 %collective-permute-start.4 = (bf16[1536,256]{1,0:T(8,128)(2,1)}, bf16[1536,256]{1,0:T(8,128)(2,1)S(1)}, u32[]{:S(2)}, u32[]{:S(2)}) collective-permute-start(bf16[1536,256]{1,0:T(8,128)(2,1)} %wa_hbm.1), channel_id=1, source_target_pairs={{0,1},{1,0},{2,3},{3,2},{4,5},{5,4},{6,7},{7,6},{8,9},{9,8},{10,11... | collective-permute-start | bytes 2359304 | tf_op jit(solution)/shard_map/ppermute | solution.py:383
  2.7 18.8 %collective-permute-start.3 = (bf16[32,512]{1,0:T(8,128)(2,1)S(1)}, bf16[32,512]{1,0:T(8,128)(2,1)S(1)}, u32[]{:S(2)}, u32[]{:S(2)}) collective-permute-start(bf16[32,512]{1,0:T(8,128)(2,1)S(1)} %slice.2), channel_id=1, source_target_pairs={{0,12},{1,15},{2,14},{3,13},{4,8},{5,11},{6,10},{7,9},{8,4},{9,7},... | collective-permute-start | bytes 98312 | tf_op jit(solution)/shard_map/ppermute | solution.py:400
  7.3 14.1 %collective-permute-start.2 = (bf16[32,512]{1,0:T(8,128)(2,1)S(1)}, bf16[32,512]{1,0:T(8,128)(2,1)S(1)}, u32[]{:S(2)}, u32[]{:S(2)}) collective-permute-start(bf16[32,512]{1,0:T(8,128)(2,1)S(1)} %slice.2), channel_id=1, source_target_pairs={{0,8},{1,11},{2,10},{3,9},{4,12},{5,15},{6,14},{7,13},{8,0},{9,3},... | collective-permute-start | bytes 98312 | tf_op jit(solution)/shard_map/ppermute | solution.py:400
  7.3 14.1 %collective-permute-start.1 = (bf16[32,512]{1,0:T(8,128)(2,1)S(1)}, bf16[32,512]{1,0:T(8,128)(2,1)S(1)}, u32[]{:S(2)}, u32[]{:S(2)}) collective-permute-start(bf16[32,512]{1,0:T(8,128)(2,1)S(1)} %slice.2), channel_id=1, source_target_pairs={{0,4},{1,7},{2,6},{3,5},{4,0},{5,3},{6,2},{7,1},{8,12},{9,15},{10,... | collective-permute-start | bytes 98312 | tf_op jit(solution)/shard_map/ppermute | solution.py:400
  8.0 13.5 %collective-permute-start = (bf16[160,512]{1,0:T(8,128)(2,1)S(1)}, bf16[160,512]{1,0:T(8,128)(2,1)S(1)}, u32[]{:S(2)}, u32[]{:S(2)}) collective-permute-start(bf16[160,512]{1,0:T(8,128)(2,1)S(1)} %get-tuple-element.40.lent_ref), channel_id=1, source_target_pairs={{0,2},{1,15},{2,0},{3,5},{4,6},{5,3},{6,4},{7,9},{8,10},{9,7},{10,... | collective-permute-start | bytes 491528 | tf_op jit(solution)/shard_map/ppermute | solution.py:398
  10.3 11.8 %collective-permute-start.6 = (bf16[256,512]{1,0:T(8,128)(2,1)}, bf16[256,512]{1,0:T(8,128)(2,1)S(1)}, u32[]{:S(2)}, u32[]{:S(2)}) collective-permute-start(bf16[256,512]{1,0:T(8,128)(2,1)} %refs_0_.1), channel_id=1, source_target_pairs={{0,1},{1,0},{2,3},{3,2},{4,5},{5,4},{6,7},{7,6},{8,9},{9,8},{10,11... | collective-permute-start | bytes 786440 | tf_op jit(solution)/shard_map/ppermute | solution.py:383
  21.5 1.6 %collective-permute-start.5 = (bf16[256,512]{1,0:T(8,128)(2,1)S(1)}, bf16[256,512]{1,0:T(8,128)(2,1)S(1)}, u32[]{:S(2)}, u32[]{:S(2)}) collective-permute-start(bf16[256,512]{1,0:T(8,128)(2,1)S(1)} %constant_dynamic-update-slice_fusion.mine_ref), channel_id=1, source_target_pairs={{0,1},{1,0},{2,3},{3,2},{4,5},{5,4},{6,7},{7,6},{8,9},{9,8},{10,11... | collective-permute-start | bytes 786440 | tf_op jit(solution)/shard_map/ppermute | solution.py:383
  21.6 12.5 %collective-permute-start.8 = (bf16[1024,256]{1,0:T(8,128)(2,1)S(1)}, bf16[1024,256]{1,0:T(8,128)(2,1)S(1)}, u32[]{:S(2)}, u32[]{:S(2)}) collective-permute-start(bf16[1024,256]{1,0:T(8,128)(2,1)S(1)} %get-tuple-element.63.wa_ref), channel_id=1, source_target_pairs={{0,1},{1,0},{2,3},{3,2},{4,5},{5,4},{6,7},{7,6},{8,9},{9,8},{10,11... | collective-permute-start | bytes 1572872 | tf_op jit(solution)/shard_map/ppermute | solution.py:383
  29.9 1.6 %collective-permute-start.7 = (bf16[256,512]{1,0:T(8,128)(2,1)S(1)}, bf16[256,512]{1,0:T(8,128)(2,1)S(1)}, u32[]{:S(2)}, u32[]{:S(2)}) collective-permute-start(bf16[256,512]{1,0:T(8,128)(2,1)S(1)} %get-tuple-element.54), channel_id=1, source_target_pairs={{0,1},{1,0},{2,3},{3,2},{4,5},{5,4},{6,7},{7,6},{8,9},{9,8},{10,11... | collective-permute-start | bytes 786440 | tf_op jit(solution)/shard_map/ppermute | solution.py:383
  31.6 12.4 %collective-permute-start.15 = (bf16[2048,256]{1,0:T(8,128)(2,1)S(1)}, bf16[2048,256]{1,0:T(8,128)(2,1)S(1)}, u32[]{:S(2)}, u32[]{:S(2)}) collective-permute-start(bf16[2048,256]{1,0:T(8,128)(2,1)S(1)} %get-tuple-element.62.other_ref), channel_id=1, source_target_pairs={{0,1},{1,0},{2,3},{3,2},{4,5},{5,4},{6,7},{7,6},{8,9},{9,8},{10,11... | collective-permute-start | bytes 3145736 | tf_op jit(solution)/shard_map/ppermute | solution.py:383
  31.8 6.5 %collective-permute-start.10 = (bf16[32,512]{1,0:T(8,128)(2,1)S(1)}, bf16[32,512]{1,0:T(8,128)(2,1)S(1)}, u32[]{:S(2)}, u32[]{:S(2)}) collective-permute-start(bf16[32,512]{1,0:T(8,128)(2,1)S(1)} %get-tuple-element.68), channel_id=1, source_target_pairs={{0,4},{1,7},{2,6},{3,5},{4,0},{5,3},{6,2},{7,1},{8,12},{9,15},{10,... | collective-permute-start | bytes 98312 | tf_op jit(solution)/shard_map/ppermute | solution.py:463
  31.8 6.5 %collective-permute-start.11 = (bf16[32,512]{1,0:T(8,128)(2,1)S(1)}, bf16[32,512]{1,0:T(8,128)(2,1)S(1)}, u32[]{:S(2)}, u32[]{:S(2)}) collective-permute-start(bf16[32,512]{1,0:T(8,128)(2,1)S(1)} %get-tuple-element.69), channel_id=1, source_target_pairs={{0,8},{1,11},{2,10},{3,9},{4,12},{5,15},{6,14},{7,13},{8,0},{9,3},... | collective-permute-start | bytes 98312 | tf_op jit(solution)/shard_map/ppermute | solution.py:463
  33.1 7.2 %collective-permute-start.9 = (bf16[160,512]{1,0:T(8,128)(2,1)S(1)}, bf16[160,512]{1,0:T(8,128)(2,1)S(1)}, u32[]{:S(2)}, u32[]{:S(2)}) collective-permute-start(bf16[160,512]{1,0:T(8,128)(2,1)S(1)} %get-tuple-element.67), channel_id=1, source_target_pairs={{0,2},{1,15},{2,0},{3,5},{4,6},{5,3},{6,4},{7,9},{8,10},{9,7},{10,... | collective-permute-start | bytes 491528 | tf_op jit(solution)/shard_map/ppermute | solution.py:463
  34.1 6.1 %collective-permute-start.12 = (bf16[32,512]{1,0:T(8,128)(2,1)S(1)}, bf16[32,512]{1,0:T(8,128)(2,1)S(1)}, u32[]{:S(2)}, u32[]{:S(2)}) collective-permute-start(bf16[32,512]{1,0:T(8,128)(2,1)S(1)} %get-tuple-element.70), channel_id=1, source_target_pairs={{0,12},{1,15},{2,14},{3,13},{4,8},{5,11},{6,10},{7,9},{8,4},{9,7},... | collective-permute-start | bytes 98312 | tf_op jit(solution)/shard_map/ppermute | solution.py:463
  40.8 3.1 %collective-permute-start.13 = (bf16[640,512]{1,0:T(8,128)(2,1)S(1)}, bf16[640,512]{1,0:T(8,128)(2,1)S(1)}, u32[]{:S(2)}, u32[]{:S(2)}) collective-permute-start(bf16[640,512]{1,0:T(8,128)(2,1)S(1)} %get-tuple-element.72), channel_id=1, source_target_pairs={{0,1},{1,0},{2,3},{3,2},{4,5},{5,4},{6,7},{7,6},{8,9},{9,8},{10,11... | collective-permute-start | bytes 1966088 | tf_op jit(solution)/shard_map/ppermute | solution.py:383
  41.8 2.1 %collective-permute-start.14 = (bf16[256,512]{1,0:T(8,128)(2,1)S(1)}, bf16[256,512]{1,0:T(8,128)(2,1)S(1)}, u32[]{:S(2)}, u32[]{:S(2)}) collective-permute-start(bf16[256,512]{1,0:T(8,128)(2,1)S(1)} %get-tuple-element.74.va_ref), channel_id=1, source_target_pairs={{0,1},{1,0},{2,3},{3,2},{4,5},{5,4},{6,7},{7,6},{8,9},{9,8},{10,11... | collective-permute-start | bytes 786440 | tf_op jit(solution)/shard_map/ppermute | solution.py:383

commit v4 on v3

--- a/solution.py
+++ b/solution.py
@@ -12,6 +12,7 @@
 BF16 = jnp.bfloat16
 MIB = 1024 * 1024
 LIMIT = 30
+BESIDE = 10
 DEAD = -1
 NOWHERE = -2
 FEAT_SWAP = [(0, 1), (1, 0)]
@@ -78,17 +79,19 @@
         self.used = node_count + coarse
         self.local_slots = -(-self.used // 256) * 256
 
-    def slots(self, rows, patch):
+    def slots(self, rows, patch, feat):
         node_count, halo, coarse, group = self.node_count, self.halo, self.coarse, self.group
         at = rows - (node_count + 2 * halo)
         owner, entry = lax.shift_right_arithmetic(at, coarse.bit_length() - 1), at & (coarse - 1)
         distance = patch ^ owner
-        odd = patch & 1
-        place = self.local_slots + (distance & 1) * group + halo + coarse * lax.shift_right_arithmetic(distance, 1)
+        even = 1 - (patch & 1)
+        core0 = self.local_slots + feat * group
+        place = self.local_slots + ((distance & 1) ^ feat) * group + halo
+        place = place + coarse * lax.shift_right_arithmetic(distance, 1)
         place = jnp.where(distance == 0, node_count, place)
-        place = jnp.where(distance == 1, self.local_slots + halo, place) + entry
-        lower = self.local_slots + (1 - odd) * group - node_count + rows
-        upper = self.local_slots + odd * group - (node_count + halo) + rows
+        place = jnp.where(distance == 1, core0 + halo, place) + entry
+        lower = self.local_slots + (even ^ feat) * group - node_count + rows
+        upper = self.local_slots + (1 - (even ^ feat)) * group - (node_count + halo) + rows
         lower = jnp.where(patch == 0, NOWHERE, lower)
         upper = jnp.where(patch == self.patches - 1, NOWHERE, upper)
         place = jnp.where(rows < node_count + 2 * halo, upper, place)
@@ -101,8 +104,23 @@
     return jnp.where(which == 0, lists[0:1], lists[1:2])
 
 
-def lend_kernel(node_ref, halo_ref, coarse_ref, lent_ref, node, halo, coarse, sems):
-    for copy in copies(((halo_ref, halo), (coarse_ref, coarse), (node_ref, node)), sems):
+def lend_kernel(*refs, share):
+    (node_hbm, halo_hbm, coarse_hbm, wa_hbm, send_hbm, recv_hbm), refs = refs[:6], refs[6:]
+    lent_ref, node, halo, coarse, wa, send, recv, sems = refs
+    rows128 = share // 128
+    mine = pl.ds(pl.multiple_of(lax.axis_index("feat") * rows128, rows128), rows128)
+    loads = copies(
+        (
+            (halo_hbm, halo),
+            (coarse_hbm, coarse),
+            (node_hbm, node),
+            (wa_hbm, wa),
+            (send_hbm.at[mine, :], send),
+            (recv_hbm.at[mine, :], recv),
+        ),
+        sems,
+    )
+    for copy in loads[:3]:
         copy.wait()
     index_row = jnp.concatenate([lent_list(halo[...]), coarse[...].reshape(1, -1)], axis=1)
     lent_ref[...] = lax.dot_general(
@@ -111,39 +129,36 @@
         (((0,), (0,)), ((), ())),
         preferred_element_type=F32,
     ).astype(BF16)
-
-
-def local_kernel(
-    node,
-    lent_ref,
-    wb_ref,
-    limit,
-    latent_hbm,
-    send_hbm,
-    recv_hbm,
-    wa_hbm,
-    *refs,
-    layout,
-    block,
-):
-    count = (len(refs) - 8) // 2
+    for copy in loads[3:]:
+        copy.wait()
+
+
+def local_part(at, block, latent, send, recv, wa, wb, table):
+    part, some = slice(at, at + block), slice(at // 128, (at + block) // 128)
+    half = wa.shape[1]
+    width = latent.shape[1]
+    slots = table.shape[0] // 2
+    picks = jnp.concatenate(
+        [one_hot_rows(index_columns(index[some, :]), 0, slots) for index in (send, recv)], axis=1
+    )
+    return jnp.concatenate(
+        [
+            0.5 * (dot(latent[part, :], weight[:width, :]) + dot(picks, table[:, col : col + half]))
+            for weight, col in ((wa, 0), (wb, half))
+        ],
+        axis=1,
+    )
+
+
+def local_kernel(node, lent_ref, wa, wb, send_in, recv_in, limit, latent_hbm, *refs, layout, block):
+    count = (len(refs) - 7) // 2
     more_hbm, refs = refs[:count], refs[count:]
-    pre_ref, latent, send, recv, wa, *more = refs[: 5 + count]
-    table, sems, block_sems = refs[5 + count :]
+    pre_ref, latent, send, recv, table, *more = refs[: 5 + count]
+    sems, block_sems = refs[5 + count :]
     share, width = latent.shape
     half = wa.shape[1]
     feat, patch = lax.axis_index("feat"), lax.axis_index("patch")
     local_slots, used = layout.local_slots, layout.used
-    rows128 = share // 128
-    mine = pl.ds(pl.multiple_of(feat * rows128, rows128), rows128)
-    first = copies(
-        (
-            (wa_hbm, wa),
-            (send_hbm.at[mine, :], send),
-            (recv_hbm.at[mine, :], recv),
-        ),
-        sems,
-    )
     blocks = copies(
         [
             (
@@ -154,41 +169,56 @@
         ],
         block_sems,
     )
-    rest = copies(list(zip(more_hbm, more)), sems.at[pl.ds(3, count)])
-    for copy in first:
-        copy.wait()
+    rest = copies(list(zip(more_hbm, more)), sems)
     rows_in = jnp.concatenate([node[...], lent_ref[lent_ref.shape[0] - layout.coarse :, :]], axis=0)
     for side in range(2):
         base = side * local_slots
         rows = slice((side + 1) * width, (side + 2) * width)
-        for weight, col in ((wa, 0), (wb_ref, half)):
+        for weight, col in ((wa, 0), (wb, half)):
             table[base : base + used, col : col + half] = dot(rows_in, weight[rows, :]).astype(BF16)
         table[base + used : base + local_slots, :] = jnp.zeros((local_slots - used, 2 * half), BF16)
-    shape = (rows128, 128)
+    shape = send.shape
     edge = lax.broadcasted_iota(jnp.int32, shape, 0) * 128 + lax.broadcasted_iota(jnp.int32, shape, 1) + feat * share
     live = edge < limit[0]
-    for index in (send, recv):
-        index[...] = jnp.where(live, layout.slots(index[...], patch), DEAD)
+    for index_in, index in ((send_in, send), (recv_in, recv)):
+        index[...] = jnp.where(live, layout.slots(index_in[...], patch, feat), DEAD)
     for i, copy in enumerate(blocks):
-        part = slice(i * block, (i + 1) * block)
-        some = slice(i * block // 128, (i + 1) * block // 128)
-        picks = jnp.concatenate(
-            [one_hot_rows(index_columns(index[some, :]), 0, local_slots) for index in (send, recv)], axis=1
-        )
         copy.wait()
-        for weight, col in ((wa, 0), (wb_ref, half)):
-            cols = slice(col, col + half)
-            pre_ref[part, cols] = 0.5 * (dot(latent[part, :], weight[:width, :]) + dot(picks, table[:, cols]))
+        at = i * block
+        if at < pre_ref.shape[0]:
+            pre_ref[at : at + block, :] = local_part(at, block, latent, send, recv, wa, wb, table)
     for copy in rest:
         copy.wait()
 
 
+def second_kernel(latent, send, recv, wa, wb, table, mine, pre_ref, projected, block):
+    share, width = latent.shape
+    half = wa.shape[1]
+    done = share - pre_ref.shape[0]
+    group = mine.shape[0]
+    for at in range(done, share, block):
+        pre_ref[at - done : at - done + block, :] = local_part(at, block, latent, send, recv, wa, wb, table)
+    project(mine, wa, wb, projected)
+
+
+def project(rows, wa, wb, out):
+    group, width = rows.shape
+    half = wa.shape[1]
+    for side in range(2):
+        part = slice((side + 1) * width, (side + 2) * width)
+        for weight, col in ((wa, 0), (wb, half)):
+            out[side * group : (side + 1) * group, col : col + half] = (
+                0.5 * dot(rows[...], weight[part, :])
+            ).astype(BF16)
+
+
 def edge_kernel(
     pre_ref,
+    pre2_ref,
     latent_ref,
     send_ref,
     recv_ref,
-    mine_ref,
+    mine_table,
     theirs_ref,
     wa_ref,
     wb_ref,
@@ -199,7 +229,7 @@
     out_other_ref,
     group_mine_ref,
     group_other_ref,
-    table,
+    theirs_table,
     sums,
     layout,
     block,
@@ -208,22 +238,19 @@
     half = wa_ref.shape[1]
     group = layout.group
     feat = lax.axis_index("feat")
-    for side in range(2):
-        rows = slice((side + 1) * width, (side + 2) * width)
-        for weight, col in ((wa_ref, 0), (wb_ref, half)):
-            cols = slice(col, col + half)
-            base = side * 2 * group
-            for source, owner in ((mine_ref, feat), (theirs_ref, 1 - feat)):
-                at = pl.multiple_of(base + owner * group, group)
-                table[pl.ds(at, group), cols] = (0.5 * dot(source[...], weight[rows, :])).astype(BF16)
+    project(theirs_ref, wa_ref, wb_ref, theirs_table)
     gain = gain_ref[...].astype(F32).reshape(1, width)
     for at in range(0, share, block):
         part = slice(at, at + block)
         some = slice(at // 128, (at + block) // 128)
         receivers = recv_ref[some, :]
         columns = [index_columns(send_ref[some, :]), index_columns(receivers)]
-        picks = jnp.concatenate([one_hot_rows(column, layout.local_slots, 2 * group) for column in columns], axis=1)
-        hidden = silu_of_double(pre_ref[part, :] + dot(picks, table[...])).astype(BF16)
+        first = pre_ref.shape[0]
+        pre = pre_ref[part, :] if at < first else pre2_ref[at - first : at - first + block, :]
+        for base, table in ((layout.local_slots, mine_table), (layout.local_slots + group, theirs_table)):
+            picks = jnp.concatenate([one_hot_rows(column, base, group) for column in columns], axis=1)
+            pre = pre + dot(picks, table[...])
+        hidden = silu_of_double(pre).astype(BF16)
         pre = dot(hidden[:, :half], va_ref[...]) + dot(hidden[:, half:], vb_ref[...])
         live = jnp.concatenate([column[:, :1] for column in columns[1]], axis=0) != DEAD
         fresh = (latent_ref[part, :].astype(F32) + layer_norm(pre, gain, live)).astype(BF16)
@@ -232,8 +259,8 @@
         out_other_ref[part, :] = jnp.where(feat == 0, high, low)
         added = dot(one_hot_columns(flat_row(receivers), layout.local_slots, 2 * group), fresh)
         sums[...] = added if at == 0 else sums[...] + added
-    group_mine_ref[...] = sums[pl.ds(pl.multiple_of(feat * group, group), group), :]
-    group_other_ref[...] = sums[pl.ds(pl.multiple_of((1 - feat) * group, group), group), :].astype(BF16)
+    group_mine_ref[...] = sums[:group, :]
+    group_other_ref[...] = sums[group:, :].astype(BF16)
 
 
 def merge_kernel(mine_ref, theirs_ref, *out_refs):
@@ -330,7 +357,7 @@
         out_specs=out_specs,
         out_shape=outputs,
         scratch_shapes=list(scratch),
-        cost_estimate=pl.CostEstimate(flops=flops, bytes_accessed=4 * MIB, transcendentals=0),
+        cost_estimate=pl.CostEstimate(flops=flops, bytes_accessed=MIB // 4, transcendentals=0),
         compiler_params=pltpu.CompilerParams(vmem_limit_bytes=limit * MIB),
     )(*operands)
 
@@ -382,70 +409,84 @@
     def swap(values):
         return lax.ppermute(values, "feat", FEAT_SWAP)
 
-    edge_w1_b, edge_w2_b = swap(edge_w1), swap(edge_w2)
-
-    lent, node, halo_lists, coarse_list = call(
-        lend_kernel,
-        [in_hbm(array) for array in (node_latent, halo_rows, coarse_rows)],
-        [ANY_SPEC] * 3,
-        [shape(halo + coarse, width), like(node_latent), like(halo_rows), like(coarse_rows)],
-        [VMEM_SPEC] * 4,
+    edge_w1_b = swap(edge_w1)
+
+    index_rows = (edge_count // 128, 128)
+    core_rows = jax.ShapeDtypeStruct((share // 128, 128), jnp.int32)
+    lent, node, halo_lists, coarse_list, w1, send, recv = call(
+        functools.partial(lend_kernel, share=share),
+        [
+            in_hbm(array)
+            for array in (
+                node_latent,
+                halo_rows,
+                coarse_rows,
+                edge_w1,
+                edge_senders.reshape(index_rows),
+                edge_receivers.reshape(index_rows),
+            )
+        ],
+        [ANY_SPEC] * 6,
+        [shape(halo + coarse, width)]
+        + [like(array) for array in (node_latent, halo_rows, coarse_rows, edge_w1)]
+        + [core_rows] * 2,
+        [VMEM_SPEC] * 7,
         2 * node_count * (halo + coarse) * width,
         8,
-        scratch=[dma((3,))],
+        scratch=[dma((6,))],
     )
     pairs = exchange_pairs(patches)
-    arrived = [lax.ppermute(lent, both, pairs[0])]
-    for some in pairs[1:]:
-        arrived.append(lax.ppermute(lent[halo:], both, some))
-
-    index_rows = (edge_count // 128, 128)
+    arrived = [
+        lax.ppermute(lent[halo:] if i else lent, both, pairs[i]) for i in reversed(range(len(pairs)))
+    ][::-1]
+
     more = (edge_w2, edge_gain, node_w1, node_w2, node_gain)
-    pre, latent, send, recv, w1, w2, e_gain, n_w1, n_w2, n_gain = call(
+    first = share // 2
+    pre, latent, send, recv, table, w2, e_gain, n_w1, n_w2, n_gain = call(
         functools.partial(local_kernel, layout=layout, block=block),
-        [node, lent, edge_w1_b, edge_counts]
-        + [
-            in_hbm(array)
-            for array in (
-                edge_latent,
-                edge_senders.reshape(index_rows),
-                edge_receivers.reshape(index_rows),
-                edge_w1,
-                *more,
-            )
-        ],
-        [VMEM_SPEC] * 3 + [pl.BlockSpec(memory_space=pltpu.SMEM)] + [ANY_SPEC] * (4 + len(more)),
+        [node, lent, w1, edge_w1_b, send, recv, edge_counts] + [in_hbm(array) for array in (edge_latent, *more)],
+        [VMEM_SPEC] * 6 + [pl.BlockSpec(memory_space=pltpu.SMEM)] + [ANY_SPEC] * (1 + len(more)),
         [
-            shape(share, width, F32),
+            shape(first, width, F32),
             shape(share, width),
-            shape(share // 128, 128, jnp.int32),
-            shape(share // 128, 128, jnp.int32),
-            like(edge_w1),
+            core_rows,
+            core_rows,
+            shape(2 * local_slots, width),
         ]
         + [like(array) for array in more],
         [VMEM_SPEC] * (5 + len(more)),
-        2 * width * width * share + 4 * used * width * width + 4 * share * local_slots * width,
+        (2 * width * width * first + 4 * used * width * width + 4 * first * local_slots * width) // BESIDE,
         LIMIT,
-        scratch=[
-            pltpu.VMEM((2 * local_slots, width), BF16),
-            dma((3 + len(more),)),
-            dma((share // block,)),
-        ],
-    )
-    *arrived, pre = lax.optimization_barrier((*arrived, pre))
+        scratch=[dma((len(more),)), dma((share // block,))],
+    )
+    pre, *arrived = lax.optimization_barrier((pre, *arrived))
     table_mine = jnp.concatenate(arrived, axis=0)
     table_theirs = swap(table_mine)
-    node_w1_b, node_w2_b = swap(n_w1), swap(n_w2)
+    edge_w2_b = swap(w2)
+    pre2, projected = call(
+        functools.partial(second_kernel, block=block),
+        (latent, send, recv, w1, edge_w1_b, table, table_mine),
+        [VMEM_SPEC] * 7,
+        [shape(share - first, width, F32), shape(2 * group, width)],
+        [VMEM_SPEC] * 2,
+        2 * width * width * (share - first) + 4 * (share - first) * local_slots * width + 4 * group * width * width,
+        LIMIT,
+    )
+    n_w1_b, n_w2_b = lax.optimization_barrier((n_w1, n_w2, pre2))[:2]
+    node_w1_b, node_w2_b = swap(n_w1_b), swap(n_w2_b)
 
     mine, other, group_mine, group_other = call(
         functools.partial(edge_kernel, layout=layout, block=block),
-        (pre, latent, send, recv, table_mine, table_theirs, w1, edge_w1_b, w2, edge_w2_b, e_gain),
-        [VMEM_SPEC] * 11,
+        (pre, pre2, latent, send, recv, projected, table_theirs, w1, edge_w1_b, w2, edge_w2_b, e_gain),
+        [VMEM_SPEC] * 12,
         [shape(share, half), shape(share, half), shape(group, width, F32), shape(group, width)],
         [VMEM_SPEC] * 4,
-        2 * share * width * (width + 6 * group) + 8 * group * width * width,
+        2 * share * width * (width + 6 * group) + 4 * group * width * width,
         LIMIT,
-        scratch=[pltpu.VMEM((4 * group, width), BF16), pltpu.VMEM((2 * group, width), F32)],
+        scratch=[pltpu.VMEM((2 * group, width), BF16), pltpu.VMEM((2 * group, width), F32)],
+    )
+    node_w1_b, node_w2_b, mine, other, group_mine, group_other = lax.optimization_barrier(
+        (node_w1_b, node_w2_b, mine, other, group_mine, group_other)
     )
 
     group_theirs = swap(group_other)
@@ -460,17 +501,19 @@
         8,
     )
     *outgoing, mine, other = lax.optimization_barrier((*outgoing, mine, other))
-    back = [lax.ppermute(part, both, some) for part, some in zip(outgoing, pairs)]
-    edges_theirs = swap(other)
+    back = [lax.ppermute(outgoing[i], both, pairs[i]) for i in reversed(range(len(pairs)))][::-1]
     local_sums, node_pre = call(
         functools.partial(local_sums_kernel, block=block),
         (mine, other, recv, node, n_w1, node_w1_b),
         [VMEM_SPEC] * 6,
         [shape(used, width, F32), shape(node_count, width, F32)],
         [VMEM_SPEC] * 2,
-        2 * share * width * used + 2 * node_count * width * width,
+        (2 * share * width * used + 2 * node_count * width * width) // BESIDE,
         16,
     )
+    edges_theirs = swap(other)
+    local_sums, *back = lax.optimization_barrier((local_sums, *back[::-1]))
+    back = back[::-1]
     own, rounded = call(
         receive_kernel,
         (local_sums, halo_lists, coarse_list, *back),

time: 47.1 us -> 44.2 us (0.938)
  waiting for transfers between devices: 6.39 us -> 2.96 us
  starting transfers between devices: 17.3 us -> 19.1 us
  Pallas kernels: 21.6 us -> 20.5 us
    ppermute x8, starting transfers between devices: 11.4 us -> 14.9 us  [the longest x4 7.93 us: on_device(): lax.ppermute(outgoing[i], both, pairs[i])]
    ppermute x8, waiting for transfers between devices: 1.94 us -> 0.06 us  [the longest x4 0.05 us: on_device(): lax.ppermute(outgoing[i], both, pairs[i])]
    ppermute x8, starting transfers between devices: 5.93 us -> 4.17 us  [swap(): return lax.ppermute(values, 'feat', FEAT_SWAP)]
    ppermute x8, waiting for transfers between devices: 4.45 us -> 2.9 us  [swap(): return lax.ppermute(values, 'feat', FEAT_SWAP)]
    pallas_call x7 -> x8, Pallas kernels: 21.6 us -> 20.5 us  [call(): pl.pallas_call(kernel, in_specs=in_specs, out_specs=out_specs, out_shape=...]
  transfers between devices with their start and end apart: 16 -> 16, of which waited for: 4 -> 2; matrix products, arithmetic and copies ran while one was open for 0% -> 0% of each run, Pallas kernels for 40% -> 40%
where the time goes in v4:
time: 44.2 us; the launch traced here: 44 us
  Pallas kernels  20.5 us (46%)
  starting transfers between devices  19.1 us (43%)
  waiting for transfers between devices  2.96 us (7%)
  between operations  1.44 us (3%)
    pallas_call x8, Pallas kernels, call(): pl.pallas_call(kernel, in_specs=in_specs, out_specs=out_specs, out_shape=...  20.5 us
    ppermute x4, starting transfers between devices, on_device(): lax.ppermute(outgoing[i], both, pairs[i])  7.93 us
    ppermute x4, starting transfers between devices, on_device(): lax.ppermute(lent[halo:] if i else lent, both, pairs[i])  6.98 us
    ppermute x8, starting transfers between devices, swap(): return lax.ppermute(values, 'feat', FEAT_SWAP)  4.17 us
    ppermute x8, waiting for transfers between devices, swap(): return lax.ppermute(values, 'feat', FEAT_SWAP)  2.9 us
  transfers between devices with their start and end apart: 16, of which 2 were waited for; matrix products, arithmetic and copies ran while one was open for 0% of the time, Pallas kernels for 40%

profile of v4, /device:TPU:0, one launch (start us, length us, event | category | flops | bytes accessed | tf_op | source)
XLA Modules:
  0.0 44.0 jit_solution(9953271147435733110)
XLA Ops:
  0.6 0.5 %collective-permute-start = (bf16[1536,256]{1,0:T(8,128)(2,1)}, bf16[1536,256]{1,0:T(8,128)(2,1)S(1)}, u32[]{:S(2)}, u32[]{:S(2)}) collective-permute-start(bf16[1536,256]{1,0:T(8,128)(2,1)} %refs_3_.2), channel_id=1, source_target_pairs={{0,1},{1,0},{2,3},{3,2},{4,5},{5,4},{6,7},{7,6},{8,9},{9,8},{10,11... | collective-permute-start | bytes 2359304 | tf_op jit(solution)/shard_map/ppermute | solution.py:410
  1.1 1.5 %shard_map.140 = (bf16[160,512]{1,0:T(8,128)(2,1)S(1)}, bf16[640,512]{1,0:T(8,128)(2,1)S(1)}, s32[2,128]{1,0:T(2,128)S(1)}, s32[32]{0:T(128)S(1)}, bf16[1536,256...) custom-call(bf16[640,512]{1,0:T(8,128)(2,1)} %refs_0_.2, s32[2,128]{1,0:T(2,128)} %refs_1_.2, ...), custom_call_target="tpu_custom_call" | custom-call | flops 104857600 | bytes 262144 | tf_op jit(solution)/shard_map/pallas_call | solution.py:354
  2.7 2.6 %collective-permute-start.1 = (bf16[160,512]{1,0:T(8,128)(2,1)S(1)}, bf16[160,512]{1,0:T(8,128)(2,1)S(1)}, u32[]{:S(2)}, u32[]{:S(2)}) collective-permute-start(bf16[160,512]{1,0:T(8,128)(2,1)S(1)} %get-tuple-element.58.lent_ref), channel_id=1, source_target_pairs={{0,2},{1,15},{2,0},{3,5},{4,6},{5,3},{6,4},{7,9},{8,10},{9,7},{10,... | collective-permute-start | bytes 491528 | tf_op jit(solution)/shard_map/ppermute | solution.py:440
  5.3 3.6 %collective-permute-start.4 = (bf16[32,512]{1,0:T(8,128)(2,1)S(1)}, bf16[32,512]{1,0:T(8,128)(2,1)S(1)}, u32[]{:S(2)}, u32[]{:S(2)}) collective-permute-start(bf16[32,512]{1,0:T(8,128)(2,1)S(1)} %slice.2), channel_id=1, source_target_pairs={{0,12},{1,15},{2,14},{3,13},{4,8},{5,11},{6,10},{7,9},{8,4},{9,7},... | collective-permute-start | bytes 98312 | tf_op jit(solution)/shard_map/ppermute | solution.py:440
  8.9 0.8 %collective-permute-start.2 = (bf16[32,512]{1,0:T(8,128)(2,1)S(1)}, bf16[32,512]{1,0:T(8,128)(2,1)S(1)}, u32[]{:S(2)}, u32[]{:S(2)}) collective-permute-start(bf16[32,512]{1,0:T(8,128)(2,1)S(1)} %slice.2), channel_id=1, source_target_pairs={{0,4},{1,7},{2,6},{3,5},{4,0},{5,3},{6,2},{7,1},{8,12},{9,15},{10,... | collective-permute-start | bytes 98312 | tf_op jit(solution)/shard_map/ppermute | solution.py:440
  10.3 4.6 %shard_map.141 = (f32[1024,512]{1,0:T(8,128)S(1)}, bf16[2048,512]{1,0:T(8,128)(2,1)S(1)}, s32[16,128]{1,0:T(8,128)S(1)}, s32[16,128]{1,0:T(8,128)S(1)}, bf16[153...) custom-call(bf16[640,512]{1,0:T(8,128)(2,1)S(1)} %get-tuple-element., ...), custom_call_target="tpu_custom_call" | custom-call | flops 285212672 | bytes 262144 | tf_op jit(solution)/shard_map/pallas_call | solution.py:354
  14.9 0.0 collective-permute-done.4
  15.0 0.0 collective-permute-done.1
  15.0 1.3 %collective-permute-start.7 = (bf16[256,512]{1,0:T(8,128)(2,1)S(1)}, bf16[256,512]{1,0:T(8,128)(2,1)S(1)}, u32[]{:S(2)}, u32[]{:S(2)}) collective-permute-start(bf16[256,512]{1,0:T(8,128)(2,1)S(1)} %constant_dynamic-update-slice_fusion.mine), channel_id=1, source_target_pairs={{0,1},{1,0},{2,3},{3,2},{4,5},{5,4},{6,7},{7,6},{8,9},{9,8},{10,11... | collective-permute-start | bytes 786440 | tf_op jit(solution)/shard_map/ppermute | solution.py:410
  16.3 0.1 collective-permute-start.8
  16.4 2.7 %shard_map.142 = (f32[1024,512]{1,0:T(8,128)S(1)}, bf16[512,512]{1,0:T(8,128)(2,1)S(1)}) custom-call(bf16[2048,512]{1,0:T(8,128)(2,1)S(1)} %get-tuple-element.64.latent.latent_ref, s32[16,128]{1,0:T(8,128)S(1)} %get-tuple-element.65.send.send_ref, s32[16,128]{1,0:T(8,128)S(1)} %get-tuple-element.66.recv.recv_ref, ...), custom_call_target="tpu_custom_call" | custom-call | flops 2415919104 | bytes 262144 | tf_op jit(solution)/shard_map/pallas_call | solution.py:354
  19.1 0.5 %collective-permute-start.5 = (bf16[1024,256]{1,0:T(8,128)(2,1)S(1)}, bf16[1024,256]{1,0:T(8,128)(2,1)S(1)}, u32[]{:S(2)}, u32[]{:S(2)}) collective-permute-start(bf16[1024,256]{1,0:T(8,128)(2,1)S(1)} %get-tuple-element.74.wa_ref), channel_id=1, source_target_pairs={{0,1},{1,0},{2,3},{3,2},{4,5},{5,4},{6,7},{7,6},{8,9},{9,8},{10,11... | collective-permute-start | bytes 1572872 | tf_op jit(solution)/shard_map/ppermute | solution.py:410
  19.6 0.1 collective-permute-start.6
  19.7 6.4 %shard_map.143 = (bf16[2048,256]{1,0:T(8,128)(2,1)S(1)}, bf16[2048,256]{1,0:T(8,128)(2,1)S(1)}, f32[256,512]{1,0:T(8,128)S(1)}, bf16[256,512]{1,0:T(8,128)(2,1)S(1)}) custom-call(f32[1024,512]{1,0:T(8,128)S(1)} %get-tuple-element.76.pre_ref, f32[1024,512]{1,0:T(8,128)S(1)} %get-tuple-element.73.pre2_ref, ...), custom_call_target="tpu_custom_call" | custom-call | flops 4563402752 | bytes 262144 | tf_op jit(solution)/shard_map/pallas_call | solution.py:354
  26.1 0.0 collective-permute-done.6.vb_ref
  26.1 0.0 collective-permute-done.5.wb_ref
  26.1 0.5 %collective-permute-start.9 = (bf16[256,512]{1,0:T(8,128)(2,1)S(1)}, bf16[256,512]{1,0:T(8,128)(2,1)S(1)}, u32[]{:S(2)}, u32[]{:S(2)}) collective-permute-start(bf16[256,512]{1,0:T(8,128)(2,1)S(1)} %get-tuple-element.85), channel_id=1, source_target_pairs={{0,1},{1,0},{2,3},{3,2},{4,5},{5,4},{6,7},{7,6},{8,9},{9,8},{10,11... | collective-permute-start | bytes 786440 | tf_op jit(solution)/shard_map/ppermute | solution.py:410
  26.6 1.2 %collective-permute-done.9.theirs_ref = bf16[256,512]{1,0:T(8,128)(2,1)S(1)} collective-permute-done((bf16[256,512]{1,0:T(8,128)(2,1)S(1)}, bf16[256,512]{1,0:T(8,128)(2,1)S(1)}, u32[]{:S(2)}, u32[]{:S(2)}) %collective-permute-start.9) | collective-permute-done | bytes 262176 | tf_op jit(solution)/shard_map/ppermute | solution.py:410
  27.8 0.1 shard_map.144
  27.8 0.4 collective-permute-start.15
  28.3 3.5 %collective-permute-start.13 = (bf16[160,512]{1,0:T(8,128)(2,1)S(1)}, bf16[160,512]{1,0:T(8,128)(2,1)S(1)}, u32[]{:S(2)}, u32[]{:S(2)}) collective-permute-start(bf16[160,512]{1,0:T(8,128)(2,1)S(1)} %get-tuple-element.99), channel_id=1, source_target_pairs={{0,2},{1,15},{2,0},{3,5},{4,6},{5,3},{6,4},{7,9},{8,10},{9,7},{10,... | collective-permute-start | bytes 491528 | tf_op jit(solution)/shard_map/ppermute | solution.py:504
  31.8 0.5 %collective-permute-start.10 = (bf16[32,512]{1,0:T(8,128)(2,1)S(1)}, bf16[32,512]{1,0:T(8,128)(2,1)S(1)}, u32[]{:S(2)}, u32[]{:S(2)}) collective-permute-start(bf16[32,512]{1,0:T(8,128)(2,1)S(1)} %get-tuple-element.96), channel_id=1, source_target_pairs={{0,12},{1,15},{2,14},{3,13},{4,8},{5,11},{6,10},{7,9},{8,4},{9,7},... | collective-permute-start | bytes 98312 | tf_op jit(solution)/shard_map/ppermute | solution.py:504
  32.3 0.0 collective-permute-start.11
  32.3 3.9 %collective-permute-start.12 = (bf16[32,512]{1,0:T(8,128)(2,1)S(1)}, bf16[32,512]{1,0:T(8,128)(2,1)S(1)}, u32[]{:S(2)}, u32[]{:S(2)}) collective-permute-start(bf16[32,512]{1,0:T(8,128)(2,1)S(1)} %get-tuple-element.98), channel_id=1, source_target_pairs={{0,4},{1,7},{2,6},{3,5},{4,0},{5,3},{6,2},{7,1},{8,12},{9,15},{10,... | collective-permute-start | bytes 98312 | tf_op jit(solution)/shard_map/ppermute | solution.py:504
  36.2 1.9 %shard_map.145 = (f32[672,512]{1,0:T(8,128)S(1)}, f32[640,512]{1,0:T(8,128)S(1)}) custom-call(bf16[2048,256]{1,0:T(8,128)(2,1)S(1)} %get-tuple-element.92.mine_ref, bf16[2048,256]{1,0:T(8,128)(2,1)S(1)} %get-tuple-element.93.other_ref, s32[16,128]{1,0:T(8,128)S(1)} %get-tuple-element.66.recv.recv_ref, bf16[640,512]{1,0:T(8,128)(2,1)S(1)} %get-tuple-element.57.node.node_ref, ...), custom_call_target="tpu_custom_call" | custom-call | flops 174483040 | bytes 262144 | tf_op jit(solution)/shard_map/pallas_call | solution.py:354
  38.1 0.0 collective-permute-done.10.refs_3_
  38.1 0.0 collective-permute-done.12.refs_1_
  38.2 0.5 %shard_map.146 = (f32[640,512]{1,0:T(8,128)S(1)}, bf16[640,512]{1,0:T(8,128)(2,1)S(1)}) custom-call(f32[672,512]{1,0:T(8,128)S(1)} %get-tuple-element.100.sums_ref, s32[2,128]{1,0:T(2,128)S(1)} %get-tuple-element.101.halo_ref, s32[32]{0:T(128)S(1)} %get-tuple-element.102.coarse_ref, bf16[160,512]{1,0:T(8,128)(2,1)S(1)} %collective-permute-done.13.refs_0_, ...), custom_call_target="tpu_custom_call" | custom-call | flops 188743680 | bytes 262144 | tf_op jit(solution)/shard_map/pallas_call | solution.py:354
  38.7 0.8 %collective-permute-start.14 = (bf16[640,512]{1,0:T(8,128)(2,1)S(1)}, bf16[640,512]{1,0:T(8,128)(2,1)S(1)}, u32[]{:S(2)}, u32[]{:S(2)}) collective-permute-start(bf16[640,512]{1,0:T(8,128)(2,1)S(1)} %get-tuple-element.108), channel_id=1, source_target_pairs={{0,1},{1,0},{2,3},{3,2},{4,5},{5,4},{6,7},{7,6},{8,9},{9,8},{10,11... | collective-permute-start | bytes 1966088 | tf_op jit(solution)/shard_map/ppermute | solution.py:410
  39.5 1.7 %collective-permute-done.14.partner_ref = bf16[640,512]{1,0:T(8,128)(2,1)S(1)} collective-permute-done((bf16[640,512]{1,0:T(8,128)(2,1)S(1)}, bf16[640,512]{1,0:T(8,128)(2,1)S(1)}, u32[]{:S(2)}, u32[]{:S(2)}) %collective-permute-start.14) | collective-permute-done | bytes 655392 | tf_op jit(solution)/shard_map/ppermute | solution.py:410
  41.2 0.0 collective-permute-done.15.theirs_ref
  41.2 2.8 %shard_map.147 = (bf16[640,256]{1,0:T(8,128)(2,1)}, bf16[4096,256]{1,0:T(8,128)(2,1)}) custom-call(bf16[640,512]{1,0:T(8,128)(2,1)S(1)} %get-tuple-element.57.node.node_ref, f32[640,512]{1,0:T(8,128)S(1)} %get-tuple-element.107.own_ref, bf16[640,512]{1,0:T(8,128)(2,1)S(1)} %collective-permute-done.14.partner_ref, f32[640,512]{1,0:T(8,128)S(1)} %get-tuple-element.109.pre_ref, ...), custom_call_target="tpu_custom_call" | custom-call | flops 671088640 | bytes 262144 | tf_op jit(solution)/shard_map/pallas_call | solution.py:354
  (13 shorter events, 0.1 us)
Async XLA Ops:
  0.6 9.7 %collective-permute-start = (bf16[1536,256]{1,0:T(8,128)(2,1)}, bf16[1536,256]{1,0:T(8,128)(2,1)S(1)}, u32[]{:S(2)}, u32[]{:S(2)}) collective-permute-start(bf16[1536,256]{1,0:T(8,128)(2,1)} %refs_3_.2), channel_id=1, source_target_pairs={{0,1},{1,0},{2,3},{3,2},{4,5},{5,4},{6,7},{7,6},{8,9},{9,8},{10,11... | collective-permute-start | bytes 2359304 | tf_op jit(solution)/shard_map/ppermute | solution.py:410
  2.7 12.3 %collective-permute-start.1 = (bf16[160,512]{1,0:T(8,128)(2,1)S(1)}, bf16[160,512]{1,0:T(8,128)(2,1)S(1)}, u32[]{:S(2)}, u32[]{:S(2)}) collective-permute-start(bf16[160,512]{1,0:T(8,128)(2,1)S(1)} %get-tuple-element.58.lent_ref), channel_id=1, source_target_pairs={{0,2},{1,15},{2,0},{3,5},{4,6},{5,3},{6,4},{7,9},{8,10},{9,7},{10,... | collective-permute-start | bytes 491528 | tf_op jit(solution)/shard_map/ppermute | solution.py:440
  5.3 9.7 %collective-permute-start.4 = (bf16[32,512]{1,0:T(8,128)(2,1)S(1)}, bf16[32,512]{1,0:T(8,128)(2,1)S(1)}, u32[]{:S(2)}, u32[]{:S(2)}) collective-permute-start(bf16[32,512]{1,0:T(8,128)(2,1)S(1)} %slice.2), channel_id=1, source_target_pairs={{0,12},{1,15},{2,14},{3,13},{4,8},{5,11},{6,10},{7,9},{8,4},{9,7},... | collective-permute-start | bytes 98312 | tf_op jit(solution)/shard_map/ppermute | solution.py:440
  8.9 6.1 %collective-permute-start.3 = (bf16[32,512]{1,0:T(8,128)(2,1)S(1)}, bf16[32,512]{1,0:T(8,128)(2,1)S(1)}, u32[]{:S(2)}, u32[]{:S(2)}) collective-permute-start(bf16[32,512]{1,0:T(8,128)(2,1)S(1)} %slice.2), channel_id=1, source_target_pairs={{0,8},{1,11},{2,10},{3,9},{4,12},{5,15},{6,14},{7,13},{8,0},{9,3},... | collective-permute-start | bytes 98312 | tf_op jit(solution)/shard_map/ppermute | solution.py:440
  8.9 6.1 %collective-permute-start.2 = (bf16[32,512]{1,0:T(8,128)(2,1)S(1)}, bf16[32,512]{1,0:T(8,128)(2,1)S(1)}, u32[]{:S(2)}, u32[]{:S(2)}) collective-permute-start(bf16[32,512]{1,0:T(8,128)(2,1)S(1)} %slice.2), channel_id=1, source_target_pairs={{0,4},{1,7},{2,6},{3,5},{4,0},{5,3},{6,2},{7,1},{8,12},{9,15},{10,... | collective-permute-start | bytes 98312 | tf_op jit(solution)/shard_map/ppermute | solution.py:440
  15.0 4.6 %collective-permute-start.7 = (bf16[256,512]{1,0:T(8,128)(2,1)S(1)}, bf16[256,512]{1,0:T(8,128)(2,1)S(1)}, u32[]{:S(2)}, u32[]{:S(2)}) collective-permute-start(bf16[256,512]{1,0:T(8,128)(2,1)S(1)} %constant_dynamic-update-slice_fusion.mine), channel_id=1, source_target_pairs={{0,1},{1,0},{2,3},{3,2},{4,5},{5,4},{6,7},{7,6},{8,9},{9,8},{10,11... | collective-permute-start | bytes 786440 | tf_op jit(solution)/shard_map/ppermute | solution.py:410
  16.3 3.3 %collective-permute-start.8 = (bf16[256,512]{1,0:T(8,128)(2,1)S(1)}, bf16[256,512]{1,0:T(8,128)(2,1)S(1)}, u32[]{:S(2)}, u32[]{:S(2)}) collective-permute-start(bf16[256,512]{1,0:T(8,128)(2,1)S(1)} %get-tuple-element.78.va_ref), channel_id=1, source_target_pairs={{0,1},{1,0},{2,3},{3,2},{4,5},{5,4},{6,7},{7,6},{8,9},{9,8},{10,11... | collective-permute-start | bytes 786440 | tf_op jit(solution)/shard_map/ppermute | solution.py:410
  19.1 7.0 %collective-permute-start.5 = (bf16[1024,256]{1,0:T(8,128)(2,1)S(1)}, bf16[1024,256]{1,0:T(8,128)(2,1)S(1)}, u32[]{:S(2)}, u32[]{:S(2)}) collective-permute-start(bf16[1024,256]{1,0:T(8,128)(2,1)S(1)} %get-tuple-element.74.wa_ref), channel_id=1, source_target_pairs={{0,1},{1,0},{2,3},{3,2},{4,5},{5,4},{6,7},{7,6},{8,9},{9,8},{10,11... | collective-permute-start | bytes 1572872 | tf_op jit(solution)/shard_map/ppermute | solution.py:410
  19.6 6.5 %collective-permute-start.6 = (bf16[256,512]{1,0:T(8,128)(2,1)S(1)}, bf16[256,512]{1,0:T(8,128)(2,1)S(1)}, u32[]{:S(2)}, u32[]{:S(2)}) collective-permute-start(bf16[256,512]{1,0:T(8,128)(2,1)S(1)} %get-tuple-element.75.va_ref), channel_id=1, source_target_pairs={{0,1},{1,0},{2,3},{3,2},{4,5},{5,4},{6,7},{7,6},{8,9},{9,8},{10,11... | collective-permute-start | bytes 786440 | tf_op jit(solution)/shard_map/ppermute | solution.py:410
  26.1 1.7 %collective-permute-start.9 = (bf16[256,512]{1,0:T(8,128)(2,1)S(1)}, bf16[256,512]{1,0:T(8,128)(2,1)S(1)}, u32[]{:S(2)}, u32[]{:S(2)}) collective-permute-start(bf16[256,512]{1,0:T(8,128)(2,1)S(1)} %get-tuple-element.85), channel_id=1, source_target_pairs={{0,1},{1,0},{2,3},{3,2},{4,5},{5,4},{6,7},{7,6},{8,9},{9,8},{10,11... | collective-permute-start | bytes 786440 | tf_op jit(solution)/shard_map/ppermute | solution.py:410
  27.8 13.4 %collective-permute-start.15 = (bf16[2048,256]{1,0:T(8,128)(2,1)S(1)}, bf16[2048,256]{1,0:T(8,128)(2,1)S(1)}, u32[]{:S(2)}, u32[]{:S(2)}) collective-permute-start(bf16[2048,256]{1,0:T(8,128)(2,1)S(1)} %get-tuple-element.93.other_ref), channel_id=1, source_target_pairs={{0,1},{1,0},{2,3},{3,2},{4,5},{5,4},{6,7},{7,6},{8,9},{9,8},{10,11... | collective-permute-start | bytes 3145736 | tf_op jit(solution)/shard_map/ppermute | solution.py:410
  28.3 9.9 %collective-permute-start.13 = (bf16[160,512]{1,0:T(8,128)(2,1)S(1)}, bf16[160,512]{1,0:T(8,128)(2,1)S(1)}, u32[]{:S(2)}, u32[]{:S(2)}) collective-permute-start(bf16[160,512]{1,0:T(8,128)(2,1)S(1)} %get-tuple-element.99), channel_id=1, source_target_pairs={{0,2},{1,15},{2,0},{3,5},{4,6},{5,3},{6,4},{7,9},{8,10},{9,7},{10,... | collective-permute-start | bytes 491528 | tf_op jit(solution)/shard_map/ppermute | solution.py:504
  31.8 6.3 %collective-permute-start.10 = (bf16[32,512]{1,0:T(8,128)(2,1)S(1)}, bf16[32,512]{1,0:T(8,128)(2,1)S(1)}, u32[]{:S(2)}, u32[]{:S(2)}) collective-permute-start(bf16[32,512]{1,0:T(8,128)(2,1)S(1)} %get-tuple-element.96), channel_id=1, source_target_pairs={{0,12},{1,15},{2,14},{3,13},{4,8},{5,11},{6,10},{7,9},{8,4},{9,7},... | collective-permute-start | bytes 98312 | tf_op jit(solution)/shard_map/ppermute | solution.py:504
  32.3 5.9 %collective-permute-start.11 = (bf16[32,512]{1,0:T(8,128)(2,1)S(1)}, bf16[32,512]{1,0:T(8,128)(2,1)S(1)}, u32[]{:S(2)}, u32[]{:S(2)}) collective-permute-start(bf16[32,512]{1,0:T(8,128)(2,1)S(1)} %get-tuple-element.97), channel_id=1, source_target_pairs={{0,8},{1,11},{2,10},{3,9},{4,12},{5,15},{6,14},{7,13},{8,0},{9,3},... | collective-permute-start | bytes 98312 | tf_op jit(solution)/shard_map/ppermute | solution.py:504
  32.3 5.9 %collective-permute-start.12 = (bf16[32,512]{1,0:T(8,128)(2,1)S(1)}, bf16[32,512]{1,0:T(8,128)(2,1)S(1)}, u32[]{:S(2)}, u32[]{:S(2)}) collective-permute-start(bf16[32,512]{1,0:T(8,128)(2,1)S(1)} %get-tuple-element.98), channel_id=1, source_target_pairs={{0,4},{1,7},{2,6},{3,5},{4,0},{5,3},{6,2},{7,1},{8,12},{9,15},{10,... | collective-permute-start | bytes 98312 | tf_op jit(solution)/shard_map/ppermute | solution.py:504
  38.7 2.5 %collective-permute-start.14 = (bf16[640,512]{1,0:T(8,128)(2,1)S(1)}, bf16[640,512]{1,0:T(8,128)(2,1)S(1)}, u32[]{:S(2)}, u32[]{:S(2)}) collective-permute-start(bf16[640,512]{1,0:T(8,128)(2,1)S(1)} %get-tuple-element.108), channel_id=1, source_target_pairs={{0,1},{1,0},{2,3},{3,2},{4,5},{5,4},{6,7},{7,6},{8,9},{9,8},{10,11... | collective-permute-start | bytes 1966088 | tf_op jit(solution)/shard_map/ppermute | solution.py:410

commit v5 on v4

--- a/solution.py
+++ b/solution.py
@@ -26,14 +26,25 @@
     return jnp.dot(a, b, preferred_element_type=F32)
 
 
+def lane_sums(x):
+    high = x.astype(BF16)
+    low = (x - high.astype(F32)).astype(BF16)
+    ones = jnp.ones((128, 128), BF16)
+    return dot(high, ones) + dot(low, ones)
+
+
 def layer_norm(pre, gain, keep=None):
     width = pre.shape[1]
-    center = jnp.sum(pre, axis=1, keepdims=True) * (1.0 / width)
-    square = jnp.sum(pre * pre, axis=1, keepdims=True) * (1.0 / width)
+    parts = [pre[:, at : at + 128] for at in range(0, width, 128)]
+    center = jnp.sum(sum(parts), axis=1, keepdims=True) * (1.0 / width)
+    square = jnp.sum(sum(part * part for part in parts), axis=1, keepdims=True) * (1.0 / width)
     scale = lax.rsqrt(square - center * center + EPSILON)
     if keep is not None:
         scale = jnp.where(keep, scale, 0.0)
-    return (pre - center) * scale * gain
+    shift = -center * scale
+    return jnp.concatenate(
+        [(part * scale + shift) * gain[:, at * 128 : at * 128 + 128] for at, part in enumerate(parts)], axis=1
+    )
 
 
 def index_columns(index):
@@ -73,23 +84,31 @@
 
 
 class Layout:
-    def __init__(self, patches, node_count, halo, coarse):
-        self.patches, self.node_count, self.halo, self.coarse = patches, node_count, halo, coarse
-        self.group = halo + coarse * (patches // 2)
+    def __init__(self, rounds, node_count, halo, coarse):
+        self.patches = len(rounds[0][0])
+        self.node_count, self.halo, self.coarse = node_count, halo, coarse
+        self.group = halo + coarse * len(rounds)
         self.used = node_count + coarse
         self.local_slots = -(-self.used // 256) * 256
+        self.code = [[0] * self.patches for _ in range(self.patches)]
+        for i, some in reversed(list(enumerate(rounds))):
+            for core, targets in enumerate(some):
+                for patch, owner in enumerate(targets):
+                    self.code[patch][owner] = (core << 16) + halo + coarse * i
 
     def slots(self, rows, patch, feat):
         node_count, halo, coarse, group = self.node_count, self.halo, self.coarse, self.group
         at = rows - (node_count + 2 * halo)
         owner, entry = lax.shift_right_arithmetic(at, coarse.bit_length() - 1), at & (coarse - 1)
-        distance = patch ^ owner
+        place = jnp.zeros_like(rows)
+        for q in range(self.patches):
+            code = jnp.int32(0)
+            for p in range(self.patches):
+                code = jnp.where(patch == p, self.code[p][q], code)
+            remote = self.local_slots + (lax.shift_right_arithmetic(code, 16) ^ feat) * group + (code & 0xFFFF)
+            place = jnp.where(owner == q, jnp.where(patch == q, node_count, remote), place)
+        place = place + entry
         even = 1 - (patch & 1)
-        core0 = self.local_slots + feat * group
-        place = self.local_slots + ((distance & 1) ^ feat) * group + halo
-        place = place + coarse * lax.shift_right_arithmetic(distance, 1)
-        place = jnp.where(distance == 0, node_count, place)
-        place = jnp.where(distance == 1, core0 + halo, place) + entry
         lower = self.local_slots + (even ^ feat) * group - node_count + rows
         upper = self.local_slots + (1 - (even ^ feat)) * group - (node_count + halo) + rows
         lower = jnp.where(patch == 0, NOWHERE, lower)
@@ -104,19 +123,20 @@
     return jnp.where(which == 0, lists[0:1], lists[1:2])
 
 
-def lend_kernel(*refs, share):
+def lend_kernel(*refs, share, layout):
     (node_hbm, halo_hbm, coarse_hbm, wa_hbm, send_hbm, recv_hbm), refs = refs[:6], refs[6:]
     lent_ref, node, halo, coarse, wa, send, recv, sems = refs
     rows128 = share // 128
-    mine = pl.ds(pl.multiple_of(lax.axis_index("feat") * rows128, rows128), rows128)
+    feat, patch = lax.axis_index("feat"), lax.axis_index("patch")
+    mine = pl.ds(pl.multiple_of(feat * rows128, rows128), rows128)
     loads = copies(
         (
             (halo_hbm, halo),
             (coarse_hbm, coarse),
             (node_hbm, node),
-            (wa_hbm, wa),
             (send_hbm.at[mine, :], send),
             (recv_hbm.at[mine, :], recv),
+            (wa_hbm, wa),
         ),
         sems,
     )
@@ -129,11 +149,14 @@
         (((0,), (0,)), ((), ())),
         preferred_element_type=F32,
     ).astype(BF16)
-    for copy in loads[3:]:
+    for copy in loads[3:5]:
         copy.wait()
-
-
-def local_part(at, block, latent, send, recv, wa, wb, table):
+    for index in (send, recv):
+        index[...] = layout.slots(index[...], patch, feat)
+    loads[5].wait()
+
+
+def local_part(at, block, latent, send, recv, wa, wb, table, before=None):
     part, some = slice(at, at + block), slice(at // 128, (at + block) // 128)
     half = wa.shape[1]
     width = latent.shape[1]
@@ -141,35 +164,30 @@
     picks = jnp.concatenate(
         [one_hot_rows(index_columns(index[some, :]), 0, slots) for index in (send, recv)], axis=1
     )
+    picked = [dot(picks, table[:, col : col + half]) for col in (0, half)]
+    if before is not None:
+        before.wait()
+    rows = latent[part, :]
     return jnp.concatenate(
-        [
-            0.5 * (dot(latent[part, :], weight[:width, :]) + dot(picks, table[:, col : col + half]))
-            for weight, col in ((wa, 0), (wb, half))
-        ],
-        axis=1,
-    )
-
-
-def local_kernel(node, lent_ref, wa, wb, send_in, recv_in, limit, latent_hbm, *refs, layout, block):
-    count = (len(refs) - 7) // 2
+        [0.5 * (some + dot(rows, weight[:width, :])) for some, weight in zip(picked, (wa, wb))], axis=1
+    )
+
+
+def local_kernel(node, lent_ref, wa, wb, send, recv, latent_hbm, *refs, layout, block):
+    count = (len(refs) - 5) // 2
     more_hbm, refs = refs[:count], refs[count:]
-    pre_ref, latent, send, recv, table, *more = refs[: 5 + count]
-    sems, block_sems = refs[5 + count :]
+    pre_ref, latent, table, *more = refs[: 3 + count]
+    sems, block_sems = refs[3 + count :]
     share, width = latent.shape
     half = wa.shape[1]
-    feat, patch = lax.axis_index("feat"), lax.axis_index("patch")
+    feat = lax.axis_index("feat")
     local_slots, used = layout.local_slots, layout.used
-    blocks = copies(
-        [
-            (
-                latent_hbm.at[pl.ds(pl.multiple_of(feat * share + at, block), block), :],
-                latent.at[pl.ds(at, block), :],
-            )
-            for at in range(0, share, block)
-        ],
-        block_sems,
-    )
-    rest = copies(list(zip(more_hbm, more)), sems)
+    first = pre_ref.shape[0]
+    blocks = [
+        (latent_hbm.at[pl.ds(pl.multiple_of(feat * share + at, block), block), :], latent.at[pl.ds(at, block), :])
+        for at in range(0, share, block)
+    ]
+    early = copies(blocks[: first // block], block_sems)
     rows_in = jnp.concatenate([node[...], lent_ref[lent_ref.shape[0] - layout.coarse :, :]], axis=0)
     for side in range(2):
         base = side * local_slots
@@ -177,16 +195,10 @@
         for weight, col in ((wa, 0), (wb, half)):
             table[base : base + used, col : col + half] = dot(rows_in, weight[rows, :]).astype(BF16)
         table[base + used : base + local_slots, :] = jnp.zeros((local_slots - used, 2 * half), BF16)
-    shape = send.shape
-    edge = lax.broadcasted_iota(jnp.int32, shape, 0) * 128 + lax.broadcasted_iota(jnp.int32, shape, 1) + feat * share
-    live = edge < limit[0]
-    for index_in, index in ((send_in, send), (recv_in, recv)):
-        index[...] = jnp.where(live, layout.slots(index_in[...], patch, feat), DEAD)
-    for i, copy in enumerate(blocks):
-        copy.wait()
+    rest = copies(blocks[first // block :] + list(zip(more_hbm, more)), sems)
+    for i, copy in enumerate(early):
         at = i * block
-        if at < pre_ref.shape[0]:
-            pre_ref[at : at + block, :] = local_part(at, block, latent, send, recv, wa, wb, table)
+        pre_ref[at : at + block, :] = local_part(at, block, latent, send, recv, wa, wb, table, copy)
     for copy in rest:
         copy.wait()
 
@@ -213,6 +225,7 @@
 
 
 def edge_kernel(
+    limit_ref,
     pre_ref,
     pre2_ref,
     latent_ref,
@@ -227,10 +240,10 @@
     gain_ref,
     out_mine_ref,
     out_other_ref,
-    group_mine_ref,
+    fresh_all,
     group_other_ref,
+    live_recv_ref,
     theirs_table,
-    sums,
     layout,
     block,
 ):
@@ -239,11 +252,14 @@
     group = layout.group
     feat = lax.axis_index("feat")
     project(theirs_ref, wa_ref, wb_ref, theirs_table)
+    shape = recv_ref.shape
+    edge = lax.broadcasted_iota(jnp.int32, shape, 0) * 128 + lax.broadcasted_iota(jnp.int32, shape, 1) + feat * share
+    live_recv_ref[...] = jnp.where(edge < limit_ref[0], recv_ref[...], DEAD)
     gain = gain_ref[...].astype(F32).reshape(1, width)
     for at in range(0, share, block):
         part = slice(at, at + block)
         some = slice(at // 128, (at + block) // 128)
-        receivers = recv_ref[some, :]
+        receivers = live_recv_ref[some, :]
         columns = [index_columns(send_ref[some, :]), index_columns(receivers)]
         first = pre_ref.shape[0]
         pre = pre_ref[part, :] if at < first else pre2_ref[at - first : at - first + block, :]
@@ -252,15 +268,18 @@
             pre = pre + dot(picks, table[...])
         hidden = silu_of_double(pre).astype(BF16)
         pre = dot(hidden[:, :half], va_ref[...]) + dot(hidden[:, half:], vb_ref[...])
-        live = jnp.concatenate([column[:, :1] for column in columns[1]], axis=0) != DEAD
+        live = jnp.concatenate(columns[1], axis=0) != DEAD
         fresh = (latent_ref[part, :].astype(F32) + layer_norm(pre, gain, live)).astype(BF16)
         low, high = fresh[:, : width // 2], fresh[:, width // 2 :]
         out_mine_ref[part, :] = jnp.where(feat == 0, low, high)
         out_other_ref[part, :] = jnp.where(feat == 0, high, low)
-        added = dot(one_hot_columns(flat_row(receivers), layout.local_slots, 2 * group), fresh)
-        sums[...] = added if at == 0 else sums[...] + added
-    group_mine_ref[...] = sums[:group, :]
-    group_other_ref[...] = sums[group:, :].astype(BF16)
+        fresh_all[part, :] = fresh
+    receivers = flat_row(live_recv_ref[...])
+    group_other_ref[...] = dot(one_hot_columns(receivers, layout.local_slots + group, group), fresh_all[...]).astype(BF16)
+
+
+def group_sums_kernel(fresh_ref, recv_ref, sums_ref, first):
+    sums_ref[...] = dot(one_hot_columns(flat_row(recv_ref[...]), first, sums_ref.shape[0]), fresh_ref[...])
 
 
 def merge_kernel(mine_ref, theirs_ref, *out_refs):
@@ -272,20 +291,10 @@
         at += rows
 
 
-def local_sums_kernel(mine_ref, other_ref, recv_ref, node_ref, wa_ref, wb_ref, sums_ref, pre_ref, block):
+def local_sums_kernel(fresh_ref, recv_ref, node_ref, wa_ref, wb_ref, sums_ref, pre_ref):
     width = node_ref.shape[1]
-    share, half = mine_ref.shape
-    used = sums_ref.shape[0]
-    feat = lax.axis_index("feat")
-    mine = other = None
-    for at in range(0, share, block):
-        part = slice(at, at + block)
-        picks = one_hot_columns(flat_row(recv_ref[at // 128 : (at + block) // 128, :]), 0, used)
-        new_mine, new_other = dot(picks, mine_ref[part, :]), dot(picks, other_ref[part, :])
-        mine = new_mine if mine is None else mine + new_mine
-        other = new_other if other is None else other + new_other
-    sums_ref[:, :half] = jnp.where(feat == 0, mine, other)
-    sums_ref[:, half:] = jnp.where(feat == 0, other, mine)
+    half = wa_ref.shape[1]
+    sums_ref[...] = dot(one_hot_columns(flat_row(recv_ref[...]), 0, sums_ref.shape[0]), fresh_ref[...])
     pre_ref[:, :half] = dot(node_ref[...], wa_ref[:width, :])
     pre_ref[:, half:] = dot(node_ref[...], wb_ref[:width, :])
 
@@ -362,11 +371,25 @@
     )(*operands)
 
 
-def exchange_pairs(count):
+def pairing(count, pairs):
+    targets = [None] * count
+    for p, q in pairs:
+        targets[p], targets[q] = q, p
+    return targets
+
+
+def exchange_rounds(count):
     across = [(p + 1 if p % 2 else p - 1) % count for p in range(count)]
-    rounds = [([p ^ 1 for p in range(count)], across)]
-    for distance in range(2, count, 2):
-        rounds.append(([p ^ distance for p in range(count)], [p ^ (distance + 1) for p in range(count)]))
+    apart = lambda distance: [p ^ distance for p in range(count)]
+    rounds = [(apart(1), across)]
+    if count == 8:
+        mixed = pairing(count, [(0, 3), (4, 7), (1, 6), (2, 5)])
+        return rounds + [(apart(4), apart(5)), (apart(2), apart(2)), (apart(6), mixed)]
+    return rounds + [(apart(distance), apart(distance + 1)) for distance in range(2, count, 2)]
+
+
+def exchange_pairs(rounds):
+    count = len(rounds[0][0])
     return [
         [(2 * p + feat, 2 * targets[p] + feat) for p in range(count) for feat, targets in enumerate(some)]
         for some in rounds
@@ -394,7 +417,8 @@
     halo, coarse = halo_rows.shape[1], coarse_rows.shape[0]
     patches = lax.axis_size("patch")
     both = ("patch", "feat")
-    layout = Layout(patches, node_count, halo, coarse)
+    rounds = exchange_rounds(patches)
+    layout = Layout(rounds, node_count, halo, coarse)
     group, used, local_slots = layout.group, layout.used, layout.local_slots
     share = edge_count // 2
     block = 512
@@ -414,7 +438,7 @@
     index_rows = (edge_count // 128, 128)
     core_rows = jax.ShapeDtypeStruct((share // 128, 128), jnp.int32)
     lent, node, halo_lists, coarse_list, w1, send, recv = call(
-        functools.partial(lend_kernel, share=share),
+        functools.partial(lend_kernel, share=share, layout=layout),
         [
             in_hbm(array)
             for array in (
@@ -435,29 +459,27 @@
         8,
         scratch=[dma((6,))],
     )
-    pairs = exchange_pairs(patches)
+    pairs = exchange_pairs(rounds)
     arrived = [
         lax.ppermute(lent[halo:] if i else lent, both, pairs[i]) for i in reversed(range(len(pairs)))
     ][::-1]
 
     more = (edge_w2, edge_gain, node_w1, node_w2, node_gain)
     first = share // 2
-    pre, latent, send, recv, table, w2, e_gain, n_w1, n_w2, n_gain = call(
+    pre, latent, table, w2, e_gain, n_w1, n_w2, n_gain = call(
         functools.partial(local_kernel, layout=layout, block=block),
-        [node, lent, w1, edge_w1_b, send, recv, edge_counts] + [in_hbm(array) for array in (edge_latent, *more)],
-        [VMEM_SPEC] * 6 + [pl.BlockSpec(memory_space=pltpu.SMEM)] + [ANY_SPEC] * (1 + len(more)),
+        [node, lent, w1, edge_w1_b, send, recv] + [in_hbm(array) for array in (edge_latent, *more)],
+        [VMEM_SPEC] * 6 + [ANY_SPEC] * (1 + len(more)),
         [
             shape(first, width, F32),
             shape(share, width),
-            core_rows,
-            core_rows,
             shape(2 * local_slots, width),
         ]
         + [like(array) for array in more],
-        [VMEM_SPEC] * (5 + len(more)),
+        [VMEM_SPEC] * (3 + len(more)),
         (2 * width * width * first + 4 * used * width * width + 4 * first * local_slots * width) // BESIDE,
         LIMIT,
-        scratch=[dma((len(more),)), dma((share // block,))],
+        scratch=[dma((len(more) + (share - first) // block,)), dma((first // block,))],
     )
     pre, *arrived = lax.optimization_barrier((pre, *arrived))
     table_mine = jnp.concatenate(arrived, axis=0)
@@ -475,21 +497,30 @@
     n_w1_b, n_w2_b = lax.optimization_barrier((n_w1, n_w2, pre2))[:2]
     node_w1_b, node_w2_b = swap(n_w1_b), swap(n_w2_b)
 
-    mine, other, group_mine, group_other = call(
+    mine, other, fresh, group_other, live_recv = call(
         functools.partial(edge_kernel, layout=layout, block=block),
-        (pre, pre2, latent, send, recv, projected, table_theirs, w1, edge_w1_b, w2, edge_w2_b, e_gain),
-        [VMEM_SPEC] * 12,
-        [shape(share, half), shape(share, half), shape(group, width, F32), shape(group, width)],
-        [VMEM_SPEC] * 4,
+        (edge_counts, pre, pre2, latent, send, recv, projected, table_theirs, w1, edge_w1_b, w2, edge_w2_b, e_gain),
+        [pl.BlockSpec(memory_space=pltpu.SMEM)] + [VMEM_SPEC] * 12,
+        [shape(share, half), shape(share, half), shape(share, width), shape(group, width), core_rows],
+        [VMEM_SPEC] * 5,
         2 * share * width * (width + 6 * group) + 4 * group * width * width,
         LIMIT,
-        scratch=[pltpu.VMEM((2 * group, width), BF16), pltpu.VMEM((2 * group, width), F32)],
-    )
-    node_w1_b, node_w2_b, mine, other, group_mine, group_other = lax.optimization_barrier(
-        (node_w1_b, node_w2_b, mine, other, group_mine, group_other)
+        scratch=[pltpu.VMEM((2 * group, width), BF16)],
+    )
+    node_w1_b, node_w2_b, mine, other, fresh, group_other = lax.optimization_barrier(
+        (node_w1_b, node_w2_b, mine, other, fresh, group_other)
     )
 
     group_theirs = swap(group_other)
+    group_mine = call(
+        functools.partial(group_sums_kernel, first=local_slots),
+        (fresh, live_recv),
+        [VMEM_SPEC] * 2,
+        shape(group, width, F32),
+        VMEM_SPEC,
+        2 * share * width * group,
+        16,
+    )
     sizes = [halo + coarse] + [coarse] * (len(pairs) - 1)
     outgoing = call(
         merge_kernel,
@@ -500,12 +531,12 @@
         group * width,
         8,
     )
-    *outgoing, mine, other = lax.optimization_barrier((*outgoing, mine, other))
+    *outgoing, mine, other, fresh = lax.optimization_barrier((*outgoing, mine, other, fresh))
     back = [lax.ppermute(outgoing[i], both, pairs[i]) for i in reversed(range(len(pairs)))][::-1]
     local_sums, node_pre = call(
-        functools.partial(local_sums_kernel, block=block),
-        (mine, other, recv, node, n_w1, node_w1_b),
-        [VMEM_SPEC] * 6,
+        local_sums_kernel,
+        (fresh, live_recv, node, n_w1, node_w1_b),
+        [VMEM_SPEC] * 5,
         [shape(used, width, F32), shape(node_count, width, F32)],
         [VMEM_SPEC] * 2,
         (2 * share * width * used + 2 * node_count * width * width) // BESIDE,

time: 44.2 us -> 41.1 us (0.930)
  starting transfers between devices: 19.1 us -> 17 us
  waiting for transfers between devices: 2.96 us -> 2.26 us
    ppermute x8, starting transfers between devices: 4.17 us -> 3.05 us  [swap(): return lax.ppermute(values, 'feat', FEAT_SWAP)]
    ppermute x4, starting transfers between devices: 7.93 us -> 6.93 us  [on_device(): lax.ppermute(outgoing[i], both, pairs[i])]
    ppermute x8, waiting for transfers between devices: 2.9 us -> 2.2 us  [swap(): return lax.ppermute(values, 'feat', FEAT_SWAP)]
    pallas_call x8 -> x9, Pallas kernels: 20.5 us -> 20.1 us  [call(): pl.pallas_call(kernel, in_specs=in_specs, out_specs=out_specs, out_shape=...]
  transfers between devices with their start and end apart: 16 -> 16, of which waited for: 2 -> 2; matrix products, arithmetic and copies ran while one was open for 0% -> 0% of each run, Pallas kernels for 40% -> 42%
where the time goes in v5:
time: 41.1 us; the launch traced here: 41 us
  Pallas kernels  20.1 us (49%)
  starting transfers between devices  17 us (41%)
  waiting for transfers between devices  2.26 us (5%)
  between operations  1.6 us (4%)
    pallas_call x9, Pallas kernels, call(): pl.pallas_call(kernel, in_specs=in_specs, out_specs=out_specs, out_shape=...  20.1 us
    ppermute x4, starting transfers between devices, on_device(): lax.ppermute(lent[halo:] if i else lent, both, pairs[i])  6.98 us
    ppermute x4, starting transfers between devices, on_device(): lax.ppermute(outgoing[i], both, pairs[i])  6.93 us
    ppermute x8, starting transfers between devices, swap(): return lax.ppermute(values, 'feat', FEAT_SWAP)  3.05 us
    ppermute x8, waiting for transfers between devices, swap(): return lax.ppermute(values, 'feat', FEAT_SWAP)  2.2 us
  transfers between devices with their start and end apart: 16, of which 2 were waited for; matrix products, arithmetic and copies ran while one was open for 0% of the time, Pallas kernels for 42%

profile of v5, /device:TPU:0, one launch (start us, length us, event | category | flops | bytes accessed | tf_op | source)
XLA Modules:
  0.0 41.0 jit_solution(16691608612184186277)
XLA Ops:
  0.6 0.5 %collective-permute-start = (bf16[1536,256]{1,0:T(8,128)(2,1)}, bf16[1536,256]{1,0:T(8,128)(2,1)S(1)}, u32[]{:S(2)}, u32[]{:S(2)}) collective-permute-start(bf16[1536,256]{1,0:T(8,128)(2,1)} %refs_3_.2), channel_id=1, source_target_pairs={{0,1},{1,0},{2,3},{3,2},{4,5},{5,4},{6,7},{7,6},{8,9},{9,8},{10,11... | collective-permute-start | bytes 2359304 | tf_op jit(solution)/shard_map/ppermute | solution.py:434
  1.1 1.5 %shard_map.140 = (bf16[160,512]{1,0:T(8,128)(2,1)S(1)}, bf16[640,512]{1,0:T(8,128)(2,1)S(1)}, s32[2,128]{1,0:T(2,128)S(1)}, s32[32]{0:T(128)S(1)}, bf16[1536,256...) custom-call(bf16[640,512]{1,0:T(8,128)(2,1)} %refs_0_.2, s32[2,128]{1,0:T(2,128)} %refs_1_.2, ...), custom_call_target="tpu_custom_call" | custom-call | flops 104857600 | bytes 262144 | tf_op jit(solution)/shard_map/pallas_call | solution.py:363
  2.7 2.6 %collective-permute-start.1 = (bf16[160,512]{1,0:T(8,128)(2,1)S(1)}, bf16[160,512]{1,0:T(8,128)(2,1)S(1)}, u32[]{:S(2)}, u32[]{:S(2)}) collective-permute-start(bf16[160,512]{1,0:T(8,128)(2,1)S(1)} %get-tuple-element.58.lent_ref), channel_id=1, source_target_pairs={{0,2},{1,15},{2,0},{3,5},{4,6},{5,3},{6,4},{7,9},{8,10},{9,7},{10,... | collective-permute-start | bytes 491528 | tf_op jit(solution)/shard_map/ppermute | solution.py:464
  5.3 3.6 %collective-permute-start.4 = (bf16[32,512]{1,0:T(8,128)(2,1)S(1)}, bf16[32,512]{1,0:T(8,128)(2,1)S(1)}, u32[]{:S(2)}, u32[]{:S(2)}) collective-permute-start(bf16[32,512]{1,0:T(8,128)(2,1)S(1)} %slice.2), channel_id=1, source_target_pairs={{0,12},{1,7},{2,14},{3,13},{4,8},{5,11},{6,10},{7,1},{8,4},{9,15},... | collective-permute-start | bytes 98312 | tf_op jit(solution)/shard_map/ppermute | solution.py:464
  8.9 0.8 %collective-permute-start.2 = (bf16[32,512]{1,0:T(8,128)(2,1)S(1)}, bf16[32,512]{1,0:T(8,128)(2,1)S(1)}, u32[]{:S(2)}, u32[]{:S(2)}) collective-permute-start(bf16[32,512]{1,0:T(8,128)(2,1)S(1)} %slice.2), channel_id=1, source_target_pairs={{0,8},{1,11},{2,10},{3,9},{4,12},{5,15},{6,14},{7,13},{8,0},{9,3},... | collective-permute-start | bytes 98312 | tf_op jit(solution)/shard_map/ppermute | solution.py:464
  9.7 0.0 collective-permute-done.wb.wb_ref
  9.7 4.0 %shard_map.141 = (f32[1024,512]{1,0:T(8,128)S(1)}, bf16[2048,512]{1,0:T(8,128)(2,1)S(1)}, bf16[1536,512]{1,0:T(8,128)(2,1)S(1)}, bf16[256,512]{1,0:T(8,128)(2,1)...) custom-call(bf16[640,512]{1,0:T(8,128)(2,1)S(1)} %get-tuple-element., ...), custom_call_target="tpu_custom_call" | custom-call | flops 285212672 | bytes 262144 | tf_op jit(solution)/shard_map/pallas_call | solution.py:363
  13.7 0.0 collective-permute-done.4
  13.7 0.0 collective-permute-done.2
  13.7 0.0 collective-permute-done.1
  13.8 0.4 %collective-permute-start.7 = (bf16[256,512]{1,0:T(8,128)(2,1)S(1)}, bf16[256,512]{1,0:T(8,128)(2,1)S(1)}, u32[]{:S(2)}, u32[]{:S(2)}) collective-permute-start(bf16[256,512]{1,0:T(8,128)(2,1)S(1)} %constant_dynamic-update-slice_fusion.mine), channel_id=1, source_target_pairs={{0,1},{1,0},{2,3},{3,2},{4,5},{5,4},{6,7},{7,6},{8,9},{9,8},{10,11... | collective-permute-start | bytes 786440 | tf_op jit(solution)/shard_map/ppermute | solution.py:434
  14.2 0.1 collective-permute-start.8
  14.4 2.7 %shard_map.142 = (f32[1024,512]{1,0:T(8,128)S(1)}, bf16[512,512]{1,0:T(8,128)(2,1)S(1)}) custom-call(bf16[2048,512]{1,0:T(8,128)(2,1)S(1)} %get-tuple-element.64.latent.latent_ref, s32[16,128]{1,0:T(8,128)S(1)} %get-tuple-element.60.send.send_ref, s32[16,128]{1,0:T(8,128)S(1)} %get-tuple-element.61.recv.recv_ref, ...), custom_call_target="tpu_custom_call" | custom-call | flops 2415919104 | bytes 262144 | tf_op jit(solution)/shard_map/pallas_call | solution.py:363
  17.0 0.4 %collective-permute-start.5 = (bf16[1024,256]{1,0:T(8,128)(2,1)S(1)}, bf16[1024,256]{1,0:T(8,128)(2,1)S(1)}, u32[]{:S(2)}, u32[]{:S(2)}) collective-permute-start(bf16[1024,256]{1,0:T(8,128)(2,1)S(1)} %get-tuple-element.72.wa_ref), channel_id=1, source_target_pairs={{0,1},{1,0},{2,3},{3,2},{4,5},{5,4},{6,7},{7,6},{8,9},{9,8},{10,11... | collective-permute-start | bytes 1572872 | tf_op jit(solution)/shard_map/ppermute | solution.py:434
  18.1 0.2 collective-permute-start.6
  18.3 0.0 collective-permute-done.7.theirs_ref
  18.3 0.0 collective-permute-done.8.vb_ref
  18.3 5.6 %shard_map.143 = (bf16[2048,256]{1,0:T(8,128)(2,1)S(1)}, bf16[2048,256]{1,0:T(8,128)(2,1)S(1)}, bf16[2048,512]{1,0:T(8,128)(2,1)S(1)}, bf16[256,512]{1,0:T(8,128)(2,1)S(1)}, s32[16,128]{1,0:T(8,128)S(1)}) custom-call(s32[1]{0:T(128)S(6)} %copy.18.limit_ref, f32[1024,512]{1,0:T(8,128)S(1)} %get-tuple-element.74.pre_ref, ...), custom_call_target="tpu_custom_call" | custom-call | flops 4563402752 | bytes 262144 | tf_op jit(solution)/shard_map/pallas_call | solution.py:363
  23.9 0.4 %collective-permute-start.9 = (bf16[256,512]{1,0:T(8,128)(2,1)S(1)}, bf16[256,512]{1,0:T(8,128)(2,1)S(1)}, u32[]{:S(2)}, u32[]{:S(2)}) collective-permute-start(bf16[256,512]{1,0:T(8,128)(2,1)S(1)} %get-tuple-element.84), channel_id=1, source_target_pairs={{0,1},{1,0},{2,3},{3,2},{4,5},{5,4},{6,7},{7,6},{8,9},{9,8},{10,11... | collective-permute-start | bytes 786440 | tf_op jit(solution)/shard_map/ppermute | solution.py:434
  24.4 0.7 %shard_map.144.mine_ref = f32[256,512]{1,0:T(8,128)S(1)} custom-call(bf16[2048,512]{1,0:T(8,128)(2,1)S(1)} %get-tuple-element.91.fresh_ref, s32[16,128]{1,0:T(8,128)S(1)} %get-tuple-element.83.recv_ref), custom_call_target="tpu_custom_call" | custom-call | flops 536870912 | bytes 262144 | tf_op jit(solution)/shard_map/pallas_call | solution.py:363
  25.1 0.5 %collective-permute-done.9.theirs_ref = bf16[256,512]{1,0:T(8,128)(2,1)S(1)} collective-permute-done((bf16[256,512]{1,0:T(8,128)(2,1)S(1)}, bf16[256,512]{1,0:T(8,128)(2,1)S(1)}, u32[]{:S(2)}, u32[]{:S(2)}) %collective-permute-start.9) | collective-permute-done | bytes 262176 | tf_op jit(solution)/shard_map/ppermute | solution.py:434
  25.5 0.1 shard_map.145
  25.6 0.4 %collective-permute-start.15 = (bf16[2048,256]{1,0:T(8,128)(2,1)S(1)}, bf16[2048,256]{1,0:T(8,128)(2,1)S(1)}, u32[]{:S(2)}, u32[]{:S(2)}) collective-permute-start(bf16[2048,256]{1,0:T(8,128)(2,1)S(1)} %get-tuple-element.111), channel_id=1, source_target_pairs={{0,1},{1,0},{2,3},{3,2},{4,5},{5,4},{6,7},{7,6},{8,9},{9,8},{10,11... | collective-permute-start | bytes 3145736 | tf_op jit(solution)/shard_map/ppermute | solution.py:434
  26.0 2.5 %collective-permute-start.13 = (bf16[160,512]{1,0:T(8,128)(2,1)S(1)}, bf16[160,512]{1,0:T(8,128)(2,1)S(1)}, u32[]{:S(2)}, u32[]{:S(2)}) collective-permute-start(bf16[160,512]{1,0:T(8,128)(2,1)S(1)} %get-tuple-element.97), channel_id=1, source_target_pairs={{0,2},{1,15},{2,0},{3,5},{4,6},{5,3},{6,4},{7,9},{8,10},{9,7},{10,... | collective-permute-start | bytes 491528 | tf_op jit(solution)/shard_map/ppermute | solution.py:535
  28.6 1.3 %collective-permute-start.10 = (bf16[32,512]{1,0:T(8,128)(2,1)S(1)}, bf16[32,512]{1,0:T(8,128)(2,1)S(1)}, u32[]{:S(2)}, u32[]{:S(2)}) collective-permute-start(bf16[32,512]{1,0:T(8,128)(2,1)S(1)} %get-tuple-element.94), channel_id=1, source_target_pairs={{0,12},{1,7},{2,14},{3,13},{4,8},{5,11},{6,10},{7,1},{8,4},{9,15},... | collective-permute-start | bytes 98312 | tf_op jit(solution)/shard_map/ppermute | solution.py:535
  29.9 0.2 collective-permute-start.11
  30.1 2.9 %collective-permute-start.12 = (bf16[32,512]{1,0:T(8,128)(2,1)S(1)}, bf16[32,512]{1,0:T(8,128)(2,1)S(1)}, u32[]{:S(2)}, u32[]{:S(2)}) collective-permute-start(bf16[32,512]{1,0:T(8,128)(2,1)S(1)} %get-tuple-element.96), channel_id=1, source_target_pairs={{0,8},{1,11},{2,10},{3,9},{4,12},{5,15},{6,14},{7,13},{8,0},{9,3},... | collective-permute-start | bytes 98312 | tf_op jit(solution)/shard_map/ppermute | solution.py:535
  33.0 2.1 %shard_map.146 = (f32[672,512]{1,0:T(8,128)S(1)}, f32[640,512]{1,0:T(8,128)S(1)}) custom-call(bf16[2048,512]{1,0:T(8,128)(2,1)S(1)} %get-tuple-element.91.fresh_ref, s32[16,128]{1,0:T(8,128)S(1)} %get-tuple-element.83.recv_ref, bf16[640,512]{1,0:T(8,128)(2,1)S(1)} %get-tuple-element.57.node.node_ref, bf16[1024,256]{1,0:T(8,128)(2,1)S(1)} %get-tuple-element.72.wa_ref, ...), custom_call_target="tpu_custom_call" | custom-call | flops 174483040 | bytes 262144 | tf_op jit(solution)/shard_map/pallas_call | solution.py:363
  35.1 0.5 %shard_map.147 = (f32[640,512]{1,0:T(8,128)S(1)}, bf16[640,512]{1,0:T(8,128)(2,1)S(1)}) custom-call(f32[672,512]{1,0:T(8,128)S(1)} %get-tuple-element.98.sums_ref, s32[2,128]{1,0:T(2,128)S(1)} %get-tuple-element.99.halo_ref, s32[32]{0:T(128)S(1)} %get-tuple-element.100.coarse_ref, bf16[160,512]{1,0:T(8,128)(2,1)S(1)} %collective-permute-done.13.refs_0_, ...), custom_call_target="tpu_custom_call" | custom-call | flops 188743680 | bytes 262144 | tf_op jit(solution)/shard_map/pallas_call | solution.py:363
  35.7 0.5 %collective-permute-start.14 = (bf16[640,512]{1,0:T(8,128)(2,1)S(1)}, bf16[640,512]{1,0:T(8,128)(2,1)S(1)}, u32[]{:S(2)}, u32[]{:S(2)}) collective-permute-start(bf16[640,512]{1,0:T(8,128)(2,1)S(1)} %get-tuple-element.106), channel_id=1, source_target_pairs={{0,1},{1,0},{2,3},{3,2},{4,5},{5,4},{6,7},{7,6},{8,9},{9,8},{10,11... | collective-permute-start | bytes 1966088 | tf_op jit(solution)/shard_map/ppermute | solution.py:434
  36.1 1.7 %collective-permute-done.14.partner_ref = bf16[640,512]{1,0:T(8,128)(2,1)S(1)} collective-permute-done((bf16[640,512]{1,0:T(8,128)(2,1)S(1)}, bf16[640,512]{1,0:T(8,128)(2,1)S(1)}, u32[]{:S(2)}, u32[]{:S(2)}) %collective-permute-start.14) | collective-permute-done | bytes 655392 | tf_op jit(solution)/shard_map/ppermute | solution.py:434
  37.9 2.9 %shard_map.148 = (bf16[640,256]{1,0:T(8,128)(2,1)}, bf16[4096,256]{1,0:T(8,128)(2,1)}) custom-call(bf16[640,512]{1,0:T(8,128)(2,1)S(1)} %get-tuple-element.57.node.node_ref, f32[640,512]{1,0:T(8,128)S(1)} %get-tuple-element.105.own_ref, bf16[640,512]{1,0:T(8,128)(2,1)S(1)} %collective-permute-done.14.partner_ref, f32[640,512]{1,0:T(8,128)S(1)} %get-tuple-element.107.pre_ref, ...), custom_call_target="tpu_custom_call" | custom-call | flops 671088640 | bytes 262144 | tf_op jit(solution)/shard_map/pallas_call | solution.py:363
  (14 shorter events, 0.1 us)
Async XLA Ops:
  0.6 9.1 %collective-permute-start = (bf16[1536,256]{1,0:T(8,128)(2,1)}, bf16[1536,256]{1,0:T(8,128)(2,1)S(1)}, u32[]{:S(2)}, u32[]{:S(2)}) collective-permute-start(bf16[1536,256]{1,0:T(8,128)(2,1)} %refs_3_.2), channel_id=1, source_target_pairs={{0,1},{1,0},{2,3},{3,2},{4,5},{5,4},{6,7},{7,6},{8,9},{9,8},{10,11... | collective-permute-start | bytes 2359304 | tf_op jit(solution)/shard_map/ppermute | solution.py:434
  2.7 11.0 %collective-permute-start.1 = (bf16[160,512]{1,0:T(8,128)(2,1)S(1)}, bf16[160,512]{1,0:T(8,128)(2,1)S(1)}, u32[]{:S(2)}, u32[]{:S(2)}) collective-permute-start(bf16[160,512]{1,0:T(8,128)(2,1)S(1)} %get-tuple-element.58.lent_ref), channel_id=1, source_target_pairs={{0,2},{1,15},{2,0},{3,5},{4,6},{5,3},{6,4},{7,9},{8,10},{9,7},{10,... | collective-permute-start | bytes 491528 | tf_op jit(solution)/shard_map/ppermute | solution.py:464
  5.3 8.4 %collective-permute-start.4 = (bf16[32,512]{1,0:T(8,128)(2,1)S(1)}, bf16[32,512]{1,0:T(8,128)(2,1)S(1)}, u32[]{:S(2)}, u32[]{:S(2)}) collective-permute-start(bf16[32,512]{1,0:T(8,128)(2,1)S(1)} %slice.2), channel_id=1, source_target_pairs={{0,12},{1,7},{2,14},{3,13},{4,8},{5,11},{6,10},{7,1},{8,4},{9,15},... | collective-permute-start | bytes 98312 | tf_op jit(solution)/shard_map/ppermute | solution.py:464
  8.9 4.8 %collective-permute-start.3 = (bf16[32,512]{1,0:T(8,128)(2,1)S(1)}, bf16[32,512]{1,0:T(8,128)(2,1)S(1)}, u32[]{:S(2)}, u32[]{:S(2)}) collective-permute-start(bf16[32,512]{1,0:T(8,128)(2,1)S(1)} %slice.2), channel_id=1, source_target_pairs={{0,4},{1,5},{2,6},{3,7},{4,0},{5,1},{6,2},{7,3},{8,12},{9,13},{10,... | collective-permute-start | bytes 98312 | tf_op jit(solution)/shard_map/ppermute | solution.py:464
  8.9 4.8 %collective-permute-start.2 = (bf16[32,512]{1,0:T(8,128)(2,1)S(1)}, bf16[32,512]{1,0:T(8,128)(2,1)S(1)}, u32[]{:S(2)}, u32[]{:S(2)}) collective-permute-start(bf16[32,512]{1,0:T(8,128)(2,1)S(1)} %slice.2), channel_id=1, source_target_pairs={{0,8},{1,11},{2,10},{3,9},{4,12},{5,15},{6,14},{7,13},{8,0},{9,3},... | collective-permute-start | bytes 98312 | tf_op jit(solution)/shard_map/ppermute | solution.py:464
  13.8 4.5 %collective-permute-start.7 = (bf16[256,512]{1,0:T(8,128)(2,1)S(1)}, bf16[256,512]{1,0:T(8,128)(2,1)S(1)}, u32[]{:S(2)}, u32[]{:S(2)}) collective-permute-start(bf16[256,512]{1,0:T(8,128)(2,1)S(1)} %constant_dynamic-update-slice_fusion.mine), channel_id=1, source_target_pairs={{0,1},{1,0},{2,3},{3,2},{4,5},{5,4},{6,7},{7,6},{8,9},{9,8},{10,11... | collective-permute-start | bytes 786440 | tf_op jit(solution)/shard_map/ppermute | solution.py:434
  14.2 4.1 %collective-permute-start.8 = (bf16[256,512]{1,0:T(8,128)(2,1)S(1)}, bf16[256,512]{1,0:T(8,128)(2,1)S(1)}, u32[]{:S(2)}, u32[]{:S(2)}) collective-permute-start(bf16[256,512]{1,0:T(8,128)(2,1)S(1)} %get-tuple-element.76.va_ref), channel_id=1, source_target_pairs={{0,1},{1,0},{2,3},{3,2},{4,5},{5,4},{6,7},{7,6},{8,9},{9,8},{10,11... | collective-permute-start | bytes 786440 | tf_op jit(solution)/shard_map/ppermute | solution.py:434
  17.0 6.9 %collective-permute-start.5 = (bf16[1024,256]{1,0:T(8,128)(2,1)S(1)}, bf16[1024,256]{1,0:T(8,128)(2,1)S(1)}, u32[]{:S(2)}, u32[]{:S(2)}) collective-permute-start(bf16[1024,256]{1,0:T(8,128)(2,1)S(1)} %get-tuple-element.72.wa_ref), channel_id=1, source_target_pairs={{0,1},{1,0},{2,3},{3,2},{4,5},{5,4},{6,7},{7,6},{8,9},{9,8},{10,11... | collective-permute-start | bytes 1572872 | tf_op jit(solution)/shard_map/ppermute | solution.py:434
  18.1 5.8 %collective-permute-start.6 = (bf16[256,512]{1,0:T(8,128)(2,1)S(1)}, bf16[256,512]{1,0:T(8,128)(2,1)S(1)}, u32[]{:S(2)}, u32[]{:S(2)}) collective-permute-start(bf16[256,512]{1,0:T(8,128)(2,1)S(1)} %get-tuple-element.73.va_ref), channel_id=1, source_target_pairs={{0,1},{1,0},{2,3},{3,2},{4,5},{5,4},{6,7},{7,6},{8,9},{9,8},{10,11... | collective-permute-start | bytes 786440 | tf_op jit(solution)/shard_map/ppermute | solution.py:434
  23.9 1.6 %collective-permute-start.9 = (bf16[256,512]{1,0:T(8,128)(2,1)S(1)}, bf16[256,512]{1,0:T(8,128)(2,1)S(1)}, u32[]{:S(2)}, u32[]{:S(2)}) collective-permute-start(bf16[256,512]{1,0:T(8,128)(2,1)S(1)} %get-tuple-element.84), channel_id=1, source_target_pairs={{0,1},{1,0},{2,3},{3,2},{4,5},{5,4},{6,7},{7,6},{8,9},{9,8},{10,11... | collective-permute-start | bytes 786440 | tf_op jit(solution)/shard_map/ppermute | solution.py:434
  25.6 12.2 %collective-permute-start.15 = (bf16[2048,256]{1,0:T(8,128)(2,1)S(1)}, bf16[2048,256]{1,0:T(8,128)(2,1)S(1)}, u32[]{:S(2)}, u32[]{:S(2)}) collective-permute-start(bf16[2048,256]{1,0:T(8,128)(2,1)S(1)} %get-tuple-element.111), channel_id=1, source_target_pairs={{0,1},{1,0},{2,3},{3,2},{4,5},{5,4},{6,7},{7,6},{8,9},{9,8},{10,11... | collective-permute-start | bytes 3145736 | tf_op jit(solution)/shard_map/ppermute | solution.py:434
  26.0 9.1 %collective-permute-start.13 = (bf16[160,512]{1,0:T(8,128)(2,1)S(1)}, bf16[160,512]{1,0:T(8,128)(2,1)S(1)}, u32[]{:S(2)}, u32[]{:S(2)}) collective-permute-start(bf16[160,512]{1,0:T(8,128)(2,1)S(1)} %get-tuple-element.97), channel_id=1, source_target_pairs={{0,2},{1,15},{2,0},{3,5},{4,6},{5,3},{6,4},{7,9},{8,10},{9,7},{10,... | collective-permute-start | bytes 491528 | tf_op jit(solution)/shard_map/ppermute | solution.py:535
  28.6 6.5 %collective-permute-start.10 = (bf16[32,512]{1,0:T(8,128)(2,1)S(1)}, bf16[32,512]{1,0:T(8,128)(2,1)S(1)}, u32[]{:S(2)}, u32[]{:S(2)}) collective-permute-start(bf16[32,512]{1,0:T(8,128)(2,1)S(1)} %get-tuple-element.94), channel_id=1, source_target_pairs={{0,12},{1,7},{2,14},{3,13},{4,8},{5,11},{6,10},{7,1},{8,4},{9,15},... | collective-permute-start | bytes 98312 | tf_op jit(solution)/shard_map/ppermute | solution.py:535
  29.9 5.2 %collective-permute-start.11 = (bf16[32,512]{1,0:T(8,128)(2,1)S(1)}, bf16[32,512]{1,0:T(8,128)(2,1)S(1)}, u32[]{:S(2)}, u32[]{:S(2)}) collective-permute-start(bf16[32,512]{1,0:T(8,128)(2,1)S(1)} %get-tuple-element.95), channel_id=1, source_target_pairs={{0,4},{1,5},{2,6},{3,7},{4,0},{5,1},{6,2},{7,3},{8,12},{9,13},{10,... | collective-permute-start | bytes 98312 | tf_op jit(solution)/shard_map/ppermute | solution.py:535
  30.1 5.0 %collective-permute-start.12 = (bf16[32,512]{1,0:T(8,128)(2,1)S(1)}, bf16[32,512]{1,0:T(8,128)(2,1)S(1)}, u32[]{:S(2)}, u32[]{:S(2)}) collective-permute-start(bf16[32,512]{1,0:T(8,128)(2,1)S(1)} %get-tuple-element.96), channel_id=1, source_target_pairs={{0,8},{1,11},{2,10},{3,9},{4,12},{5,15},{6,14},{7,13},{8,0},{9,3},... | collective-permute-start | bytes 98312 | tf_op jit(solution)/shard_map/ppermute | solution.py:535
  35.7 2.2 %collective-permute-start.14 = (bf16[640,512]{1,0:T(8,128)(2,1)S(1)}, bf16[640,512]{1,0:T(8,128)(2,1)S(1)}, u32[]{:S(2)}, u32[]{:S(2)}) collective-permute-start(bf16[640,512]{1,0:T(8,128)(2,1)S(1)} %get-tuple-element.106), channel_id=1, source_target_pairs={{0,1},{1,0},{2,3},{3,2},{4,5},{5,4},{6,7},{7,6},{8,9},{9,8},{10,11... | collective-permute-start | bytes 1966088 | tf_op jit(solution)/shard_map/ppermute | solution.py:434

commit v6 on v5

--- a/solution.py
+++ b/solution.py
@@ -88,15 +88,14 @@
         self.patches = len(rounds[0][0])
         self.node_count, self.halo, self.coarse = node_count, halo, coarse
         self.group = halo + coarse * len(rounds)
-        self.used = node_count + coarse
-        self.local_slots = -(-self.used // 256) * 256
+        self.local_slots = -(-node_count // 128) * 128
         self.code = [[0] * self.patches for _ in range(self.patches)]
         for i, some in reversed(list(enumerate(rounds))):
             for core, targets in enumerate(some):
                 for patch, owner in enumerate(targets):
                     self.code[patch][owner] = (core << 16) + halo + coarse * i
 
-    def slots(self, rows, patch, feat):
+    def slots(self, rows, patch, feat, own):
         node_count, halo, coarse, group = self.node_count, self.halo, self.coarse, self.group
         at = rows - (node_count + 2 * halo)
         owner, entry = lax.shift_right_arithmetic(at, coarse.bit_length() - 1), at & (coarse - 1)
@@ -106,8 +105,10 @@
             for p in range(self.patches):
                 code = jnp.where(patch == p, self.code[p][q], code)
             remote = self.local_slots + (lax.shift_right_arithmetic(code, 16) ^ feat) * group + (code & 0xFFFF)
-            place = jnp.where(owner == q, jnp.where(patch == q, node_count, remote), place)
+            place = jnp.where(owner == q, remote, place)
         place = place + entry
+        for i in range(coarse):
+            place = jnp.where((owner == patch) & (entry == i), own[i], place)
         even = 1 - (patch & 1)
         lower = self.local_slots + (even ^ feat) * group - node_count + rows
         upper = self.local_slots + (1 - (even ^ feat)) * group - (node_count + halo) + rows
@@ -124,8 +125,8 @@
 
 
 def lend_kernel(*refs, share, layout):
-    (node_hbm, halo_hbm, coarse_hbm, wa_hbm, send_hbm, recv_hbm), refs = refs[:6], refs[6:]
-    lent_ref, node, halo, coarse, wa, send, recv, sems = refs
+    (node_hbm, halo_hbm, coarse_hbm, wa_hbm, send_hbm, recv_hbm, latent_hbm), refs = refs[:7], refs[7:]
+    lent_ref, node, halo, coarse, wa, send, recv, latent, own, sems = refs
     rows128 = share // 128
     feat, patch = lax.axis_index("feat"), lax.axis_index("patch")
     mine = pl.ds(pl.multiple_of(feat * rows128, rows128), rows128)
@@ -136,7 +137,9 @@
             (node_hbm, node),
             (send_hbm.at[mine, :], send),
             (recv_hbm.at[mine, :], recv),
+            (coarse_hbm, own),
             (wa_hbm, wa),
+            (latent_hbm.at[pl.ds(pl.multiple_of(feat * share, share), latent.shape[0]), :], latent),
         ),
         sems,
     )
@@ -149,11 +152,12 @@
         (((0,), (0,)), ((), ())),
         preferred_element_type=F32,
     ).astype(BF16)
-    for copy in loads[3:5]:
+    for copy in loads[3:6]:
         copy.wait()
     for index in (send, recv):
-        index[...] = layout.slots(index[...], patch, feat)
-    loads[5].wait()
+        index[...] = layout.slots(index[...], patch, feat, own)
+    for copy in loads[6:]:
+        copy.wait()
 
 
 def local_part(at, block, latent, send, recv, wa, wb, table, before=None):
@@ -173,7 +177,7 @@
     )
 
 
-def local_kernel(node, lent_ref, wa, wb, send, recv, latent_hbm, *refs, layout, block):
+def local_kernel(node, wa, wb, send, recv, early_latent, latent_hbm, *refs, layout, block):
     count = (len(refs) - 5) // 2
     more_hbm, refs = refs[:count], refs[count:]
     pre_ref, latent, table, *more = refs[: 3 + count]
@@ -181,29 +185,34 @@
     share, width = latent.shape
     half = wa.shape[1]
     feat = lax.axis_index("feat")
-    local_slots, used = layout.local_slots, layout.used
+    local_slots, used = layout.local_slots, layout.node_count
     first = pre_ref.shape[0]
     blocks = [
         (latent_hbm.at[pl.ds(pl.multiple_of(feat * share + at, block), block), :], latent.at[pl.ds(at, block), :])
-        for at in range(0, share, block)
+        for at in range(block, share, block)
     ]
-    early = copies(blocks[: first // block], block_sems)
-    rows_in = jnp.concatenate([node[...], lent_ref[lent_ref.shape[0] - layout.coarse :, :]], axis=0)
+    wanted = first // block - 1
+    early = copies(blocks[:wanted], block_sems)
+    latent[:block, :] = early_latent[...]
     for side in range(2):
         base = side * local_slots
         rows = slice((side + 1) * width, (side + 2) * width)
         for weight, col in ((wa, 0), (wb, half)):
-            table[base : base + used, col : col + half] = dot(rows_in, weight[rows, :]).astype(BF16)
-        table[base + used : base + local_slots, :] = jnp.zeros((local_slots - used, 2 * half), BF16)
-    rest = copies(blocks[first // block :] + list(zip(more_hbm, more)), sems)
-    for i, copy in enumerate(early):
+            table[base : base + used, col : col + half] = dot(node[...], weight[rows, :]).astype(BF16)
+        if used < local_slots:
+            table[base + used : base + local_slots, :] = jnp.zeros((local_slots - used, 2 * half), BF16)
+    rest = copies(blocks[wanted:] + list(zip(more_hbm, more)), sems)
+    for i, copy in enumerate([None] + early):
         at = i * block
         pre_ref[at : at + block, :] = local_part(at, block, latent, send, recv, wa, wb, table, copy)
     for copy in rest:
         copy.wait()
 
 
-def second_kernel(latent, send, recv, wa, wb, table, mine, pre_ref, projected, block):
+def second_kernel(latent, send, recv, wa, wb, table, mine, *refs, block):
+    count = (len(refs) - 3) // 2
+    more_hbm, pre_ref, projected, more, sems = refs[:count], refs[count], refs[count + 1], refs[count + 2 : -1], refs[-1]
+    rest = copies(list(zip(more_hbm, more)), sems)
     share, width = latent.shape
     half = wa.shape[1]
     done = share - pre_ref.shape[0]
@@ -211,15 +220,17 @@
     for at in range(done, share, block):
         pre_ref[at - done : at - done + block, :] = local_part(at, block, latent, send, recv, wa, wb, table)
     project(mine, wa, wb, projected)
-
-
-def project(rows, wa, wb, out):
+    for copy in rest:
+        copy.wait()
+
+
+def project(rows, wa, wb, out, at=0):
     group, width = rows.shape
     half = wa.shape[1]
     for side in range(2):
         part = slice((side + 1) * width, (side + 2) * width)
         for weight, col in ((wa, 0), (wb, half)):
-            out[side * group : (side + 1) * group, col : col + half] = (
+            out[at + side * group : at + (side + 1) * group, col : col + half] = (
                 0.5 * dot(rows[...], weight[part, :])
             ).astype(BF16)
 
@@ -243,7 +254,7 @@
     fresh_all,
     group_other_ref,
     live_recv_ref,
-    theirs_table,
+    table,
     layout,
     block,
 ):
@@ -251,10 +262,11 @@
     half = wa_ref.shape[1]
     group = layout.group
     feat = lax.axis_index("feat")
-    project(theirs_ref, wa_ref, wb_ref, theirs_table)
+    table[: 2 * group, :] = mine_table[...]
+    project(theirs_ref, wa_ref, wb_ref, table, 2 * group)
     shape = recv_ref.shape
     edge = lax.broadcasted_iota(jnp.int32, shape, 0) * 128 + lax.broadcasted_iota(jnp.int32, shape, 1) + feat * share
-    live_recv_ref[...] = jnp.where(edge < limit_ref[0], recv_ref[...], DEAD)
+    live_recv_ref[...] = jnp.where(edge < limit_ref[...], recv_ref[...], DEAD)
     gain = gain_ref[...].astype(F32).reshape(1, width)
     for at in range(0, share, block):
         part = slice(at, at + block)
@@ -263,10 +275,15 @@
         columns = [index_columns(send_ref[some, :]), index_columns(receivers)]
         first = pre_ref.shape[0]
         pre = pre_ref[part, :] if at < first else pre2_ref[at - first : at - first + block, :]
-        for base, table in ((layout.local_slots, mine_table), (layout.local_slots + group, theirs_table)):
-            picks = jnp.concatenate([one_hot_rows(column, base, group) for column in columns], axis=1)
-            pre = pre + dot(picks, table[...])
-        hidden = silu_of_double(pre).astype(BF16)
+        picks = jnp.concatenate(
+            [
+                one_hot_rows(column, base, group)
+                for base in (layout.local_slots, layout.local_slots + group)
+                for column in columns
+            ],
+            axis=1,
+        )
+        hidden = silu_of_double(pre + dot(picks, table[...])).astype(BF16)
         pre = dot(hidden[:, :half], va_ref[...]) + dot(hidden[:, half:], vb_ref[...])
         live = jnp.concatenate(columns[1], axis=0) != DEAD
         fresh = (latent_ref[part, :].astype(F32) + layer_norm(pre, gain, live)).astype(BF16)
@@ -291,43 +308,12 @@
         at += rows
 
 
-def local_sums_kernel(fresh_ref, recv_ref, node_ref, wa_ref, wb_ref, sums_ref, pre_ref):
+def local_sums_kernel(fresh_ref, recv_ref, sums_ref):
+    sums_ref[...] = dot(one_hot_columns(flat_row(recv_ref[...]), 0, sums_ref.shape[0]), fresh_ref[...])
+
+
+def beside_kernel(node_ref, wa_ref, wb_ref, mine_ref, theirs_ref, pre_ref, edges_ref, sems):
     width = node_ref.shape[1]
-    half = wa_ref.shape[1]
-    sums_ref[...] = dot(one_hot_columns(flat_row(recv_ref[...]), 0, sums_ref.shape[0]), fresh_ref[...])
-    pre_ref[:, :half] = dot(node_ref[...], wa_ref[:width, :])
-    pre_ref[:, half:] = dot(node_ref[...], wb_ref[:width, :])
-
-
-def receive_kernel(sums_ref, halo_ref, coarse_ref, *refs):
-    *parts, own_ref, rounded_ref = refs
-    node_count = own_ref.shape[0]
-    coarse = coarse_ref.shape[0]
-    coarse_row = coarse_ref[...].reshape(1, coarse)
-    index_row = jnp.concatenate([lent_list(halo_ref[...])] + [coarse_row] * (len(parts) + 1), axis=1)
-    returned = jnp.concatenate([part[...] for part in parts] + [sums_ref[node_count:, :].astype(BF16)], axis=0)
-    own = sums_ref[:node_count, :] + dot(one_hot_columns(index_row, 0, node_count), returned)
-    own_ref[...] = own
-    rounded_ref[...] = own.astype(BF16)
-
-
-def node_kernel(
-    node_ref,
-    own_ref,
-    partner_ref,
-    pre_ref,
-    wa_ref,
-    wb_ref,
-    va_ref,
-    vb_ref,
-    gain_ref,
-    mine_ref,
-    theirs_ref,
-    out_ref,
-    edges_ref,
-    sems,
-):
-    node_count, width = node_ref.shape
     half = wa_ref.shape[1]
     share = mine_ref.shape[0]
     feat = lax.axis_index("feat")
@@ -338,17 +324,36 @@
         ],
         sems,
     )
+    for weight, col in ((wa_ref, 0), (wb_ref, half)):
+        pre_ref[:, col : col + half] = 0.5 * dot(node_ref[...], weight[:width, :])
+    for copy in placed:
+        copy.wait()
+
+
+def receive_kernel(sums_ref, halo_ref, coarse_ref, *refs):
+    *parts, own_ref, rounded_ref = refs
+    coarse = coarse_ref.shape[0]
+    coarse_row = coarse_ref[...].reshape(1, coarse)
+    index_row = jnp.concatenate([lent_list(halo_ref[...])] + [coarse_row] * len(parts), axis=1)
+    returned = jnp.concatenate([part[...] for part in parts], axis=0)
+    own = sums_ref[...] + dot(one_hot_columns(index_row, 0, own_ref.shape[0]), returned)
+    own_ref[...] = own
+    rounded_ref[...] = own.astype(BF16)
+
+
+def node_kernel(node_ref, own_ref, partner_ref, pre_ref, wa_ref, wb_ref, va_ref, vb_ref, gain_ref, out_ref):
+    width = node_ref.shape[1]
+    half = wa_ref.shape[1]
+    feat = lax.axis_index("feat")
     received = (own_ref[...] + partner_ref[...].astype(F32)).astype(BF16)
     total = None
     for weight, second, col in ((wa_ref, va_ref, 0), (wb_ref, vb_ref, half)):
-        pre = pre_ref[:, col : col + half] + dot(received, weight[width:, :])
-        part = dot(silu_of_double(0.5 * pre).astype(BF16), second[...])
+        pre = pre_ref[:, col : col + half] + 0.5 * dot(received, weight[width:, :])
+        part = dot(silu_of_double(pre).astype(BF16), second[...])
         total = part if total is None else total + part
     update = layer_norm(total, gain_ref[...].astype(F32).reshape(1, width))
     fresh = (node_ref[...].astype(F32) + update).astype(BF16)
     out_ref[...] = jnp.where(feat == 0, fresh[:, : width // 2], fresh[:, width // 2 :])
-    for copy in placed:
-        copy.wait()
 
 
 def in_hbm(array):
@@ -419,7 +424,7 @@
     both = ("patch", "feat")
     rounds = exchange_rounds(patches)
     layout = Layout(rounds, node_count, halo, coarse)
-    group, used, local_slots = layout.group, layout.used, layout.local_slots
+    group, local_slots = layout.group, layout.local_slots
     share = edge_count // 2
     block = 512
     dma = pltpu.SemaphoreType.DMA
@@ -437,7 +442,7 @@
 
     index_rows = (edge_count // 128, 128)
     core_rows = jax.ShapeDtypeStruct((share // 128, 128), jnp.int32)
-    lent, node, halo_lists, coarse_list, w1, send, recv = call(
+    lent, node, halo_lists, coarse_list, w1, send, recv, early_latent = call(
         functools.partial(lend_kernel, share=share, layout=layout),
         [
             in_hbm(array)
@@ -448,27 +453,30 @@
                 edge_w1,
                 edge_senders.reshape(index_rows),
                 edge_receivers.reshape(index_rows),
+                edge_latent,
             )
         ],
-        [ANY_SPEC] * 6,
+        [ANY_SPEC] * 7,
         [shape(halo + coarse, width)]
         + [like(array) for array in (node_latent, halo_rows, coarse_rows, edge_w1)]
-        + [core_rows] * 2,
-        [VMEM_SPEC] * 7,
+        + [core_rows] * 2
+        + [shape(block, width)],
+        [VMEM_SPEC] * 8,
         2 * node_count * (halo + coarse) * width,
         8,
-        scratch=[dma((6,))],
+        scratch=[pltpu.SMEM((coarse,), jnp.int32), dma((8,))],
     )
     pairs = exchange_pairs(rounds)
     arrived = [
         lax.ppermute(lent[halo:] if i else lent, both, pairs[i]) for i in reversed(range(len(pairs)))
     ][::-1]
 
-    more = (edge_w2, edge_gain, node_w1, node_w2, node_gain)
-    first = share // 2
-    pre, latent, table, w2, e_gain, n_w1, n_w2, n_gain = call(
+    more = (edge_w2, edge_gain)
+    later = (node_w1, node_w2, node_gain)
+    first = share * 3 // 4
+    pre, latent, table, w2, e_gain = call(
         functools.partial(local_kernel, layout=layout, block=block),
-        [node, lent, w1, edge_w1_b, send, recv] + [in_hbm(array) for array in (edge_latent, *more)],
+        [node, w1, edge_w1_b, send, recv, early_latent] + [in_hbm(array) for array in (edge_latent, *more)],
         [VMEM_SPEC] * 6 + [ANY_SPEC] * (1 + len(more)),
         [
             shape(first, width, F32),
@@ -477,7 +485,7 @@
         ]
         + [like(array) for array in more],
         [VMEM_SPEC] * (3 + len(more)),
-        (2 * width * width * first + 4 * used * width * width + 4 * first * local_slots * width) // BESIDE,
+        (2 * width * width * first + 4 * node_count * width * width + 4 * first * local_slots * width) // BESIDE,
         LIMIT,
         scratch=[dma((len(more) + (share - first) // block,)), dma((first // block,))],
     )
@@ -485,27 +493,28 @@
     table_mine = jnp.concatenate(arrived, axis=0)
     table_theirs = swap(table_mine)
     edge_w2_b = swap(w2)
-    pre2, projected = call(
+    pre2, projected, n_w1, n_w2, n_gain = call(
         functools.partial(second_kernel, block=block),
-        (latent, send, recv, w1, edge_w1_b, table, table_mine),
-        [VMEM_SPEC] * 7,
-        [shape(share - first, width, F32), shape(2 * group, width)],
-        [VMEM_SPEC] * 2,
+        [latent, send, recv, w1, edge_w1_b, table, table_mine] + [in_hbm(array) for array in later],
+        [VMEM_SPEC] * 7 + [ANY_SPEC] * len(later),
+        [shape(share - first, width, F32), shape(2 * group, width)] + [like(array) for array in later],
+        [VMEM_SPEC] * (2 + len(later)),
         2 * width * width * (share - first) + 4 * (share - first) * local_slots * width + 4 * group * width * width,
         LIMIT,
+        scratch=[dma((len(later),))],
     )
     n_w1_b, n_w2_b = lax.optimization_barrier((n_w1, n_w2, pre2))[:2]
     node_w1_b, node_w2_b = swap(n_w1_b), swap(n_w2_b)
 
     mine, other, fresh, group_other, live_recv = call(
         functools.partial(edge_kernel, layout=layout, block=block),
-        (edge_counts, pre, pre2, latent, send, recv, projected, table_theirs, w1, edge_w1_b, w2, edge_w2_b, e_gain),
-        [pl.BlockSpec(memory_space=pltpu.SMEM)] + [VMEM_SPEC] * 12,
+        (edge_counts.reshape(1, 1), pre, pre2, latent, send, recv, projected, table_theirs, w1, edge_w1_b, w2, edge_w2_b, e_gain),
+        [VMEM_SPEC] * 13,
         [shape(share, half), shape(share, half), shape(share, width), shape(group, width), core_rows],
         [VMEM_SPEC] * 5,
         2 * share * width * (width + 6 * group) + 4 * group * width * width,
         LIMIT,
-        scratch=[pltpu.VMEM((2 * group, width), BF16)],
+        scratch=[pltpu.VMEM((4 * group, width), BF16)],
     )
     node_w1_b, node_w2_b, mine, other, fresh, group_other = lax.optimization_barrier(
         (node_w1_b, node_w2_b, mine, other, fresh, group_other)
@@ -533,13 +542,13 @@
     )
     *outgoing, mine, other, fresh = lax.optimization_barrier((*outgoing, mine, other, fresh))
     back = [lax.ppermute(outgoing[i], both, pairs[i]) for i in reversed(range(len(pairs)))][::-1]
-    local_sums, node_pre = call(
+    local_sums = call(
         local_sums_kernel,
-        (fresh, live_recv, node, n_w1, node_w1_b),
-        [VMEM_SPEC] * 5,
-        [shape(used, width, F32), shape(node_count, width, F32)],
+        (fresh, live_recv),
         [VMEM_SPEC] * 2,
-        (2 * share * width * used + 2 * node_count * width * width) // BESIDE,
+        shape(node_count, width, F32),
+        VMEM_SPEC,
+        2 * share * width * node_count // BESIDE,
         16,
     )
     edges_theirs = swap(other)
@@ -551,19 +560,29 @@
         [VMEM_SPEC] * (3 + len(sizes)),
         [shape(node_count, width, F32), shape(node_count, width)],
         [VMEM_SPEC] * 2,
-        2 * node_count * width * (group + coarse),
+        2 * node_count * width * group,
         16,
     )
     partner = swap(rounded)
-    nodes_out, edges_out = call(
+    mine, edges_theirs, node = lax.optimization_barrier((mine, edges_theirs, node, rounded))[:3]
+    node_pre, edges_out = call(
+        beside_kernel,
+        (node, n_w1, node_w1_b, mine, edges_theirs),
+        [VMEM_SPEC] * 3 + [ANY_SPEC] * 2,
+        [shape(node_count, width, F32), shape(edge_count, half)],
+        [VMEM_SPEC, ANY_SPEC],
+        2 * node_count * width * width,
+        16,
+        scratch=[dma((2,))],
+    )
+    nodes_out = call(
         node_kernel,
-        (node, own, partner, node_pre, n_w1, node_w1_b, n_w2, node_w2_b, n_gain, mine, edges_theirs),
-        [VMEM_SPEC] * 9 + [ANY_SPEC] * 2,
-        [shape(node_count, half), shape(edge_count, half)],
-        [VMEM_SPEC, ANY_SPEC],
+        (node, own, partner, node_pre, n_w1, node_w1_b, n_w2, node_w2_b, n_gain),
+        [VMEM_SPEC] * 9,
+        shape(node_count, half),
+        VMEM_SPEC,
         4 * node_count * width * width,
         16,
-        scratch=[dma((2,))],
     )
     return nodes_out, edges_out
 

time: 41.1 us -> 39.2 us (0.954)
  Pallas kernels: 20.1 us -> 19.1 us
  waiting for transfers between devices: 2.26 us -> 1.67 us
    ppermute x8, waiting for transfers between devices: 2.2 us -> 0.79 us  [swap(): return lax.ppermute(values, 'feat', FEAT_SWAP)]
    pallas_call x9 -> x10, Pallas kernels: 20.1 us -> 19.1 us  [call(): pl.pallas_call(kernel, in_specs=in_specs, out_specs=out_specs, out_shape=...]
    ppermute x4, waiting for transfers between devices: 0.01 us -> 0.87 us  [on_device(): lax.ppermute(outgoing[i], both, pairs[i])]
    ppermute x4, starting transfers between devices: 6.93 us -> 6.48 us  [on_device(): lax.ppermute(outgoing[i], both, pairs[i])]
  transfers between devices with their start and end apart: 16 -> 16, of which waited for: 2 -> 4; matrix products, arithmetic and copies ran while one was open for 0% -> 0% of each run, Pallas kernels for 42% -> 44%
where the time goes in v6:
time: 39.2 us; the launch traced here: 39 us
  Pallas kernels  19.1 us (49%)
  starting transfers between devices  16.8 us (43%)
  waiting for transfers between devices  1.67 us (4%)
  between operations  1.44 us (4%)
    pallas_call x10, Pallas kernels, call(): pl.pallas_call(kernel, in_specs=in_specs, out_specs=out_specs, out_shape=...  19.1 us
    ppermute x4, starting transfers between devices, on_device(): lax.ppermute(lent[halo:] if i else lent, both, pairs[i])  6.98 us
    ppermute x4, starting transfers between devices, on_device(): lax.ppermute(outgoing[i], both, pairs[i])  6.48 us
    ppermute x8, starting transfers between devices, swap(): return lax.ppermute(values, 'feat', FEAT_SWAP)  3.3 us
    ppermute x4, waiting for transfers between devices, on_device(): lax.ppermute(outgoing[i], both, pairs[i])  0.87 us
    ppermute x8, waiting for transfers between devices, swap(): return lax.ppermute(values, 'feat', FEAT_SWAP)  0.79 us
  transfers between devices with their start and end apart: 16, of which 4 were waited for; matrix products, arithmetic and copies ran while one was open for 0% of the time, Pallas kernels for 44%

profile of v6, /device:TPU:0, one launch (start us, length us, event | category | flops | bytes accessed | tf_op | source)
XLA Modules:
  0.0 39.0 jit_solution(14352748590924634643)
XLA Ops:
  0.6 0.5 %collective-permute-start = (bf16[1536,256]{1,0:T(8,128)(2,1)}, bf16[1536,256]{1,0:T(8,128)(2,1)S(1)}, u32[]{:S(2)}, u32[]{:S(2)}) collective-permute-start(bf16[1536,256]{1,0:T(8,128)(2,1)} %refs_3_.1), channel_id=1, source_target_pairs={{0,1},{1,0},{2,3},{3,2},{4,5},{5,4},{6,7},{7,6},{8,9},{9,8},{10,11... | collective-permute-start | bytes 2359304 | tf_op jit(solution)/shard_map/ppermute | solution.py:439
  1.1 1.6 %shard_map.140 = (bf16[160,512]{1,0:T(8,128)(2,1)S(1)}, bf16[640,512]{1,0:T(8,128)(2,1)S(1)}, s32[2,128]{1,0:T(2,128)S(1)}, s32[32]{0:T(128)S(1)}, bf16[1536,256...) custom-call(bf16[640,512]{1,0:T(8,128)(2,1)} %refs_0_.3, ...), custom_call_target="tpu_custom_call" | custom-call | flops 104857600 | bytes 262144 | tf_op jit(solution)/shard_map/pallas_call | solution.py:368
  2.8 2.6 %collective-permute-start.1 = (bf16[160,512]{1,0:T(8,128)(2,1)S(1)}, bf16[160,512]{1,0:T(8,128)(2,1)S(1)}, u32[]{:S(2)}, u32[]{:S(2)}) collective-permute-start(bf16[160,512]{1,0:T(8,128)(2,1)S(1)} %get-tuple-element.69), channel_id=1, source_target_pairs={{0,2},{1,15},{2,0},{3,5},{4,6},{5,3},{6,4},{7,9},{8,10},{9,7},{10,... | collective-permute-start | bytes 491528 | tf_op jit(solution)/shard_map/ppermute | solution.py:471
  5.4 3.6 %collective-permute-start.4 = (bf16[32,512]{1,0:T(8,128)(2,1)S(1)}, bf16[32,512]{1,0:T(8,128)(2,1)S(1)}, u32[]{:S(2)}, u32[]{:S(2)}) collective-permute-start(bf16[32,512]{1,0:T(8,128)(2,1)S(1)} %slice.2), channel_id=1, source_target_pairs={{0,12},{1,7},{2,14},{3,13},{4,8},{5,11},{6,10},{7,1},{8,4},{9,15},... | collective-permute-start | bytes 98312 | tf_op jit(solution)/shard_map/ppermute | solution.py:471
  9.0 0.8 %collective-permute-start.2 = (bf16[32,512]{1,0:T(8,128)(2,1)S(1)}, bf16[32,512]{1,0:T(8,128)(2,1)S(1)}, u32[]{:S(2)}, u32[]{:S(2)}) collective-permute-start(bf16[32,512]{1,0:T(8,128)(2,1)S(1)} %slice.2), channel_id=1, source_target_pairs={{0,8},{1,11},{2,10},{3,9},{4,12},{5,15},{6,14},{7,13},{8,0},{9,3},... | collective-permute-start | bytes 98312 | tf_op jit(solution)/shard_map/ppermute | solution.py:471
  9.8 4.4 %shard_map.141 = (f32[1536,512]{1,0:T(8,128)S(1)}, bf16[2048,512]{1,0:T(8,128)(2,1)S(1)}, bf16[1280,512]{1,0:T(8,128)(2,1)S(1)}, bf16[256,512]{1,0:T(8,128)(2,1)S(1)}, bf16[512]{0:T(512)(128)(2,1)S(1)}) custom-call(bf16[640,512]{1,0:T(8,128)(2,1)S(1)} %get-tuple-element.111.node.node_ref, bf16[1536,256]{1,0:T(8,128)(2,1)S(1)} %get-tuple-element.62.wa.wa_ref, ...), custom_call_target="tpu_custom_call" | custom-call | flops 348966080 | bytes 262144 | tf_op jit(solution)/shard_map/pallas_call | solution.py:368
  14.2 0.0 collective-permute-done.4
  14.2 0.0 collective-permute-done.3
  14.2 0.0 collective-permute-done.1
  14.3 0.4 %collective-permute-start.7 = (bf16[256,512]{1,0:T(8,128)(2,1)S(1)}, bf16[256,512]{1,0:T(8,128)(2,1)S(1)}, u32[]{:S(2)}, u32[]{:S(2)}) collective-permute-start(bf16[256,512]{1,0:T(8,128)(2,1)S(1)} %constant_dynamic-update-slice_fusion.mine), channel_id=1, source_target_pairs={{0,1},{1,0},{2,3},{3,2},{4,5},{5,4},{6,7},{7,6},{8,9},{9,8},{10,11... | collective-permute-start | bytes 786440 | tf_op jit(solution)/shard_map/ppermute | solution.py:439
  14.8 0.1 collective-permute-start.8
  14.9 1.6 %shard_map.142 = (f32[512,512]{1,0:T(8,128)S(1)}, bf16[512,512]{1,0:T(8,128)(2,1)S(1)}, bf16[1024,256]{1,0:T(8,128)(2,1)S(1)}, bf16[256,512]{1,0:T(8,128)(2,1)S(1)}, bf16[512]{0:T(512)(128)(2,1)S(1)}) custom-call(bf16[2048,512]{1,0:T(8,128)(2,1)S(1)} %get-tuple-element.66.latent.latent_ref, s32[16,128]{1,0:T(8,128)S(1)} %get-tuple-element.63.send.send_ref, ...), custom_call_target="tpu_custom_call" | custom-call | flops 1207959552 | bytes 262144 | tf_op jit(solution)/shard_map/pallas_call | solution.py:368
  16.5 0.4 %collective-permute-start.5 = (bf16[1024,256]{1,0:T(8,128)(2,1)S(1)}, bf16[1024,256]{1,0:T(8,128)(2,1)S(1)}, u32[]{:S(2)}, u32[]{:S(2)}) collective-permute-start(bf16[1024,256]{1,0:T(8,128)(2,1)S(1)} %get-tuple-element.77.wa_ref), channel_id=1, source_target_pairs={{0,1},{1,0},{2,3},{3,2},{4,5},{5,4},{6,7},{7,6},{8,9},{9,8},{10,11... | collective-permute-start | bytes 1572872 | tf_op jit(solution)/shard_map/ppermute | solution.py:439
  17.6 0.2 collective-permute-start.6
  17.8 5.4 %shard_map.143 = (bf16[2048,256]{1,0:T(8,128)(2,1)S(1)}, bf16[2048,256]{1,0:T(8,128)(2,1)S(1)}, bf16[2048,512]{1,0:T(8,128)(2,1)S(1)}, bf16[256,512]{1,0:T(8,128)(2,1)S(1)}, s32[16,128]{1,0:T(8,128)S(1)}) custom-call(s32[1,1]{1,0:T(1,128)} %bitcast.3.limit_ref, f32[1536,512]{1,0:T(8,128)S(1)} %get-tuple-element.79.pre_ref, ...), custom_call_target="tpu_custom_call" | custom-call | flops 4563402752 | bytes 262144 | tf_op jit(solution)/shard_map/pallas_call | solution.py:368
  23.2 0.4 %collective-permute-start.9 = (bf16[256,512]{1,0:T(8,128)(2,1)S(1)}, bf16[256,512]{1,0:T(8,128)(2,1)S(1)}, u32[]{:S(2)}, u32[]{:S(2)}) collective-permute-start(bf16[256,512]{1,0:T(8,128)(2,1)S(1)} %get-tuple-element.89), channel_id=1, source_target_pairs={{0,1},{1,0},{2,3},{3,2},{4,5},{5,4},{6,7},{7,6},{8,9},{9,8},{10,11... | collective-permute-start | bytes 786440 | tf_op jit(solution)/shard_map/ppermute | solution.py:439
  23.7 0.7 %shard_map.144.mine_ref = f32[256,512]{1,0:T(8,128)S(1)} custom-call(bf16[2048,512]{1,0:T(8,128)(2,1)S(1)} %get-tuple-element.98.fresh_ref, s32[16,128]{1,0:T(8,128)S(1)} %get-tuple-element.88.recv_ref), custom_call_target="tpu_custom_call" | custom-call | flops 536870912 | bytes 262144 | tf_op jit(solution)/shard_map/pallas_call | solution.py:368
  24.4 0.5 %collective-permute-done.9.theirs_ref = bf16[256,512]{1,0:T(8,128)(2,1)S(1)} collective-permute-done((bf16[256,512]{1,0:T(8,128)(2,1)S(1)}, bf16[256,512]{1,0:T(8,128)(2,1)S(1)}, u32[]{:S(2)}, u32[]{:S(2)}) %collective-permute-start.9) | collective-permute-done | bytes 262176 | tf_op jit(solution)/shard_map/ppermute | solution.py:439
  24.9 0.1 shard_map.145
  24.9 0.4 %collective-permute-start.10 = (bf16[2048,256]{1,0:T(8,128)(2,1)S(1)}, bf16[2048,256]{1,0:T(8,128)(2,1)S(1)}, u32[]{:S(2)}, u32[]{:S(2)}) collective-permute-start(bf16[2048,256]{1,0:T(8,128)(2,1)S(1)} %get-tuple-element.97), channel_id=1, source_target_pairs={{0,1},{1,0},{2,3},{3,2},{4,5},{5,4},{6,7},{7,6},{8,9},{9,8},{10,11... | collective-permute-start | bytes 3145736 | tf_op jit(solution)/shard_map/ppermute | solution.py:439
  25.4 2.1 %collective-permute-start.14 = (bf16[160,512]{1,0:T(8,128)(2,1)S(1)}, bf16[160,512]{1,0:T(8,128)(2,1)S(1)}, u32[]{:S(2)}, u32[]{:S(2)}) collective-permute-start(bf16[160,512]{1,0:T(8,128)(2,1)S(1)} %get-tuple-element.102), channel_id=1, source_target_pairs={{0,2},{1,15},{2,0},{3,5},{4,6},{5,3},{6,4},{7,9},{8,10},{9,7},{10,... | collective-permute-start | bytes 491528 | tf_op jit(solution)/shard_map/ppermute | solution.py:544
  27.5 1.8 %collective-permute-start.11 = (bf16[32,512]{1,0:T(8,128)(2,1)S(1)}, bf16[32,512]{1,0:T(8,128)(2,1)S(1)}, u32[]{:S(2)}, u32[]{:S(2)}) collective-permute-start(bf16[32,512]{1,0:T(8,128)(2,1)S(1)} %get-tuple-element.99), channel_id=1, source_target_pairs={{0,12},{1,7},{2,14},{3,13},{4,8},{5,11},{6,10},{7,1},{8,4},{9,15},... | collective-permute-start | bytes 98312 | tf_op jit(solution)/shard_map/ppermute | solution.py:544
  29.2 0.2 collective-permute-start.12
  29.4 2.4 %collective-permute-start.13 = (bf16[32,512]{1,0:T(8,128)(2,1)S(1)}, bf16[32,512]{1,0:T(8,128)(2,1)S(1)}, u32[]{:S(2)}, u32[]{:S(2)}) collective-permute-start(bf16[32,512]{1,0:T(8,128)(2,1)S(1)} %get-tuple-element.101), channel_id=1, source_target_pairs={{0,8},{1,11},{2,10},{3,9},{4,12},{5,15},{6,14},{7,13},{8,0},{9,3},... | collective-permute-start | bytes 98312 | tf_op jit(solution)/shard_map/ppermute | solution.py:544
  31.8 1.5 %shard_map.146.sums_ref = f32[640,512]{1,0:T(8,128)S(1)} custom-call(bf16[2048,512]{1,0:T(8,128)(2,1)S(1)} %get-tuple-element.98.fresh_ref, s32[16,128]{1,0:T(8,128)S(1)} %get-tuple-element.88.recv_ref), custom_call_target="tpu_custom_call" | custom-call | flops 134217728 | bytes 262144 | tf_op jit(solution)/shard_map/pallas_call | solution.py:368
  33.4 0.2 collective-permute-done.12.refs_2_
  33.5 0.7 %collective-permute-done.13.refs_1_ = bf16[32,512]{1,0:T(8,128)(2,1)S(1)} collective-permute-done((bf16[32,512]{1,0:T(8,128)(2,1)S(1)}, bf16[32,512]{1,0:T(8,128)(2,1)S(1)}, u32[]{:S(2)}, u32[]{:S(2)}) %collective-permute-start.13) | collective-permute-done | bytes 32800 | tf_op jit(solution)/shard_map/ppermute | solution.py:544
  34.2 0.4 shard_map.147
  34.6 0.7 %collective-permute-start.15 = (bf16[640,512]{1,0:T(8,128)(2,1)S(1)}, bf16[640,512]{1,0:T(8,128)(2,1)S(1)}, u32[]{:S(2)}, u32[]{:S(2)}) collective-permute-start(bf16[640,512]{1,0:T(8,128)(2,1)S(1)} %get-tuple-element.110), channel_id=1, source_target_pairs={{0,1},{1,0},{2,3},{3,2},{4,5},{5,4},{6,7},{7,6},{8,9},{9,8},{10,11... | collective-permute-start | bytes 1966088 | tf_op jit(solution)/shard_map/ppermute | solution.py:439
  35.3 1.4 %shard_map.148 = (f32[640,512]{1,0:T(8,128)S(1)}, bf16[4096,256]{1,0:T(8,128)(2,1)}) custom-call(bf16[640,512]{1,0:T(8,128)(2,1)S(1)} %get-tuple-element.111.node.node_ref, bf16[1024,256]{1,0:T(8,128)(2,1)S(1)} %get-tuple-element.77.wa_ref, bf16[1024,256]{1,0:T(8,128)(2,1)S(1)} %collective-permute-done.5.wb_ref, ...), custom_call_target="tpu_custom_call" | custom-call | flops 335544320 | bytes 262144 | tf_op jit(solution)/shard_map/pallas_call | solution.py:368
  36.7 0.3 collective-permute-done.15.partner_ref
  37.0 2.0 %shard_map.149 = bf16[640,256]{1,0:T(8,128)(2,1)} custom-call(bf16[640,512]{1,0:T(8,128)(2,1)S(1)} %get-tuple-element.111.node.node_ref, f32[640,512]{1,0:T(8,128)S(1)} %get-tuple-element.112.own_ref, bf16[640,512]{1,0:T(8,128)(2,1)S(1)} %collective-permute-done.15.partner_ref, f32[640,512]{1,0:T(8,128)S(1)} %get-tuple-element.116.pre_ref, ...), custom_call_target="tpu_custom_call" | custom-call | flops 671088640 | bytes 262144 | tf_op jit(solution)/shard_map/pallas_call | solution.py:368
  (15 shorter events, 0.1 us)
Async XLA Ops:
  0.6 9.2 %collective-permute-start = (bf16[1536,256]{1,0:T(8,128)(2,1)}, bf16[1536,256]{1,0:T(8,128)(2,1)S(1)}, u32[]{:S(2)}, u32[]{:S(2)}) collective-permute-start(bf16[1536,256]{1,0:T(8,128)(2,1)} %refs_3_.1), channel_id=1, source_target_pairs={{0,1},{1,0},{2,3},{3,2},{4,5},{5,4},{6,7},{7,6},{8,9},{9,8},{10,11... | collective-permute-start | bytes 2359304 | tf_op jit(solution)/shard_map/ppermute | solution.py:439
  2.8 11.4 %collective-permute-start.1 = (bf16[160,512]{1,0:T(8,128)(2,1)S(1)}, bf16[160,512]{1,0:T(8,128)(2,1)S(1)}, u32[]{:S(2)}, u32[]{:S(2)}) collective-permute-start(bf16[160,512]{1,0:T(8,128)(2,1)S(1)} %get-tuple-element.69), channel_id=1, source_target_pairs={{0,2},{1,15},{2,0},{3,5},{4,6},{5,3},{6,4},{7,9},{8,10},{9,7},{10,... | collective-permute-start | bytes 491528 | tf_op jit(solution)/shard_map/ppermute | solution.py:471
  5.4 8.8 %collective-permute-start.4 = (bf16[32,512]{1,0:T(8,128)(2,1)S(1)}, bf16[32,512]{1,0:T(8,128)(2,1)S(1)}, u32[]{:S(2)}, u32[]{:S(2)}) collective-permute-start(bf16[32,512]{1,0:T(8,128)(2,1)S(1)} %slice.2), channel_id=1, source_target_pairs={{0,12},{1,7},{2,14},{3,13},{4,8},{5,11},{6,10},{7,1},{8,4},{9,15},... | collective-permute-start | bytes 98312 | tf_op jit(solution)/shard_map/ppermute | solution.py:471
  9.0 5.2 %collective-permute-start.3 = (bf16[32,512]{1,0:T(8,128)(2,1)S(1)}, bf16[32,512]{1,0:T(8,128)(2,1)S(1)}, u32[]{:S(2)}, u32[]{:S(2)}) collective-permute-start(bf16[32,512]{1,0:T(8,128)(2,1)S(1)} %slice.2), channel_id=1, source_target_pairs={{0,4},{1,5},{2,6},{3,7},{4,0},{5,1},{6,2},{7,3},{8,12},{9,13},{10,... | collective-permute-start | bytes 98312 | tf_op jit(solution)/shard_map/ppermute | solution.py:471
  9.0 5.2 %collective-permute-start.2 = (bf16[32,512]{1,0:T(8,128)(2,1)S(1)}, bf16[32,512]{1,0:T(8,128)(2,1)S(1)}, u32[]{:S(2)}, u32[]{:S(2)}) collective-permute-start(bf16[32,512]{1,0:T(8,128)(2,1)S(1)} %slice.2), channel_id=1, source_target_pairs={{0,8},{1,11},{2,10},{3,9},{4,12},{5,15},{6,14},{7,13},{8,0},{9,3},... | collective-permute-start | bytes 98312 | tf_op jit(solution)/shard_map/ppermute | solution.py:471
  14.3 3.5 %collective-permute-start.7 = (bf16[256,512]{1,0:T(8,128)(2,1)S(1)}, bf16[256,512]{1,0:T(8,128)(2,1)S(1)}, u32[]{:S(2)}, u32[]{:S(2)}) collective-permute-start(bf16[256,512]{1,0:T(8,128)(2,1)S(1)} %constant_dynamic-update-slice_fusion.mine), channel_id=1, source_target_pairs={{0,1},{1,0},{2,3},{3,2},{4,5},{5,4},{6,7},{7,6},{8,9},{9,8},{10,11... | collective-permute-start | bytes 786440 | tf_op jit(solution)/shard_map/ppermute | solution.py:439
  14.8 3.0 %collective-permute-start.8 = (bf16[256,512]{1,0:T(8,128)(2,1)S(1)}, bf16[256,512]{1,0:T(8,128)(2,1)S(1)}, u32[]{:S(2)}, u32[]{:S(2)}) collective-permute-start(bf16[256,512]{1,0:T(8,128)(2,1)S(1)} %get-tuple-element.81.va_ref), channel_id=1, source_target_pairs={{0,1},{1,0},{2,3},{3,2},{4,5},{5,4},{6,7},{7,6},{8,9},{9,8},{10,11... | collective-permute-start | bytes 786440 | tf_op jit(solution)/shard_map/ppermute | solution.py:439
  16.5 6.8 %collective-permute-start.5 = (bf16[1024,256]{1,0:T(8,128)(2,1)S(1)}, bf16[1024,256]{1,0:T(8,128)(2,1)S(1)}, u32[]{:S(2)}, u32[]{:S(2)}) collective-permute-start(bf16[1024,256]{1,0:T(8,128)(2,1)S(1)} %get-tuple-element.77.wa_ref), channel_id=1, source_target_pairs={{0,1},{1,0},{2,3},{3,2},{4,5},{5,4},{6,7},{7,6},{8,9},{9,8},{10,11... | collective-permute-start | bytes 1572872 | tf_op jit(solution)/shard_map/ppermute | solution.py:439
  17.6 5.7 %collective-permute-start.6 = (bf16[256,512]{1,0:T(8,128)(2,1)S(1)}, bf16[256,512]{1,0:T(8,128)(2,1)S(1)}, u32[]{:S(2)}, u32[]{:S(2)}) collective-permute-start(bf16[256,512]{1,0:T(8,128)(2,1)S(1)} %get-tuple-element.78.va_ref), channel_id=1, source_target_pairs={{0,1},{1,0},{2,3},{3,2},{4,5},{5,4},{6,7},{7,6},{8,9},{9,8},{10,11... | collective-permute-start | bytes 786440 | tf_op jit(solution)/shard_map/ppermute | solution.py:439
  23.2 1.6 %collective-permute-start.9 = (bf16[256,512]{1,0:T(8,128)(2,1)S(1)}, bf16[256,512]{1,0:T(8,128)(2,1)S(1)}, u32[]{:S(2)}, u32[]{:S(2)}) collective-permute-start(bf16[256,512]{1,0:T(8,128)(2,1)S(1)} %get-tuple-element.89), channel_id=1, source_target_pairs={{0,1},{1,0},{2,3},{3,2},{4,5},{5,4},{6,7},{7,6},{8,9},{9,8},{10,11... | collective-permute-start | bytes 786440 | tf_op jit(solution)/shard_map/ppermute | solution.py:439
  24.9 10.4 %collective-permute-start.10 = (bf16[2048,256]{1,0:T(8,128)(2,1)S(1)}, bf16[2048,256]{1,0:T(8,128)(2,1)S(1)}, u32[]{:S(2)}, u32[]{:S(2)}) collective-permute-start(bf16[2048,256]{1,0:T(8,128)(2,1)S(1)} %get-tuple-element.97), channel_id=1, source_target_pairs={{0,1},{1,0},{2,3},{3,2},{4,5},{5,4},{6,7},{7,6},{8,9},{9,8},{10,11... | collective-permute-start | bytes 3145736 | tf_op jit(solution)/shard_map/ppermute | solution.py:439
  25.4 8.9 %collective-permute-start.14 = (bf16[160,512]{1,0:T(8,128)(2,1)S(1)}, bf16[160,512]{1,0:T(8,128)(2,1)S(1)}, u32[]{:S(2)}, u32[]{:S(2)}) collective-permute-start(bf16[160,512]{1,0:T(8,128)(2,1)S(1)} %get-tuple-element.102), channel_id=1, source_target_pairs={{0,2},{1,15},{2,0},{3,5},{4,6},{5,3},{6,4},{7,9},{8,10},{9,7},{10,... | collective-permute-start | bytes 491528 | tf_op jit(solution)/shard_map/ppermute | solution.py:544
  27.5 5.9 %collective-permute-start.11 = (bf16[32,512]{1,0:T(8,128)(2,1)S(1)}, bf16[32,512]{1,0:T(8,128)(2,1)S(1)}, u32[]{:S(2)}, u32[]{:S(2)}) collective-permute-start(bf16[32,512]{1,0:T(8,128)(2,1)S(1)} %get-tuple-element.99), channel_id=1, source_target_pairs={{0,12},{1,7},{2,14},{3,13},{4,8},{5,11},{6,10},{7,1},{8,4},{9,15},... | collective-permute-start | bytes 98312 | tf_op jit(solution)/shard_map/ppermute | solution.py:544
  29.2 4.3 %collective-permute-start.12 = (bf16[32,512]{1,0:T(8,128)(2,1)S(1)}, bf16[32,512]{1,0:T(8,128)(2,1)S(1)}, u32[]{:S(2)}, u32[]{:S(2)}) collective-permute-start(bf16[32,512]{1,0:T(8,128)(2,1)S(1)} %get-tuple-element.100), channel_id=1, source_target_pairs={{0,4},{1,5},{2,6},{3,7},{4,0},{5,1},{6,2},{7,3},{8,12},{9,13},{10,... | collective-permute-start | bytes 98312 | tf_op jit(solution)/shard_map/ppermute | solution.py:544
  29.4 4.8 %collective-permute-start.13 = (bf16[32,512]{1,0:T(8,128)(2,1)S(1)}, bf16[32,512]{1,0:T(8,128)(2,1)S(1)}, u32[]{:S(2)}, u32[]{:S(2)}) collective-permute-start(bf16[32,512]{1,0:T(8,128)(2,1)S(1)} %get-tuple-element.101), channel_id=1, source_target_pairs={{0,8},{1,11},{2,10},{3,9},{4,12},{5,15},{6,14},{7,13},{8,0},{9,3},... | collective-permute-start | bytes 98312 | tf_op jit(solution)/shard_map/ppermute | solution.py:544
  34.6 2.4 %collective-permute-start.15 = (bf16[640,512]{1,0:T(8,128)(2,1)S(1)}, bf16[640,512]{1,0:T(8,128)(2,1)S(1)}, u32[]{:S(2)}, u32[]{:S(2)}) collective-permute-start(bf16[640,512]{1,0:T(8,128)(2,1)S(1)} %get-tuple-element.110), channel_id=1, source_target_pairs={{0,1},{1,0},{2,3},{3,2},{4,5},{5,4},{6,7},{7,6},{8,9},{9,8},{10,11... | collective-permute-start | bytes 1966088 | tf_op jit(solution)/shard_map/ppermute | solution.py:439

commit v7 on v6

--- a/solution.py
+++ b/solution.py
@@ -177,11 +177,11 @@
     )
 
 
-def local_kernel(node, wa, wb, send, recv, early_latent, latent_hbm, *refs, layout, block):
-    count = (len(refs) - 5) // 2
+def local_kernel(limit_ref, node, wa, wb, send, recv, early_latent, latent_hbm, *refs, layout, block):
+    count = (len(refs) - 6) // 2
     more_hbm, refs = refs[:count], refs[count:]
-    pre_ref, latent, table, *more = refs[: 3 + count]
-    sems, block_sems = refs[3 + count :]
+    pre_ref, latent, table, live_ref, *more = refs[: 4 + count]
+    sems, block_sems = refs[4 + count :]
     share, width = latent.shape
     half = wa.shape[1]
     feat = lax.axis_index("feat")
@@ -201,6 +201,9 @@
             table[base : base + used, col : col + half] = dot(node[...], weight[rows, :]).astype(BF16)
         if used < local_slots:
             table[base + used : base + local_slots, :] = jnp.zeros((local_slots - used, 2 * half), BF16)
+    shape = recv.shape
+    edge = lax.broadcasted_iota(jnp.int32, shape, 0) * 128 + lax.broadcasted_iota(jnp.int32, shape, 1) + feat * share
+    live_ref[...] = jnp.where(edge < limit_ref[...], recv[...], DEAD)
     rest = copies(blocks[wanted:] + list(zip(more_hbm, more)), sems)
     for i, copy in enumerate([None] + early):
         at = i * block
@@ -209,10 +212,7 @@
         copy.wait()
 
 
-def second_kernel(latent, send, recv, wa, wb, table, mine, *refs, block):
-    count = (len(refs) - 3) // 2
-    more_hbm, pre_ref, projected, more, sems = refs[:count], refs[count], refs[count + 1], refs[count + 2 : -1], refs[-1]
-    rest = copies(list(zip(more_hbm, more)), sems)
+def second_kernel(latent, send, recv, wa, wb, table, mine, pre_ref, projected, block):
     share, width = latent.shape
     half = wa.shape[1]
     done = share - pre_ref.shape[0]
@@ -220,8 +220,6 @@
     for at in range(done, share, block):
         pre_ref[at - done : at - done + block, :] = local_part(at, block, latent, send, recv, wa, wb, table)
     project(mine, wa, wb, projected)
-    for copy in rest:
-        copy.wait()
 
 
 def project(rows, wa, wb, out, at=0):
@@ -236,7 +234,7 @@
 
 
 def edge_kernel(
-    limit_ref,
+    live_ref,
     pre_ref,
     pre2_ref,
     latent_ref,
@@ -264,9 +262,7 @@
     feat = lax.axis_index("feat")
     table[: 2 * group, :] = mine_table[...]
     project(theirs_ref, wa_ref, wb_ref, table, 2 * group)
-    shape = recv_ref.shape
-    edge = lax.broadcasted_iota(jnp.int32, shape, 0) * 128 + lax.broadcasted_iota(jnp.int32, shape, 1) + feat * share
-    live_recv_ref[...] = jnp.where(edge < limit_ref[...], recv_ref[...], DEAD)
+    live_recv_ref[...] = live_ref[...]
     gain = gain_ref[...].astype(F32).reshape(1, width)
     for at in range(0, share, block):
         part = slice(at, at + block)
@@ -308,25 +304,24 @@
         at += rows
 
 
-def local_sums_kernel(fresh_ref, recv_ref, sums_ref):
-    sums_ref[...] = dot(one_hot_columns(flat_row(recv_ref[...]), 0, sums_ref.shape[0]), fresh_ref[...])
-
-
-def beside_kernel(node_ref, wa_ref, wb_ref, mine_ref, theirs_ref, pre_ref, edges_ref, sems):
+def core_rows_of(edges, core):
+    share = edges.shape[0] // 2
+    return edges.at[pl.ds(pl.multiple_of(core * share, share), share), :]
+
+
+def local_sums_kernel(fresh_ref, recv_ref, node_ref, wa_ref, wb_ref, mine_ref, sums_ref, pre_ref, edges_ref, sems):
+    placed = copies([(mine_ref, core_rows_of(edges_ref, lax.axis_index("feat")))], sems)
     width = node_ref.shape[1]
     half = wa_ref.shape[1]
-    share = mine_ref.shape[0]
-    feat = lax.axis_index("feat")
-    placed = copies(
-        [
-            (source, edges_ref.at[pl.ds(pl.multiple_of(owner * share, share), share), :])
-            for source, owner in ((mine_ref, feat), (theirs_ref, 1 - feat))
-        ],
-        sems,
-    )
+    sums_ref[...] = dot(one_hot_columns(flat_row(recv_ref[...]), 0, sums_ref.shape[0]), fresh_ref[...])
     for weight, col in ((wa_ref, 0), (wb_ref, half)):
         pre_ref[:, col : col + half] = 0.5 * dot(node_ref[...], weight[:width, :])
     for copy in placed:
+        copy.wait()
+
+
+def beside_kernel(theirs_ref, edges_in_ref, edges_ref, sems):
+    for copy in copies([(theirs_ref, core_rows_of(edges_ref, 1 - lax.axis_index("feat")))], sems):
         copy.wait()
 
 
@@ -364,13 +359,14 @@
 ANY_SPEC = pl.BlockSpec(memory_space=pl.ANY)
 
 
-def call(kernel, operands, in_specs, outputs, out_specs, flops, limit, scratch=()):
+def call(kernel, operands, in_specs, outputs, out_specs, flops, limit, scratch=(), aliases=None):
     return pl.pallas_call(
         kernel,
         in_specs=in_specs,
         out_specs=out_specs,
         out_shape=outputs,
         scratch_shapes=list(scratch),
+        input_output_aliases=aliases or {},
         cost_estimate=pl.CostEstimate(flops=flops, bytes_accessed=MIB // 4, transcendentals=0),
         compiler_params=pltpu.CompilerParams(vmem_limit_bytes=limit * MIB),
     )(*operands)
@@ -471,20 +467,20 @@
         lax.ppermute(lent[halo:] if i else lent, both, pairs[i]) for i in reversed(range(len(pairs)))
     ][::-1]
 
-    more = (edge_w2, edge_gain)
-    later = (node_w1, node_w2, node_gain)
-    first = share * 3 // 4
-    pre, latent, table, w2, e_gain = call(
+    more = (edge_w2, edge_gain, node_w1, node_w2, node_gain)
+    first = share // 2
+    pre, latent, table, live, w2, e_gain, n_w1, n_w2, n_gain = call(
         functools.partial(local_kernel, layout=layout, block=block),
-        [node, w1, edge_w1_b, send, recv, early_latent] + [in_hbm(array) for array in (edge_latent, *more)],
-        [VMEM_SPEC] * 6 + [ANY_SPEC] * (1 + len(more)),
+        [edge_counts.reshape(1, 1), node, w1, edge_w1_b, send, recv, early_latent] + [in_hbm(array) for array in (edge_latent, *more)],
+        [VMEM_SPEC] * 7 + [ANY_SPEC] * (1 + len(more)),
         [
             shape(first, width, F32),
             shape(share, width),
             shape(2 * local_slots, width),
+            core_rows,
         ]
         + [like(array) for array in more],
-        [VMEM_SPEC] * (3 + len(more)),
+        [VMEM_SPEC] * (4 + len(more)),
         (2 * width * width * first + 4 * node_count * width * width + 4 * first * local_slots * width) // BESIDE,
         LIMIT,
         scratch=[dma((len(more) + (share - first) // block,)), dma((first // block,))],
@@ -493,22 +489,20 @@
     table_mine = jnp.concatenate(arrived, axis=0)
     table_theirs = swap(table_mine)
     edge_w2_b = swap(w2)
-    pre2, projected, n_w1, n_w2, n_gain = call(
+    pre2, projected = call(
         functools.partial(second_kernel, block=block),
-        [latent, send, recv, w1, edge_w1_b, table, table_mine] + [in_hbm(array) for array in later],
-        [VMEM_SPEC] * 7 + [ANY_SPEC] * len(later),
-        [shape(share - first, width, F32), shape(2 * group, width)] + [like(array) for array in later],
-        [VMEM_SPEC] * (2 + len(later)),
+        [latent, send, recv, w1, edge_w1_b, table, table_mine],
+        [VMEM_SPEC] * 7,
+        [shape(share - first, width, F32), shape(2 * group, width)],
+        [VMEM_SPEC] * 2,
         2 * width * width * (share - first) + 4 * (share - first) * local_slots * width + 4 * group * width * width,
         LIMIT,
-        scratch=[dma((len(later),))],
-    )
-    n_w1_b, n_w2_b = lax.optimization_barrier((n_w1, n_w2, pre2))[:2]
-    node_w1_b, node_w2_b = swap(n_w1_b), swap(n_w2_b)
+    )
+    node_w1_b, node_w2_b = swap(n_w1), swap(n_w2)
 
     mine, other, fresh, group_other, live_recv = call(
         functools.partial(edge_kernel, layout=layout, block=block),
-        (edge_counts.reshape(1, 1), pre, pre2, latent, send, recv, projected, table_theirs, w1, edge_w1_b, w2, edge_w2_b, e_gain),
+        (live, pre, pre2, latent, send, recv, projected, table_theirs, w1, edge_w1_b, w2, edge_w2_b, e_gain),
         [VMEM_SPEC] * 13,
         [shape(share, half), shape(share, half), shape(share, width), shape(group, width), core_rows],
         [VMEM_SPEC] * 5,
@@ -530,6 +524,8 @@
         2 * share * width * group,
         16,
     )
+    group_mine, other = lax.optimization_barrier((group_mine, other))
+    edges_theirs = swap(other)
     sizes = [halo + coarse] + [coarse] * (len(pairs) - 1)
     outgoing = call(
         merge_kernel,
@@ -540,18 +536,18 @@
         group * width,
         8,
     )
-    *outgoing, mine, other, fresh = lax.optimization_barrier((*outgoing, mine, other, fresh))
+    *outgoing, fresh = lax.optimization_barrier((*outgoing, fresh))
     back = [lax.ppermute(outgoing[i], both, pairs[i]) for i in reversed(range(len(pairs)))][::-1]
-    local_sums = call(
+    local_sums, node_pre, edges = call(
         local_sums_kernel,
-        (fresh, live_recv),
-        [VMEM_SPEC] * 2,
-        shape(node_count, width, F32),
-        VMEM_SPEC,
+        (fresh, live_recv, node, n_w1, node_w1_b, mine),
+        [VMEM_SPEC] * 5 + [ANY_SPEC],
+        [shape(node_count, width, F32), shape(node_count, width, F32), shape(edge_count, half)],
+        [VMEM_SPEC] * 2 + [ANY_SPEC],
         2 * share * width * node_count // BESIDE,
         16,
-    )
-    edges_theirs = swap(other)
+        scratch=[dma((1,))],
+    )
     local_sums, *back = lax.optimization_barrier((local_sums, *back[::-1]))
     back = back[::-1]
     own, rounded = call(
@@ -564,16 +560,17 @@
         16,
     )
     partner = swap(rounded)
-    mine, edges_theirs, node = lax.optimization_barrier((mine, edges_theirs, node, rounded))[:3]
-    node_pre, edges_out = call(
+    edges_theirs = lax.optimization_barrier((edges_theirs, rounded))[0]
+    edges_out = call(
         beside_kernel,
-        (node, n_w1, node_w1_b, mine, edges_theirs),
-        [VMEM_SPEC] * 3 + [ANY_SPEC] * 2,
-        [shape(node_count, width, F32), shape(edge_count, half)],
-        [VMEM_SPEC, ANY_SPEC],
+        (edges_theirs, edges),
+        [ANY_SPEC] * 2,
+        shape(edge_count, half),
+        ANY_SPEC,
         2 * node_count * width * width,
-        16,
-        scratch=[dma((2,))],
+        8,
+        scratch=[dma((1,))],
+        aliases={1: 0},
     )
     nodes_out = call(
         node_kernel,

time: 39.2 us -> 38.6 us (0.985)
  starting transfers between devices: 16.8 us -> 14.6 us
  waiting for transfers between devices: 1.67 us -> 2.81 us
  Pallas kernels: 19.1 us -> 19.5 us
    ppermute x4, waiting for transfers between devices: 0.01 us -> 1.68 us  [on_device(): lax.ppermute(lent[halo:] if i else lent, both, pairs[i])]
    ppermute x4, starting transfers between devices: 6.48 us -> 5.01 us  [on_device(): lax.ppermute(outgoing[i], both, pairs[i])]
    ppermute x4, waiting for transfers between devices: 0.87 us -> 0.01 us  [on_device(): lax.ppermute(outgoing[i], both, pairs[i])]
    ppermute x8, starting transfers between devices: 3.3 us -> 2.56 us  [swap(): return lax.ppermute(values, 'feat', FEAT_SWAP)]
    pallas_call x10, Pallas kernels: 19.1 us -> 19.5 us  [call(): pl.pallas_call(kernel, in_specs=in_specs, out_specs=out_specs, out_shape=...]
  transfers between devices with their start and end apart: 16 -> 16, of which waited for: 4 -> 3; matrix products, arithmetic and copies ran while one was open for 0% -> 0% of each run, Pallas kernels for 44% -> 46%
where the time goes in v7:
time: 38.6 us; the launch traced here: 38.4 us
  Pallas kernels  19.5 us (51%)
  starting transfers between devices  14.6 us (38%)
  waiting for transfers between devices  2.81 us (7%)
  between operations  1.48 us (4%)
    pallas_call x10, Pallas kernels, call(): pl.pallas_call(kernel, in_specs=in_specs, out_specs=out_specs, out_shape=...  19.5 us
    ppermute x4, starting transfers between devices, on_device(): lax.ppermute(lent[halo:] if i else lent, both, pairs[i])  6.98 us
    ppermute x4, starting transfers between devices, on_device(): lax.ppermute(outgoing[i], both, pairs[i])  5.01 us
    ppermute x8, starting transfers between devices, swap(): return lax.ppermute(values, 'feat', FEAT_SWAP)  2.56 us
    ppermute x4, waiting for transfers between devices, on_device(): lax.ppermute(lent[halo:] if i else lent, both, pairs[i])  1.68 us
    ppermute x8, waiting for transfers between devices, swap(): return lax.ppermute(values, 'feat', FEAT_SWAP)  1.12 us
  transfers between devices with their start and end apart: 16, of which 3 were waited for; matrix products, arithmetic and copies ran while one was open for 0% of the time, Pallas kernels for 46%

profile of v7, /device:TPU:0, one launch (start us, length us, event | category | flops | bytes accessed | tf_op | source)
XLA Modules:
  0.0 38.4 jit_solution(14457058552122003213)
XLA Ops:
  0.6 0.5 %collective-permute-start = (bf16[1536,256]{1,0:T(8,128)(2,1)}, bf16[1536,256]{1,0:T(8,128)(2,1)S(1)}, u32[]{:S(2)}, u32[]{:S(2)}) collective-permute-start(bf16[1536,256]{1,0:T(8,128)(2,1)} %refs_3_.2), channel_id=1, source_target_pairs={{0,1},{1,0},{2,3},{3,2},{4,5},{5,4},{6,7},{7,6},{8,9},{9,8},{10,11... | collective-permute-start | bytes 2359304 | tf_op jit(solution)/shard_map/ppermute | solution.py:435
  1.1 1.6 %shard_map.140 = (bf16[160,512]{1,0:T(8,128)(2,1)S(1)}, bf16[640,512]{1,0:T(8,128)(2,1)S(1)}, s32[2,128]{1,0:T(2,128)S(1)}, s32[32]{0:T(128)S(1)}, bf16[1536,256...) custom-call(bf16[640,512]{1,0:T(8,128)(2,1)} %refs_0_.2, ...), custom_call_target="tpu_custom_call" | custom-call | flops 104857600 | bytes 262144 | tf_op jit(solution)/shard_map/pallas_call | solution.py:363
  2.8 2.6 %collective-permute-start.3 = (bf16[160,512]{1,0:T(8,128)(2,1)S(1)}, bf16[160,512]{1,0:T(8,128)(2,1)S(1)}, u32[]{:S(2)}, u32[]{:S(2)}) collective-permute-start(bf16[160,512]{1,0:T(8,128)(2,1)S(1)} %get-tuple-element.68), channel_id=1, source_target_pairs={{0,2},{1,15},{2,0},{3,5},{4,6},{5,3},{6,4},{7,9},{8,10},{9,7},{10,... | collective-permute-start | bytes 491528 | tf_op jit(solution)/shard_map/ppermute | solution.py:467
  5.4 2.6 %collective-permute-start.4 = (bf16[32,512]{1,0:T(8,128)(2,1)S(1)}, bf16[32,512]{1,0:T(8,128)(2,1)S(1)}, u32[]{:S(2)}, u32[]{:S(2)}) collective-permute-start(bf16[32,512]{1,0:T(8,128)(2,1)S(1)} %slice.2), channel_id=1, source_target_pairs={{0,8},{1,11},{2,10},{3,9},{4,12},{5,15},{6,14},{7,13},{8,0},{9,3},... | collective-permute-start | bytes 98312 | tf_op jit(solution)/shard_map/ppermute | solution.py:467
  8.0 1.6 %collective-permute-start.5 = (bf16[32,512]{1,0:T(8,128)(2,1)S(1)}, bf16[32,512]{1,0:T(8,128)(2,1)S(1)}, u32[]{:S(2)}, u32[]{:S(2)}) collective-permute-start(bf16[32,512]{1,0:T(8,128)(2,1)S(1)} %slice.2), channel_id=1, source_target_pairs={{0,4},{1,5},{2,6},{3,7},{4,0},{5,1},{6,2},{7,3},{8,12},{9,13},{10,... | collective-permute-start | bytes 98312 | tf_op jit(solution)/shard_map/ppermute | solution.py:467
  9.6 0.2 collective-permute-start.6
  10.4 3.1 %shard_map.141 = (f32[1024,512]{1,0:T(8,128)S(1)}, bf16[2048,512]{1,0:T(8,128)(2,1)S(1)}, bf16[1280,512]{1,0:T(8,128)(2,1)S(1)}, s32[16,128]{1,0:T(8,128)S(1)}, ...) custom-call(s32[1,1]{1,0:T(1,128)} %bitcast.3.limit_ref, ...), custom_call_target="tpu_custom_call" | custom-call | flops 255013680 | bytes 262144 | tf_op jit(solution)/shard_map/pallas_call | solution.py:363
  13.6 0.0 collective-permute-done.4
  13.6 1.7 %collective-permute-done.6 = bf16[32,512]{1,0:T(8,128)(2,1)S(1)} collective-permute-done((bf16[32,512]{1,0:T(8,128)(2,1)S(1)}, bf16[32,512]{1,0:T(8,128)(2,1)S(1)}, u32[]{:S(2)}, u32[]{:S(2)}) %collective-permute-start.6) | collective-permute-done | bytes 32800 | tf_op jit(solution)/shard_map/ppermute | solution.py:467
  15.3 0.0 collective-permute-done.3
  15.3 0.1 collective-permute-start.7
  15.4 0.5 %collective-permute-start.8 = (bf16[256,512]{1,0:T(8,128)(2,1)S(1)}, bf16[256,512]{1,0:T(8,128)(2,1)S(1)}, u32[]{:S(2)}, u32[]{:S(2)}) collective-permute-start(bf16[256,512]{1,0:T(8,128)(2,1)S(1)} %get-tuple-element.78.va_ref), channel_id=1, source_target_pairs={{0,1},{1,0},{2,3},{3,2},{4,5},{5,4},{6,7},{7,6},{8,9},{9,8},{10,11... | collective-permute-start | bytes 786440 | tf_op jit(solution)/shard_map/ppermute | solution.py:435
  15.9 0.1 collective-permute-start.1
  16.0 0.4 %collective-permute-start.2 = (bf16[256,512]{1,0:T(8,128)(2,1)S(1)}, bf16[256,512]{1,0:T(8,128)(2,1)S(1)}, u32[]{:S(2)}, u32[]{:S(2)}) collective-permute-start(bf16[256,512]{1,0:T(8,128)(2,1)S(1)} %get-tuple-element.65.va_ref), channel_id=1, source_target_pairs={{0,1},{1,0},{2,3},{3,2},{4,5},{5,4},{6,7},{7,6},{8,9},{9,8},{10,11... | collective-permute-start | bytes 786440 | tf_op jit(solution)/shard_map/ppermute | solution.py:435
  16.4 2.4 %shard_map.142 = (f32[1024,512]{1,0:T(8,128)S(1)}, bf16[512,512]{1,0:T(8,128)(2,1)S(1)}) custom-call(bf16[2048,512]{1,0:T(8,128)(2,1)S(1)} %get-tuple-element.70.latent.latent_ref, s32[16,128]{1,0:T(8,128)S(1)} %get-tuple-element.61.send.send_ref, s32[16,128]{1,0:T(8,128)S(1)} %get-tuple-element.62.recv.recv_ref, ...), custom_call_target="tpu_custom_call" | custom-call | flops 2147483648 | bytes 262144 | tf_op jit(solution)/shard_map/pallas_call | solution.py:363
  18.8 0.0 collective-permute-done.7.theirs_ref
  18.8 5.6 %shard_map.143 = (bf16[2048,256]{1,0:T(8,128)(2,1)S(1)}, bf16[2048,256]{1,0:T(8,128)(2,1)S(1)}, bf16[2048,512]{1,0:T(8,128)(2,1)S(1)}, bf16[256,512]{1,0:T(8,128)(2,1)S(1)}, s32[16,128]{1,0:T(8,128)S(1)}) custom-call(s32[16,128]{1,0:T(8,128)S(1)} %get-tuple-element.66.live_ref, f32[1024,512]{1,0:T(8,128)S(1)} %get-tuple-element.69.pre_ref, ...), custom_call_target="tpu_custom_call" | custom-call | flops 4563402752 | bytes 262144 | tf_op jit(solution)/shard_map/pallas_call | solution.py:363
  24.4 0.2 collective-permute-start.9
  24.6 0.7 %shard_map.144.mine_ref = f32[256,512]{1,0:T(8,128)S(1)} custom-call(bf16[2048,512]{1,0:T(8,128)(2,1)S(1)} %get-tuple-element.93.fresh_ref, s32[16,128]{1,0:T(8,128)S(1)} %get-tuple-element.85.recv_ref), custom_call_target="tpu_custom_call" | custom-call | flops 536870912 | bytes 262144 | tf_op jit(solution)/shard_map/pallas_call | solution.py:363
  25.3 0.5 %collective-permute-start.15 = (bf16[2048,256]{1,0:T(8,128)(2,1)S(1)}, bf16[2048,256]{1,0:T(8,128)(2,1)S(1)}, u32[]{:S(2)}, u32[]{:S(2)}) collective-permute-start(bf16[2048,256]{1,0:T(8,128)(2,1)S(1)} %get-tuple-element.113), channel_id=1, source_target_pairs={{0,1},{1,0},{2,3},{3,2},{4,5},{5,4},{6,7},{7,6},{8,9},{9,8},{10,11... | collective-permute-start | bytes 3145736 | tf_op jit(solution)/shard_map/ppermute | solution.py:435
  25.8 0.3 collective-permute-done.9.theirs_ref
  26.0 0.1 shard_map.145
  26.1 0.6 %collective-permute-start.13 = (bf16[160,512]{1,0:T(8,128)(2,1)S(1)}, bf16[160,512]{1,0:T(8,128)(2,1)S(1)}, u32[]{:S(2)}, u32[]{:S(2)}) collective-permute-start(bf16[160,512]{1,0:T(8,128)(2,1)S(1)} %get-tuple-element.100), channel_id=1, source_target_pairs={{0,2},{1,15},{2,0},{3,5},{4,6},{5,3},{6,4},{7,9},{8,10},{9,7},{10,... | collective-permute-start | bytes 491528 | tf_op jit(solution)/shard_map/ppermute | solution.py:540
  26.7 1.9 %collective-permute-start.10 = (bf16[32,512]{1,0:T(8,128)(2,1)S(1)}, bf16[32,512]{1,0:T(8,128)(2,1)S(1)}, u32[]{:S(2)}, u32[]{:S(2)}) collective-permute-start(bf16[32,512]{1,0:T(8,128)(2,1)S(1)} %get-tuple-element.97), channel_id=1, source_target_pairs={{0,12},{1,7},{2,14},{3,13},{4,8},{5,11},{6,10},{7,1},{8,4},{9,15},... | collective-permute-start | bytes 98312 | tf_op jit(solution)/shard_map/ppermute | solution.py:540
  28.6 0.0 collective-permute-start.11
  28.7 2.4 %collective-permute-start.12 = (bf16[32,512]{1,0:T(8,128)(2,1)S(1)}, bf16[32,512]{1,0:T(8,128)(2,1)S(1)}, u32[]{:S(2)}, u32[]{:S(2)}) collective-permute-start(bf16[32,512]{1,0:T(8,128)(2,1)S(1)} %get-tuple-element.99), channel_id=1, source_target_pairs={{0,8},{1,11},{2,10},{3,9},{4,12},{5,15},{6,14},{7,13},{8,0},{9,3},... | collective-permute-start | bytes 98312 | tf_op jit(solution)/shard_map/ppermute | solution.py:540
  31.1 2.7 %shard_map.146 = (f32[640,512]{1,0:T(8,128)S(1)}, f32[640,512]{1,0:T(8,128)S(1)}, bf16[4096,256]{1,0:T(8,128)(2,1)}) custom-call(bf16[2048,512]{1,0:T(8,128)(2,1)S(1)} %get-tuple-element.93.fresh_ref, s32[16,128]{1,0:T(8,128)S(1)} %get-tuple-element.85.recv_ref, bf16[640,512]{1,0:T(8,128)(2,1)S(1)} %get-tuple-element.59.node.node_ref, ...), custom_call_target="tpu_custom_call" | custom-call | flops 134217728 | bytes 262144 | tf_op jit(solution)/shard_map/pallas_call | solution.py:363
  33.9 0.4 shard_map.147
  34.3 0.3 collective-permute-start.14
  34.6 1.0 %shard_map.149 = bf16[4096,256]{1,0:T(8,128)(2,1)} custom-call(bf16[2048,256]{1,0:T(8,128)(2,1)S(1)} %collective-permute-done.15.theirs_ref, bf16[4096,256]{1,0:T(8,128)(2,1)} %get-tuple-element.115.edges_in_ref), custom_call_target="tpu_custom_call", output_to_operand_aliasing={{}: (1, {})} | custom-call | flops 335544320 | bytes 262144 | tf_op jit(solution)/shard_map/pallas_call | solution.py:363
  35.6 0.8 %collective-permute-done.14.partner_ref = bf16[640,512]{1,0:T(8,128)(2,1)S(1)} collective-permute-done((bf16[640,512]{1,0:T(8,128)(2,1)S(1)}, bf16[640,512]{1,0:T(8,128)(2,1)S(1)}, u32[]{:S(2)}, u32[]{:S(2)}) %collective-permute-start.14) | collective-permute-done | bytes 655392 | tf_op jit(solution)/shard_map/ppermute | solution.py:435
  36.4 2.0 %shard_map.148 = bf16[640,256]{1,0:T(8,128)(2,1)} custom-call(bf16[640,512]{1,0:T(8,128)(2,1)S(1)} %get-tuple-element.59.node.node_ref, f32[640,512]{1,0:T(8,128)S(1)} %get-tuple-element.108.own_ref, bf16[640,512]{1,0:T(8,128)(2,1)S(1)} %collective-permute-done.14.partner_ref, f32[640,512]{1,0:T(8,128)S(1)} %get-tuple-element.110.pre_ref, ...), custom_call_target="tpu_custom_call" | custom-call | flops 671088640 | bytes 262144 | tf_op jit(solution)/shard_map/pallas_call | solution.py:363
  (15 shorter events, 0.1 us)
Async XLA Ops:
  0.6 9.8 %collective-permute-start = (bf16[1536,256]{1,0:T(8,128)(2,1)}, bf16[1536,256]{1,0:T(8,128)(2,1)S(1)}, u32[]{:S(2)}, u32[]{:S(2)}) collective-permute-start(bf16[1536,256]{1,0:T(8,128)(2,1)} %refs_3_.2), channel_id=1, source_target_pairs={{0,1},{1,0},{2,3},{3,2},{4,5},{5,4},{6,7},{7,6},{8,9},{9,8},{10,11... | collective-permute-start | bytes 2359304 | tf_op jit(solution)/shard_map/ppermute | solution.py:435
  2.8 12.5 %collective-permute-start.3 = (bf16[160,512]{1,0:T(8,128)(2,1)S(1)}, bf16[160,512]{1,0:T(8,128)(2,1)S(1)}, u32[]{:S(2)}, u32[]{:S(2)}) collective-permute-start(bf16[160,512]{1,0:T(8,128)(2,1)S(1)} %get-tuple-element.68), channel_id=1, source_target_pairs={{0,2},{1,15},{2,0},{3,5},{4,6},{5,3},{6,4},{7,9},{8,10},{9,7},{10,... | collective-permute-start | bytes 491528 | tf_op jit(solution)/shard_map/ppermute | solution.py:467
  5.4 8.2 %collective-permute-start.4 = (bf16[32,512]{1,0:T(8,128)(2,1)S(1)}, bf16[32,512]{1,0:T(8,128)(2,1)S(1)}, u32[]{:S(2)}, u32[]{:S(2)}) collective-permute-start(bf16[32,512]{1,0:T(8,128)(2,1)S(1)} %slice.2), channel_id=1, source_target_pairs={{0,8},{1,11},{2,10},{3,9},{4,12},{5,15},{6,14},{7,13},{8,0},{9,3},... | collective-permute-start | bytes 98312 | tf_op jit(solution)/shard_map/ppermute | solution.py:467
  8.0 5.6 %collective-permute-start.5 = (bf16[32,512]{1,0:T(8,128)(2,1)S(1)}, bf16[32,512]{1,0:T(8,128)(2,1)S(1)}, u32[]{:S(2)}, u32[]{:S(2)}) collective-permute-start(bf16[32,512]{1,0:T(8,128)(2,1)S(1)} %slice.2), channel_id=1, source_target_pairs={{0,4},{1,5},{2,6},{3,7},{4,0},{5,1},{6,2},{7,3},{8,12},{9,13},{10,... | collective-permute-start | bytes 98312 | tf_op jit(solution)/shard_map/ppermute | solution.py:467
  9.6 5.7 %collective-permute-start.6 = (bf16[32,512]{1,0:T(8,128)(2,1)S(1)}, bf16[32,512]{1,0:T(8,128)(2,1)S(1)}, u32[]{:S(2)}, u32[]{:S(2)}) collective-permute-start(bf16[32,512]{1,0:T(8,128)(2,1)S(1)} %slice.2), channel_id=1, source_target_pairs={{0,12},{1,7},{2,14},{3,13},{4,8},{5,11},{6,10},{7,1},{8,4},{9,15},... | collective-permute-start | bytes 98312 | tf_op jit(solution)/shard_map/ppermute | solution.py:467
  15.3 3.5 %collective-permute-start.7 = (bf16[256,512]{1,0:T(8,128)(2,1)S(1)}, bf16[256,512]{1,0:T(8,128)(2,1)S(1)}, u32[]{:S(2)}, u32[]{:S(2)}) collective-permute-start(bf16[256,512]{1,0:T(8,128)(2,1)S(1)} %constant_dynamic-update-slice_fusion.mine), channel_id=1, source_target_pairs={{0,1},{1,0},{2,3},{3,2},{4,5},{5,4},{6,7},{7,6},{8,9},{9,8},{10,11... | collective-permute-start | bytes 786440 | tf_op jit(solution)/shard_map/ppermute | solution.py:435
  15.4 3.4 %collective-permute-start.8 = (bf16[256,512]{1,0:T(8,128)(2,1)S(1)}, bf16[256,512]{1,0:T(8,128)(2,1)S(1)}, u32[]{:S(2)}, u32[]{:S(2)}) collective-permute-start(bf16[256,512]{1,0:T(8,128)(2,1)S(1)} %get-tuple-element.78.va_ref), channel_id=1, source_target_pairs={{0,1},{1,0},{2,3},{3,2},{4,5},{5,4},{6,7},{7,6},{8,9},{9,8},{10,11... | collective-permute-start | bytes 786440 | tf_op jit(solution)/shard_map/ppermute | solution.py:435
  15.9 8.5 %collective-permute-start.1 = (bf16[1024,256]{1,0:T(8,128)(2,1)S(1)}, bf16[1024,256]{1,0:T(8,128)(2,1)S(1)}, u32[]{:S(2)}, u32[]{:S(2)}) collective-permute-start(bf16[1024,256]{1,0:T(8,128)(2,1)S(1)} %get-tuple-element.64.wa_ref), channel_id=1, source_target_pairs={{0,1},{1,0},{2,3},{3,2},{4,5},{5,4},{6,7},{7,6},{8,9},{9,8},{10,11... | collective-permute-start | bytes 1572872 | tf_op jit(solution)/shard_map/ppermute | solution.py:435
  16.0 8.4 %collective-permute-start.2 = (bf16[256,512]{1,0:T(8,128)(2,1)S(1)}, bf16[256,512]{1,0:T(8,128)(2,1)S(1)}, u32[]{:S(2)}, u32[]{:S(2)}) collective-permute-start(bf16[256,512]{1,0:T(8,128)(2,1)S(1)} %get-tuple-element.65.va_ref), channel_id=1, source_target_pairs={{0,1},{1,0},{2,3},{3,2},{4,5},{5,4},{6,7},{7,6},{8,9},{9,8},{10,11... | collective-permute-start | bytes 786440 | tf_op jit(solution)/shard_map/ppermute | solution.py:435
  24.4 1.6 %collective-permute-start.9 = (bf16[256,512]{1,0:T(8,128)(2,1)S(1)}, bf16[256,512]{1,0:T(8,128)(2,1)S(1)}, u32[]{:S(2)}, u32[]{:S(2)}) collective-permute-start(bf16[256,512]{1,0:T(8,128)(2,1)S(1)} %get-tuple-element.88), channel_id=1, source_target_pairs={{0,1},{1,0},{2,3},{3,2},{4,5},{5,4},{6,7},{7,6},{8,9},{9,8},{10,11... | collective-permute-start | bytes 786440 | tf_op jit(solution)/shard_map/ppermute | solution.py:435
  25.3 9.3 %collective-permute-start.15 = (bf16[2048,256]{1,0:T(8,128)(2,1)S(1)}, bf16[2048,256]{1,0:T(8,128)(2,1)S(1)}, u32[]{:S(2)}, u32[]{:S(2)}) collective-permute-start(bf16[2048,256]{1,0:T(8,128)(2,1)S(1)} %get-tuple-element.113), channel_id=1, source_target_pairs={{0,1},{1,0},{2,3},{3,2},{4,5},{5,4},{6,7},{7,6},{8,9},{9,8},{10,11... | collective-permute-start | bytes 3145736 | tf_op jit(solution)/shard_map/ppermute | solution.py:435
  26.1 7.8 %collective-permute-start.13 = (bf16[160,512]{1,0:T(8,128)(2,1)S(1)}, bf16[160,512]{1,0:T(8,128)(2,1)S(1)}, u32[]{:S(2)}, u32[]{:S(2)}) collective-permute-start(bf16[160,512]{1,0:T(8,128)(2,1)S(1)} %get-tuple-element.100), channel_id=1, source_target_pairs={{0,2},{1,15},{2,0},{3,5},{4,6},{5,3},{6,4},{7,9},{8,10},{9,7},{10,... | collective-permute-start | bytes 491528 | tf_op jit(solution)/shard_map/ppermute | solution.py:540
  26.7 7.1 %collective-permute-start.10 = (bf16[32,512]{1,0:T(8,128)(2,1)S(1)}, bf16[32,512]{1,0:T(8,128)(2,1)S(1)}, u32[]{:S(2)}, u32[]{:S(2)}) collective-permute-start(bf16[32,512]{1,0:T(8,128)(2,1)S(1)} %get-tuple-element.97), channel_id=1, source_target_pairs={{0,12},{1,7},{2,14},{3,13},{4,8},{5,11},{6,10},{7,1},{8,4},{9,15},... | collective-permute-start | bytes 98312 | tf_op jit(solution)/shard_map/ppermute | solution.py:540
  28.6 5.2 %collective-permute-start.11 = (bf16[32,512]{1,0:T(8,128)(2,1)S(1)}, bf16[32,512]{1,0:T(8,128)(2,1)S(1)}, u32[]{:S(2)}, u32[]{:S(2)}) collective-permute-start(bf16[32,512]{1,0:T(8,128)(2,1)S(1)} %get-tuple-element.98), channel_id=1, source_target_pairs={{0,4},{1,5},{2,6},{3,7},{4,0},{5,1},{6,2},{7,3},{8,12},{9,13},{10,... | collective-permute-start | bytes 98312 | tf_op jit(solution)/shard_map/ppermute | solution.py:540
  28.7 5.2 %collective-permute-start.12 = (bf16[32,512]{1,0:T(8,128)(2,1)S(1)}, bf16[32,512]{1,0:T(8,128)(2,1)S(1)}, u32[]{:S(2)}, u32[]{:S(2)}) collective-permute-start(bf16[32,512]{1,0:T(8,128)(2,1)S(1)} %get-tuple-element.99), channel_id=1, source_target_pairs={{0,8},{1,11},{2,10},{3,9},{4,12},{5,15},{6,14},{7,13},{8,0},{9,3},... | collective-permute-start | bytes 98312 | tf_op jit(solution)/shard_map/ppermute | solution.py:540
  34.3 2.2 %collective-permute-start.14 = (bf16[640,512]{1,0:T(8,128)(2,1)S(1)}, bf16[640,512]{1,0:T(8,128)(2,1)S(1)}, u32[]{:S(2)}, u32[]{:S(2)}) collective-permute-start(bf16[640,512]{1,0:T(8,128)(2,1)S(1)} %get-tuple-element.109), channel_id=1, source_target_pairs={{0,1},{1,0},{2,3},{3,2},{4,5},{5,4},{6,7},{7,6},{8,9},{9,8},{10,11... | collective-permute-start | bytes 1966088 | tf_op jit(solution)/shard_map/ppermute | solution.py:435

commit v8 on v7

--- a/solution.py
+++ b/solution.py
@@ -247,7 +247,6 @@
     va_ref,
     vb_ref,
     gain_ref,
-    out_mine_ref,
     out_other_ref,
     fresh_all,
     group_other_ref,
@@ -284,7 +283,6 @@
         live = jnp.concatenate(columns[1], axis=0) != DEAD
         fresh = (latent_ref[part, :].astype(F32) + layer_norm(pre, gain, live)).astype(BF16)
         low, high = fresh[:, : width // 2], fresh[:, width // 2 :]
-        out_mine_ref[part, :] = jnp.where(feat == 0, low, high)
         out_other_ref[part, :] = jnp.where(feat == 0, high, low)
         fresh_all[part, :] = fresh
     receivers = flat_row(live_recv_ref[...])
@@ -309,10 +307,12 @@
     return edges.at[pl.ds(pl.multiple_of(core * share, share), share), :]
 
 
-def local_sums_kernel(fresh_ref, recv_ref, node_ref, wa_ref, wb_ref, mine_ref, sums_ref, pre_ref, edges_ref, sems):
-    placed = copies([(mine_ref, core_rows_of(edges_ref, lax.axis_index("feat")))], sems)
+def local_sums_kernel(fresh_ref, recv_ref, node_ref, wa_ref, wb_ref, sums_ref, pre_ref, edges_ref, sems):
     width = node_ref.shape[1]
     half = wa_ref.shape[1]
+    feat = lax.axis_index("feat")
+    columns = pl.ds(pl.multiple_of(feat * half, half), half)
+    placed = copies([(fresh_ref.at[:, columns], core_rows_of(edges_ref, feat))], sems)
     sums_ref[...] = dot(one_hot_columns(flat_row(recv_ref[...]), 0, sums_ref.shape[0]), fresh_ref[...])
     for weight, col in ((wa_ref, 0), (wb_ref, half)):
         pre_ref[:, col : col + half] = 0.5 * dot(node_ref[...], weight[:width, :])
@@ -500,18 +500,18 @@
     )
     node_w1_b, node_w2_b = swap(n_w1), swap(n_w2)
 
-    mine, other, fresh, group_other, live_recv = call(
+    other, fresh, group_other, live_recv = call(
         functools.partial(edge_kernel, layout=layout, block=block),
         (live, pre, pre2, latent, send, recv, projected, table_theirs, w1, edge_w1_b, w2, edge_w2_b, e_gain),
         [VMEM_SPEC] * 13,
-        [shape(share, half), shape(share, half), shape(share, width), shape(group, width), core_rows],
-        [VMEM_SPEC] * 5,
+        [shape(share, half), shape(share, width), shape(group, width), core_rows],
+        [VMEM_SPEC] * 4,
         2 * share * width * (width + 6 * group) + 4 * group * width * width,
         LIMIT,
         scratch=[pltpu.VMEM((4 * group, width), BF16)],
     )
-    node_w1_b, node_w2_b, mine, other, fresh, group_other = lax.optimization_barrier(
-        (node_w1_b, node_w2_b, mine, other, fresh, group_other)
+    node_w1_b, node_w2_b, other, fresh, group_other = lax.optimization_barrier(
+        (node_w1_b, node_w2_b, other, fresh, group_other)
     )
 
     group_theirs = swap(group_other)
@@ -540,8 +540,8 @@
     back = [lax.ppermute(outgoing[i], both, pairs[i]) for i in reversed(range(len(pairs)))][::-1]
     local_sums, node_pre, edges = call(
         local_sums_kernel,
-        (fresh, live_recv, node, n_w1, node_w1_b, mine),
-        [VMEM_SPEC] * 5 + [ANY_SPEC],
+        (fresh, live_recv, node, n_w1, node_w1_b),
+        [VMEM_SPEC] * 5,
         [shape(node_count, width, F32), shape(node_count, width, F32), shape(edge_count, half)],
         [VMEM_SPEC] * 2 + [ANY_SPEC],
         2 * share * width * node_count // BESIDE,

time: 38.6 us -> 38.5 us (level)
  transfers between devices with their start and end apart: 16 -> 16, of which waited for: 3 -> 4; matrix products, arithmetic and copies ran while one was open for 0% -> 0% of each run, Pallas kernels for 46% -> 45%
where the time goes in v8:
time: 38.5 us; the launch traced here: 38.3 us
  Pallas kernels  19.3 us (50%)
  starting transfers between devices  14.8 us (38%)
  waiting for transfers between devices  2.75 us (7%)
  between operations  1.46 us (4%)
    pallas_call x10, Pallas kernels, call(): pl.pallas_call(kernel, in_specs=in_specs, out_specs=out_specs, out_shape=...  19.3 us
    ppermute x4, starting transfers between devices, on_device(): lax.ppermute(lent[halo:] if i else lent, both, pairs[i])  6.98 us
    ppermute x4, starting transfers between devices, on_device(): lax.ppermute(outgoing[i], both, pairs[i])  5.01 us
    ppermute x8, starting transfers between devices, swap(): return lax.ppermute(values, 'feat', FEAT_SWAP)  2.78 us
    ppermute x4, waiting for transfers between devices, on_device(): lax.ppermute(lent[halo:] if i else lent, both, pairs[i])  1.68 us
    ppermute x8, waiting for transfers between devices, swap(): return lax.ppermute(values, 'feat', FEAT_SWAP)  1.01 us
  transfers between devices with their start and end apart: 16, of which 4 were waited for; matrix products, arithmetic and copies ran while one was open for 0% of the time, Pallas kernels for 45%

profile of v8, /device:TPU:0, one launch (start us, length us, event | category | flops | bytes accessed | tf_op | source)
XLA Modules:
  0.0 38.3 jit_solution(9810589214699031216)
XLA Ops:
  0.6 0.5 %collective-permute-start = (bf16[1536,256]{1,0:T(8,128)(2,1)}, bf16[1536,256]{1,0:T(8,128)(2,1)S(1)}, u32[]{:S(2)}, u32[]{:S(2)}) collective-permute-start(bf16[1536,256]{1,0:T(8,128)(2,1)} %refs_3_.2), channel_id=1, source_target_pairs={{0,1},{1,0},{2,3},{3,2},{4,5},{5,4},{6,7},{7,6},{8,9},{9,8},{10,11... | collective-permute-start | bytes 2359304 | tf_op jit(solution)/shard_map/ppermute | solution.py:435
  1.1 1.6 %shard_map.140 = (bf16[160,512]{1,0:T(8,128)(2,1)S(1)}, bf16[640,512]{1,0:T(8,128)(2,1)S(1)}, s32[2,128]{1,0:T(2,128)S(1)}, s32[32]{0:T(128)S(1)}, bf16[1536,256...) custom-call(bf16[640,512]{1,0:T(8,128)(2,1)} %refs_0_.2, ...), custom_call_target="tpu_custom_call" | custom-call | flops 104857600 | bytes 262144 | tf_op jit(solution)/shard_map/pallas_call | solution.py:363
  2.8 2.6 %collective-permute-start.3 = (bf16[160,512]{1,0:T(8,128)(2,1)S(1)}, bf16[160,512]{1,0:T(8,128)(2,1)S(1)}, u32[]{:S(2)}, u32[]{:S(2)}) collective-permute-start(bf16[160,512]{1,0:T(8,128)(2,1)S(1)} %get-tuple-element.66), channel_id=1, source_target_pairs={{0,2},{1,15},{2,0},{3,5},{4,6},{5,3},{6,4},{7,9},{8,10},{9,7},{10,... | collective-permute-start | bytes 491528 | tf_op jit(solution)/shard_map/ppermute | solution.py:467
  5.4 2.6 %collective-permute-start.4 = (bf16[32,512]{1,0:T(8,128)(2,1)S(1)}, bf16[32,512]{1,0:T(8,128)(2,1)S(1)}, u32[]{:S(2)}, u32[]{:S(2)}) collective-permute-start(bf16[32,512]{1,0:T(8,128)(2,1)S(1)} %slice.2), channel_id=1, source_target_pairs={{0,8},{1,11},{2,10},{3,9},{4,12},{5,15},{6,14},{7,13},{8,0},{9,3},... | collective-permute-start | bytes 98312 | tf_op jit(solution)/shard_map/ppermute | solution.py:467
  8.0 1.6 %collective-permute-start.5 = (bf16[32,512]{1,0:T(8,128)(2,1)S(1)}, bf16[32,512]{1,0:T(8,128)(2,1)S(1)}, u32[]{:S(2)}, u32[]{:S(2)}) collective-permute-start(bf16[32,512]{1,0:T(8,128)(2,1)S(1)} %slice.2), channel_id=1, source_target_pairs={{0,4},{1,5},{2,6},{3,7},{4,0},{5,1},{6,2},{7,3},{8,12},{9,13},{10,... | collective-permute-start | bytes 98312 | tf_op jit(solution)/shard_map/ppermute | solution.py:467
  9.6 0.2 collective-permute-start.6
  10.4 3.1 %shard_map.141 = (f32[1024,512]{1,0:T(8,128)S(1)}, bf16[2048,512]{1,0:T(8,128)(2,1)S(1)}, bf16[1280,512]{1,0:T(8,128)(2,1)S(1)}, s32[16,128]{1,0:T(8,128)S(1)}, ...) custom-call(s32[1,1]{1,0:T(1,128)} %bitcast.3.limit_ref, ...), custom_call_target="tpu_custom_call" | custom-call | flops 255013680 | bytes 262144 | tf_op jit(solution)/shard_map/pallas_call | solution.py:363
  13.6 0.0 collective-permute-done.4
  13.6 1.7 %collective-permute-done.6 = bf16[32,512]{1,0:T(8,128)(2,1)S(1)} collective-permute-done((bf16[32,512]{1,0:T(8,128)(2,1)S(1)}, bf16[32,512]{1,0:T(8,128)(2,1)S(1)}, u32[]{:S(2)}, u32[]{:S(2)}) %collective-permute-start.6) | collective-permute-done | bytes 32800 | tf_op jit(solution)/shard_map/ppermute | solution.py:467
  15.3 0.1 collective-permute-start.7
  15.4 0.5 %collective-permute-start.8 = (bf16[256,512]{1,0:T(8,128)(2,1)S(1)}, bf16[256,512]{1,0:T(8,128)(2,1)S(1)}, u32[]{:S(2)}, u32[]{:S(2)}) collective-permute-start(bf16[256,512]{1,0:T(8,128)(2,1)S(1)} %get-tuple-element.76.va_ref), channel_id=1, source_target_pairs={{0,1},{1,0},{2,3},{3,2},{4,5},{5,4},{6,7},{7,6},{8,9},{9,8},{10,11... | collective-permute-start | bytes 786440 | tf_op jit(solution)/shard_map/ppermute | solution.py:435
  15.9 0.1 collective-permute-start.1
  16.0 0.4 %collective-permute-start.2 = (bf16[256,512]{1,0:T(8,128)(2,1)S(1)}, bf16[256,512]{1,0:T(8,128)(2,1)S(1)}, u32[]{:S(2)}, u32[]{:S(2)}) collective-permute-start(bf16[256,512]{1,0:T(8,128)(2,1)S(1)} %get-tuple-element.63.va_ref), channel_id=1, source_target_pairs={{0,1},{1,0},{2,3},{3,2},{4,5},{5,4},{6,7},{7,6},{8,9},{9,8},{10,11... | collective-permute-start | bytes 786440 | tf_op jit(solution)/shard_map/ppermute | solution.py:435
  16.4 2.4 %shard_map.142 = (f32[1024,512]{1,0:T(8,128)S(1)}, bf16[512,512]{1,0:T(8,128)(2,1)S(1)}) custom-call(bf16[2048,512]{1,0:T(8,128)(2,1)S(1)} %get-tuple-element.68.latent.latent_ref, s32[16,128]{1,0:T(8,128)S(1)} %get-tuple-element.59.send.send_ref, s32[16,128]{1,0:T(8,128)S(1)} %get-tuple-element.60.recv.recv_ref, ...), custom_call_target="tpu_custom_call" | custom-call | flops 2147483648 | bytes 262144 | tf_op jit(solution)/shard_map/pallas_call | solution.py:363
  18.8 0.0 collective-permute-done.7.theirs_ref
  18.8 5.6 %shard_map.143 = (bf16[2048,256]{1,0:T(8,128)(2,1)S(1)}, bf16[2048,512]{1,0:T(8,128)(2,1)S(1)}, bf16[256,512]{1,0:T(8,128)(2,1)S(1)}, s32[16,128]{1,0:T(8,128)S(1)}) custom-call(s32[16,128]{1,0:T(8,128)S(1)} %get-tuple-element.64.live_ref, f32[1024,512]{1,0:T(8,128)S(1)} %get-tuple-element.67.pre_ref, f32[1024,512]{1,0:T(8,128)S(1)} %get-tuple-element.74.pre2_ref, ...), custom_call_target="tpu_custom_call" | custom-call | flops 4563402752 | bytes 262144 | tf_op jit(solution)/shard_map/pallas_call | solution.py:363
  24.5 0.1 collective-permute-start.9
  24.6 0.7 %shard_map.144.mine_ref = f32[256,512]{1,0:T(8,128)S(1)} custom-call(bf16[2048,512]{1,0:T(8,128)(2,1)S(1)} %get-tuple-element.90.fresh_ref, s32[16,128]{1,0:T(8,128)S(1)} %get-tuple-element.82.recv_ref), custom_call_target="tpu_custom_call" | custom-call | flops 536870912 | bytes 262144 | tf_op jit(solution)/shard_map/pallas_call | solution.py:363
  25.3 0.5 %collective-permute-start.15 = (bf16[2048,256]{1,0:T(8,128)(2,1)S(1)}, bf16[2048,256]{1,0:T(8,128)(2,1)S(1)}, u32[]{:S(2)}, u32[]{:S(2)}) collective-permute-start(bf16[2048,256]{1,0:T(8,128)(2,1)S(1)} %get-tuple-element.109), channel_id=1, source_target_pairs={{0,1},{1,0},{2,3},{3,2},{4,5},{5,4},{6,7},{7,6},{8,9},{9,8},{10,11... | collective-permute-start | bytes 3145736 | tf_op jit(solution)/shard_map/ppermute | solution.py:435
  25.8 0.3 collective-permute-done.9.theirs_ref
  26.1 0.1 shard_map.145
  26.2 0.6 %collective-permute-start.13 = (bf16[160,512]{1,0:T(8,128)(2,1)S(1)}, bf16[160,512]{1,0:T(8,128)(2,1)S(1)}, u32[]{:S(2)}, u32[]{:S(2)}) collective-permute-start(bf16[160,512]{1,0:T(8,128)(2,1)S(1)} %get-tuple-element.96), channel_id=1, source_target_pairs={{0,2},{1,15},{2,0},{3,5},{4,6},{5,3},{6,4},{7,9},{8,10},{9,7},{10,... | collective-permute-start | bytes 491528 | tf_op jit(solution)/shard_map/ppermute | solution.py:540
  26.8 1.9 %collective-permute-start.10 = (bf16[32,512]{1,0:T(8,128)(2,1)S(1)}, bf16[32,512]{1,0:T(8,128)(2,1)S(1)}, u32[]{:S(2)}, u32[]{:S(2)}) collective-permute-start(bf16[32,512]{1,0:T(8,128)(2,1)S(1)} %get-tuple-element.93), channel_id=1, source_target_pairs={{0,12},{1,7},{2,14},{3,13},{4,8},{5,11},{6,10},{7,1},{8,4},{9,15},... | collective-permute-start | bytes 98312 | tf_op jit(solution)/shard_map/ppermute | solution.py:540
  28.7 0.0 collective-permute-start.11
  28.7 2.5 %collective-permute-start.12 = (bf16[32,512]{1,0:T(8,128)(2,1)S(1)}, bf16[32,512]{1,0:T(8,128)(2,1)S(1)}, u32[]{:S(2)}, u32[]{:S(2)}) collective-permute-start(bf16[32,512]{1,0:T(8,128)(2,1)S(1)} %get-tuple-element.95), channel_id=1, source_target_pairs={{0,8},{1,11},{2,10},{3,9},{4,12},{5,15},{6,14},{7,13},{8,0},{9,3},... | collective-permute-start | bytes 98312 | tf_op jit(solution)/shard_map/ppermute | solution.py:540
  31.2 2.5 %shard_map.146 = (f32[640,512]{1,0:T(8,128)S(1)}, f32[640,512]{1,0:T(8,128)S(1)}, bf16[4096,256]{1,0:T(8,128)(2,1)}) custom-call(bf16[2048,512]{1,0:T(8,128)(2,1)S(1)} %get-tuple-element.90.fresh_ref, s32[16,128]{1,0:T(8,128)S(1)} %get-tuple-element.82.recv_ref, bf16[640,512]{1,0:T(8,128)(2,1)S(1)} %get-tuple-element.57.node.node_ref, ...), custom_call_target="tpu_custom_call" | custom-call | flops 134217728 | bytes 262144 | tf_op jit(solution)/shard_map/pallas_call | solution.py:363
  33.6 0.1 collective-permute-done.11.refs_2_
  33.7 0.4 shard_map.147
  34.1 0.5 %collective-permute-start.14 = (bf16[640,512]{1,0:T(8,128)(2,1)S(1)}, bf16[640,512]{1,0:T(8,128)(2,1)S(1)}, u32[]{:S(2)}, u32[]{:S(2)}) collective-permute-start(bf16[640,512]{1,0:T(8,128)(2,1)S(1)} %get-tuple-element.105), channel_id=1, source_target_pairs={{0,1},{1,0},{2,3},{3,2},{4,5},{5,4},{6,7},{7,6},{8,9},{9,8},{10,11... | collective-permute-start | bytes 1966088 | tf_op jit(solution)/shard_map/ppermute | solution.py:435
  34.6 1.0 %shard_map.149 = bf16[4096,256]{1,0:T(8,128)(2,1)} custom-call(bf16[2048,256]{1,0:T(8,128)(2,1)S(1)} %collective-permute-done.15.theirs_ref, bf16[4096,256]{1,0:T(8,128)(2,1)} %get-tuple-element.111.edges_in_ref), custom_call_target="tpu_custom_call", output_to_operand_aliasing={{}: (1, {})} | custom-call | flops 335544320 | bytes 262144 | tf_op jit(solution)/shard_map/pallas_call | solution.py:363
  35.6 0.7 %collective-permute-done.14.partner_ref = bf16[640,512]{1,0:T(8,128)(2,1)S(1)} collective-permute-done((bf16[640,512]{1,0:T(8,128)(2,1)S(1)}, bf16[640,512]{1,0:T(8,128)(2,1)S(1)}, u32[]{:S(2)}, u32[]{:S(2)}) %collective-permute-start.14) | collective-permute-done | bytes 655392 | tf_op jit(solution)/shard_map/ppermute | solution.py:435
  36.4 2.0 %shard_map.148 = bf16[640,256]{1,0:T(8,128)(2,1)} custom-call(bf16[640,512]{1,0:T(8,128)(2,1)S(1)} %get-tuple-element.57.node.node_ref, f32[640,512]{1,0:T(8,128)S(1)} %get-tuple-element.104.own_ref, bf16[640,512]{1,0:T(8,128)(2,1)S(1)} %collective-permute-done.14.partner_ref, f32[640,512]{1,0:T(8,128)S(1)} %get-tuple-element.106.pre_ref, ...), custom_call_target="tpu_custom_call" | custom-call | flops 671088640 | bytes 262144 | tf_op jit(solution)/shard_map/pallas_call | solution.py:363
  (15 shorter events, 0.1 us)
Async XLA Ops:
  0.6 9.8 %collective-permute-start = (bf16[1536,256]{1,0:T(8,128)(2,1)}, bf16[1536,256]{1,0:T(8,128)(2,1)S(1)}, u32[]{:S(2)}, u32[]{:S(2)}) collective-permute-start(bf16[1536,256]{1,0:T(8,128)(2,1)} %refs_3_.2), channel_id=1, source_target_pairs={{0,1},{1,0},{2,3},{3,2},{4,5},{5,4},{6,7},{7,6},{8,9},{9,8},{10,11... | collective-permute-start | bytes 2359304 | tf_op jit(solution)/shard_map/ppermute | solution.py:435
  2.8 12.5 %collective-permute-start.3 = (bf16[160,512]{1,0:T(8,128)(2,1)S(1)}, bf16[160,512]{1,0:T(8,128)(2,1)S(1)}, u32[]{:S(2)}, u32[]{:S(2)}) collective-permute-start(bf16[160,512]{1,0:T(8,128)(2,1)S(1)} %get-tuple-element.66), channel_id=1, source_target_pairs={{0,2},{1,15},{2,0},{3,5},{4,6},{5,3},{6,4},{7,9},{8,10},{9,7},{10,... | collective-permute-start | bytes 491528 | tf_op jit(solution)/shard_map/ppermute | solution.py:467
  5.4 8.2 %collective-permute-start.4 = (bf16[32,512]{1,0:T(8,128)(2,1)S(1)}, bf16[32,512]{1,0:T(8,128)(2,1)S(1)}, u32[]{:S(2)}, u32[]{:S(2)}) collective-permute-start(bf16[32,512]{1,0:T(8,128)(2,1)S(1)} %slice.2), channel_id=1, source_target_pairs={{0,8},{1,11},{2,10},{3,9},{4,12},{5,15},{6,14},{7,13},{8,0},{9,3},... | collective-permute-start | bytes 98312 | tf_op jit(solution)/shard_map/ppermute | solution.py:467
  8.0 5.6 %collective-permute-start.5 = (bf16[32,512]{1,0:T(8,128)(2,1)S(1)}, bf16[32,512]{1,0:T(8,128)(2,1)S(1)}, u32[]{:S(2)}, u32[]{:S(2)}) collective-permute-start(bf16[32,512]{1,0:T(8,128)(2,1)S(1)} %slice.2), channel_id=1, source_target_pairs={{0,4},{1,5},{2,6},{3,7},{4,0},{5,1},{6,2},{7,3},{8,12},{9,13},{10,... | collective-permute-start | bytes 98312 | tf_op jit(solution)/shard_map/ppermute | solution.py:467
  9.6 5.7 %collective-permute-start.6 = (bf16[32,512]{1,0:T(8,128)(2,1)S(1)}, bf16[32,512]{1,0:T(8,128)(2,1)S(1)}, u32[]{:S(2)}, u32[]{:S(2)}) collective-permute-start(bf16[32,512]{1,0:T(8,128)(2,1)S(1)} %slice.2), channel_id=1, source_target_pairs={{0,12},{1,7},{2,14},{3,13},{4,8},{5,11},{6,10},{7,1},{8,4},{9,15},... | collective-permute-start | bytes 98312 | tf_op jit(solution)/shard_map/ppermute | solution.py:467
  15.3 3.5 %collective-permute-start.7 = (bf16[256,512]{1,0:T(8,128)(2,1)S(1)}, bf16[256,512]{1,0:T(8,128)(2,1)S(1)}, u32[]{:S(2)}, u32[]{:S(2)}) collective-permute-start(bf16[256,512]{1,0:T(8,128)(2,1)S(1)} %constant_dynamic-update-slice_fusion.mine), channel_id=1, source_target_pairs={{0,1},{1,0},{2,3},{3,2},{4,5},{5,4},{6,7},{7,6},{8,9},{9,8},{10,11... | collective-permute-start | bytes 786440 | tf_op jit(solution)/shard_map/ppermute | solution.py:435
  15.4 3.4 %collective-permute-start.8 = (bf16[256,512]{1,0:T(8,128)(2,1)S(1)}, bf16[256,512]{1,0:T(8,128)(2,1)S(1)}, u32[]{:S(2)}, u32[]{:S(2)}) collective-permute-start(bf16[256,512]{1,0:T(8,128)(2,1)S(1)} %get-tuple-element.76.va_ref), channel_id=1, source_target_pairs={{0,1},{1,0},{2,3},{3,2},{4,5},{5,4},{6,7},{7,6},{8,9},{9,8},{10,11... | collective-permute-start | bytes 786440 | tf_op jit(solution)/shard_map/ppermute | solution.py:435
  15.9 8.6 %collective-permute-start.1 = (bf16[1024,256]{1,0:T(8,128)(2,1)S(1)}, bf16[1024,256]{1,0:T(8,128)(2,1)S(1)}, u32[]{:S(2)}, u32[]{:S(2)}) collective-permute-start(bf16[1024,256]{1,0:T(8,128)(2,1)S(1)} %get-tuple-element.62.wa_ref), channel_id=1, source_target_pairs={{0,1},{1,0},{2,3},{3,2},{4,5},{5,4},{6,7},{7,6},{8,9},{9,8},{10,11... | collective-permute-start | bytes 1572872 | tf_op jit(solution)/shard_map/ppermute | solution.py:435
  16.0 8.5 %collective-permute-start.2 = (bf16[256,512]{1,0:T(8,128)(2,1)S(1)}, bf16[256,512]{1,0:T(8,128)(2,1)S(1)}, u32[]{:S(2)}, u32[]{:S(2)}) collective-permute-start(bf16[256,512]{1,0:T(8,128)(2,1)S(1)} %get-tuple-element.63.va_ref), channel_id=1, source_target_pairs={{0,1},{1,0},{2,3},{3,2},{4,5},{5,4},{6,7},{7,6},{8,9},{9,8},{10,11... | collective-permute-start | bytes 786440 | tf_op jit(solution)/shard_map/ppermute | solution.py:435
  24.5 1.6 %collective-permute-start.9 = (bf16[256,512]{1,0:T(8,128)(2,1)S(1)}, bf16[256,512]{1,0:T(8,128)(2,1)S(1)}, u32[]{:S(2)}, u32[]{:S(2)}) collective-permute-start(bf16[256,512]{1,0:T(8,128)(2,1)S(1)} %get-tuple-element.85), channel_id=1, source_target_pairs={{0,1},{1,0},{2,3},{3,2},{4,5},{5,4},{6,7},{7,6},{8,9},{9,8},{10,11... | collective-permute-start | bytes 786440 | tf_op jit(solution)/shard_map/ppermute | solution.py:435
  25.3 9.3 %collective-permute-start.15 = (bf16[2048,256]{1,0:T(8,128)(2,1)S(1)}, bf16[2048,256]{1,0:T(8,128)(2,1)S(1)}, u32[]{:S(2)}, u32[]{:S(2)}) collective-permute-start(bf16[2048,256]{1,0:T(8,128)(2,1)S(1)} %get-tuple-element.109), channel_id=1, source_target_pairs={{0,1},{1,0},{2,3},{3,2},{4,5},{5,4},{6,7},{7,6},{8,9},{9,8},{10,11... | collective-permute-start | bytes 3145736 | tf_op jit(solution)/shard_map/ppermute | solution.py:435
  26.2 7.5 %collective-permute-start.13 = (bf16[160,512]{1,0:T(8,128)(2,1)S(1)}, bf16[160,512]{1,0:T(8,128)(2,1)S(1)}, u32[]{:S(2)}, u32[]{:S(2)}) collective-permute-start(bf16[160,512]{1,0:T(8,128)(2,1)S(1)} %get-tuple-element.96), channel_id=1, source_target_pairs={{0,2},{1,15},{2,0},{3,5},{4,6},{5,3},{6,4},{7,9},{8,10},{9,7},{10,... | collective-permute-start | bytes 491528 | tf_op jit(solution)/shard_map/ppermute | solution.py:540
  26.8 6.9 %collective-permute-start.10 = (bf16[32,512]{1,0:T(8,128)(2,1)S(1)}, bf16[32,512]{1,0:T(8,128)(2,1)S(1)}, u32[]{:S(2)}, u32[]{:S(2)}) collective-permute-start(bf16[32,512]{1,0:T(8,128)(2,1)S(1)} %get-tuple-element.93), channel_id=1, source_target_pairs={{0,12},{1,7},{2,14},{3,13},{4,8},{5,11},{6,10},{7,1},{8,4},{9,15},... | collective-permute-start | bytes 98312 | tf_op jit(solution)/shard_map/ppermute | solution.py:540
  28.7 5.0 %collective-permute-start.11 = (bf16[32,512]{1,0:T(8,128)(2,1)S(1)}, bf16[32,512]{1,0:T(8,128)(2,1)S(1)}, u32[]{:S(2)}, u32[]{:S(2)}) collective-permute-start(bf16[32,512]{1,0:T(8,128)(2,1)S(1)} %get-tuple-element.94), channel_id=1, source_target_pairs={{0,4},{1,5},{2,6},{3,7},{4,0},{5,1},{6,2},{7,3},{8,12},{9,13},{10,... | collective-permute-start | bytes 98312 | tf_op jit(solution)/shard_map/ppermute | solution.py:540
  28.7 5.0 %collective-permute-start.12 = (bf16[32,512]{1,0:T(8,128)(2,1)S(1)}, bf16[32,512]{1,0:T(8,128)(2,1)S(1)}, u32[]{:S(2)}, u32[]{:S(2)}) collective-permute-start(bf16[32,512]{1,0:T(8,128)(2,1)S(1)} %get-tuple-element.95), channel_id=1, source_target_pairs={{0,8},{1,11},{2,10},{3,9},{4,12},{5,15},{6,14},{7,13},{8,0},{9,3},... | collective-permute-start | bytes 98312 | tf_op jit(solution)/shard_map/ppermute | solution.py:540
  34.1 2.3 %collective-permute-start.14 = (bf16[640,512]{1,0:T(8,128)(2,1)S(1)}, bf16[640,512]{1,0:T(8,128)(2,1)S(1)}, u32[]{:S(2)}, u32[]{:S(2)}) collective-permute-start(bf16[640,512]{1,0:T(8,128)(2,1)S(1)} %get-tuple-element.105), channel_id=1, source_target_pairs={{0,1},{1,0},{2,3},{3,2},{4,5},{5,4},{6,7},{7,6},{8,9},{9,8},{10,11... | collective-permute-start | bytes 1966088 | tf_op jit(solution)/shard_map/ppermute | solution.py:435

commit v9 on v8

--- a/solution.py
+++ b/solution.py
@@ -234,12 +234,11 @@
 
 
 def edge_kernel(
-    live_ref,
     pre_ref,
     pre2_ref,
     latent_ref,
     send_ref,
-    recv_ref,
+    live_ref,
     mine_table,
     theirs_ref,
     wa_ref,
@@ -250,7 +249,6 @@
     out_other_ref,
     fresh_all,
     group_other_ref,
-    live_recv_ref,
     table,
     layout,
     block,
@@ -261,12 +259,11 @@
     feat = lax.axis_index("feat")
     table[: 2 * group, :] = mine_table[...]
     project(theirs_ref, wa_ref, wb_ref, table, 2 * group)
-    live_recv_ref[...] = live_ref[...]
     gain = gain_ref[...].astype(F32).reshape(1, width)
     for at in range(0, share, block):
         part = slice(at, at + block)
         some = slice(at // 128, (at + block) // 128)
-        receivers = live_recv_ref[some, :]
+        receivers = live_ref[some, :]
         columns = [index_columns(send_ref[some, :]), index_columns(receivers)]
         first = pre_ref.shape[0]
         pre = pre_ref[part, :] if at < first else pre2_ref[at - first : at - first + block, :]
@@ -285,7 +282,7 @@
         low, high = fresh[:, : width // 2], fresh[:, width // 2 :]
         out_other_ref[part, :] = jnp.where(feat == 0, high, low)
         fresh_all[part, :] = fresh
-    receivers = flat_row(live_recv_ref[...])
+    receivers = flat_row(live_ref[...])
     group_other_ref[...] = dot(one_hot_columns(receivers, layout.local_slots + group, group), fresh_all[...]).astype(BF16)
 
 
@@ -500,12 +497,12 @@
     )
     node_w1_b, node_w2_b = swap(n_w1), swap(n_w2)
 
-    other, fresh, group_other, live_recv = call(
+    other, fresh, group_other = call(
         functools.partial(edge_kernel, layout=layout, block=block),
-        (live, pre, pre2, latent, send, recv, projected, table_theirs, w1, edge_w1_b, w2, edge_w2_b, e_gain),
-        [VMEM_SPEC] * 13,
-        [shape(share, half), shape(share, width), shape(group, width), core_rows],
-        [VMEM_SPEC] * 4,
+        (pre, pre2, latent, send, live, projected, table_theirs, w1, edge_w1_b, w2, edge_w2_b, e_gain),
+        [VMEM_SPEC] * 12,
+        [shape(share, half), shape(share, width), shape(group, width)],
+        [VMEM_SPEC] * 3,
         2 * share * width * (width + 6 * group) + 4 * group * width * width,
         LIMIT,
         scratch=[pltpu.VMEM((4 * group, width), BF16)],
@@ -517,7 +514,7 @@
     group_theirs = swap(group_other)
     group_mine = call(
         functools.partial(group_sums_kernel, first=local_slots),
-        (fresh, live_recv),
+        (fresh, live),
         [VMEM_SPEC] * 2,
         shape(group, width, F32),
         VMEM_SPEC,
@@ -540,7 +537,7 @@
     back = [lax.ppermute(outgoing[i], both, pairs[i]) for i in reversed(range(len(pairs)))][::-1]
     local_sums, node_pre, edges = call(
         local_sums_kernel,
-        (fresh, live_recv, node, n_w1, node_w1_b),
+        (fresh, live, node, n_w1, node_w1_b),
         [VMEM_SPEC] * 5,
         [shape(node_count, width, F32), shape(node_count, width, F32), shape(edge_count, half)],
         [VMEM_SPEC] * 2 + [ANY_SPEC],

time: 38.5 us -> 38.6 us (level)
  no operation moved by 1% of the time
where the time goes in v9:
time: 38.6 us; the launch traced here: 38.4 us
  Pallas kernels  19.4 us (50%)
  starting transfers between devices  14.8 us (38%)
  waiting for transfers between devices  2.74 us (7%)
  between operations  1.46 us (4%)
    pallas_call x10, Pallas kernels, call(): pl.pallas_call(kernel, in_specs=in_specs, out_specs=out_specs, out_shape=...  19.4 us
    ppermute x4, starting transfers between devices, on_device(): lax.ppermute(lent[halo:] if i else lent, both, pairs[i])  6.98 us
    ppermute x4, starting transfers between devices, on_device(): lax.ppermute(outgoing[i], both, pairs[i])  5.02 us
    ppermute x8, starting transfers between devices, swap(): return lax.ppermute(values, 'feat', FEAT_SWAP)  2.79 us
    ppermute x4, waiting for transfers between devices, on_device(): lax.ppermute(lent[halo:] if i else lent, both, pairs[i])  1.68 us
    ppermute x8, waiting for transfers between devices, swap(): return lax.ppermute(values, 'feat', FEAT_SWAP)  1 us
  transfers between devices with their start and end apart: 16, of which 4 were waited for; matrix products, arithmetic and copies ran while one was open for 0% of the time, Pallas kernels for 45%

profile of v9, /device:TPU:0, one launch (start us, length us, event | category | flops | bytes accessed | tf_op | source)
XLA Modules:
  0.0 38.4 jit_solution(5604770717396239791)
XLA Ops:
  0.6 0.5 %collective-permute-start = (bf16[1536,256]{1,0:T(8,128)(2,1)}, bf16[1536,256]{1,0:T(8,128)(2,1)S(1)}, u32[]{:S(2)}, u32[]{:S(2)}) collective-permute-start(bf16[1536,256]{1,0:T(8,128)(2,1)} %refs_3_.2), channel_id=1, source_target_pairs={{0,1},{1,0},{2,3},{3,2},{4,5},{5,4},{6,7},{7,6},{8,9},{9,8},{10,11... | collective-permute-start | bytes 2359304 | tf_op jit(solution)/shard_map/ppermute | solution.py:432
  1.1 1.6 %shard_map.140 = (bf16[160,512]{1,0:T(8,128)(2,1)S(1)}, bf16[640,512]{1,0:T(8,128)(2,1)S(1)}, s32[2,128]{1,0:T(2,128)S(1)}, s32[32]{0:T(128)S(1)}, bf16[1536,256...) custom-call(bf16[640,512]{1,0:T(8,128)(2,1)} %refs_0_.2, ...), custom_call_target="tpu_custom_call" | custom-call | flops 104857600 | bytes 262144 | tf_op jit(solution)/shard_map/pallas_call | solution.py:360
  2.8 2.6 %collective-permute-start.3 = (bf16[160,512]{1,0:T(8,128)(2,1)S(1)}, bf16[160,512]{1,0:T(8,128)(2,1)S(1)}, u32[]{:S(2)}, u32[]{:S(2)}) collective-permute-start(bf16[160,512]{1,0:T(8,128)(2,1)S(1)} %get-tuple-element.64), channel_id=1, source_target_pairs={{0,2},{1,15},{2,0},{3,5},{4,6},{5,3},{6,4},{7,9},{8,10},{9,7},{10,... | collective-permute-start | bytes 491528 | tf_op jit(solution)/shard_map/ppermute | solution.py:464
  5.4 2.6 %collective-permute-start.4 = (bf16[32,512]{1,0:T(8,128)(2,1)S(1)}, bf16[32,512]{1,0:T(8,128)(2,1)S(1)}, u32[]{:S(2)}, u32[]{:S(2)}) collective-permute-start(bf16[32,512]{1,0:T(8,128)(2,1)S(1)} %slice.2), channel_id=1, source_target_pairs={{0,8},{1,11},{2,10},{3,9},{4,12},{5,15},{6,14},{7,13},{8,0},{9,3},... | collective-permute-start | bytes 98312 | tf_op jit(solution)/shard_map/ppermute | solution.py:464
  8.0 1.6 %collective-permute-start.5 = (bf16[32,512]{1,0:T(8,128)(2,1)S(1)}, bf16[32,512]{1,0:T(8,128)(2,1)S(1)}, u32[]{:S(2)}, u32[]{:S(2)}) collective-permute-start(bf16[32,512]{1,0:T(8,128)(2,1)S(1)} %slice.2), channel_id=1, source_target_pairs={{0,4},{1,5},{2,6},{3,7},{4,0},{5,1},{6,2},{7,3},{8,12},{9,13},{10,... | collective-permute-start | bytes 98312 | tf_op jit(solution)/shard_map/ppermute | solution.py:464
  9.6 0.2 collective-permute-start.6
  10.4 3.1 %shard_map.141 = (f32[1024,512]{1,0:T(8,128)S(1)}, bf16[2048,512]{1,0:T(8,128)(2,1)S(1)}, bf16[1280,512]{1,0:T(8,128)(2,1)S(1)}, s32[16,128]{1,0:T(8,128)S(1)}, ...) custom-call(s32[1,1]{1,0:T(1,128)} %bitcast.3.limit_ref, ...), custom_call_target="tpu_custom_call" | custom-call | flops 255013680 | bytes 262144 | tf_op jit(solution)/shard_map/pallas_call | solution.py:360
  13.6 0.0 collective-permute-done.4
  13.6 1.7 %collective-permute-done.6 = bf16[32,512]{1,0:T(8,128)(2,1)S(1)} collective-permute-done((bf16[32,512]{1,0:T(8,128)(2,1)S(1)}, bf16[32,512]{1,0:T(8,128)(2,1)S(1)}, u32[]{:S(2)}, u32[]{:S(2)}) %collective-permute-start.6) | collective-permute-done | bytes 32800 | tf_op jit(solution)/shard_map/ppermute | solution.py:464
  15.3 0.0 collective-permute-done.3
  15.3 0.1 collective-permute-start.7
  15.4 0.5 %collective-permute-start.8 = (bf16[256,512]{1,0:T(8,128)(2,1)S(1)}, bf16[256,512]{1,0:T(8,128)(2,1)S(1)}, u32[]{:S(2)}, u32[]{:S(2)}) collective-permute-start(bf16[256,512]{1,0:T(8,128)(2,1)S(1)} %get-tuple-element.75.va_ref), channel_id=1, source_target_pairs={{0,1},{1,0},{2,3},{3,2},{4,5},{5,4},{6,7},{7,6},{8,9},{9,8},{10,11... | collective-permute-start | bytes 786440 | tf_op jit(solution)/shard_map/ppermute | solution.py:432
  15.9 0.1 collective-permute-start.1
  16.0 0.4 %collective-permute-start.2 = (bf16[256,512]{1,0:T(8,128)(2,1)S(1)}, bf16[256,512]{1,0:T(8,128)(2,1)S(1)}, u32[]{:S(2)}, u32[]{:S(2)}) collective-permute-start(bf16[256,512]{1,0:T(8,128)(2,1)S(1)} %get-tuple-element.62.va_ref), channel_id=1, source_target_pairs={{0,1},{1,0},{2,3},{3,2},{4,5},{5,4},{6,7},{7,6},{8,9},{9,8},{10,11... | collective-permute-start | bytes 786440 | tf_op jit(solution)/shard_map/ppermute | solution.py:432
  16.4 2.4 %shard_map.142 = (f32[1024,512]{1,0:T(8,128)S(1)}, bf16[512,512]{1,0:T(8,128)(2,1)S(1)}) custom-call(bf16[2048,512]{1,0:T(8,128)(2,1)S(1)} %get-tuple-element.66.latent.latent_ref, s32[16,128]{1,0:T(8,128)S(1)} %get-tuple-element.58.send.send_ref, s32[16,128]{1,0:T(8,128)S(1)} %get-tuple-element.59.recv, bf16[1536,256]{1,0:T(8,128)(2,1)S(1)} %get-tuple-element.57.wa.wa_ref, ...), custom_call_target="tpu_custom_call" | custom-call | flops 2147483648 | bytes 262144 | tf_op jit(solution)/shard_map/pallas_call | solution.py:360
  18.8 5.7 %shard_map.143 = (bf16[2048,256]{1,0:T(8,128)(2,1)S(1)}, bf16[2048,512]{1,0:T(8,128)(2,1)S(1)}, bf16[256,512]{1,0:T(8,128)(2,1)S(1)}) custom-call(f32[1024,512]{1,0:T(8,128)S(1)} %get-tuple-element.65.pre_ref, f32[1024,512]{1,0:T(8,128)S(1)} %get-tuple-element.72.pre2_ref, bf16[2048,512]{1,0:T(8,128)(2,1)S(1)} %get-tuple-element.66.latent.latent_ref, ...), custom_call_target="tpu_custom_call" | custom-call | flops 4563402752 | bytes 262144 | tf_op jit(solution)/shard_map/pallas_call | solution.py:360
  24.5 0.1 collective-permute-start.9
  24.7 0.7 %shard_map.144.mine_ref = f32[256,512]{1,0:T(8,128)S(1)} custom-call(bf16[2048,512]{1,0:T(8,128)(2,1)S(1)} %get-tuple-element.88.fresh_ref, s32[16,128]{1,0:T(8,128)S(1)} %get-tuple-element.73.live_ref.recv_ref), custom_call_target="tpu_custom_call" | custom-call | flops 536870912 | bytes 262144 | tf_op jit(solution)/shard_map/pallas_call | solution.py:360
  25.4 0.5 %collective-permute-start.15 = (bf16[2048,256]{1,0:T(8,128)(2,1)S(1)}, bf16[2048,256]{1,0:T(8,128)(2,1)S(1)}, u32[]{:S(2)}, u32[]{:S(2)}) collective-permute-start(bf16[2048,256]{1,0:T(8,128)(2,1)S(1)} %get-tuple-element.107), channel_id=1, source_target_pairs={{0,1},{1,0},{2,3},{3,2},{4,5},{5,4},{6,7},{7,6},{8,9},{9,8},{10,11... | collective-permute-start | bytes 3145736 | tf_op jit(solution)/shard_map/ppermute | solution.py:432
  25.9 0.3 collective-permute-done.9.theirs_ref
  26.1 0.1 shard_map.145
  26.2 0.6 %collective-permute-start.13 = (bf16[160,512]{1,0:T(8,128)(2,1)S(1)}, bf16[160,512]{1,0:T(8,128)(2,1)S(1)}, u32[]{:S(2)}, u32[]{:S(2)}) collective-permute-start(bf16[160,512]{1,0:T(8,128)(2,1)S(1)} %get-tuple-element.94), channel_id=1, source_target_pairs={{0,2},{1,15},{2,0},{3,5},{4,6},{5,3},{6,4},{7,9},{8,10},{9,7},{10,... | collective-permute-start | bytes 491528 | tf_op jit(solution)/shard_map/ppermute | solution.py:537
  26.8 1.9 %collective-permute-start.10 = (bf16[32,512]{1,0:T(8,128)(2,1)S(1)}, bf16[32,512]{1,0:T(8,128)(2,1)S(1)}, u32[]{:S(2)}, u32[]{:S(2)}) collective-permute-start(bf16[32,512]{1,0:T(8,128)(2,1)S(1)} %get-tuple-element.91), channel_id=1, source_target_pairs={{0,12},{1,7},{2,14},{3,13},{4,8},{5,11},{6,10},{7,1},{8,4},{9,15},... | collective-permute-start | bytes 98312 | tf_op jit(solution)/shard_map/ppermute | solution.py:537
  28.7 0.0 collective-permute-start.11
  28.8 2.5 %collective-permute-start.12 = (bf16[32,512]{1,0:T(8,128)(2,1)S(1)}, bf16[32,512]{1,0:T(8,128)(2,1)S(1)}, u32[]{:S(2)}, u32[]{:S(2)}) collective-permute-start(bf16[32,512]{1,0:T(8,128)(2,1)S(1)} %get-tuple-element.93), channel_id=1, source_target_pairs={{0,8},{1,11},{2,10},{3,9},{4,12},{5,15},{6,14},{7,13},{8,0},{9,3},... | collective-permute-start | bytes 98312 | tf_op jit(solution)/shard_map/ppermute | solution.py:537
  31.2 2.5 %shard_map.146 = (f32[640,512]{1,0:T(8,128)S(1)}, f32[640,512]{1,0:T(8,128)S(1)}, bf16[4096,256]{1,0:T(8,128)(2,1)}) custom-call(bf16[2048,512]{1,0:T(8,128)(2,1)S(1)} %get-tuple-element.88.fresh_ref, s32[16,128]{1,0:T(8,128)S(1)} %get-tuple-element.73.live_ref.recv_ref, bf16[640,512]{1,0:T(8,128)(2,1)S(1)} %get-tuple-element.56.node.node_ref, ...), custom_call_target="tpu_custom_call" | custom-call | flops 134217728 | bytes 262144 | tf_op jit(solution)/shard_map/pallas_call | solution.py:360
  33.7 0.1 collective-permute-done.11.refs_2_
  33.8 0.4 shard_map.147
  34.1 0.6 %collective-permute-start.14 = (bf16[640,512]{1,0:T(8,128)(2,1)S(1)}, bf16[640,512]{1,0:T(8,128)(2,1)S(1)}, u32[]{:S(2)}, u32[]{:S(2)}) collective-permute-start(bf16[640,512]{1,0:T(8,128)(2,1)S(1)} %get-tuple-element.103), channel_id=1, source_target_pairs={{0,1},{1,0},{2,3},{3,2},{4,5},{5,4},{6,7},{7,6},{8,9},{9,8},{10,11... | collective-permute-start | bytes 1966088 | tf_op jit(solution)/shard_map/ppermute | solution.py:432
  34.7 1.0 %shard_map.149 = bf16[4096,256]{1,0:T(8,128)(2,1)} custom-call(bf16[2048,256]{1,0:T(8,128)(2,1)S(1)} %collective-permute-done.15.theirs_ref, bf16[4096,256]{1,0:T(8,128)(2,1)} %get-tuple-element.109.edges_in_ref), custom_call_target="tpu_custom_call", output_to_operand_aliasing={{}: (1, {})} | custom-call | flops 335544320 | bytes 262144 | tf_op jit(solution)/shard_map/pallas_call | solution.py:360
  35.7 0.7 %collective-permute-done.14.partner_ref = bf16[640,512]{1,0:T(8,128)(2,1)S(1)} collective-permute-done((bf16[640,512]{1,0:T(8,128)(2,1)S(1)}, bf16[640,512]{1,0:T(8,128)(2,1)S(1)}, u32[]{:S(2)}, u32[]{:S(2)}) %collective-permute-start.14) | collective-permute-done | bytes 655392 | tf_op jit(solution)/shard_map/ppermute | solution.py:432
  36.4 2.0 %shard_map.148 = bf16[640,256]{1,0:T(8,128)(2,1)} custom-call(bf16[640,512]{1,0:T(8,128)(2,1)S(1)} %get-tuple-element.56.node.node_ref, f32[640,512]{1,0:T(8,128)S(1)} %get-tuple-element.102.own_ref, bf16[640,512]{1,0:T(8,128)(2,1)S(1)} %collective-permute-done.14.partner_ref, f32[640,512]{1,0:T(8,128)S(1)} %get-tuple-element.104.pre_ref, ...), custom_call_target="tpu_custom_call" | custom-call | flops 671088640 | bytes 262144 | tf_op jit(solution)/shard_map/pallas_call | solution.py:360
  (15 shorter events, 0.1 us)
Async XLA Ops:
  0.6 9.8 %collective-permute-start = (bf16[1536,256]{1,0:T(8,128)(2,1)}, bf16[1536,256]{1,0:T(8,128)(2,1)S(1)}, u32[]{:S(2)}, u32[]{:S(2)}) collective-permute-start(bf16[1536,256]{1,0:T(8,128)(2,1)} %refs_3_.2), channel_id=1, source_target_pairs={{0,1},{1,0},{2,3},{3,2},{4,5},{5,4},{6,7},{7,6},{8,9},{9,8},{10,11... | collective-permute-start | bytes 2359304 | tf_op jit(solution)/shard_map/ppermute | solution.py:432
  2.8 12.5 %collective-permute-start.3 = (bf16[160,512]{1,0:T(8,128)(2,1)S(1)}, bf16[160,512]{1,0:T(8,128)(2,1)S(1)}, u32[]{:S(2)}, u32[]{:S(2)}) collective-permute-start(bf16[160,512]{1,0:T(8,128)(2,1)S(1)} %get-tuple-element.64), channel_id=1, source_target_pairs={{0,2},{1,15},{2,0},{3,5},{4,6},{5,3},{6,4},{7,9},{8,10},{9,7},{10,... | collective-permute-start | bytes 491528 | tf_op jit(solution)/shard_map/ppermute | solution.py:464
  5.4 8.2 %collective-permute-start.4 = (bf16[32,512]{1,0:T(8,128)(2,1)S(1)}, bf16[32,512]{1,0:T(8,128)(2,1)S(1)}, u32[]{:S(2)}, u32[]{:S(2)}) collective-permute-start(bf16[32,512]{1,0:T(8,128)(2,1)S(1)} %slice.2), channel_id=1, source_target_pairs={{0,8},{1,11},{2,10},{3,9},{4,12},{5,15},{6,14},{7,13},{8,0},{9,3},... | collective-permute-start | bytes 98312 | tf_op jit(solution)/shard_map/ppermute | solution.py:464
  8.0 5.6 %collective-permute-start.5 = (bf16[32,512]{1,0:T(8,128)(2,1)S(1)}, bf16[32,512]{1,0:T(8,128)(2,1)S(1)}, u32[]{:S(2)}, u32[]{:S(2)}) collective-permute-start(bf16[32,512]{1,0:T(8,128)(2,1)S(1)} %slice.2), channel_id=1, source_target_pairs={{0,4},{1,5},{2,6},{3,7},{4,0},{5,1},{6,2},{7,3},{8,12},{9,13},{10,... | collective-permute-start | bytes 98312 | tf_op jit(solution)/shard_map/ppermute | solution.py:464
  9.6 5.7 %collective-permute-start.6 = (bf16[32,512]{1,0:T(8,128)(2,1)S(1)}, bf16[32,512]{1,0:T(8,128)(2,1)S(1)}, u32[]{:S(2)}, u32[]{:S(2)}) collective-permute-start(bf16[32,512]{1,0:T(8,128)(2,1)S(1)} %slice.2), channel_id=1, source_target_pairs={{0,12},{1,7},{2,14},{3,13},{4,8},{5,11},{6,10},{7,1},{8,4},{9,15},... | collective-permute-start | bytes 98312 | tf_op jit(solution)/shard_map/ppermute | solution.py:464
  15.3 3.5 %collective-permute-start.7 = (bf16[256,512]{1,0:T(8,128)(2,1)S(1)}, bf16[256,512]{1,0:T(8,128)(2,1)S(1)}, u32[]{:S(2)}, u32[]{:S(2)}) collective-permute-start(bf16[256,512]{1,0:T(8,128)(2,1)S(1)} %constant_dynamic-update-slice_fusion.mine), channel_id=1, source_target_pairs={{0,1},{1,0},{2,3},{3,2},{4,5},{5,4},{6,7},{7,6},{8,9},{9,8},{10,11... | collective-permute-start | bytes 786440 | tf_op jit(solution)/shard_map/ppermute | solution.py:432
  15.4 3.4 %collective-permute-start.8 = (bf16[256,512]{1,0:T(8,128)(2,1)S(1)}, bf16[256,512]{1,0:T(8,128)(2,1)S(1)}, u32[]{:S(2)}, u32[]{:S(2)}) collective-permute-start(bf16[256,512]{1,0:T(8,128)(2,1)S(1)} %get-tuple-element.75.va_ref), channel_id=1, source_target_pairs={{0,1},{1,0},{2,3},{3,2},{4,5},{5,4},{6,7},{7,6},{8,9},{9,8},{10,11... | collective-permute-start | bytes 786440 | tf_op jit(solution)/shard_map/ppermute | solution.py:432
  15.9 8.6 %collective-permute-start.1 = (bf16[1024,256]{1,0:T(8,128)(2,1)S(1)}, bf16[1024,256]{1,0:T(8,128)(2,1)S(1)}, u32[]{:S(2)}, u32[]{:S(2)}) collective-permute-start(bf16[1024,256]{1,0:T(8,128)(2,1)S(1)} %get-tuple-element.61.wa_ref), channel_id=1, source_target_pairs={{0,1},{1,0},{2,3},{3,2},{4,5},{5,4},{6,7},{7,6},{8,9},{9,8},{10,11... | collective-permute-start | bytes 1572872 | tf_op jit(solution)/shard_map/ppermute | solution.py:432
  16.0 8.5 %collective-permute-start.2 = (bf16[256,512]{1,0:T(8,128)(2,1)S(1)}, bf16[256,512]{1,0:T(8,128)(2,1)S(1)}, u32[]{:S(2)}, u32[]{:S(2)}) collective-permute-start(bf16[256,512]{1,0:T(8,128)(2,1)S(1)} %get-tuple-element.62.va_ref), channel_id=1, source_target_pairs={{0,1},{1,0},{2,3},{3,2},{4,5},{5,4},{6,7},{7,6},{8,9},{9,8},{10,11... | collective-permute-start | bytes 786440 | tf_op jit(solution)/shard_map/ppermute | solution.py:432
  24.5 1.6 %collective-permute-start.9 = (bf16[256,512]{1,0:T(8,128)(2,1)S(1)}, bf16[256,512]{1,0:T(8,128)(2,1)S(1)}, u32[]{:S(2)}, u32[]{:S(2)}) collective-permute-start(bf16[256,512]{1,0:T(8,128)(2,1)S(1)} %get-tuple-element.83), channel_id=1, source_target_pairs={{0,1},{1,0},{2,3},{3,2},{4,5},{5,4},{6,7},{7,6},{8,9},{9,8},{10,11... | collective-permute-start | bytes 786440 | tf_op jit(solution)/shard_map/ppermute | solution.py:432
  25.4 9.3 %collective-permute-start.15 = (bf16[2048,256]{1,0:T(8,128)(2,1)S(1)}, bf16[2048,256]{1,0:T(8,128)(2,1)S(1)}, u32[]{:S(2)}, u32[]{:S(2)}) collective-permute-start(bf16[2048,256]{1,0:T(8,128)(2,1)S(1)} %get-tuple-element.107), channel_id=1, source_target_pairs={{0,1},{1,0},{2,3},{3,2},{4,5},{5,4},{6,7},{7,6},{8,9},{9,8},{10,11... | collective-permute-start | bytes 3145736 | tf_op jit(solution)/shard_map/ppermute | solution.py:432
  26.2 7.6 %collective-permute-start.13 = (bf16[160,512]{1,0:T(8,128)(2,1)S(1)}, bf16[160,512]{1,0:T(8,128)(2,1)S(1)}, u32[]{:S(2)}, u32[]{:S(2)}) collective-permute-start(bf16[160,512]{1,0:T(8,128)(2,1)S(1)} %get-tuple-element.94), channel_id=1, source_target_pairs={{0,2},{1,15},{2,0},{3,5},{4,6},{5,3},{6,4},{7,9},{8,10},{9,7},{10,... | collective-permute-start | bytes 491528 | tf_op jit(solution)/shard_map/ppermute | solution.py:537
  26.8 6.9 %collective-permute-start.10 = (bf16[32,512]{1,0:T(8,128)(2,1)S(1)}, bf16[32,512]{1,0:T(8,128)(2,1)S(1)}, u32[]{:S(2)}, u32[]{:S(2)}) collective-permute-start(bf16[32,512]{1,0:T(8,128)(2,1)S(1)} %get-tuple-element.91), channel_id=1, source_target_pairs={{0,12},{1,7},{2,14},{3,13},{4,8},{5,11},{6,10},{7,1},{8,4},{9,15},... | collective-permute-start | bytes 98312 | tf_op jit(solution)/shard_map/ppermute | solution.py:537
  28.7 5.0 %collective-permute-start.11 = (bf16[32,512]{1,0:T(8,128)(2,1)S(1)}, bf16[32,512]{1,0:T(8,128)(2,1)S(1)}, u32[]{:S(2)}, u32[]{:S(2)}) collective-permute-start(bf16[32,512]{1,0:T(8,128)(2,1)S(1)} %get-tuple-element.92), channel_id=1, source_target_pairs={{0,4},{1,5},{2,6},{3,7},{4,0},{5,1},{6,2},{7,3},{8,12},{9,13},{10,... | collective-permute-start | bytes 98312 | tf_op jit(solution)/shard_map/ppermute | solution.py:537
  28.8 5.0 %collective-permute-start.12 = (bf16[32,512]{1,0:T(8,128)(2,1)S(1)}, bf16[32,512]{1,0:T(8,128)(2,1)S(1)}, u32[]{:S(2)}, u32[]{:S(2)}) collective-permute-start(bf16[32,512]{1,0:T(8,128)(2,1)S(1)} %get-tuple-element.93), channel_id=1, source_target_pairs={{0,8},{1,11},{2,10},{3,9},{4,12},{5,15},{6,14},{7,13},{8,0},{9,3},... | collective-permute-start | bytes 98312 | tf_op jit(solution)/shard_map/ppermute | solution.py:537
  34.1 2.3 %collective-permute-start.14 = (bf16[640,512]{1,0:T(8,128)(2,1)S(1)}, bf16[640,512]{1,0:T(8,128)(2,1)S(1)}, u32[]{:S(2)}, u32[]{:S(2)}) collective-permute-start(bf16[640,512]{1,0:T(8,128)(2,1)S(1)} %get-tuple-element.103), channel_id=1, source_target_pairs={{0,1},{1,0},{2,3},{3,2},{4,5},{5,4},{6,7},{7,6},{8,9},{9,8},{10,11... | collective-permute-start | bytes 1966088 | tf_op jit(solution)/shard_map/ppermute | solution.py:432
